TPU v7x, 32 devices: a whole 2x2x4 slice. The times are simulated.
32 devices in a mesh: parts: 2 (over x), row: 16 (over z, y, core).
Axes of the slice: x: 2, y: 2, z: 4, core: 2. Of those that a mesh axis runs over, the one named last changes fastest.
Arguments:
- latent: bfloat16 [64, 256, 512], P(('parts', 'row')), parts along dimension 0, may hold values from -6 to 6
- conv_first: bfloat16 [3, 3, 512, 512], P(None, None, 'row'), may hold values from -0.09375 to 0.09375
- conv_second: bfloat16 [3, 3, 512, 512], P(None, None, 'row'), may hold values from -0.09375 to 0.09375
- w_query: bfloat16 [512, 512], replicated
- w_key: bfloat16 [512, 512], replicated
- w_value: bfloat16 [512, 512], replicated, may hold values from -0.25 to 0.25
- w_out: bfloat16 [512, 512], replicated, may hold values from -0.25 to 0.25
- w_in: bfloat16 [512, 2048], replicated, may hold values from -0.25 to 0.25
- w_down: bfloat16 [2048, 512], replicated, may hold values from -0.125 to 0.125
- conv_up: bfloat16 [3, 3, 512, 512], P(None, None, 'row'), may hold values from -0.09375 to 0.09375
Outputs:
- latent_out: bfloat16 [64, 256, 512], P(('parts', 'row')), parts along dimension 0
- upsampled: bfloat16 [64, 256, 512], P('parts', 'row'), parts along dimension 0
There are 2 independent parts, one for each index of `parts`. A program takes and returns all parts, laid end to end along the dimension named above; an argument that names none is the same for every part. Nothing has to cross between parts.
All inputs are finite; a program needn't handle non-finite values.
Results may differ from a plain program's by a relative error of at most 0.015.
Values may be sent and summed in bfloat16 or wider, within the bound.
No kernel may reach another device: no remote copies, remote signals or barrier semaphores. Data moves between devices by JAX's collectives and lax.ppermute only.
A program may use at most 128 MiB of HBM per device.

v0:
```python
import jax
import jax.numpy as jnp
from jax import lax
from jax.sharding import PartitionSpec as P

HD = 64
GRID = 16


def padded_2(value, sides, width):
    for axis, dim in sides:
        size, length = (lax.axis_size(axis), value.shape[dim])
        up = [(i, (i + 1) % size) for i in range(size - 1)]
        down = [(j, i) for i, j in up]
        last = lax.slice_in_dim(value, length - width, length, axis=dim)
        initial = lax.slice_in_dim(value, 0, width, axis=dim)
        before = lax.ppermute(last, axis, up)
        after = lax.ppermute(initial, axis, down)
        value = jnp.concatenate([before, value, after], axis=dim)
    return value


def rms_round(values):
    meansq = jnp.mean(values * values, axis=-1, keepdims=True)
    return (values * lax.rsqrt(meansq + 1e-06)).astype(jnp.bfloat16)


def softmax_round(scores):
    highest = jnp.max(scores, axis=-1, keepdims=True)
    lifted = jnp.exp(scores - highest)
    return (lifted / jnp.sum(lifted, axis=-1, keepdims=True)).astype(jnp.bfloat16)


def whole_kernel(kernel_piece):
    return lax.all_gather(kernel_piece, "row", axis=2, tiled=True)


def convolve(padded, kernel, out_rows, out_cols):
    tap_stack = jnp.stack(
        [
            padded[shift_row : shift_row + out_rows, shift_col : shift_col + out_cols]
            for shift_row in range(3)
            for shift_col in range(3)
        ],
        axis=2,
    )
    in_chans = tap_stack.shape[3]
    return jnp.dot(
        tap_stack.reshape(-1, 9 * in_chans),
        kernel.reshape(9 * in_chans, kernel.shape[3]),
        preferred_element_type=jnp.float32,
    )


def on_device(
    latent, conv_first, conv_second, w_query, w_key, w_value, w_out, w_in, w_down, conv_up
):
    devices = lax.axis_size("row")
    grid_rows, grid_cols, channels = latent.shape
    first_kernel, second_kernel, up_kernel = (conv_first, conv_second, conv_up)
    current = latent
    for kernel in (first_kernel, second_kernel):
        active = jax.nn.gelu(current.astype(jnp.float32)).astype(jnp.bfloat16)
        padded = padded_2(active, (("row", 0),), 1)
        padded = jnp.pad(padded, ((0, 0), (1, 1), (0, 0)))
        kernel = whole_kernel(kernel)
        mixing = convolve(padded, kernel, grid_rows, grid_cols)
        current = (
            current.astype(jnp.float32) + mixing.reshape(grid_rows, grid_cols, channels)
        ).astype(jnp.bfloat16)
    normed = rms_round(current.astype(jnp.float32)).reshape(-1, channels)
    send_shape = (grid_rows, GRID, devices, -1)
    queries = (
        jnp.dot(normed, w_query, preferred_element_type=jnp.float32)
        .astype(jnp.bfloat16)
        .reshape(send_shape)
    )
    keys_local = (
        jnp.dot(normed, w_key, preferred_element_type=jnp.float32)
        .astype(jnp.bfloat16)
        .reshape(send_shape)
    )
    values_local = (
        jnp.dot(normed, w_value, preferred_element_type=jnp.float32)
        .astype(jnp.bfloat16)
        .reshape(send_shape)
    )
    query_win, key_win, value_win = (
        lax.all_to_all(queries, "row", split_axis=2, concat_axis=0, tiled=True),
        lax.all_to_all(keys_local, "row", split_axis=2, concat_axis=0, tiled=True),
        lax.all_to_all(values_local, "row", split_axis=2, concat_axis=0, tiled=True),
    )
    all_rows = query_win.shape[0]
    band_rows = all_rows // GRID
    per_heads = query_win.shape[3] // HD
    window_shape = (GRID, band_rows, GRID, per_heads, HD)
    scores = jnp.einsum(
        "arbhd,erfhd->rhabef",
        query_win.reshape(window_shape),
        key_win.reshape(window_shape),
        preferred_element_type=jnp.float32,
    ) * HD ** (-0.5)
    scores = scores.reshape(band_rows, per_heads, GRID * GRID, GRID * GRID)
    probs = softmax_round(scores).reshape(band_rows, per_heads, GRID, GRID, GRID, GRID)
    attended = jnp.einsum(
        "rhabef,erfhd->arbhd",
        probs,
        value_win.reshape(window_shape),
        preferred_element_type=jnp.float32,
    )
    attended = attended.astype(jnp.bfloat16).reshape(all_rows, GRID, 1, -1)
    returned = lax.all_to_all(attended, "row", split_axis=0, concat_axis=2, tiled=True).reshape(
        -1, channels
    )
    projected = jnp.dot(returned, w_out, preferred_element_type=jnp.float32).reshape(
        grid_rows, grid_cols, channels
    )
    current = (current.astype(jnp.float32) + projected).astype(jnp.bfloat16)
    normed_two = rms_round(current.astype(jnp.float32)).reshape(-1, channels)
    hidden = jax.nn.gelu(jnp.dot(normed_two, w_in, preferred_element_type=jnp.float32)).astype(
        jnp.bfloat16
    )
    lowered = jnp.dot(hidden, w_down, preferred_element_type=jnp.float32).reshape(
        grid_rows, grid_cols, channels
    )
    latent_out = (current.astype(jnp.float32) + lowered).astype(jnp.bfloat16)
    central = latent_out[:, grid_cols // 4 : 3 * grid_cols // 4]
    central_cols = central.shape[1]
    slice_cols = central_cols // devices
    padded_central = jnp.pad(central, ((0, 0), (1, 1), (0, 0)))
    left_part = padded_central[:, :central_cols].reshape(grid_rows, devices, slice_cols, channels)
    first_extra = padded_central[:, slice_cols::slice_cols]
    second_extra = padded_central[:, slice_cols + 1 :: slice_cols]
    outgoing = jnp.concatenate(
        [left_part, first_extra[:, :, None], second_extra[:, :, None]], axis=2
    )
    arrived = lax.all_to_all(outgoing, "row", split_axis=1, concat_axis=0, tiled=True)
    total_rows = arrived.shape[0]
    framed = arrived[total_rows // 4 : 3 * total_rows // 4, 0]
    doubled = jnp.repeat(jnp.repeat(framed, 2, axis=0), 2, axis=1)[:, 1:-1]
    doubled = jnp.pad(doubled, ((1, 1), (0, 0), (0, 0)))
    out_cols = 2 * slice_cols
    up_kernel = whole_kernel(up_kernel)
    upsampled = (
        convolve(doubled, up_kernel, total_rows, out_cols)
        .reshape(total_rows, out_cols, channels)
        .astype(jnp.bfloat16)
    )
    return (latent_out, upsampled)


def solution(mesh):
    placed = (
        P(("parts", "row"), None, None),
        P(None, None, "row", None),
        P(None, None, "row", None),
        P(),
        P(),
        P(),
        P(),
        P(),
        P(),
        P(None, None, "row", None),
    )
    return jax.shard_map(
        on_device,
        mesh=mesh,
        in_specs=placed,
        out_specs=(P(("parts", "row"), None, None), P("parts", "row", None)),
        check_vma=False,
    )
```

profile of v0, /device:TPU:9, one launch (start us, length us, event | category | flops | bytes accessed | tf_op | source)
XLA Modules:
  0.0 310.4 jit_solution(8963559756864305286)
XLA Ops:
  8.7 1.4 fusion.28
  10.1 3.7 %collective-permute-start = (bf16[1,256,512]{2,1,0:T(8,128)(2,1)S(1)}, bf16[1,256,512]{2,1,0:T(8,128)(2,1)S(1)}, u32[]{:S(2)}, u32[]{:S(2)}) collective-permute-start(bf16[1,256,512]{2,1,0:T(8,128)(2,1)S(1)} %get-tuple-element.4), channel_id=1, source_target_pairs={{0,1},{1,2},{2,3},{3,4},{4,5},{5,6},{6,7},{7,8},{8,9},{9,10},{10,1... | collective-permute-start | bytes 786440 | tf_op jit(solution)/shard_map/ppermute | solution.py:17
  13.8 1.9 collective-permute-start.1
  15.8 1.4 collective-permute-done
  17.1 4.4 %collective-permute-done.1 = bf16[1,256,512]{2,1,0:T(8,128)(2,1)S(1)} collective-permute-done((bf16[1,256,512]{2,1,0:T(8,128)(2,1)S(1)}, bf16[1,256,512]{2,1,0:T(8,128)(2,1)S(1)}, u32[]{:S(2)}, u32[]{:S(2)}) %collective-permute-start.1) | collective-permute-done | bytes 262176 | tf_op jit(solution)/shard_map/ppermute | solution.py:18
  23.5 0.9 fusion.70
  25.3 1.2 bitcast_dynamic-update-slice_fusion.1
  29.0 0.9 fusion.64
  29.9 6.6 %copy.43 = bf16[2,256,9,512]{1,3,2,0:T(8,128)(2,1)} copy(bf16[2,256,9,512]{3,1,0,2:T(8,128)(2,1)} %fusion.64) | data formatting | bytes 9437184 | tf_op jit(solution)/shard_map/stack | solution.py:39
  36.6 28.6 %all-gather.4.cloned.1.call-done = bf16[3,3,512,512]{3,2,1,0:T(8,128)(2,1)} async-done(((bf16[3,3,32,512]{3,2,1,0:T(8,128)(2,1)}), bf16[3,3,512,512]{3,2,1,0:T(8,128)(2,1)}) %all-gather.4.cloned.1.call-update) | async-done | bytes 4718608 | tf_op jit(solution)/shard_map/all_gather | solution.py:35
  65.1 6.7 %fusion.34 = (bf16[2,256,512]{2,1,0:T(8,128)(2,1)S(1)}, bf16[2,256,512]{2,1,0:T(8,128)(2,1)S(1)}) fusion(bf16[2,256,4608]{1,2,0:T(8,128)(2,1)} %bitcast.203, bf16[4608,512,1]{1,0,2:T(8,128)(2,1)} %bitcast.219, bf16[2,256,512]{2,1,0:T(8,128)(2,1)S(1)} %copy-done.2), kind=kOutput, calls=%fused_computation.64 | convolution fusion | flops 2419326976 | bytes 11010048 | tf_op jit(solution)/shard_map/dot_general | solution.py:48
  71.8 2.3 collective-permute-start.2
  74.2 2.0 collective-permute-start.3
  76.2 4.8 %collective-permute-done.2 = bf16[1,256,512]{2,1,0:T(8,128)(2,1)S(1)} collective-permute-done((bf16[1,256,512]{2,1,0:T(8,128)(2,1)S(1)}, bf16[1,256,512]{2,1,0:T(8,128)(2,1)S(1)}, u32[]{:S(2)}, u32[]{:S(2)}) %collective-permute-start.2) | collective-permute-done | bytes 262176 | tf_op jit(solution)/shard_map/ppermute | solution.py:17
  81.0 4.1 %collective-permute-done.3 = bf16[1,256,512]{2,1,0:T(8,128)(2,1)S(1)} collective-permute-done((bf16[1,256,512]{2,1,0:T(8,128)(2,1)S(1)}, bf16[1,256,512]{2,1,0:T(8,128)(2,1)S(1)}, u32[]{:S(2)}, u32[]{:S(2)}) %collective-permute-start.3) | collective-permute-done | bytes 262176 | tf_op jit(solution)/shard_map/ppermute | solution.py:18
  88.8 1.2 bitcast_dynamic-update-slice_fusion
  89.9 0.9 fusion.58
  92.6 0.9 fusion.54
  93.5 6.7 %copy.45 = bf16[2,256,9,512]{1,3,2,0:T(8,128)(2,1)} copy(bf16[2,256,9,512]{3,1,0,2:T(8,128)(2,1)} %fusion.54) | data formatting | bytes 9437184 | tf_op jit(solution)/shard_map/stack | solution.py:39
  100.3 20.7 %all-gather.6.cloned.1.call-done = bf16[3,3,512,512]{3,2,1,0:T(8,128)(2,1)} async-done(((bf16[3,3,32,512]{3,2,1,0:T(8,128)(2,1)}), bf16[3,3,512,512]{3,2,1,0:T(8,128)(2,1)}) %all-gather.6.cloned.1.call-update) | async-done | bytes 4718608 | tf_op jit(solution)/shard_map/all_gather | solution.py:35
  120.9 6.5 %fusion.18 = (f32[2,256]{1,0:T(2,128)S(1)}, bf16[2,256,512]{2,1,0:T(8,128)(2,1)S(1)}) fusion(bf16[2,256,4608]{1,2,0:T(8,128)(2,1)} %bitcast.202, bf16[4608,512,1]{1,0,2:T(8,128)(2,1)} %bitcast.218, bf16[2,256,512]{2,1,0:T(8,128)(2,1)S(1)} %get-tuple-element.7), kind=kOutput, calls=%fused_computation.48 | convolution fusion | flops 2417491456 | bytes 10487808 | tf_op jit(solution)/shard_map/dot_general | solution.py:48
  128.3 1.1 copy.48
  129.4 3.8 %all-to-all-start.1 = ((bf16[2,16,16,512]{3,1,0,2:T(8,128)(2,1)}), bf16[2,16,16,512]{3,1,0,2:T(8,128)(2,1)S(1)}, u32[]{:S(2)}, u32[]{:S(2)}) async-start(bf16[2,16,16,512]{3,1,0,2:T(8,128)(2,1)} %copy.48), calls=%async_computation.1 | async-start | bytes 1048576 | tf_op jit(solution)/shard_map/all_to_all | solution.py:89
  133.1 1.5 convolution_convert_fusion.1
  134.6 1.1 copy.49
  135.7 11.6 %all-to-all-done.1 = bf16[2,16,16,512]{3,1,0,2:T(8,128)(2,1)S(1)} async-done(((bf16[2,16,16,512]{3,1,0,2:T(8,128)(2,1)}), bf16[2,16,16,512]{3,1,0,2:T(8,128)(2,1)S(1)}, u32[]{:S(2)}, u32[]{:S(2)}) %all-to-all-start.1) | async-done | bytes 524320 | tf_op jit(solution)/shard_map/all_to_all | solution.py:89
  147.3 4.4 %all-to-all-start.2 = ((bf16[2,16,16,512]{3,1,0,2:T(8,128)(2,1)}), bf16[2,16,16,512]{3,1,0,2:T(8,128)(2,1)}, u32[]{:S(2)}, u32[]{:S(2)}) async-start(bf16[2,16,16,512]{3,1,0,2:T(8,128)(2,1)} %copy.49), calls=%async_computation.2 | async-start | bytes 1048576 | tf_op jit(solution)/shard_map/all_to_all | solution.py:90
  151.8 1.5 convolution_convert_fusion.3
  153.2 1.1 copy.47
  154.4 11.7 %all-to-all-done.2 = bf16[2,16,16,512]{3,1,0,2:T(8,128)(2,1)} async-done(((bf16[2,16,16,512]{3,1,0,2:T(8,128)(2,1)}), bf16[2,16,16,512]{3,1,0,2:T(8,128)(2,1)}, u32[]{:S(2)}, u32[]{:S(2)}) %all-to-all-start.2) | async-done | bytes 524320 | tf_op jit(solution)/shard_map/all_to_all | solution.py:90
  166.0 4.4 %all-to-all-start = ((bf16[2,16,16,512]{3,1,0,2:T(8,128)(2,1)}), bf16[2,16,16,512]{3,1,0,2:T(8,128)(2,1)}, u32[]{:S(2)}, u32[]{:S(2)}) async-start(bf16[2,16,16,512]{3,1,0,2:T(8,128)(2,1)} %copy.47), calls=%async_computation | async-start | bytes 1048576 | tf_op jit(solution)/shard_map/all_to_all | solution.py:91
  171.2 1.6 reshape.110
  172.9 2.4 reshape.112
  175.3 9.5 %all-to-all-done = bf16[2,16,16,512]{3,1,0,2:T(8,128)(2,1)} async-done(((bf16[2,16,16,512]{3,1,0,2:T(8,128)(2,1)}), bf16[2,16,16,512]{3,1,0,2:T(8,128)(2,1)}, u32[]{:S(2)}, u32[]{:S(2)}) %all-to-all-start) | async-done | bytes 524320 | tf_op jit(solution)/shard_map/all_to_all | solution.py:91
  184.8 2.4 reshape.108
  187.2 14.4 %multiply_reduce_fusion = (f32[2,8,16,16]{3,2,1,0:T(8,128)S(1)}, f32[2,8,16,16,16,16]{3,5,4,2,1,0:T(8,128)}) fusion(bf16[16,2,16,8,64,1]{4,3,2,1,0,5:T(8,128)(2,1)} %bitcast.201, bf16[16,2,16,8,64,1]{4,3,2,1,0,5:T(8,128)(2,1)S(1)} %bitcast.200), kind=kOutput, calls=%fused_computation.2 | convolution fusion | flops 136310784 | bytes 5259264 | tf_op jit(solution)/shard_map/arbhd,erfhd->rhabef/dot_general | solution.py:97
  201.6 14.7 %fusion = f32[2,8,16,16]{3,2,1,0:T(8,128)S(1)} fusion(f32[2,8,16,16,16,16]{3,5,4,2,1,0:T(8,128)} %get-tuple-element.11, f32[2,8,16,16]{3,2,1,0:T(8,128)S(1)} %get-tuple-element.10), kind=kLoop, calls=%fused_computation.3 | loop fusion | flops 3141632 | bytes 4227072 | tf_op jit(solution)/shard_map/reduce_sum | solution.py:31
  216.3 15.3 %fusion.13 = bf16[16,2,16,8,64]{4,2,0,3,1:T(8,128)(2,1)} fusion(f32[2,8,16,16,16,16]{3,5,4,2,1,0:T(8,128)} %get-tuple-element.11, f32[2,8,16,16]{3,2,1,0:T(8,128)S(1)} %fusion, f32[2,8,16,16]{3,2,1,0:T(8,128)S(1)} %get-tuple-element.10, bf16[16,2,16,8,64,1]{4,3,2,1,0,5:T(8,128)(2,1)S(1)} %bitcast.210), kind=kOutput, calls=%fused_computation.35 | convolution fusion | flops 138674176 | bytes 5275648 | tf_op jit(solution)/shard_map/rhabef,erfhd->arbhd/dot_general | solution.py:105
  231.7 2.4 copy.54
  234.1 1.4 reshape.113
  235.5 18.5 %all_to_all.75 = bf16[32,16,1,512]{3,1,2,0:T(8,128)(2,1)S(1)} all-to-all(bf16[32,16,1,512]{3,1,2,0:T(8,128)(2,1)} %bitcast.206), channel_id=1, replica_groups=mesh['parts'=2,'row'=16] {'row'}, dimensions={0} | all-to-all | bytes 1048576 | tf_op jit(solution)/shard_map/all_to_all | solution.py:112
  254.3 1.7 fusion.20
  256.2 5.2 %fusion.11 = f32[512,512]{1,0:T(8,128)} fusion(bf16[2048,512]{1,0:T(8,128)(2,1)S(1)} %copy-done, bf16[512,512]{1,0:T(8,128)(2,1)S(1)} %bitcast.214, bf16[512,2048]{1,0:T(8,128)(2,1)} %param.17), kind=kOutput, calls=%fused_computation.28 | convolution fusion | flops 2156920832 | bytes 5767168 | tf_op jit(solution)/shard_map/dot_general | solution.py:123
  261.4 1.4 fusion.22
  264.0 14.3 %all_to_all.76 = bf16[2,16,10,512]{3,0,2,1:T(2,128)(2,1)S(1)} all-to-all(bf16[2,16,10,512]{3,0,2,1:T(2,128)(2,1)S(1)} %pad_maximum_fusion.4), channel_id=1, replica_groups=mesh['parts'=2,'row'=16] {'row'}, dimensions={1} | all-to-all | bytes 655360 | tf_op jit(solution)/shard_map/all_to_all | solution.py:137
  280.1 6.4 %copy.63 = bf16[32,16,9,512]{3,2,1,0:T(8,128)(2,1)} copy(bf16[32,16,9,512]{3,0,1,2:T(8,128)(2,1)S(1)} %fusion.50) | data formatting | bytes 9437184 | tf_op jit(solution)/shard_map/stack | solution.py:39
  286.5 10.2 %dot_general.54 = bf16[32,16,4608]{2,1,0:T(8,128)(2,1)} reshape(bf16[32,16,9,512]{3,2,1,0:T(8,128)(2,1)} %copy.63) | data formatting | bytes 9437184 | tf_op jit(solution)/shard_map/dot_general | solution.py:48
  296.7 7.2 %convolution_convert_fusion = bf16[32,16,512]{2,1,0:T(8,128)(2,1)} fusion(bf16[32,16,4608]{2,1,0:T(8,128)(2,1)} %dot_general.54, bf16[4608,512,1]{1,0,2:T(8,128)(2,1)} %bitcast.217), kind=kOutput, calls=%fused_computation.38 | convolution fusion | flops 2416181248 | bytes 9961472 | tf_op jit(solution)/shard_map/dot_general | solution.py:48
  (68 shorter events, 17.1 us)
Async XLA Ops:
  7.2 249.1 %copy-start = (bf16[2048,512]{1,0:T(8,128)(2,1)S(1)}, bf16[2048,512]{1,0:T(8,128)(2,1)}, u32[]{:S(2)}) copy-start(bf16[2048,512]{1,0:T(8,128)(2,1)} %param.18) | copy-start | bytes 6291460
  7.2 18.1 %copy-start.2 = (bf16[2,256,512]{2,1,0:T(8,128)(2,1)S(1)}, bf16[2,256,512]{2,1,0:T(8,128)(2,1)}, u32[]{:S(2)}) copy-start(bf16[2,256,512]{2,1,0:T(8,128)(2,1)} %param.10) | copy-start | bytes 1572868
  7.2 57.9 %all-gather.4.cloned.1.call-start = ((), (), s32[]{:S(2)}) async-start(), calls=%async_computation.5 | async-start | bytes 5013504 | tf_op jit(solution)/shard_map/all_gather | solution.py:35
  7.9 113.0 %all-gather.6.cloned.1.call-start = ((), (), s32[]{:S(2)}) async-start(), calls=%async_computation.6 | async-start | bytes 5013504 | tf_op jit(solution)/shard_map/all_gather | solution.py:35
  10.1 7.0 %collective-permute-start = (bf16[1,256,512]{2,1,0:T(8,128)(2,1)S(1)}, bf16[1,256,512]{2,1,0:T(8,128)(2,1)S(1)}, u32[]{:S(2)}, u32[]{:S(2)}) collective-permute-start(bf16[1,256,512]{2,1,0:T(8,128)(2,1)S(1)} %get-tuple-element.4), channel_id=1, source_target_pairs={{0,1},{1,2},{2,3},{3,4},{4,5},{5,6},{6,7},{7,8},{8,9},{9,10},{10,1... | collective-permute-start | bytes 786440 | tf_op jit(solution)/shard_map/ppermute | solution.py:17
  13.8 7.7 %collective-permute-start.1 = (bf16[1,256,512]{2,1,0:T(8,128)(2,1)S(1)}, bf16[1,256,512]{2,1,0:T(8,128)(2,1)S(1)}, u32[]{:S(2)}, u32[]{:S(2)}) collective-permute-start(bf16[1,256,512]{2,1,0:T(8,128)(2,1)S(1)} %get-tuple-element.5), channel_id=1, source_target_pairs={{1,0},{2,1},{3,2},{4,3},{5,4},{6,5},{7,6},{8,7},{9,8},{10,9},{11,1... | collective-permute-start | bytes 786440 | tf_op jit(solution)/shard_map/ppermute | solution.py:18
  71.8 9.2 %collective-permute-start.2 = (bf16[1,256,512]{2,1,0:T(8,128)(2,1)S(1)}, bf16[1,256,512]{2,1,0:T(8,128)(2,1)S(1)}, u32[]{:S(2)}, u32[]{:S(2)}) collective-permute-start(bf16[1,256,512]{2,1,0:T(8,128)(2,1)S(1)} %get-tuple-element.2), channel_id=1, source_target_pairs={{0,1},{1,2},{2,3},{3,4},{4,5},{5,6},{6,7},{7,8},{8,9},{9,10},{10,1... | collective-permute-start | bytes 786440 | tf_op jit(solution)/shard_map/ppermute | solution.py:17
  74.2 10.9 %collective-permute-start.3 = (bf16[1,256,512]{2,1,0:T(8,128)(2,1)S(1)}, bf16[1,256,512]{2,1,0:T(8,128)(2,1)S(1)}, u32[]{:S(2)}, u32[]{:S(2)}) collective-permute-start(bf16[1,256,512]{2,1,0:T(8,128)(2,1)S(1)} %get-tuple-element.3), channel_id=1, source_target_pairs={{1,0},{2,1},{3,2},{4,3},{5,4},{6,5},{7,6},{8,7},{9,8},{10,9},{11,1... | collective-permute-start | bytes 786440 | tf_op jit(solution)/shard_map/ppermute | solution.py:18
  120.9 6.7 %copy-start.5 = (bf16[512,512]{1,0:T(8,128)(2,1)S(1)}, bf16[512,512]{1,0:T(8,128)(2,1)}, u32[]{:S(2)}) copy-start(bf16[512,512]{1,0:T(8,128)(2,1)} %param.13) | copy-start | bytes 1572868
  127.5 0.8 copy-start.6
  129.4 18.0 %all-to-all-start.1 = ((bf16[2,16,16,512]{3,1,0,2:T(8,128)(2,1)}), bf16[2,16,16,512]{3,1,0,2:T(8,128)(2,1)S(1)}, u32[]{:S(2)}, u32[]{:S(2)}) async-start(bf16[2,16,16,512]{3,1,0,2:T(8,128)(2,1)} %copy.48), calls=%async_computation.1 | async-start | bytes 1048576 | tf_op jit(solution)/shard_map/all_to_all | solution.py:89
  147.3 23.9 %copy-start.1 = (bf16[2,16,16,512]{3,1,0,2:T(8,128)(2,1)}, bf16[2,16,16,512]{3,1,0,2:T(8,128)(2,1)S(1)}, u32[]{:S(2)}) copy-start(bf16[2,16,16,512]{3,1,0,2:T(8,128)(2,1)S(1)} %all-to-all-done.1) | copy-start | bytes 1572868
  147.3 18.7 %all-to-all-start.2 = ((bf16[2,16,16,512]{3,1,0,2:T(8,128)(2,1)}), bf16[2,16,16,512]{3,1,0,2:T(8,128)(2,1)}, u32[]{:S(2)}, u32[]{:S(2)}) async-start(bf16[2,16,16,512]{3,1,0,2:T(8,128)(2,1)} %copy.49), calls=%async_computation.2 | async-start | bytes 1048576 | tf_op jit(solution)/shard_map/all_to_all | solution.py:90
  166.0 18.7 %all-to-all-start = ((bf16[2,16,16,512]{3,1,0,2:T(8,128)(2,1)}), bf16[2,16,16,512]{3,1,0,2:T(8,128)(2,1)}, u32[]{:S(2)}, u32[]{:S(2)}) async-start(bf16[2,16,16,512]{3,1,0,2:T(8,128)(2,1)} %copy.47), calls=%async_computation | async-start | bytes 1048576 | tf_op jit(solution)/shard_map/all_to_all | solution.py:91
  170.5 126.2 %all-gather.8.cloned.1.call-start = ((), (), s32[]{:S(2)}) async-start(), calls=%async_computation.7 | async-start | bytes 5013504 | tf_op jit(solution)/shard_map/all_gather | solution.py:35
  201.6 14.7 %copy-start.4 = (bf16[16,2,16,8,64]{4,3,2,1,0:T(8,128)(2,1)S(1)}, bf16[16,2,16,8,64]{4,3,2,1,0:T(8,128)(2,1)}, u32[]{:S(2)}) copy-start(bf16[16,2,16,8,64]{4,3,2,1,0:T(8,128)(2,1)} %reshape.108) | copy-start | bytes 1572868
  262.8 16.5 %copy-start.3 = (bf16[2,256,512]{2,1,0:T(8,128)(2,1)}, bf16[2,256,512]{2,1,0:T(8,128)(2,1)S(1)}, u32[]{:S(2)}) copy-start(bf16[2,256,512]{2,1,0:T(8,128)(2,1)S(1)} %fusion.22) | copy-start | bytes 1572868
Sparse Core Ops, SparseCore 0:
  10.2 54.8 all-gather.3
  67.3 53.5 all-gather.5
  173.5 54.4 all-gather.7
where the time goes:
time: 314 us; the launch traced here: 310 us
  waiting for transfers between devices  98.5 us (31%)
  matrix products  60.5 us (19%)
  local copies, waits for them, and re-layouts  57 us (18%)
  blocking collectives  32.7 us (10%)
  other arithmetic  24.6 us (8%)
  starting transfers between devices  22.9 us (7%)
  between operations  14.1 us (4%)
    all_gather x3, waiting for transfers between devices, whole_kernel(): return lax.all_gather(kernel_piece, 'row', axis=2, tiled=True)  49.2 us
    another operation x6, local copies, waits for them, and re-layouts, convolve(): jnp.stack([padded[shift_row:shift_row + out_rows, shift_col:shift_col + o...  21.8 us
    dot_general x3, matrix products, convolve(): jnp.dot(tap_stack.reshape(-1, 9 * in_chans), kernel.reshape(9 * in_chans,...  20.4 us
    all_to_all x1, blocking collectives, on_device(): lax.all_to_all(attended, 'row', split_axis=0, concat_axis=2, tiled=True)  18.5 us
    dot_general x1, matrix products, on_device(): jnp.einsum('rhabef,erfhd->arbhd', probs, value_win.reshape(window_shape),...  15.3 us
    reduce_sum x1, other arithmetic, softmax_round(): jnp.sum(lifted, axis=-1, keepdims=True)  14.7 us
    dot_general x1, matrix products, on_device(): jnp.einsum('arbhd,erfhd->rhabef', query_win.reshape(window_shape), key_wi...  14.4 us
    all_to_all x1, blocking collectives, on_device(): lax.all_to_all(outgoing, 'row', split_axis=1, concat_axis=0, tiled=True)  14.3 us
  transfers between devices with their start and end apart: 10, of which 9 were waited for; matrix products, arithmetic and copies ran while one was open for 41% of the time, Pallas kernels for 0%

commit v1 on v0

v1 whole, which is shorter than its diff:
```python
import functools

import jax
import jax.numpy as jnp
from jax import lax
from jax.experimental import pallas as pl
from jax.experimental.pallas import tpu as pltpu
from jax.sharding import PartitionSpec as P

HD = 64
GRID = 16
F32, BF16 = jnp.float32, jnp.bfloat16
ANY = pl.BlockSpec(memory_space=pl.ANY)
VMEM = pl.BlockSpec(memory_space=pltpu.VMEM)
SMEM = pl.BlockSpec(memory_space=pltpu.SMEM)


def gelu(x):
    return jax.nn.gelu(x, approximate=True)


def params(mib):
    return pltpu.CompilerParams(vmem_limit_bytes=mib << 20)


def cost(flops, size, transcendentals=0):
    return pl.CostEstimate(
        flops=int(flops), bytes_accessed=int(size), transcendentals=int(transcendentals)
    )


def ring_of(chips):
    return list(range(0, chips, 2)) + list(range(1, chips, 2))[::-1]


def ring_positions(chips):
    steps = [0]
    for step in range(1, chips // 2 + 1):
        steps.append(-step)
        if step <= (chips - 1) // 2:
            steps.append(step)
    return steps


def gather_pieces(unit, flip):
    n = lax.axis_size("row")
    chips = n // 2
    ring = ring_of(chips)
    forward = [
        (2 * ring[i] + core, 2 * ring[(i + 1) % chips] + core)
        for i in range(chips)
        for core in (0, 1)
    ]
    backward = [(b, a) for a, b in forward]
    across = [(i, i ^ 1) for i in range(lax.axis_size("parts"))]
    turned = jnp.where(flip, unit[::-1], unit)
    own, rest = turned[:2], turned[2]
    pieces, up, down = [own], own, own
    for step in range(1, chips // 2 + 1):
        up = lax.ppermute(up, "row", forward)
        pieces.append(up)
        if step <= (chips - 1) // 2:
            down = lax.ppermute(down, "row", backward)
            pieces.append(down)
    others = pieces[1:]
    half = (len(others) + 1) // 2
    batches = [
        lax.ppermute(jnp.stack([piece[0] for piece in batch]), "parts", across)
        for batch in (others[:half], others[half:])
    ]
    return pieces + [rest] + batches


def start_copies(where, refs, target, sems):
    count = (len(refs) - 3) if len(refs) > 3 else 1
    pieces, rest, batches = refs[:count], refs[count], refs[count + 1 :]
    first = where[0]
    share = pieces[0].shape[2]
    jobs = []
    for index, piece in enumerate(pieces):
        rows = pl.ds(pl.multiple_of(where[1 + index] * share, share), share)
        jobs.append((piece.at[0], target.at[first, :, rows, :]))
        jobs.append((piece.at[1], target.at[1, :, rows, :]))
        if index == 0:
            jobs.append((rest, target.at[2 - first, :, rows, :]))
        else:
            place = index - 1
            batch = batches[0]
            if place >= batch.shape[0]:
                place -= batch.shape[0]
                batch = batches[1]
            jobs.append((batch.at[place], target.at[2 - first, :, rows, :]))
    copies = [
        pltpu.make_async_copy(source, dest, sems.at[i]) for i, (source, dest) in enumerate(jobs)
    ]
    for copy in copies:
        copy.start()
    return copies


def assemble_kernel(where, *refs):
    target, sems = refs[-2:]
    for copy in start_copies(where, refs[:-2], target, sems):
        copy.wait()


def assemble(where, pieces, chips):
    share, outs = pieces[0].shape[2:]
    shape = (3, 3, share * chips, outs)
    return pl.pallas_call(
        assemble_kernel,
        out_shape=jax.ShapeDtypeStruct(shape, BF16),
        in_specs=[SMEM] + [ANY] * len(pieces),
        out_specs=ANY,
        scratch_shapes=[pltpu.SemaphoreType.DMA((3 * chips,))],
        cost_estimate=cost(0, 4 * 9 * share * chips * outs),
        name="assemble",
    )(where, *pieces)


def conv_rows(lefts, weights, depths, row, rows, cols):
    total = []
    for b in range(3):
        part = None
        for a in range(3):
            for left, depth in zip(lefts, depths):
                block = left(row + a, rows).reshape(rows * cols, -1)
                term = jnp.dot(block, weights[a, b, depth, :], preferred_element_type=F32)
                part = term if part is None else part + term
        total.append(part)
    size = rows * cols
    col = lax.broadcasted_iota(jnp.int32, total[0].shape, 0) % cols
    left = jnp.where(col == 0, 0.0, pltpu.roll(total[0], 1, 0))
    right = jnp.where(col == cols - 1, 0.0, pltpu.roll(total[2], size - 1, 0))
    return left + total[1] + right


def first_conv_kernel(step, where, act, lat, *refs):
    pieces, (y_out, act_out, weights, sems) = refs[:-4], refs[-4:]
    copies = start_copies(where, pieces, weights, sems)
    core, top, bottom = where[where.shape[0] - 3], where[where.shape[0] - 2], where[where.shape[0] - 1]
    rows, cols, half = y_out.shape
    lanes = pl.ds(pl.multiple_of(core * half, half), half)
    for copy in copies:
        copy.wait()

    def body(i, carry):
        row = i * step
        mixed = conv_rows(
            [lambda r, k: act[pl.ds(r, k)]], weights, [slice(None)], row, step, cols
        ).reshape(step, cols, half)
        y = (lat[pl.ds(row + 1, step), :, lanes].astype(F32) + mixed).astype(BF16)
        y_out[pl.ds(row, step)] = y
        active = gelu(y.astype(F32))
        place = row + lax.broadcasted_iota(jnp.int32, active.shape, 0)
        active = jnp.where((place >= top) & (place < bottom), active, 0.0)
        act_out[pl.ds(row, step)] = active.astype(BF16)
        return carry

    lax.fori_loop(0, rows // step, body, 0)


def first_conv(where, act, lat, pieces, step):
    total_rows, cols, channels = act.shape
    rows, half, chips = total_rows - 2, channels // 2, channels // pieces[0].shape[2]
    out = jax.ShapeDtypeStruct((rows, cols, half), BF16)
    return pl.pallas_call(
        functools.partial(first_conv_kernel, step),
        out_shape=(out, out),
        in_specs=[SMEM, VMEM, VMEM] + [ANY] * len(pieces),
        out_specs=(VMEM, VMEM),
        scratch_shapes=[
            pltpu.VMEM((3, 3, channels, half), BF16),
            pltpu.SemaphoreType.DMA((3 * chips,)),
        ],
        compiler_params=params(40),
        cost_estimate=cost(
            18 * rows * cols * channels * half, 18 * channels * half, rows * cols * half
        ),
        name="first_conv",
    )(where, act, lat, *pieces)


def second_conv_kernel(step, where, y1, mine, theirs, *refs):
    pieces, (send, weights, sems, spread) = refs[:-4], refs[-4:]
    copies = start_copies(where, pieces, weights, sems)
    core = where[where.shape[0] - 3]
    groups, rows, _, half = send.shape
    cols = mine.shape[1]
    own = pl.ds(pl.multiple_of(core * half, half), half)
    other = pl.ds(pl.multiple_of((1 - core) * half, half), half)
    for copy in copies:
        copy.wait()
    lefts = [lambda r, k: mine[pl.ds(r, k)], lambda r, k: theirs[pl.ds(r, k)]]
    for row in range(0, rows, step):
        mixed = conv_rows(lefts, weights, [own, other], row, step, cols)
        before = y1[pl.ds(row + 1, step)].reshape(step * cols, half).astype(F32)
        rounded = (before + mixed).astype(BF16).astype(F32)
        for lane in range(0, half, 128):
            spread[...] = rounded[:, lane : lane + 128]
            for r in range(step):
                for c in range(groups):
                    send[c, row + r, :, lane : lane + 128] = spread[
                        pl.ds(r * cols + c, cols // groups, stride=groups), :
                    ].astype(BF16)


def second_conv(where, y1, mine, theirs, pieces, step):
    padded_rows, cols, half = y1.shape
    rows, channels = padded_rows - 2, 2 * half
    groups, chips = cols // GRID, channels // pieces[0].shape[2]
    return pl.pallas_call(
        functools.partial(second_conv_kernel, step),
        out_shape=jax.ShapeDtypeStruct((groups, rows, GRID, half), BF16),
        in_specs=[SMEM, VMEM, VMEM, VMEM] + [ANY] * len(pieces),
        out_specs=VMEM,
        scratch_shapes=[
            pltpu.VMEM((3, 3, channels, half), BF16),
            pltpu.SemaphoreType.DMA((3 * chips,)),
            pltpu.VMEM((step * cols, 128), F32),
        ],
        compiler_params=params(40),
        cost_estimate=cost(18 * rows * cols * channels * half, 18 * channels * half),
        name="second_conv",
    )(where, y1, mine, theirs, *pieces)


def rms_round(values):
    meansq = jnp.mean(values * values, axis=-1, keepdims=True)
    return (values * lax.rsqrt(meansq + 1e-06)).astype(BF16)


def window_kernel(picks, y2, w_query, w_key, w_value, w_out, w_in, w_down, out, edge, att, wide, thin):
    grid, per, _, channels = y2.shape
    cells = grid * GRID
    current = jnp.concatenate([y2[:, r].reshape(cells, channels) for r in range(per)], axis=0)
    current = current.astype(F32)
    normed = rms_round(current)
    dot = functools.partial(jnp.dot, preferred_element_type=F32)
    queries = (dot(normed, w_query[...]).astype(BF16) * BF16(HD**-0.5)).astype(BF16)
    keys = dot(normed, w_key[...]).astype(BF16)
    values = dot(normed, w_value[...]).astype(BF16)
    pair = 2 * HD
    low = lax.broadcasted_iota(jnp.int32, (cells, pair), 1) < HD
    zero = jnp.zeros((cells, pair), BF16)
    for r in range(per):
        for lane in range(0, channels, pair):
            spot = (slice(r * cells, (r + 1) * cells), slice(lane, lane + pair))
            query, key, value = queries[spot], keys[spot], values[spot]
            halves = []
            for keep in (jnp.where(low, query, zero), jnp.where(low, zero, query)):
                scores = lax.dot_general(
                    keep, key, (((1,), (1,)), ((), ())), preferred_element_type=F32
                )
                lifted = jnp.exp(scores - jnp.max(scores, axis=-1, keepdims=True))
                probs = lifted * (1.0 / jnp.sum(lifted, axis=-1, keepdims=True))
                halves.append(dot(probs.astype(BF16), value))
            att[spot] = jnp.where(low, halves[0], halves[1]).astype(BF16)
    current = (current + dot(att[...], w_out[...])).astype(BF16).astype(F32)
    normed = rms_round(current)
    units = w_in.shape[1]
    lowered = None
    for start in range(0, units, channels):
        span = slice(start, start + channels)
        hidden = gelu(dot(normed, w_in[:, span])).astype(BF16)
        term = dot(hidden, w_down[span, :])
        lowered = term if lowered is None else lowered + term
    latent = (current + lowered).astype(BF16)
    wide_values = latent.astype(F32)
    for r in range(per):
        out[:, r] = latent[r * cells : (r + 1) * cells].reshape(grid, GRID, channels)
    kept = grid // 2
    for lane in range(0, channels, 128):
        wide[...] = wide_values[:, lane : lane + 128]
        for d in range(edge.shape[0]):
            for r in range(per):
                first = r * cells + (grid // 4) * GRID + picks[d]
                thin[pl.ds(d * kept * per + r, kept, stride=per), :] = wide[
                    pl.ds(first, kept, stride=GRID), :
                ]
        edge[:, :, lane : lane + 128] = thin[...].astype(BF16).reshape(
            edge.shape[0], kept * per, 128
        )


def windows(picks, y2, w_query, w_key, w_value, w_out, w_in, w_down):
    grid, per, _, channels = y2.shape
    cells, units, dests = grid * GRID, w_in.shape[1], picks.shape[0]
    total = per * cells
    kept = per * grid // 2
    flops = 2 * total * channels * (4 * channels + 2 * units + 2 * cells)
    return pl.pallas_call(
        window_kernel,
        out_shape=(
            jax.ShapeDtypeStruct(y2.shape, BF16),
            jax.ShapeDtypeStruct((dests, kept, channels), BF16),
        ),
        in_specs=[SMEM] + [VMEM] * 7,
        out_specs=(VMEM, VMEM),
        scratch_shapes=[
            pltpu.VMEM((total, channels), BF16),
            pltpu.VMEM((total, 128), F32),
            pltpu.VMEM((dests * kept, 128), F32),
        ],
        compiler_params=params(40),
        cost_estimate=cost(flops, 8 * total * channels, total * (cells * 8 + units)),
        name="windows",
    )(picks, y2, w_query, w_key, w_value, w_out, w_in, w_down)


def upsample_kernel(info, arrived, mine, theirs, out, field, weights, spread, sems):
    taps, depth, half = mine.shape[0], mine.shape[2], mine.shape[3]
    core = info[0]
    copies = []
    for index, (source, side) in enumerate(((mine, core), (theirs, 1 - core))):
        lanes = pl.ds(pl.multiple_of(side * half, half), half)
        copies.append(pltpu.make_async_copy(source, weights.at[:, :, :, lanes], sems.at[index]))
    for copy in copies:
        copy.start()
    framed, rows, channels = field.shape
    width = framed - 2
    for j in range(framed):
        column = arrived[info[3 + j]]
        if j == 0:
            column = column * info[1].astype(F32).astype(BF16)
        if j == framed - 1:
            column = column * info[2].astype(F32).astype(BF16)
        field[j] = column
    for copy in copies:
        copy.wait()
    flat = field[...].reshape(framed * rows, channels)
    size = width * rows
    place = lax.broadcasted_iota(jnp.int32, (size, 128), 0) % rows
    out_cols = 2 * width
    for start in range(0, channels, 256):
        span = slice(start, start + 256)
        columns = []
        for a in range(3):
            p0, p1, p2 = [
                jnp.dot(flat, weights[a, b, :, span], preferred_element_type=F32)
                for b in range(3)
            ]
            middle = p1[rows : rows + size]
            columns.append(
                (
                    p0[:size] + middle + p2[rows : rows + size],
                    p0[rows : rows + size] + middle + p2[2 * rows : 2 * rows + size],
                )
            )
        for lane in range(0, 256, 128):
            for dj in range(2):
                c0, c1, c2 = [columns[a][dj][:, lane : lane + 128] for a in range(3)]
                above = jnp.where(place == 0, 0.0, pltpu.roll(c0, 1, 0))
                below = jnp.where(place == rows - 1, 0.0, pltpu.roll(c2, size - 1, 0))
                for di, value in enumerate((above + c1 + c2, c0 + c1 + below)):
                    for j in range(width):
                        first = di * out_cols + 2 * j + dj
                        spread[pl.ds(first, rows, stride=2 * out_cols), :] = value[
                            j * rows : (j + 1) * rows
                        ]
            out[:, :, start + lane : start + lane + 128] = (
                spread[...].astype(BF16).reshape(2 * rows, out_cols, 128)
            )


def upsample(info, arrived, mine, theirs, width):
    _, rows, channels = arrived.shape
    framed = width + 2
    return pl.pallas_call(
        upsample_kernel,
        out_shape=jax.ShapeDtypeStruct((2 * rows, 2 * width, channels), BF16),
        in_specs=[SMEM, VMEM, ANY, ANY],
        out_specs=VMEM,
        scratch_shapes=[
            pltpu.VMEM((framed, rows, channels), BF16),
            pltpu.VMEM((3, 3, channels, channels), BF16),
            pltpu.VMEM((4 * rows * width, 128), F32),
            pltpu.SemaphoreType.DMA((2,)),
        ],
        compiler_params=params(40),
        cost_estimate=cost(18 * framed * rows * channels * channels, 18 * channels * channels),
        name="upsample",
    )(info, arrived, mine, theirs)


def on_device(
    latent, conv_first, conv_second, w_query, w_key, w_value, w_out, w_in, w_down, conv_up
):
    n = lax.axis_size("row")
    chips = n // 2
    device = lax.axis_index("row")
    core, chip = device % 2, device // 2
    per, cols, channels = latent.shape
    half = channels // 2
    flip = lax.axis_index("parts") % 2 == 1
    swap = [(i, i ^ 1) for i in range(n)]

    shares = jnp.stack([conv_first, conv_second, conv_up])
    mine = lax.dynamic_slice_in_dim(shares, core * half, half, axis=4)
    given = lax.dynamic_slice_in_dim(shares, (1 - core) * half, half, axis=4)
    got = lax.ppermute(given, "row", swap)
    units = jnp.where(
        core == 0, jnp.concatenate([mine, got], axis=3), jnp.concatenate([got, mine], axis=3)
    )
    first_pieces, second_pieces, up_pieces = [gather_pieces(units[k], flip) for k in range(3)]
    ring = jnp.array(ring_of(chips), jnp.int32)
    position = jnp.argmax(ring == chip).astype(jnp.int32)
    steps = jnp.array(ring_positions(chips), jnp.int32)
    owners = ring[(position + steps) % chips]
    top = jnp.where(chip == 0, 1, 0)
    bottom = 2 * per + 2 - jnp.where(chip == chips - 1, 1, 0)
    where = jnp.concatenate(
        [jnp.where(flip, 2, 0)[None], owners, jnp.stack([core, top, bottom])]
    ).astype(jnp.int32)

    up = lax.ppermute(latent, "row", [(i, i + 1) for i in range(n - 1)])
    down = lax.ppermute(latent, "row", [(i + 1, i) for i in range(n - 1)])
    far = lax.ppermute(jnp.where(core == 0, up[-2:], down[:2]), "row", swap)
    field = jnp.where(
        core == 0,
        jnp.concatenate([up[-2:], latent, down, far], axis=0),
        jnp.concatenate([far, up, latent, down[:2]], axis=0),
    )
    active = gelu(field.astype(F32)).astype(BF16)

    y1, active2 = first_conv(where, active, field, first_pieces, 2)
    theirs = lax.ppermute(active2, "row", swap)
    y2 = second_conv(where, y1, active2, theirs, second_pieces, 2)

    groups = cols // GRID
    subs = n // groups
    index_groups = None
    if subs > 1:
        index_groups = [[k * subs + s for k in range(groups)] for s in range(subs)]
    kept = lax.dynamic_slice_in_dim(y2, core * per, per, axis=1)
    passed = lax.dynamic_slice_in_dim(y2, (1 - core) * per, per, axis=1)
    partner = lax.ppermute(passed, "row", swap)
    y2 = jnp.where(
        core == 0,
        jnp.concatenate([kept, partner], axis=3),
        jnp.concatenate([partner, kept], axis=3),
    )
    owned = lax.all_to_all(
        y2, "row", split_axis=0, concat_axis=0, axis_index_groups=index_groups, tiled=True
    )
    width = cols // 2 // n
    dests = jnp.arange(n, dtype=jnp.int32)
    starts = cols // 4 + width * dests - 1
    column = device // subs
    picks = jnp.clip((starts - column + groups - 1) // groups, 0, GRID - 1).astype(jnp.int32)
    latent_window, edge = windows(
        picks, owned, w_query, w_key, w_value, w_out, w_in, w_down
    )

    arrived = lax.all_to_all(edge, "row", split_axis=0, concat_axis=0, tiled=True)
    if subs > 1:
        arrived = arrived.reshape(groups, subs, GRID // 2, per, channels)
        arrived = arrived.transpose(0, 2, 1, 3, 4)
    arrived = arrived.reshape(groups, subs * per * GRID // 2, channels)
    returned = lax.all_to_all(
        latent_window,
        "row",
        split_axis=0,
        concat_axis=0,
        axis_index_groups=index_groups,
        tiled=True,
    )
    latent_out = returned.transpose(1, 2, 0, 3).reshape(per, cols, channels)

    up_mine = assemble(where, up_pieces, chips)
    up_theirs = lax.ppermute(up_mine, "row", swap)
    sources = (cols // 4 + width * device - 1 + jnp.arange(width + 2, dtype=jnp.int32)) % groups
    info = jnp.concatenate(
        [jnp.stack([core, (device > 0).astype(jnp.int32), (device < n - 1).astype(jnp.int32)]), sources]
    ).astype(jnp.int32)
    upsampled = upsample(info, arrived, up_mine, up_theirs, width)
    return (latent_out, upsampled)


def solution(mesh):
    placed = (
        P(("parts", "row"), None, None),
        P(None, None, "row", None),
        P(None, None, "row", None),
        P(),
        P(),
        P(),
        P(),
        P(),
        P(),
        P(None, None, "row", None),
    )
    return jax.shard_map(
        on_device,
        mesh=mesh,
        in_specs=placed,
        out_specs=(P(("parts", "row"), None, None), P("parts", "row", None)),
        check_vma=False,
    )
```

time: 314 us -> 241 us (0.77)
  Pallas kernels: 0 us -> 99.6 us
  matrix products: 60.5 us -> 0 us
  waiting for transfers between devices: 98.5 us -> 43.1 us
  local copies, waits for them, and re-layouts: 57 us -> 15.1 us
  starting transfers between devices: 22.9 us -> 55.7 us
  blocking collectives: 32.7 us -> 14.2 us
  other arithmetic: 24.6 us -> 9.86 us
  between operations: 14.1 us -> 1.14 us
    pallas_call x0 -> x5, Pallas kernels: none -> 99.6 us  [the longest x1 73.5 us: assemble(): pl.pallas_call(assemble_kernel, out_shape=jax.ShapeDtypeStruct(shape, BF1...]
    dot_general x10 -> x0, matrix products: 60.5 us -> none  [the longest x3 20.4 us: convolve(): jnp.dot(tap_stack.reshape(-1, 9 * in_chans), kernel.reshape(9 * in_chans,...]
    all_gather x3 -> x0, waiting for transfers between devices: 49.2 us -> none  [whole_kernel(): return lax.all_gather(kernel_piece, 'row', axis=2, tiled=True)]
    ppermute x4 -> x34, starting transfers between devices: 9.96 us -> 44.8 us  [the longest x12 21 us: gather_pieces(): up = lax.ppermute(up, 'row', forward)]
    all_to_all x3 -> x2, waiting for transfers between devices: 32.8 us -> 9.2 us  [the longest x1 9.2 us: on_device(): lax.all_to_all(latent_window, 'row', split_axis=0, concat_axis=0, axis_in...]
    another operation x6 -> x0, local copies, waits for them, and re-layouts: 21.8 us -> none  [convolve(): jnp.stack([padded[shift_row:shift_row + out_rows, shift_col:shift_col + o...]
    ppermute x4 -> x34, waiting for transfers between devices: 14.7 us -> 33.9 us  [the longest x6 17.4 us: gather_pieces(): lax.ppermute(jnp.stack([piece[0] for piece in batch]), 'parts', across)]
    all_to_all x2 -> x1, blocking collectives: 32.7 us -> 14.2 us  [on_device(): lax.all_to_all(edge, 'row', split_axis=0, concat_axis=0, tiled=True)]
  transfers between devices with their start and end apart: 10 -> 36, of which waited for: 9 -> 13; matrix products, arithmetic and copies ran while one was open for 41% -> 6% of each run, Pallas kernels for 0% -> 42%
where the time goes in v1:
time: 241 us; the launch traced here: 239 us
  Pallas kernels  99.6 us (41%)
  starting transfers between devices  55.7 us (23%)
  waiting for transfers between devices  43.1 us (18%)
  local copies, waits for them, and re-layouts  15.1 us (6%)
  blocking collectives  14.2 us (6%)
  other arithmetic  9.86 us (4%)
    pallas_call x1, Pallas kernels, assemble(): pl.pallas_call(assemble_kernel, out_shape=jax.ShapeDtypeStruct(shape, BF1...  73.5 us
    ppermute x12, starting transfers between devices, gather_pieces(): up = lax.ppermute(up, 'row', forward)  21 us
    ppermute x6, waiting for transfers between devices, gather_pieces(): lax.ppermute(jnp.stack([piece[0] for piece in batch]), 'parts', across)  17.4 us
    all_to_all x1, blocking collectives, on_device(): lax.all_to_all(edge, 'row', split_axis=0, concat_axis=0, tiled=True)  14.2 us
    ppermute x12, waiting for transfers between devices, gather_pieces(): up = lax.ppermute(up, 'row', forward)  11.1 us
    all_to_all x1, waiting for transfers between devices, on_device(): lax.all_to_all(latent_window, 'row', split_axis=0, concat_axis=0, axis_in...  9.2 us
    unnamed x46, local copies, waits for them, and re-layouts  8.2 us
    pallas_call x1, Pallas kernels, windows(): pl.pallas_call(window_kernel, out_shape=(jax.ShapeDtypeStruct(y2.shape, B...  8.09 us
  transfers between devices with their start and end apart: 36, of which 13 were waited for; matrix products, arithmetic and copies ran while one was open for 6% of the time, Pallas kernels for 42%

profile of v1, /device:TPU:9, one launch (start us, length us, event | category | flops | bytes accessed | tf_op | source)
XLA Modules:
  0.0 238.7 jit_solution(17047825531401625314)
XLA Ops:
  0.7 1.2 pad_maximum_fusion
  2.7 1.9 collective-permute-start.1
  4.7 3.6 %collective-permute-start = (bf16[2,256,512]{2,1,0:T(8,128)(2,1)}, bf16[2,256,512]{2,1,0:T(8,128)(2,1)S(1)}, u32[]{:S(2)}, u32[]{:S(2)}) collective-permute-start(bf16[2,256,512]{2,1,0:T(8,128)(2,1)} %param.12), channel_id=1, source_target_pairs={{0,1},{1,2},{2,3},{3,4},{4,5},{5,6},{6,7},{7,8},{8,9},{9,10},{10,1... | collective-permute-start | bytes 1572872 | tf_op jit(solution)/shard_map/ppermute | solution.py:416
  10.2 1.3 collective-permute-start.4
  12.5 4.5 %collective-permute-done.4.refs_1_ = bf16[2,3,64,256]{3,2,1,0:T(8,128)(2,1)S(1)} collective-permute-done((bf16[2,3,64,256]{3,2,1,0:T(8,128)(2,1)S(1)}, bf16[2,3,64,256]{3,2,1,0:T(8,128)(2,1)S(1)}, u32[]{:S(2)}, u32[]{:S(2)}) %collective-permute-start.4) | collective-permute-done | bytes 196640 | tf_op jit(solution)/shard_map/ppermute | solution.py:60
  17.0 1.3 collective-permute-start.6
  18.3 3.2 %collective-permute-start.14 = (bf16[2,3,64,256]{3,2,1,0:T(8,128)(2,1)S(1)}, bf16[2,3,64,256]{3,2,1,0:T(8,128)(2,1)S(1)}, u32[]{:S(2)}, u32[]{:S(2)}) collective-permute-start(bf16[2,3,64,256]{3,2,1,0:T(8,128)(2,1)S(1)} %slice.133.refs_0_), channel_id=1, source_target_pairs={{0,4},{1,5},{4,8},{5,9},{8,12},{9,13},{12,14},{13,15},{14,10},{15,... | collective-permute-start | bytes 589832 | tf_op jit(solution)/shard_map/ppermute | solution.py:60
  21.6 3.5 %collective-permute-start.7 = (bf16[2,3,64,256]{3,2,1,0:T(8,128)(2,1)S(1)}, bf16[2,3,64,256]{3,2,1,0:T(8,128)(2,1)S(1)}, u32[]{:S(2)}, u32[]{:S(2)}) collective-permute-start(bf16[2,3,64,256]{3,2,1,0:T(8,128)(2,1)S(1)} %collective-permute-done.5.refs_2_), channel_id=1, source_target_pairs={{4,0},{5,1},{8,4},{9,5},{12,8},{13,9},{14,12},{15,13},{10,14},{11,... | collective-permute-start | bytes 589832 | tf_op jit(solution)/shard_map/ppermute | solution.py:63
  28.9 1.4 collective-permute-start.16
  30.4 2.2 collective-permute-done.8.refs_5_
  32.7 1.4 collective-permute-start.10
  35.2 1.5 collective-permute-done.16.refs_3_
  36.7 1.2 collective-permute-start.11
  39.0 2.0 collective-permute-start.18
  41.1 1.3 collective-permute-start.12
  42.3 3.1 %fusion.5 = (bf16[8,256,512]{2,1,0:T(8,128)(2,1)S(1)}, bf16[8,256,512]{2,1,0:T(8,128)(2,1)S(1)}) fusion(bf16[2,256,512]{2,1,0:T(8,128)(2,1)S(1)} %collective-permute-done.1, bf16[2,256,512]{2,1,0:T(8,128)(2,1)} %param.12, bf16[2,256,512]{2,1,0:T(8,128)(2,1)S(1)} %collective-permute-done, bf16[2,256,512]{2,1,0:T(8,128)(2,1)} %collective-permute-done.2, ...), kind=kLoop, calls=%fused_computation.10 | loop fusion | flops 17825792 | bytes 6291457 | tf_op jit(solution)/shard_map/convert_element_type | solution.py:424
  46.5 6.3 %collective-permute-done.12.refs_10_ = bf16[3,3,64,256]{3,2,1,0:T(8,128)(2,1)S(1)} collective-permute-done((bf16[3,3,64,256]{3,2,1,0:T(8,128)(2,1)S(1)}, bf16[3,3,64,256]{3,2,1,0:T(8,128)(2,1)S(1)}, u32[]{:S(2)}, u32[]{:S(2)}) %collective-permute-start.12) | collective-permute-done | bytes 294944 | tf_op jit(solution)/shard_map/ppermute | solution.py:68
  52.8 7.6 %first_conv.1 = (bf16[6,256,256]{2,1,0:T(8,128)(2,1)S(1)}, bf16[6,256,256]{2,1,0:T(8,128)(2,1)}) custom-call(s32[12]{0:T(128)S(1)} %concatenate.24.where, bf16[8,256,512]{2,1,0:T(8,128)(2,1)S(1)} %get-tuple-element.12.act, bf16[8,256,512]{2,1,0:T(8,128)(2,1)S(1)} %get-tuple-element.13.lat, bf16[2,3,64,256]{3,2,1,0:T(8,128)(2,1)S(1)} %slice.123.refs_0_, ...), custom_call_target="tpu_custom_call" | custom-call | flops 3623878656 | bytes 2359296 | tf_op jit(solution)/shard_map/first_conv/pallas_call | solution.py:167
  60.4 1.8 collective-permute-start.13
  62.4 1.5 collective-permute-start.20
  64.6 2.2 collective-permute-start.24
  67.7 1.2 collective-permute-start.21
  69.7 1.2 collective-permute-start.22
  71.1 1.7 collective-permute-done.24.refs_1_
  72.8 1.9 collective-permute-start.26
  75.6 1.6 collective-permute-done.25.refs_2_
  77.2 1.1 collective-permute-done.26.refs_3_
  78.4 2.2 collective-permute-start.28
  80.6 3.7 %collective-permute-done.22.refs_10_ = bf16[3,3,64,256]{3,2,1,0:T(8,128)(2,1)S(1)} collective-permute-done((bf16[3,3,64,256]{3,2,1,0:T(8,128)(2,1)}, bf16[3,3,64,256]{3,2,1,0:T(8,128)(2,1)S(1)}, u32[]{:S(2)}, u32[]{:S(2)}) %collective-permute-start.22) | collective-permute-done | bytes 294944 | tf_op jit(solution)/shard_map/ppermute | solution.py:68
  84.3 1.1 copy-done.9
  85.4 5.6 %second_conv.1 = bf16[16,4,16,256]{3,2,1,0:T(8,128)(2,1)S(1)} custom-call(s32[12]{0:T(128)S(1)} %concatenate.24.where, bf16[6,256,256]{2,1,0:T(8,128)(2,1)S(1)} %copy-done.9, bf16[6,256,256]{2,1,0:T(8,128)(2,1)} %get-tuple-element.9.mine, bf16[6,256,256]{2,1,0:T(8,128)(2,1)S(1)} %collective-permute-done.13.theirs, ...), custom_call_target="tpu_custom_call" | custom-call | flops 2415919104 | bytes 2359296 | tf_op jit(solution)/shard_map/second_conv/pallas_call | solution.py:212
  91.0 1.6 collective-permute-start.23
  92.6 1.5 collective-permute-start.30
  95.1 1.3 collective-permute-start.31
  96.4 2.7 %collective-permute-done.29.refs_6_ = bf16[2,3,64,256]{3,2,1,0:T(8,128)(2,1)S(1)} collective-permute-done((bf16[2,3,64,256]{3,2,1,0:T(8,128)(2,1)S(1)}, bf16[2,3,64,256]{3,2,1,0:T(8,128)(2,1)S(1)}, u32[]{:S(2)}, u32[]{:S(2)}) %collective-permute-start.29) | collective-permute-done | bytes 196640 | tf_op jit(solution)/shard_map/ppermute | solution.py:63
  100.1 6.0 %all-to-all-start = ((bf16[16,2,16,512]{3,2,1,0:T(8,128)(2,1)}), bf16[16,2,16,512]{3,2,1,0:T(8,128)(2,1)S(1)}, u32[]{:S(2)}, u32[]{:S(2)}) async-start(bf16[16,2,16,512]{3,2,1,0:T(8,128)(2,1)} %maximum_select_fusion.2), calls=%async_computation | async-start | bytes 1048576 | tf_op jit(solution)/shard_map/all_to_all | solution.py:443
  106.2 1.3 collective-permute-start.32
  108.1 6.4 %collective-permute-done.32.refs_10_ = bf16[3,3,64,256]{3,2,1,0:T(8,128)(2,1)S(1)} collective-permute-done((bf16[3,3,64,256]{3,2,1,0:T(8,128)(2,1)S(1)}, bf16[3,3,64,256]{3,2,1,0:T(8,128)(2,1)S(1)}, u32[]{:S(2)}, u32[]{:S(2)}) %collective-permute-start.32) | collective-permute-done | bytes 294944 | tf_op jit(solution)/shard_map/ppermute | solution.py:68
  115.2 73.5 %assemble.1.mine = bf16[3,3,512,256]{3,2,1,0:T(8,128)(2,1)} custom-call(s32[12]{0:T(128)} %copy-done.1, bf16[2,3,64,256]{3,2,1,0:T(8,128)(2,1)} %slice.143.refs_0_, bf16[2,3,64,256]{3,2,1,0:T(8,128)(2,1)} %collective-permute-done.24.refs_1_, bf16[2,3,64,256]{3,2,1,0:T(8,128)(2,1)} %copy-done.14, bf16[2,3,64,256]{3,2,1,0:T(8,128)(2,1)} %copy-done.15, ...), custom_call_target="tpu_custom_call" | custom-call | bytes 4718592 | tf_op jit(solution)/shard_map/assemble/pallas_call | solution.py:110
  188.7 1.3 collective-permute-start.33
  190.0 1.6 copy-done.2
  191.6 1.6 copy-done.3
  196.3 8.1 %windows.1 = (bf16[16,2,16,512]{3,2,1,0:T(8,128)(2,1)}, bf16[16,16,512]{2,1,0:T(8,128)(2,1)S(1)}) custom-call(s32[16]{0:T(128)S(1)} %fusion.8.picks, bf16[16,2,16,512]{3,2,1,0:T(8,128)(2,1)S(1)} %all-to-all-done.y2, bf16[512,512]{1,0:T(8,128)(2,1)S(1)} %copy-done.4, bf16[512,512]{1,0:T(8,128)(2,1)S(1)} %copy-done.5, bf16[512,512]{1,0:T(8,128)(2,1)S(1)} %copy-done.6, ...), custom_call_target="tpu_custom_call" | custom-call | flops 3489660928 | bytes 2097152 | tf_op jit(solution)/shard_map/windows/pallas_call | solution.py:292
  204.4 14.2 %all_to_all.15.arrived = bf16[16,16,512]{2,1,0:T(8,128)(2,1)S(1)} all-to-all(bf16[16,16,512]{2,1,0:T(8,128)(2,1)S(1)} %get-tuple-element.11), channel_id=1, replica_groups=mesh['parts'=2,'row'=16] {'row'}, dimensions={0} | all-to-all | bytes 524288 | tf_op jit(solution)/shard_map/all_to_all | solution.py:455
  218.6 4.8 %all-to-all-start.1 = ((bf16[16,2,16,512]{3,2,1,0:T(8,128)(2,1)}), bf16[16,2,16,512]{3,2,1,0:T(8,128)(2,1)S(1)}, u32[]{:S(2)}, u32[]{:S(2)}) async-start(bf16[16,2,16,512]{3,2,1,0:T(8,128)(2,1)} %get-tuple-element.10), calls=%async_computation.1 | async-start | bytes 1048576 | tf_op jit(solution)/shard_map/all_to_all | solution.py:460
  223.6 4.9 %upsample.1 = bf16[32,16,512]{2,1,0:T(8,128)(2,1)} custom-call(s32[13]{0:T(128)S(1)} %pad_add_fusion.info, bf16[16,16,512]{2,1,0:T(8,128)(2,1)S(1)} %all_to_all.15.arrived, bf16[3,3,512,256]{3,2,1,0:T(8,128)(2,1)S(1)} %copy-done, bf16[3,3,512,256]{3,2,1,0:T(8,128)(2,1)} %collective-permute-done.33.theirs), custom_call_target="tpu_custom_call" | custom-call | flops 754974720 | bytes 4718592 | tf_op jit(solution)/shard_map/upsample/pallas_call | solution.py:369
  228.4 9.2 %all-to-all-done.1 = bf16[16,2,16,512]{3,2,1,0:T(8,128)(2,1)S(1)} async-done(((bf16[16,2,16,512]{3,2,1,0:T(8,128)(2,1)}), bf16[16,2,16,512]{3,2,1,0:T(8,128)(2,1)S(1)}, u32[]{:S(2)}, u32[]{:S(2)}) %all-to-all-start.1) | async-done | bytes 524320 | tf_op jit(solution)/shard_map/all_to_all | solution.py:460
  237.6 1.1 copy.14
  (129 shorter events, 21.0 us)
Async XLA Ops:
  0.6 7.7 %copy-start.10 = (s32[8]{0:T(128)S(1)}, s32[8]{0:T(128)}, u32[]{:S(2)}) copy-start(s32[8]{0:T(128)} %constant.126.clone) | copy-start | bytes 100
  2.0 7.1 %collective-permute-start.3 = (bf16[3,3,3,32,256]{4,3,2,1,0:T(8,128)(2,1)S(1)}, bf16[3,3,3,32,256]{4,3,2,1,0:T(8,128)(2,1)S(1)}, u32[]{:S(2)}, u32[]{:S(2)}) collective-permute-start(bf16[3,3,3,32,256]{4,3,2,1,0:T(8,128)(2,1)S(1)} %get-tuple-element.18), channel_id=1, source_target_pairs={{0,1},{1,0},{2,3},{3,2},{4,5},{5,4},{6,7},{7,6},{8,9},{9,8},{10,11... | collective-permute-start | bytes 1327112 | tf_op jit(solution)/shard_map/ppermute | solution.py:401
  2.7 23.4 %collective-permute-start.1 = (bf16[2,256,512]{2,1,0:T(8,128)(2,1)}, bf16[2,256,512]{2,1,0:T(8,128)(2,1)S(1)}, u32[]{:S(2)}, u32[]{:S(2)}) collective-permute-start(bf16[2,256,512]{2,1,0:T(8,128)(2,1)} %param.12), channel_id=1, source_target_pairs={{1,0},{2,1},{3,2},{4,3},{5,4},{6,5},{7,6},{8,7},{9,8},{10,9},{11,1... | collective-permute-start | bytes 1572872 | tf_op jit(solution)/shard_map/ppermute | solution.py:417
  4.7 21.4 %collective-permute-start = (bf16[2,256,512]{2,1,0:T(8,128)(2,1)}, bf16[2,256,512]{2,1,0:T(8,128)(2,1)S(1)}, u32[]{:S(2)}, u32[]{:S(2)}) collective-permute-start(bf16[2,256,512]{2,1,0:T(8,128)(2,1)} %param.12), channel_id=1, source_target_pairs={{0,1},{1,2},{2,3},{3,4},{4,5},{5,6},{6,7},{7,8},{8,9},{9,10},{10,1... | collective-permute-start | bytes 1572872 | tf_op jit(solution)/shard_map/ppermute | solution.py:416
  10.2 8.1 %copy-start.13 = (bf16[3,3,64,256]{3,2,1,0:T(8,128)(2,1)}, bf16[3,3,64,256]{3,2,1,0:T(8,128)(2,1)S(1)}, u32[]{:S(2)}) copy-start(bf16[3,3,64,256]{3,2,1,0:T(8,128)(2,1)S(1)} %reverse_select_fusion.2) | copy-start | bytes 884740
  10.2 6.7 %collective-permute-start.4 = (bf16[2,3,64,256]{3,2,1,0:T(8,128)(2,1)S(1)}, bf16[2,3,64,256]{3,2,1,0:T(8,128)(2,1)S(1)}, u32[]{:S(2)}, u32[]{:S(2)}) collective-permute-start(bf16[2,3,64,256]{3,2,1,0:T(8,128)(2,1)S(1)} %slice.123.refs_0_), channel_id=1, source_target_pairs={{0,4},{1,5},{4,8},{5,9},{8,12},{9,13},{12,14},{13,15},{14,10},{15,... | collective-permute-start | bytes 589832 | tf_op jit(solution)/shard_map/ppermute | solution.py:60
  12.3 9.3 %collective-permute-start.5 = (bf16[2,3,64,256]{3,2,1,0:T(8,128)(2,1)S(1)}, bf16[2,3,64,256]{3,2,1,0:T(8,128)(2,1)S(1)}, u32[]{:S(2)}, u32[]{:S(2)}) collective-permute-start(bf16[2,3,64,256]{3,2,1,0:T(8,128)(2,1)S(1)} %slice.123.refs_0_), channel_id=1, source_target_pairs={{4,0},{5,1},{8,4},{9,5},{12,8},{13,9},{14,12},{15,13},{10,14},{11,... | collective-permute-start | bytes 589832 | tf_op jit(solution)/shard_map/ppermute | solution.py:63
  17.0 8.1 %collective-permute-start.6 = (bf16[2,3,64,256]{3,2,1,0:T(8,128)(2,1)S(1)}, bf16[2,3,64,256]{3,2,1,0:T(8,128)(2,1)S(1)}, u32[]{:S(2)}, u32[]{:S(2)}) collective-permute-start(bf16[2,3,64,256]{3,2,1,0:T(8,128)(2,1)S(1)} %collective-permute-done.4.refs_1_), channel_id=1, source_target_pairs={{0,4},{1,5},{4,8},{5,9},{8,12},{9,13},{12,14},{13,15},{14,10},{15,... | collective-permute-start | bytes 589832 | tf_op jit(solution)/shard_map/ppermute | solution.py:60
  18.3 9.9 %copy-start.12 = (bf16[3,3,64,256]{3,2,1,0:T(8,128)(2,1)}, bf16[3,3,64,256]{3,2,1,0:T(8,128)(2,1)S(1)}, u32[]{:S(2)}) copy-start(bf16[3,3,64,256]{3,2,1,0:T(8,128)(2,1)S(1)} %reverse_select_fusion.1) | copy-start | bytes 884740
  18.3 10.6 %collective-permute-start.14 = (bf16[2,3,64,256]{3,2,1,0:T(8,128)(2,1)S(1)}, bf16[2,3,64,256]{3,2,1,0:T(8,128)(2,1)S(1)}, u32[]{:S(2)}, u32[]{:S(2)}) collective-permute-start(bf16[2,3,64,256]{3,2,1,0:T(8,128)(2,1)S(1)} %slice.133.refs_0_), channel_id=1, source_target_pairs={{0,4},{1,5},{4,8},{5,9},{8,12},{9,13},{12,14},{13,15},{14,10},{15,... | collective-permute-start | bytes 589832 | tf_op jit(solution)/shard_map/ppermute | solution.py:60
  21.6 8.8 %collective-permute-start.7 = (bf16[2,3,64,256]{3,2,1,0:T(8,128)(2,1)S(1)}, bf16[2,3,64,256]{3,2,1,0:T(8,128)(2,1)S(1)}, u32[]{:S(2)}, u32[]{:S(2)}) collective-permute-start(bf16[2,3,64,256]{3,2,1,0:T(8,128)(2,1)S(1)} %collective-permute-done.5.refs_2_), channel_id=1, source_target_pairs={{4,0},{5,1},{8,4},{9,5},{12,8},{13,9},{14,12},{15,13},{10,14},{11,... | collective-permute-start | bytes 589832 | tf_op jit(solution)/shard_map/ppermute | solution.py:63
  25.1 7.6 %collective-permute-start.8 = (bf16[2,3,64,256]{3,2,1,0:T(8,128)(2,1)S(1)}, bf16[2,3,64,256]{3,2,1,0:T(8,128)(2,1)S(1)}, u32[]{:S(2)}, u32[]{:S(2)}) collective-permute-start(bf16[2,3,64,256]{3,2,1,0:T(8,128)(2,1)S(1)} %collective-permute-done.6.refs_3_), channel_id=1, source_target_pairs={{0,4},{1,5},{4,8},{5,9},{8,12},{9,13},{12,14},{13,15},{14,10},{15,... | collective-permute-start | bytes 589832 | tf_op jit(solution)/shard_map/ppermute | solution.py:60
  27.0 15.4 %collective-permute-start.2 = (bf16[2,256,512]{2,1,0:T(8,128)(2,1)}, bf16[2,256,512]{2,1,0:T(8,128)(2,1)}, u32[]{:S(2)}, u32[]{:S(2)}) collective-permute-start(bf16[2,256,512]{2,1,0:T(8,128)(2,1)} %broadcast_select_fusion), channel_id=1, source_target_pairs={{0,1},{1,0},{2,3},{3,2},{4,5},{5,4},{6,7},{7,6},{8,9},{9,8},{10,11... | collective-permute-start | bytes 1572872 | tf_op jit(solution)/shard_map/ppermute | solution.py:418
  28.3 55.9 %copy-start.1 = (s32[12]{0:T(128)}, s32[12]{0:T(128)S(1)}, u32[]{:S(2)}) copy-start(s32[12]{0:T(128)S(1)} %concatenate.24.where) | copy-start | bytes 148
  28.3 6.7 %collective-permute-start.15 = (bf16[2,3,64,256]{3,2,1,0:T(8,128)(2,1)S(1)}, bf16[2,3,64,256]{3,2,1,0:T(8,128)(2,1)S(1)}, u32[]{:S(2)}, u32[]{:S(2)}) collective-permute-start(bf16[2,3,64,256]{3,2,1,0:T(8,128)(2,1)S(1)} %slice.133.refs_0_), channel_id=1, source_target_pairs={{4,0},{5,1},{8,4},{9,5},{12,8},{13,9},{14,12},{15,13},{10,14},{11,... | collective-permute-start | bytes 589832 | tf_op jit(solution)/shard_map/ppermute | solution.py:63
  28.9 7.8 %collective-permute-start.16 = (bf16[2,3,64,256]{3,2,1,0:T(8,128)(2,1)S(1)}, bf16[2,3,64,256]{3,2,1,0:T(8,128)(2,1)S(1)}, u32[]{:S(2)}, u32[]{:S(2)}) collective-permute-start(bf16[2,3,64,256]{3,2,1,0:T(8,128)(2,1)S(1)} %collective-permute-done.14.refs_1_), channel_id=1, source_target_pairs={{0,4},{1,5},{4,8},{5,9},{8,12},{9,13},{12,14},{13,15},{14,10},{15,... | collective-permute-start | bytes 589832 | tf_op jit(solution)/shard_map/ppermute | solution.py:60
  30.3 8.7 %collective-permute-start.9 = (bf16[2,3,64,256]{3,2,1,0:T(8,128)(2,1)S(1)}, bf16[2,3,64,256]{3,2,1,0:T(8,128)(2,1)S(1)}, u32[]{:S(2)}, u32[]{:S(2)}) collective-permute-start(bf16[2,3,64,256]{3,2,1,0:T(8,128)(2,1)S(1)} %collective-permute-done.7.refs_4_), channel_id=1, source_target_pairs={{4,0},{5,1},{8,4},{9,5},{12,8},{13,9},{14,12},{15,13},{10,14},{11,... | collective-permute-start | bytes 589832 | tf_op jit(solution)/shard_map/ppermute | solution.py:63
  32.7 8.3 %collective-permute-start.10 = (bf16[2,3,64,256]{3,2,1,0:T(8,128)(2,1)S(1)}, bf16[2,3,64,256]{3,2,1,0:T(8,128)(2,1)S(1)}, u32[]{:S(2)}, u32[]{:S(2)}) collective-permute-start(bf16[2,3,64,256]{3,2,1,0:T(8,128)(2,1)S(1)} %collective-permute-done.8.refs_5_), channel_id=1, source_target_pairs={{0,4},{1,5},{4,8},{5,9},{8,12},{9,13},{12,14},{13,15},{14,10},{15,... | collective-permute-start | bytes 589832 | tf_op jit(solution)/shard_map/ppermute | solution.py:60
  35.0 27.3 %collective-permute-start.17 = (bf16[2,3,64,256]{3,2,1,0:T(8,128)(2,1)S(1)}, bf16[2,3,64,256]{3,2,1,0:T(8,128)(2,1)S(1)}, u32[]{:S(2)}, u32[]{:S(2)}) collective-permute-start(bf16[2,3,64,256]{3,2,1,0:T(8,128)(2,1)S(1)} %collective-permute-done.15.refs_2_), channel_id=1, source_target_pairs={{4,0},{5,1},{8,4},{9,5},{12,8},{13,9},{14,12},{15,13},{10,14},{11,... | collective-permute-start | bytes 589832 | tf_op jit(solution)/shard_map/ppermute | solution.py:63
  36.7 9.7 %collective-permute-start.11 = (bf16[4,3,64,256]{3,2,1,0:T(8,128)(2,1)S(1)}, bf16[4,3,64,256]{3,2,1,0:T(8,128)(2,1)S(1)}, u32[]{:S(2)}, u32[]{:S(2)}) collective-permute-start(bf16[4,3,64,256]{3,2,1,0:T(8,128)(2,1)S(1)} %pad_maximum_fusion.1), channel_id=1, source_target_pairs={{0,16},{16,0},{1,17},{17,1},{2,18},{18,2},{3,19},{19,3},{4,20},{20... | collective-permute-start | bytes 1179656 | tf_op jit(solution)/shard_map/ppermute | solution.py:68
  39.0 23.4 %collective-permute-start.18 = (bf16[2,3,64,256]{3,2,1,0:T(8,128)(2,1)S(1)}, bf16[2,3,64,256]{3,2,1,0:T(8,128)(2,1)S(1)}, u32[]{:S(2)}, u32[]{:S(2)}) collective-permute-start(bf16[2,3,64,256]{3,2,1,0:T(8,128)(2,1)S(1)} %collective-permute-done.16.refs_3_), channel_id=1, source_target_pairs={{0,4},{1,5},{4,8},{5,9},{8,12},{9,13},{12,14},{13,15},{14,10},{15,... | collective-permute-start | bytes 589832 | tf_op jit(solution)/shard_map/ppermute | solution.py:60
  41.1 11.7 %collective-permute-start.12 = (bf16[3,3,64,256]{3,2,1,0:T(8,128)(2,1)S(1)}, bf16[3,3,64,256]{3,2,1,0:T(8,128)(2,1)S(1)}, u32[]{:S(2)}, u32[]{:S(2)}) collective-permute-start(bf16[3,3,64,256]{3,2,1,0:T(8,128)(2,1)S(1)} %pad_maximum_fusion.4), channel_id=1, source_target_pairs={{0,16},{16,0},{1,17},{17,1},{2,18},{18,2},{3,19},{19,3},{4,20},{20... | collective-permute-start | bytes 884744 | tf_op jit(solution)/shard_map/ppermute | solution.py:68
  52.8 11.1 %copy-start.11 = (bf16[3,3,64,256]{3,2,1,0:T(8,128)(2,1)S(1)}, bf16[3,3,64,256]{3,2,1,0:T(8,128)(2,1)}, u32[]{:S(2)}) copy-start(bf16[3,3,64,256]{3,2,1,0:T(8,128)(2,1)} %get-tuple-element.14) | copy-start | bytes 884740
  60.4 8.5 %copy-start.8 = (bf16[6,256,256]{2,1,0:T(8,128)(2,1)}, bf16[6,256,256]{2,1,0:T(8,128)(2,1)S(1)}, u32[]{:S(2)}) copy-start(bf16[6,256,256]{2,1,0:T(8,128)(2,1)S(1)} %get-tuple-element.8.y1) | copy-start | bytes 2359300
  60.4 23.8 %collective-permute-start.13 = (bf16[6,256,256]{2,1,0:T(8,128)(2,1)}, bf16[6,256,256]{2,1,0:T(8,128)(2,1)S(1)}, u32[]{:S(2)}, u32[]{:S(2)}) collective-permute-start(bf16[6,256,256]{2,1,0:T(8,128)(2,1)} %get-tuple-element.9.mine), channel_id=1, source_target_pairs={{0,1},{1,0},{2,3},{3,2},{4,5},{5,4},{6,7},{7,6},{8,9},{9,8},{10,11... | collective-permute-start | bytes 2359304 | tf_op jit(solution)/shard_map/ppermute | solution.py:427
  62.3 6.7 %collective-permute-start.19 = (bf16[2,3,64,256]{3,2,1,0:T(8,128)(2,1)S(1)}, bf16[2,3,64,256]{3,2,1,0:T(8,128)(2,1)S(1)}, u32[]{:S(2)}, u32[]{:S(2)}) collective-permute-start(bf16[2,3,64,256]{3,2,1,0:T(8,128)(2,1)S(1)} %collective-permute-done.17.refs_4_), channel_id=1, source_target_pairs={{4,0},{5,1},{8,4},{9,5},{12,8},{13,9},{14,12},{15,13},{10,14},{11,... | collective-permute-start | bytes 589832 | tf_op jit(solution)/shard_map/ppermute | solution.py:63
  62.4 6.6 %collective-permute-start.20 = (bf16[2,3,64,256]{3,2,1,0:T(8,128)(2,1)S(1)}, bf16[2,3,64,256]{3,2,1,0:T(8,128)(2,1)S(1)}, u32[]{:S(2)}, u32[]{:S(2)}) collective-permute-start(bf16[2,3,64,256]{3,2,1,0:T(8,128)(2,1)S(1)} %collective-permute-done.18.refs_5_), channel_id=1, source_target_pairs={{0,4},{1,5},{4,8},{5,9},{8,12},{9,13},{12,14},{13,15},{14,10},{15,... | collective-permute-start | bytes 589832 | tf_op jit(solution)/shard_map/ppermute | solution.py:60
  64.6 8.2 %collective-permute-start.24 = (bf16[2,3,64,256]{3,2,1,0:T(8,128)(2,1)}, bf16[2,3,64,256]{3,2,1,0:T(8,128)(2,1)}, u32[]{:S(2)}, u32[]{:S(2)}) collective-permute-start(bf16[2,3,64,256]{3,2,1,0:T(8,128)(2,1)} %slice.143.refs_0_), channel_id=1, source_target_pairs={{0,4},{1,5},{4,8},{5,9},{8,12},{9,13},{12,14},{13,15},{14,10},{15,... | collective-permute-start | bytes 589832 | tf_op jit(solution)/shard_map/ppermute | solution.py:60
  67.7 12.9 %collective-permute-start.21 = (bf16[4,3,64,256]{3,2,1,0:T(8,128)(2,1)}, bf16[4,3,64,256]{3,2,1,0:T(8,128)(2,1)S(1)}, u32[]{:S(2)}, u32[]{:S(2)}) collective-permute-start(bf16[4,3,64,256]{3,2,1,0:T(8,128)(2,1)} %pad_maximum_fusion.2), channel_id=1, source_target_pairs={{0,16},{16,0},{1,17},{17,1},{2,18},{18,2},{3,19},{19,3},{4,20},{20... | collective-permute-start | bytes 1179656 | tf_op jit(solution)/shard_map/ppermute | solution.py:68
  69.7 14.5 %collective-permute-start.22 = (bf16[3,3,64,256]{3,2,1,0:T(8,128)(2,1)}, bf16[3,3,64,256]{3,2,1,0:T(8,128)(2,1)S(1)}, u32[]{:S(2)}, u32[]{:S(2)}) collective-permute-start(bf16[3,3,64,256]{3,2,1,0:T(8,128)(2,1)} %pad_maximum_fusion.5), channel_id=1, source_target_pairs={{0,16},{16,0},{1,17},{17,1},{2,18},{18,2},{3,19},{19,3},{4,20},{20... | collective-permute-start | bytes 884744 | tf_op jit(solution)/shard_map/ppermute | solution.py:68
  70.9 6.2 %collective-permute-start.25 = (bf16[2,3,64,256]{3,2,1,0:T(8,128)(2,1)}, bf16[2,3,64,256]{3,2,1,0:T(8,128)(2,1)S(1)}, u32[]{:S(2)}, u32[]{:S(2)}) collective-permute-start(bf16[2,3,64,256]{3,2,1,0:T(8,128)(2,1)} %slice.143.refs_0_), channel_id=1, source_target_pairs={{4,0},{5,1},{8,4},{9,5},{12,8},{13,9},{14,12},{15,13},{10,14},{11,... | collective-permute-start | bytes 589832 | tf_op jit(solution)/shard_map/ppermute | solution.py:63
  72.8 5.5 %collective-permute-start.26 = (bf16[2,3,64,256]{3,2,1,0:T(8,128)(2,1)}, bf16[2,3,64,256]{3,2,1,0:T(8,128)(2,1)S(1)}, u32[]{:S(2)}, u32[]{:S(2)}) collective-permute-start(bf16[2,3,64,256]{3,2,1,0:T(8,128)(2,1)} %collective-permute-done.24.refs_1_), channel_id=1, source_target_pairs={{0,4},{1,5},{4,8},{5,9},{8,12},{9,13},{12,14},{13,15},{14,10},{15,... | collective-permute-start | bytes 589832 | tf_op jit(solution)/shard_map/ppermute | solution.py:60
  77.2 16.9 %copy-start.14 = (bf16[2,3,64,256]{3,2,1,0:T(8,128)(2,1)}, bf16[2,3,64,256]{3,2,1,0:T(8,128)(2,1)S(1)}, u32[]{:S(2)}) copy-start(bf16[2,3,64,256]{3,2,1,0:T(8,128)(2,1)S(1)} %collective-permute-done.25.refs_2_) | copy-start | bytes 589828
  77.2 15.4 %collective-permute-start.27 = (bf16[2,3,64,256]{3,2,1,0:T(8,128)(2,1)S(1)}, bf16[2,3,64,256]{3,2,1,0:T(8,128)(2,1)S(1)}, u32[]{:S(2)}, u32[]{:S(2)}) collective-permute-start(bf16[2,3,64,256]{3,2,1,0:T(8,128)(2,1)S(1)} %collective-permute-done.25.refs_2_), channel_id=1, source_target_pairs={{4,0},{5,1},{8,4},{9,5},{12,8},{13,9},{14,12},{15,13},{10,14},{11,... | collective-permute-start | bytes 589832 | tf_op jit(solution)/shard_map/ppermute | solution.py:63
  78.3 16.6 %copy-start.15 = (bf16[2,3,64,256]{3,2,1,0:T(8,128)(2,1)}, bf16[2,3,64,256]{3,2,1,0:T(8,128)(2,1)S(1)}, u32[]{:S(2)}) copy-start(bf16[2,3,64,256]{3,2,1,0:T(8,128)(2,1)S(1)} %collective-permute-done.26.refs_3_) | copy-start | bytes 589828
  78.4 14.2 %collective-permute-start.28 = (bf16[2,3,64,256]{3,2,1,0:T(8,128)(2,1)S(1)}, bf16[2,3,64,256]{3,2,1,0:T(8,128)(2,1)S(1)}, u32[]{:S(2)}, u32[]{:S(2)}) collective-permute-start(bf16[2,3,64,256]{3,2,1,0:T(8,128)(2,1)S(1)} %collective-permute-done.26.refs_3_), channel_id=1, source_target_pairs={{0,4},{1,5},{4,8},{5,9},{8,12},{9,13},{12,14},{13,15},{14,10},{15,... | collective-permute-start | bytes 589832 | tf_op jit(solution)/shard_map/ppermute | solution.py:60
  91.0 8.1 %collective-permute-start.23 = (bf16[16,2,16,256]{3,2,1,0:T(8,128)(2,1)S(1)}, bf16[16,2,16,256]{3,2,1,0:T(8,128)(2,1)S(1)}, u32[]{:S(2)}, u32[]{:S(2)}) collective-permute-start(bf16[16,2,16,256]{3,2,1,0:T(8,128)(2,1)S(1)} %get-tuple-element.20), channel_id=1, source_target_pairs={{0,1},{1,0},{2,3},{3,2},{4,5},{5,4},{6,7},{7,6},{8,9},{9,8},{10,11... | collective-permute-start | bytes 786440 | tf_op jit(solution)/shard_map/ppermute | solution.py:437
  92.6 6.5 %collective-permute-start.29 = (bf16[2,3,64,256]{3,2,1,0:T(8,128)(2,1)S(1)}, bf16[2,3,64,256]{3,2,1,0:T(8,128)(2,1)S(1)}, u32[]{:S(2)}, u32[]{:S(2)}) collective-permute-start(bf16[2,3,64,256]{3,2,1,0:T(8,128)(2,1)S(1)} %collective-permute-done.27.refs_4_), channel_id=1, source_target_pairs={{4,0},{5,1},{8,4},{9,5},{12,8},{13,9},{14,12},{15,13},{10,14},{11,... | collective-permute-start | bytes 589832 | tf_op jit(solution)/shard_map/ppermute | solution.py:63
  92.6 6.5 %collective-permute-start.30 = (bf16[2,3,64,256]{3,2,1,0:T(8,128)(2,1)S(1)}, bf16[2,3,64,256]{3,2,1,0:T(8,128)(2,1)S(1)}, u32[]{:S(2)}, u32[]{:S(2)}) collective-permute-start(bf16[2,3,64,256]{3,2,1,0:T(8,128)(2,1)S(1)} %collective-permute-done.28.refs_5_), channel_id=1, source_target_pairs={{0,4},{1,5},{4,8},{5,9},{8,12},{9,13},{12,14},{13,15},{14,10},{15,... | collective-permute-start | bytes 589832 | tf_op jit(solution)/shard_map/ppermute | solution.py:60
  95.1 13.0 %collective-permute-start.31 = (bf16[4,3,64,256]{3,2,1,0:T(8,128)(2,1)S(1)}, bf16[4,3,64,256]{3,2,1,0:T(8,128)(2,1)S(1)}, u32[]{:S(2)}, u32[]{:S(2)}) collective-permute-start(bf16[4,3,64,256]{3,2,1,0:T(8,128)(2,1)S(1)} %pad_maximum_fusion.3), channel_id=1, source_target_pairs={{0,16},{16,0},{1,17},{17,1},{2,18},{18,2},{3,19},{19,3},{4,20},{20... | collective-permute-start | bytes 1179656 | tf_op jit(solution)/shard_map/ppermute | solution.py:68
  99.1 15.4 %copy-start.18 = (bf16[2,3,64,256]{3,2,1,0:T(8,128)(2,1)}, bf16[2,3,64,256]{3,2,1,0:T(8,128)(2,1)S(1)}, u32[]{:S(2)}) copy-start(bf16[2,3,64,256]{3,2,1,0:T(8,128)(2,1)S(1)} %collective-permute-done.29.refs_6_) | copy-start | bytes 589828
  99.1 15.4 %copy-start.19 = (bf16[2,3,64,256]{3,2,1,0:T(8,128)(2,1)}, bf16[2,3,64,256]{3,2,1,0:T(8,128)(2,1)S(1)}, u32[]{:S(2)}) copy-start(bf16[2,3,64,256]{3,2,1,0:T(8,128)(2,1)S(1)} %collective-permute-done.30.refs_7_) | copy-start | bytes 589828
  100.1 89.8 %all-to-all-start = ((bf16[16,2,16,512]{3,2,1,0:T(8,128)(2,1)}), bf16[16,2,16,512]{3,2,1,0:T(8,128)(2,1)S(1)}, u32[]{:S(2)}, u32[]{:S(2)}) async-start(bf16[16,2,16,512]{3,2,1,0:T(8,128)(2,1)} %maximum_select_fusion.2), calls=%async_computation | async-start | bytes 1048576 | tf_op jit(solution)/shard_map/all_to_all | solution.py:443
  106.2 8.3 %collective-permute-start.32 = (bf16[3,3,64,256]{3,2,1,0:T(8,128)(2,1)S(1)}, bf16[3,3,64,256]{3,2,1,0:T(8,128)(2,1)S(1)}, u32[]{:S(2)}, u32[]{:S(2)}) collective-permute-start(bf16[3,3,64,256]{3,2,1,0:T(8,128)(2,1)S(1)} %pad_maximum_fusion.6), channel_id=1, source_target_pairs={{0,16},{16,0},{1,17},{17,1},{2,18},{18,2},{3,19},{19,3},{4,20},{20... | collective-permute-start | bytes 884744 | tf_op jit(solution)/shard_map/ppermute | solution.py:68
  108.1 81.8 %copy-start.4 = (bf16[512,512]{1,0:T(8,128)(2,1)S(1)}, bf16[512,512]{1,0:T(8,128)(2,1)}, u32[]{:S(2)}) copy-start(bf16[512,512]{1,0:T(8,128)(2,1)} %w_query.1) | copy-start | bytes 1572868
  188.7 34.9 %collective-permute-start.33 = (bf16[3,3,512,256]{3,2,1,0:T(8,128)(2,1)}, bf16[3,3,512,256]{3,2,1,0:T(8,128)(2,1)}, u32[]{:S(2)}, u32[]{:S(2)}) collective-permute-start(bf16[3,3,512,256]{3,2,1,0:T(8,128)(2,1)} %assemble.1.mine), channel_id=1, source_target_pairs={{0,1},{1,0},{2,3},{3,2},{4,5},{5,4},{6,7},{7,6},{8,9},{9,8},{10,11... | collective-permute-start | bytes 7077896 | tf_op jit(solution)/shard_map/ppermute | solution.py:471
  196.3 27.3 %copy-start = (bf16[3,3,512,256]{3,2,1,0:T(8,128)(2,1)S(1)}, bf16[3,3,512,256]{3,2,1,0:T(8,128)(2,1)}, u32[]{:S(2)}) copy-start(bf16[3,3,512,256]{3,2,1,0:T(8,128)(2,1)} %assemble.1.mine) | copy-start | bytes 7077892
  218.6 19.0 %all-to-all-start.1 = ((bf16[16,2,16,512]{3,2,1,0:T(8,128)(2,1)}), bf16[16,2,16,512]{3,2,1,0:T(8,128)(2,1)S(1)}, u32[]{:S(2)}, u32[]{:S(2)}) async-start(bf16[16,2,16,512]{3,2,1,0:T(8,128)(2,1)} %get-tuple-element.10), calls=%async_computation.1 | async-start | bytes 1048576 | tf_op jit(solution)/shard_map/all_to_all | solution.py:460
  (11 other events, 26.0 us)

commit v2 on v1

--- a/solution.py
+++ b/solution.py
@@ -27,6 +27,10 @@
     return pl.CostEstimate(
         flops=int(flops), bytes_accessed=int(size), transcendentals=int(transcendentals)
     )
+
+
+def chip_at(position, chips):
+    return jnp.where(position < chips // 2, 2 * position, 2 * (chips - 1 - position) + 1)
 
 
 def ring_of(chips):
@@ -42,54 +46,68 @@
     return steps
 
 
-def gather_pieces(unit, flip):
-    n = lax.axis_size("row")
-    chips = n // 2
-    ring = ring_of(chips)
-    forward = [
-        (2 * ring[i] + core, 2 * ring[(i + 1) % chips] + core)
-        for i in range(chips)
-        for core in (0, 1)
-    ]
-    backward = [(b, a) for a, b in forward]
-    across = [(i, i ^ 1) for i in range(lax.axis_size("parts"))]
-    turned = jnp.where(flip, unit[::-1], unit)
-    own, rest = turned[:2], turned[2]
-    pieces, up, down = [own], own, own
-    for step in range(1, chips // 2 + 1):
-        up = lax.ppermute(up, "row", forward)
-        pieces.append(up)
-        if step <= (chips - 1) // 2:
-            down = lax.ppermute(down, "row", backward)
-            pieces.append(down)
-    others = pieces[1:]
-    half = (len(others) + 1) // 2
-    batches = [
-        lax.ppermute(jnp.stack([piece[0] for piece in batch]), "parts", across)
-        for batch in (others[:half], others[half:])
-    ]
-    return pieces + [rest] + batches
-
-
-def start_copies(where, refs, target, sems):
-    count = (len(refs) - 3) if len(refs) > 3 else 1
-    pieces, rest, batches = refs[:count], refs[count], refs[count + 1 :]
+class Gather:
+    def __init__(self, unit, flip):
+        turned = jnp.where(flip, unit[::-1], unit)
+        self.chips = lax.axis_size("row") // 2
+        self.up = self.down = turned[:2]
+        self.rest = turned[2]
+        self.pieces, self.finals, self.batches, self.sent = [self.up], [], [], 1
+
+    def after(self, value):
+        self.up, self.down, _ = lax.optimization_barrier((self.up, self.down, value))
+
+    def before(self, value):
+        held = (value, self.up, self.down, self.finals, self.batches[:-1])
+        return lax.optimization_barrier(held)[0]
+
+    def step(self, index):
+        ring = ring_of(self.chips)
+        forward = [
+            (2 * ring[i] + core, 2 * ring[(i + 1) % self.chips] + core)
+            for i in range(self.chips)
+            for core in (0, 1)
+        ]
+        backward = [(b, a) for a, b in forward]
+        across = [(i, i ^ 1) for i in range(lax.axis_size("parts"))]
+        if index == self.chips // 2:
+            ways = ((self.up, forward), (self.down, backward))
+            for kernel in range(self.up.shape[1]):
+                value, pairs = ways[kernel % 2]
+                self.finals.append(lax.ppermute(value[:, kernel : kernel + 1], "row", pairs))
+            batch = jnp.concatenate([piece[0] for piece in self.finals], axis=0)[None]
+            self.batches.append(lax.ppermute(batch, "parts", across))
+            return
+        self.up = lax.ppermute(self.up, "row", forward)
+        self.down = lax.ppermute(self.down, "row", backward)
+        self.pieces += [self.up, self.down]
+        count = len(self.pieces)
+        if count == self.chips - 1 or count - self.sent >= self.chips // 4:
+            batch = jnp.stack([piece[0] for piece in self.pieces[self.sent :]])
+            self.batches.append(lax.ppermute(batch, "parts", across))
+            self.sent = count
+
+    def result(self):
+        return self.pieces + self.finals + [self.rest] + self.batches
+
+
+def start_copies(where, refs, index, target, sems):
+    chips = target.shape[2] // refs[0].shape[3]
+    near, kernels = chips - 1, refs[0].shape[1]
+    finals, rest = refs[near : near + kernels], refs[near + kernels]
+    batches = refs[near + kernels + 1 :]
+    pieces = [piece.at[:, index] for piece in refs[:near]] + [finals[index].at[:, 0]]
+    thirds = [rest.at[index]]
+    for batch in batches:
+        thirds += [batch.at[i, index] for i in range(batch.shape[0])]
     first = where[0]
-    share = pieces[0].shape[2]
+    share = refs[0].shape[3]
     jobs = []
-    for index, piece in enumerate(pieces):
-        rows = pl.ds(pl.multiple_of(where[1 + index] * share, share), share)
+    for i, piece in enumerate(pieces):
+        rows = pl.ds(pl.multiple_of(where[1 + i] * share, share), share)
         jobs.append((piece.at[0], target.at[first, :, rows, :]))
         jobs.append((piece.at[1], target.at[1, :, rows, :]))
-        if index == 0:
-            jobs.append((rest, target.at[2 - first, :, rows, :]))
-        else:
-            place = index - 1
-            batch = batches[0]
-            if place >= batch.shape[0]:
-                place -= batch.shape[0]
-                batch = batches[1]
-            jobs.append((batch.at[place], target.at[2 - first, :, rows, :]))
+        jobs.append((thirds[i], target.at[2 - first, :, rows, :]))
     copies = [
         pltpu.make_async_copy(source, dest, sems.at[i]) for i, (source, dest) in enumerate(jobs)
     ]
@@ -100,19 +118,20 @@
 
 def assemble_kernel(where, *refs):
     target, sems = refs[-2:]
-    for copy in start_copies(where, refs[:-2], target, sems):
+    for copy in start_copies(where, refs[:-2], 0, target, sems):
         copy.wait()
 
 
 def assemble(where, pieces, chips):
-    share, outs = pieces[0].shape[2:]
+    share, outs = pieces[0].shape[3:]
     shape = (3, 3, share * chips, outs)
     return pl.pallas_call(
         assemble_kernel,
         out_shape=jax.ShapeDtypeStruct(shape, BF16),
         in_specs=[SMEM] + [ANY] * len(pieces),
-        out_specs=ANY,
+        out_specs=VMEM,
         scratch_shapes=[pltpu.SemaphoreType.DMA((3 * chips,))],
+        compiler_params=params(12),
         cost_estimate=cost(0, 4 * 9 * share * chips * outs),
         name="assemble",
     )(where, *pieces)
@@ -137,7 +156,7 @@
 
 def first_conv_kernel(step, where, act, lat, *refs):
     pieces, (y_out, act_out, weights, sems) = refs[:-4], refs[-4:]
-    copies = start_copies(where, pieces, weights, sems)
+    copies = start_copies(where, pieces, 0, weights, sems)
     core, top, bottom = where[where.shape[0] - 3], where[where.shape[0] - 2], where[where.shape[0] - 1]
     rows, cols, half = y_out.shape
     lanes = pl.ds(pl.multiple_of(core * half, half), half)
@@ -162,7 +181,7 @@
 
 def first_conv(where, act, lat, pieces, step):
     total_rows, cols, channels = act.shape
-    rows, half, chips = total_rows - 2, channels // 2, channels // pieces[0].shape[2]
+    rows, half, chips = total_rows - 2, channels // 2, channels // pieces[0].shape[3]
     out = jax.ShapeDtypeStruct((rows, cols, half), BF16)
     return pl.pallas_call(
         functools.partial(first_conv_kernel, step),
@@ -183,7 +202,7 @@
 
 def second_conv_kernel(step, where, y1, mine, theirs, *refs):
     pieces, (send, weights, sems, spread) = refs[:-4], refs[-4:]
-    copies = start_copies(where, pieces, weights, sems)
+    copies = start_copies(where, pieces, 1, weights, sems)
     core = where[where.shape[0] - 3]
     groups, rows, _, half = send.shape
     cols = mine.shape[1]
@@ -208,7 +227,7 @@
 def second_conv(where, y1, mine, theirs, pieces, step):
     padded_rows, cols, half = y1.shape
     rows, channels = padded_rows - 2, 2 * half
-    groups, chips = cols // GRID, channels // pieces[0].shape[2]
+    groups, chips = cols // GRID, channels // pieces[0].shape[3]
     return pl.pallas_call(
         functools.partial(second_conv_kernel, step),
         out_shape=jax.ShapeDtypeStruct((groups, rows, GRID, half), BF16),
@@ -230,13 +249,31 @@
     return (values * lax.rsqrt(meansq + 1e-06)).astype(BF16)
 
 
-def window_kernel(picks, y2, w_query, w_key, w_value, w_out, w_in, w_down, out, edge, att, wide, thin):
-    grid, per, _, channels = y2.shape
+def window_kernel(picks, y2, *refs):
+    sources, (out, edge), (att, wide, thin) = refs[:6], refs[6:8], refs[8:11]
+    weights, sems = refs[11:17], refs[17]
+    copies = [
+        pltpu.make_async_copy(source, dest, sems.at[i])
+        for i, (source, dest) in enumerate(zip(sources, weights))
+    ]
+    for copy in copies:
+        copy.start()
+    w_query, w_key, w_value, w_out, w_in, w_down = weights
+    grid, per, _, channels = out.shape
     cells = grid * GRID
-    current = jnp.concatenate([y2[:, r].reshape(cells, channels) for r in range(per)], axis=0)
-    current = current.astype(F32)
+    current = jnp.concatenate(
+        [
+            jnp.concatenate(
+                [y2[:, side, :, r].reshape(cells, -1) for side in range(y2.shape[1])], axis=1
+            )
+            for r in range(per)
+        ],
+        axis=0,
+    ).astype(F32)
     normed = rms_round(current)
     dot = functools.partial(jnp.dot, preferred_element_type=F32)
+    for copy in copies[:3]:
+        copy.wait()
     queries = (dot(normed, w_query[...]).astype(BF16) * BF16(HD**-0.5)).astype(BF16)
     keys = dot(normed, w_key[...]).astype(BF16)
     values = dot(normed, w_value[...]).astype(BF16)
@@ -256,6 +293,8 @@
                 probs = lifted * (1.0 / jnp.sum(lifted, axis=-1, keepdims=True))
                 halves.append(dot(probs.astype(BF16), value))
             att[spot] = jnp.where(low, halves[0], halves[1]).astype(BF16)
+    for copy in copies[3:]:
+        copy.wait()
     current = (current + dot(att[...], w_out[...])).astype(BF16).astype(F32)
     normed = rms_round(current)
     units = w_in.shape[1]
@@ -284,7 +323,7 @@
 
 
 def windows(picks, y2, w_query, w_key, w_value, w_out, w_in, w_down):
-    grid, per, _, channels = y2.shape
+    grid, per, channels = y2.shape[0] * y2.shape[2], y2.shape[3], w_query.shape[0]
     cells, units, dests = grid * GRID, w_in.shape[1], picks.shape[0]
     total = per * cells
     kept = per * grid // 2
@@ -292,17 +331,22 @@
     return pl.pallas_call(
         window_kernel,
         out_shape=(
-            jax.ShapeDtypeStruct(y2.shape, BF16),
+            jax.ShapeDtypeStruct((grid, per, GRID, channels), BF16),
             jax.ShapeDtypeStruct((dests, kept, channels), BF16),
         ),
-        in_specs=[SMEM] + [VMEM] * 7,
+        in_specs=[SMEM, VMEM] + [ANY] * 6,
         out_specs=(VMEM, VMEM),
         scratch_shapes=[
             pltpu.VMEM((total, channels), BF16),
             pltpu.VMEM((total, 128), F32),
             pltpu.VMEM((dests * kept, 128), F32),
-        ],
-        compiler_params=params(40),
+        ]
+        + [
+            pltpu.VMEM(weight.shape, BF16)
+            for weight in (w_query, w_key, w_value, w_out, w_in, w_down)
+        ]
+        + [pltpu.SemaphoreType.DMA((6,))],
+        compiler_params=params(56),
         cost_estimate=cost(flops, 8 * total * channels, total * (cells * 8 + units)),
         name="windows",
     )(picks, y2, w_query, w_key, w_value, w_out, w_in, w_down)
@@ -383,6 +427,30 @@
     )(info, arrived, mine, theirs)
 
 
+def settle_kernel(arrived, earlier, out, spread):
+    groups, per, cells, channels = arrived.shape
+    for r in range(per):
+        for lane in range(0, channels, 128):
+            for c in range(groups):
+                spread[pl.ds(c, cells, stride=groups), :] = arrived[
+                    c, r, :, lane : lane + 128
+                ].astype(F32)
+            out[r, :, lane : lane + 128] = spread[...].astype(BF16)
+
+
+def settle(arrived, earlier):
+    groups, per, cells, channels = arrived.shape
+    return pl.pallas_call(
+        settle_kernel,
+        out_shape=jax.ShapeDtypeStruct((per, groups * cells, channels), BF16),
+        in_specs=[VMEM, ANY],
+        out_specs=VMEM,
+        scratch_shapes=[pltpu.VMEM((groups * cells, 128), F32)],
+        compiler_params=params(8),
+        name="settle",
+    )(arrived, earlier)
+
+
 def on_device(
     latent, conv_first, conv_second, w_query, w_key, w_value, w_out, w_in, w_down, conv_up
 ):
@@ -395,54 +463,85 @@
     flip = lax.axis_index("parts") % 2 == 1
     swap = [(i, i ^ 1) for i in range(n)]
 
-    shares = jnp.stack([conv_first, conv_second, conv_up])
-    mine = lax.dynamic_slice_in_dim(shares, core * half, half, axis=4)
-    given = lax.dynamic_slice_in_dim(shares, (1 - core) * half, half, axis=4)
-    got = lax.ppermute(given, "row", swap)
-    units = jnp.where(
-        core == 0, jnp.concatenate([mine, got], axis=3), jnp.concatenate([got, mine], axis=3)
+    def unit_of(share):
+        mine = lax.dynamic_slice_in_dim(share, core * half, half, axis=share.ndim - 1)
+        given = lax.dynamic_slice_in_dim(share, (1 - core) * half, half, axis=share.ndim - 1)
+        got = lax.ppermute(given, "row", swap)
+        depth = share.ndim - 2
+        return jnp.where(
+            core == 0,
+            jnp.concatenate([mine, got], axis=depth),
+            jnp.concatenate([got, mine], axis=depth),
+        )
+
+    pair = Gather(unit_of(jnp.stack([conv_first, conv_second], axis=1)), flip)
+    latent_later, conv_later, _ = lax.optimization_barrier((latent, conv_up, pair.up))
+    last = Gather(unit_of(conv_later[:, None]), flip)
+
+    edges = []
+    for i in range(chips - 1):
+        edges += [(2 * i + 1, 2 * i + 2), (2 * i + 2, 2 * i + 1)]
+    beside = jnp.where(core == 0, latent_later[:2], latent_later[-2:])
+    near = lax.ppermute(beside, "row", edges)
+    partner = lax.ppermute(latent_later, "row", swap)
+    count = chips // 2
+    for index in range(1, count):
+        if len(pair.batches) > 1:
+            pair.after(pair.batches[-2])
+        pair.step(index)
+    near_later, _ = lax.optimization_barrier((near, pair.up))
+    far = lax.ppermute(near_later, "row", swap)
+    pair.after(pair.batches[-2])
+    pair.step(count)
+    last.after(pair.finals)
+    last.step(1)
+    field = jnp.where(
+        core == 0,
+        jnp.concatenate([near, latent, partner, far], axis=0),
+        jnp.concatenate([far, partner, latent, near], axis=0),
     )
-    first_pieces, second_pieces, up_pieces = [gather_pieces(units[k], flip) for k in range(3)]
-    ring = jnp.array(ring_of(chips), jnp.int32)
-    position = jnp.argmax(ring == chip).astype(jnp.int32)
-    steps = jnp.array(ring_positions(chips), jnp.int32)
-    owners = ring[(position + steps) % chips]
+    active = last.before(gelu(field.astype(F32)).astype(BF16))
+    last.after(active)
+    last.step(2)
+
+    place = jnp.where(chip % 2 == 0, chip // 2, chips - 1 - chip // 2)
+    owners = chip_at((place + jnp.array(ring_positions(chips), jnp.int32)) % chips, chips)
     top = jnp.where(chip == 0, 1, 0)
     bottom = 2 * per + 2 - jnp.where(chip == chips - 1, 1, 0)
     where = jnp.concatenate(
         [jnp.where(flip, 2, 0)[None], owners, jnp.stack([core, top, bottom])]
     ).astype(jnp.int32)
 
-    up = lax.ppermute(latent, "row", [(i, i + 1) for i in range(n - 1)])
-    down = lax.ppermute(latent, "row", [(i + 1, i) for i in range(n - 1)])
-    far = lax.ppermute(jnp.where(core == 0, up[-2:], down[:2]), "row", swap)
-    field = jnp.where(
-        core == 0,
-        jnp.concatenate([up[-2:], latent, down, far], axis=0),
-        jnp.concatenate([far, up, latent, down[:2]], axis=0),
-    )
-    active = gelu(field.astype(F32)).astype(BF16)
-
-    y1, active2 = first_conv(where, active, field, first_pieces, 2)
+    y1, active2 = first_conv(where, active, field, pair.result(), 2)
+    active2 = last.before(active2)
     theirs = lax.ppermute(active2, "row", swap)
-    y2 = second_conv(where, y1, active2, theirs, second_pieces, 2)
-
+    last.after(active2)
+    last.step(3)
+    y2 = second_conv(where, y1, active2, theirs, pair.result(), 2)
+
+    y2 = last.before(y2)
     groups = cols // GRID
     subs = n // groups
     index_groups = None
     if subs > 1:
         index_groups = [[k * subs + s for k in range(groups)] for s in range(subs)]
-    kept = lax.dynamic_slice_in_dim(y2, core * per, per, axis=1)
-    passed = lax.dynamic_slice_in_dim(y2, (1 - core) * per, per, axis=1)
-    partner = lax.ppermute(passed, "row", swap)
-    y2 = jnp.where(
-        core == 0,
-        jnp.concatenate([kept, partner], axis=3),
-        jnp.concatenate([partner, kept], axis=3),
-    )
+    if subs > 1:
+        kept = lax.dynamic_slice_in_dim(y2, core * per, per, axis=1)
+        passed = lax.dynamic_slice_in_dim(y2, (1 - core) * per, per, axis=1)
+        partner = lax.ppermute(passed, "row", swap)
+        y2 = jnp.where(
+            core == 0,
+            jnp.concatenate([kept, partner], axis=3),
+            jnp.concatenate([partner, kept], axis=3),
+        )
     owned = lax.all_to_all(
         y2, "row", split_axis=0, concat_axis=0, axis_index_groups=index_groups, tiled=True
     )
+    last.after(owned)
+    for index in range(4, count + 1):
+        last.step(index)
+    sides = 2 if subs == 1 else 1
+    owned = owned.reshape(GRID // 2, sides, 2, per, GRID, channels // sides)
     width = cols // 2 // n
     dests = jnp.arange(n, dtype=jnp.int32)
     starts = cols // 4 + width * dests - 1
@@ -452,7 +551,10 @@
         picks, owned, w_query, w_key, w_value, w_out, w_in, w_down
     )
 
+    edge = last.before(edge)
+    edge = edge.reshape(n, per, -1, channels)
     arrived = lax.all_to_all(edge, "row", split_axis=0, concat_axis=0, tiled=True)
+    arrived, latent_window = lax.optimization_barrier((arrived, latent_window))
     if subs > 1:
         arrived = arrived.reshape(groups, subs, GRID // 2, per, channels)
         arrived = arrived.transpose(0, 2, 1, 3, 4)
@@ -465,16 +567,15 @@
         axis_index_groups=index_groups,
         tiled=True,
     )
-    latent_out = returned.transpose(1, 2, 0, 3).reshape(per, cols, channels)
-
-    up_mine = assemble(where, up_pieces, chips)
+    where_later = lax.optimization_barrier((where, edge))[0]
+    up_mine = assemble(where_later, last.result(), chips)
     up_theirs = lax.ppermute(up_mine, "row", swap)
     sources = (cols // 4 + width * device - 1 + jnp.arange(width + 2, dtype=jnp.int32)) % groups
     info = jnp.concatenate(
         [jnp.stack([core, (device > 0).astype(jnp.int32), (device < n - 1).astype(jnp.int32)]), sources]
     ).astype(jnp.int32)
     upsampled = upsample(info, arrived, up_mine, up_theirs, width)
-    return (latent_out, upsampled)
+    return (settle(returned, upsampled), upsampled)
 
 
 def solution(mesh):

time: 241 us -> 159 us (0.66)
  Pallas kernels: 99.6 us -> 30.7 us
  waiting for transfers between devices: 43.1 us -> 59.6 us
  starting transfers between devices: 55.7 us -> 42.2 us
  local copies, waits for them, and re-layouts: 15.1 us -> 5.86 us
  other arithmetic: 9.86 us -> 4.61 us
    pallas_call x1, Pallas kernels: 73.5 us -> 1.95 us  [assemble(): pl.pallas_call(assemble_kernel, out_shape=jax.ShapeDtypeStruct(shape, BF1...]
    all_to_all x1, waiting for transfers between devices: 0.01 us -> 13.6 us  [on_device(): lax.all_to_all(y2, 'row', split_axis=0, concat_axis=0, axis_index_groups=...]
    ppermute x32 -> x28, starting transfers between devices: 41.7 us -> 28.3 us  [the longest x6 6.48 us: step(): self.down = lax.ppermute(self.down, 'row', backward)]
    unnamed x46 -> x38, local copies, waits for them, and re-layouts: 8.2 us -> 2.7 us
    pallas_call x1 -> x2, Pallas kernels: 8.09 us -> 11.3 us  [the longest x1 10.1 us: windows(): pl.pallas_call(window_kernel, out_shape=(jax.ShapeDtypeStruct((grid, per,...]
    ppermute x32 -> x28, waiting for transfers between devices: 33.9 us -> 36.8 us  [the longest x6 15.5 us: step(): self.down = lax.ppermute(self.down, 'row', backward)]
  transfers between devices with their start and end apart: 36 -> 32, of which waited for: 13 -> 11; matrix products, arithmetic and copies ran while one was open for 6% -> 4% of each run, Pallas kernels for 42% -> 18%
where the time goes in v2:
time: 159 us; the launch traced here: 157 us
  waiting for transfers between devices  59.6 us (37%)
  starting transfers between devices  42.2 us (27%)
  Pallas kernels  30.7 us (19%)
  blocking collectives  12.8 us (8%)
  local copies, waits for them, and re-layouts  5.86 us (4%)
  other arithmetic  4.61 us (3%)
    ppermute x6, waiting for transfers between devices, step(): self.down = lax.ppermute(self.down, 'row', backward)  15.5 us
    all_to_all x1, waiting for transfers between devices, on_device(): lax.all_to_all(y2, 'row', split_axis=0, concat_axis=0, axis_index_groups=...  13.6 us
    all_to_all x1, blocking collectives, on_device(): lax.all_to_all(edge, 'row', split_axis=0, concat_axis=0, tiled=True)  12.8 us
    pallas_call x1, Pallas kernels, windows(): pl.pallas_call(window_kernel, out_shape=(jax.ShapeDtypeStruct((grid, per,...  10.1 us
    all_to_all x1, waiting for transfers between devices, on_device(): lax.all_to_all(latent_window, 'row', split_axis=0, concat_axis=0, axis_in...  9.2 us
    ppermute x1, waiting for transfers between devices, on_device(): near = lax.ppermute(beside, 'row', edges)  8.25 us
    pallas_call x1, Pallas kernels, first_conv(): pl.pallas_call(functools.partial(first_conv_kernel, step), out_shape=(out...  6.75 us
    ppermute x6, starting transfers between devices, step(): self.down = lax.ppermute(self.down, 'row', backward)  6.48 us
  transfers between devices with their start and end apart: 32, of which 11 were waited for; matrix products, arithmetic and copies ran while one was open for 4% of the time, Pallas kernels for 18%

profile of v2, /device:TPU:9, one launch (start us, length us, event | category | flops | bytes accessed | tf_op | source)
XLA Modules:
  0.0 157.0 jit_solution(12674421443123565892)
XLA Ops:
  0.7 1.2 fusion.7
  1.9 0.7 collective-permute-start
  2.6 1.2 collective-permute-done
  4.3 1.5 collective-permute-start.3
  5.8 8.9 %collective-permute-done.5.refs_2_ = bf16[2,2,3,64,256]{4,3,2,1,0:T(8,128)(2,1)S(1)} collective-permute-done((bf16[2,2,3,64,256]{4,3,2,1,0:T(8,128)(2,1)S(1)}, bf16[2,2,3,64,256]{4,3,2,1,0:T(8,128)(2,1)S(1)}, u32[]{:S(2)}, u32[]{:S(2)}) %collective-permute-start.5) | collective-permute-done | bytes 393248 | tf_op jit(solution)/shard_map/ppermute | solution.py:82
  14.8 1.1 collective-permute-start.6
  15.9 1.2 collective-permute-start.7
  17.6 6.7 %collective-permute-done.6.refs_4_ = bf16[2,2,3,64,256]{4,3,2,1,0:T(8,128)(2,1)S(1)} collective-permute-done((bf16[2,2,3,64,256]{4,3,2,1,0:T(8,128)(2,1)S(1)}, bf16[2,2,3,64,256]{4,3,2,1,0:T(8,128)(2,1)S(1)}, u32[]{:S(2)}, u32[]{:S(2)}) %collective-permute-start.6) | collective-permute-done | bytes 393248 | tf_op jit(solution)/shard_map/ppermute | solution.py:82
  24.2 0.4 collective-permute-done.7.refs_10_
  24.7 0.9 collective-permute-done.4.refs_3_
  26.0 0.7 collective-permute-start.8
  26.8 0.7 collective-permute-start.11
  27.5 1.0 dynamic-slice_bitcast_fusion.1
  28.5 3.9 %collective-permute-start.10 = (bf16[3,1,3,32,256]{4,3,2,1,0:T(8,128)(2,1)S(1)}, bf16[3,1,3,32,256]{4,3,2,1,0:T(8,128)(2,1)S(1)}, u32[]{:S(2)}, u32[]{:S(2)}) collective-permute-start(bf16[3,1,3,32,256]{4,3,2,1,0:T(8,128)(2,1)S(1)} %get-tuple-element.57), channel_id=1, source_target_pairs={{0,1},{1,0},{2,3},{3,2},{4,5},{5,4},{6,7},{7,6},{8,9},{9,8},{10,11... | collective-permute-start | bytes 442376 | tf_op jit(solution)/shard_map/ppermute | solution.py:469
  32.4 4.2 %collective-permute-start.1 = (bf16[2,256,512]{2,1,0:T(8,128)(2,1)}, bf16[2,256,512]{2,1,0:T(8,128)(2,1)S(1)}, u32[]{:S(2)}, u32[]{:S(2)}) collective-permute-start(bf16[2,256,512]{2,1,0:T(8,128)(2,1)} %param.11), channel_id=1, source_target_pairs={{1,2},{2,1},{3,4},{4,3},{5,6},{6,5},{7,8},{8,7},{9,10},{10,9},{11,... | collective-permute-start | bytes 1572872 | tf_op jit(solution)/shard_map/ppermute | solution.py:485
  36.6 0.9 slice_bitcast_fusion.refs_9_
  37.6 0.4 collective-permute-start.2
  38.3 1.5 collective-permute-start.13
  39.9 1.3 collective-permute-start.17
  41.2 8.3 %collective-permute-done.1 = bf16[2,256,512]{2,1,0:T(8,128)(2,1)S(1)} collective-permute-done((bf16[2,256,512]{2,1,0:T(8,128)(2,1)}, bf16[2,256,512]{2,1,0:T(8,128)(2,1)S(1)}, u32[]{:S(2)}, u32[]{:S(2)}) %collective-permute-start.1) | collective-permute-done | bytes 524320 | tf_op jit(solution)/shard_map/ppermute | solution.py:485
  49.5 0.5 collective-permute-start.15
  50.0 3.2 %collective-permute-start.16 = (bf16[2,1,3,64,256]{4,3,2,1,0:T(8,128)(2,1)S(1)}, bf16[2,1,3,64,256]{4,3,2,1,0:T(8,128)(2,1)S(1)}, u32[]{:S(2)}, u32[]{:S(2)}) collective-permute-start(bf16[2,1,3,64,256]{4,3,2,1,0:T(8,128)(2,1)S(1)} %slice.87.refs_0_), channel_id=1, source_target_pairs={{4,0},{5,1},{8,4},{9,5},{12,8},{13,9},{14,12},{15,13},{10,14},{11,... | collective-permute-start | bytes 589832 | tf_op jit(solution)/shard_map/ppermute | solution.py:82
  53.2 4.0 %collective-permute-done.15.refs_1_ = bf16[2,1,3,64,256]{4,3,2,1,0:T(8,128)(2,1)S(1)} collective-permute-done((bf16[2,1,3,64,256]{4,3,2,1,0:T(8,128)(2,1)S(1)}, bf16[2,1,3,64,256]{4,3,2,1,0:T(8,128)(2,1)S(1)}, u32[]{:S(2)}, u32[]{:S(2)}) %collective-permute-start.15) | collective-permute-done | bytes 196640 | tf_op jit(solution)/shard_map/ppermute | solution.py:81
  57.3 1.2 collective-permute-start.18
  58.9 2.0 %fusion.5 = (bf16[8,256,512]{2,1,0:T(8,128)(2,1)S(1)}, bf16[8,256,512]{2,1,0:T(8,128)(2,1)S(1)}) fusion(bf16[2,256,512]{2,1,0:T(8,128)(2,1)S(1)} %collective-permute-done.1, bf16[2,256,512]{2,1,0:T(8,128)(2,1)S(1)} %copy-done.15, bf16[2,256,512]{2,1,0:T(8,128)(2,1)S(1)} %collective-permute-done.2, bf16[2,256,512]{2,1,0:T(8,128)(2,1)S(1)} %collective-permute-done.9, ...), kind=kLoop, calls=%fused_computation.9 | loop fusion | flops 17825792 | bytes 6291457 | tf_op jit(solution)/shard_map/convert_element_type | solution.py:503
  60.9 0.5 collective-permute-start.19
  61.4 1.5 collective-permute-start.20
  62.9 1.3 collective-permute-done.18.refs_13_
  64.1 6.8 %first_conv.1 = (bf16[6,256,256]{2,1,0:T(8,128)(2,1)S(1)}, bf16[6,256,256]{2,1,0:T(8,128)(2,1)S(1)}) custom-call(s32[12]{0:T(128)S(1)} %concatenate.45.where, bf16[8,256,512]{2,1,0:T(8,128)(2,1)S(1)} %get-tuple-element.36.act, bf16[8,256,512]{2,1,0:T(8,128)(2,1)S(1)} %get-tuple-element.53.lat, bf16[2,2,3,64,256]{4,3,2,1,0:T(8,128)(2,1)S(1)} %slice.84.refs_0_, ...), custom_call_target="tpu_custom_call" | custom-call | flops 3623878656 | bytes 2359296 | tf_op jit(solution)/shard_map/first_conv/pallas_call | solution.py:186
  71.0 2.1 %collective-permute-start.22 = (bf16[6,256,256]{2,1,0:T(8,128)(2,1)S(1)}, bf16[6,256,256]{2,1,0:T(8,128)(2,1)S(1)}, u32[]{:S(2)}, u32[]{:S(2)}) collective-permute-start(bf16[6,256,256]{2,1,0:T(8,128)(2,1)S(1)} %get-tuple-element.41.mine), channel_id=1, source_target_pairs={{0,1},{1,0},{2,3},{3,2},{4,5},{5,4},{6,7},{7,6},{8,9},{9,8},{10,11... | collective-permute-start | bytes 2359304 | tf_op jit(solution)/shard_map/ppermute | solution.py:517
  73.5 1.7 %collective-permute-start.23 = (bf16[2,1,3,64,256]{4,3,2,1,0:T(8,128)(2,1)S(1)}, bf16[2,1,3,64,256]{4,3,2,1,0:T(8,128)(2,1)S(1)}, u32[]{:S(2)}, u32[]{:S(2)}) collective-permute-start(bf16[2,1,3,64,256]{4,3,2,1,0:T(8,128)(2,1)S(1)} %collective-permute-done.19.refs_3_), channel_id=1, source_target_pairs={{0,4},{1,5},{4,8},{5,9},{8,12},{9,13},{12,14},{13,15},{14,10},{15,... | collective-permute-start | bytes 589832 | tf_op jit(solution)/shard_map/ppermute | solution.py:81
  75.2 5.8 %second_conv.1 = bf16[16,4,16,256]{3,2,1,0:T(8,128)(2,1)} custom-call(s32[12]{0:T(128)S(1)} %concatenate.45.where, bf16[6,256,256]{2,1,0:T(8,128)(2,1)S(1)} %get-tuple-element.37.y1, bf16[6,256,256]{2,1,0:T(8,128)(2,1)S(1)} %get-tuple-element.41.mine, bf16[6,256,256]{2,1,0:T(8,128)(2,1)S(1)} %collective-permute-done.22.theirs, ...), custom_call_target="tpu_custom_call" | custom-call | flops 2415919104 | bytes 2359296 | tf_op jit(solution)/shard_map/second_conv/pallas_call | solution.py:231
  81.0 0.7 copy-done.5
  81.7 5.9 %all-to-all-start = ((bf16[16,4,16,256]{3,2,1,0:T(8,128)(2,1)}), bf16[16,4,16,256]{3,2,1,0:T(8,128)(2,1)S(1)}, u32[]{:S(2)}, u32[]{:S(2)}) async-start(bf16[16,4,16,256]{3,2,1,0:T(8,128)(2,1)} %second_conv.1), calls=%async_computation | async-start | bytes 1048576 | tf_op jit(solution)/shard_map/all_to_all | solution.py:537
  87.6 0.5 fusion.10.picks
  88.2 13.6 %all-to-all-done = bf16[16,4,16,256]{3,2,1,0:T(8,128)(2,1)S(1)} async-done(((bf16[16,4,16,256]{3,2,1,0:T(8,128)(2,1)}), bf16[16,4,16,256]{3,2,1,0:T(8,128)(2,1)S(1)}, u32[]{:S(2)}, u32[]{:S(2)}) %all-to-all-start) | async-done | bytes 524320 | tf_op jit(solution)/shard_map/all_to_all | solution.py:537
  102.0 0.9 slice_bitcast_fusion.1.refs_8_
  103.3 5.1 %collective-permute-done.26.refs_7_ = bf16[2,1,3,64,256]{4,3,2,1,0:T(8,128)(2,1)S(1)} collective-permute-done((bf16[2,1,3,64,256]{4,3,2,1,0:T(8,128)(2,1)S(1)}, bf16[2,1,3,64,256]{4,3,2,1,0:T(8,128)(2,1)S(1)}, u32[]{:S(2)}, u32[]{:S(2)}) %collective-permute-start.26) | collective-permute-done | bytes 196640 | tf_op jit(solution)/shard_map/ppermute | solution.py:77
  108.8 10.1 %windows.1 = (bf16[16,2,16,512]{3,2,1,0:T(8,128)(2,1)}, bf16[16,16,512]{2,1,0:T(8,128)(2,1)}) custom-call(s32[16]{0:T(128)} %fusion.10.picks, bf16[8,2,2,2,16,256]{5,4,3,2,1,0:T(8,128)(2,1)} %bitcast.26, bf16[512,512]{1,0:T(8,128)(2,1)} %refs_0_.1, bf16[512,512]{1,0:T(8,128)(2,1)} %refs_1_.1, bf16[512,512]{1,0:T(8,128)(2,1)} %refs_2_.1, ...), custom_call_target="tpu_custom_call" | custom-call | flops 3489660928 | bytes 2097152 | tf_op jit(solution)/shard_map/windows/pallas_call | solution.py:331
  118.9 0.9 copy-done.2
  119.9 1.9 %assemble.1.mine = bf16[3,3,512,256]{3,2,1,0:T(8,128)(2,1)S(1)} custom-call(s32[12]{0:T(128)S(1)} %concatenate.45.where, bf16[2,1,3,64,256]{4,3,2,1,0:T(8,128)(2,1)S(1)} %slice.87.refs_0_, bf16[2,1,3,64,256]{4,3,2,1,0:T(8,128)(2,1)S(1)} %collective-permute-done.15.refs_1_, bf16[2,1,3,64,256]{4,3,2,1,0:T(8,128)(2,1)S(1)} %collective-permute-done.16.refs_2_, ...), custom_call_target="tpu_custom_call" | custom-call | bytes 4718592 | tf_op jit(solution)/shard_map/assemble/pallas_call | solution.py:128
  121.8 1.1 collective-permute-start.29
  122.9 12.8 %all_to_all.15 = bf16[16,2,8,512]{3,2,1,0:T(8,128)(2,1)S(1)} all-to-all(bf16[16,2,8,512]{3,2,1,0:T(8,128)(2,1)S(1)} %bitcast.29), channel_id=1, replica_groups=mesh['parts'=2,'row'=16] {'row'}, dimensions={0} | all-to-all | bytes 524288 | tf_op jit(solution)/shard_map/all_to_all | solution.py:556
  135.7 4.8 %all-to-all-start.2 = ((bf16[16,2,16,512]{3,2,1,0:T(8,128)(2,1)}), bf16[16,2,16,512]{3,2,1,0:T(8,128)(2,1)S(1)}, u32[]{:S(2)}, u32[]{:S(2)}) async-start(bf16[16,2,16,512]{3,2,1,0:T(8,128)(2,1)} %get-tuple-element.49), calls=%async_computation.2 | async-start | bytes 1048576 | tf_op jit(solution)/shard_map/all_to_all | solution.py:562
  140.6 4.9 %upsample.1.earlier = bf16[32,16,512]{2,1,0:T(8,128)(2,1)} custom-call(s32[13]{0:T(128)S(1)} %pad_add_fusion.info, bf16[16,16,512]{2,1,0:T(8,128)(2,1)S(1)} %bitcast.25, bf16[3,3,512,256]{3,2,1,0:T(8,128)(2,1)S(1)} %assemble.1.mine, bf16[3,3,512,256]{3,2,1,0:T(8,128)(2,1)} %collective-permute-done.29.theirs), custom_call_target="tpu_custom_call" | custom-call | flops 754974720 | bytes 4718592 | tf_op jit(solution)/shard_map/upsample/pallas_call | solution.py:413
  145.5 9.2 %all-to-all-done.2.arrived = bf16[16,2,16,512]{3,2,1,0:T(8,128)(2,1)S(1)} async-done(((bf16[16,2,16,512]{3,2,1,0:T(8,128)(2,1)}), bf16[16,2,16,512]{3,2,1,0:T(8,128)(2,1)S(1)}, u32[]{:S(2)}, u32[]{:S(2)}) %all-to-all-start.2) | async-done | bytes 524320 | tf_op jit(solution)/shard_map/all_to_all | solution.py:562
  154.7 1.0 copy-done
  155.7 1.2 settle.1
  (101 shorter events, 3.9 us)
Async XLA Ops:
  1.9 1.9 %collective-permute-start = (bf16[3,2,3,32,256]{4,3,2,1,0:T(8,128)(2,1)S(1)}, bf16[3,2,3,32,256]{4,3,2,1,0:T(8,128)(2,1)S(1)}, u32[]{:S(2)}, u32[]{:S(2)}) collective-permute-start(bf16[3,2,3,32,256]{4,3,2,1,0:T(8,128)(2,1)S(1)} %get-tuple-element.55), channel_id=1, source_target_pairs={{0,1},{1,0},{2,3},{3,2},{4,5},{5,4},{6,7},{7,6},{8,9},{9,8},{10,11... | collective-permute-start | bytes 884744 | tf_op jit(solution)/shard_map/ppermute | solution.py:469
  4.1 13.4 %copy-start.18 = (s32[8]{0:T(128)S(1)}, s32[8]{0:T(128)}, u32[]{:S(2)}) copy-start(s32[8]{0:T(128)} %constant.133.clone) | copy-start | bytes 100
  4.2 11.6 %copy-start.13 = (bf16[3,2,3,64,256]{4,3,2,1,0:T(8,128)(2,1)}, bf16[3,2,3,64,256]{4,3,2,1,0:T(8,128)(2,1)S(1)}, u32[]{:S(2)}) copy-start(bf16[3,2,3,64,256]{4,3,2,1,0:T(8,128)(2,1)S(1)} %reverse_select_fusion) | copy-start | bytes 1769476
  4.3 10.4 %collective-permute-start.5 = (bf16[2,2,3,64,256]{4,3,2,1,0:T(8,128)(2,1)S(1)}, bf16[2,2,3,64,256]{4,3,2,1,0:T(8,128)(2,1)S(1)}, u32[]{:S(2)}, u32[]{:S(2)}) collective-permute-start(bf16[2,2,3,64,256]{4,3,2,1,0:T(8,128)(2,1)S(1)} %slice.84.refs_0_), channel_id=1, source_target_pairs={{4,0},{5,1},{8,4},{9,5},{12,8},{13,9},{14,12},{15,13},{10,14},{11,... | collective-permute-start | bytes 1179656 | tf_op jit(solution)/shard_map/ppermute | solution.py:82
  4.3 10.4 %collective-permute-start.3 = (bf16[2,2,3,64,256]{4,3,2,1,0:T(8,128)(2,1)S(1)}, bf16[2,2,3,64,256]{4,3,2,1,0:T(8,128)(2,1)S(1)}, u32[]{:S(2)}, u32[]{:S(2)}) collective-permute-start(bf16[2,2,3,64,256]{4,3,2,1,0:T(8,128)(2,1)S(1)} %slice.84.refs_0_), channel_id=1, source_target_pairs={{0,4},{1,5},{4,8},{5,9},{8,12},{9,13},{12,14},{13,15},{14,10},{15,... | collective-permute-start | bytes 1179656 | tf_op jit(solution)/shard_map/ppermute | solution.py:81
  14.8 9.5 %collective-permute-start.6 = (bf16[2,2,3,64,256]{4,3,2,1,0:T(8,128)(2,1)S(1)}, bf16[2,2,3,64,256]{4,3,2,1,0:T(8,128)(2,1)S(1)}, u32[]{:S(2)}, u32[]{:S(2)}) collective-permute-start(bf16[2,2,3,64,256]{4,3,2,1,0:T(8,128)(2,1)S(1)} %collective-permute-done.5.refs_2_), channel_id=1, source_target_pairs={{4,0},{5,1},{8,4},{9,5},{12,8},{13,9},{14,12},{15,13},{10,14},{11,... | collective-permute-start | bytes 1179656 | tf_op jit(solution)/shard_map/ppermute | solution.py:82
  15.9 8.8 %collective-permute-start.7 = (bf16[2,2,3,64,256]{4,3,2,1,0:T(8,128)(2,1)S(1)}, bf16[2,2,3,64,256]{4,3,2,1,0:T(8,128)(2,1)S(1)}, u32[]{:S(2)}, u32[]{:S(2)}) collective-permute-start(bf16[2,2,3,64,256]{4,3,2,1,0:T(8,128)(2,1)S(1)} %pad_maximum_fusion), channel_id=1, source_target_pairs={{0,16},{16,0},{1,17},{17,1},{2,18},{18,2},{3,19},{19,3},{4,20},{20... | collective-permute-start | bytes 1179656 | tf_op jit(solution)/shard_map/ppermute | solution.py:87
  17.1 8.5 %collective-permute-start.4 = (bf16[2,2,3,64,256]{4,3,2,1,0:T(8,128)(2,1)S(1)}, bf16[2,2,3,64,256]{4,3,2,1,0:T(8,128)(2,1)S(1)}, u32[]{:S(2)}, u32[]{:S(2)}) collective-permute-start(bf16[2,2,3,64,256]{4,3,2,1,0:T(8,128)(2,1)S(1)} %collective-permute-done.3.refs_1_), channel_id=1, source_target_pairs={{0,4},{1,5},{4,8},{5,9},{8,12},{9,13},{12,14},{13,15},{14,10},{15,... | collective-permute-start | bytes 1179656 | tf_op jit(solution)/shard_map/ppermute | solution.py:81
  24.2 15.5 %copy-start.7 = (bf16[2,2,3,64,256]{4,3,2,1,0:T(8,128)(2,1)}, bf16[2,2,3,64,256]{4,3,2,1,0:T(8,128)(2,1)S(1)}, u32[]{:S(2)}) copy-start(bf16[2,2,3,64,256]{4,3,2,1,0:T(8,128)(2,1)S(1)} %collective-permute-done.6.refs_4_) | copy-start | bytes 1179652
  24.7 15.1 %copy-start.11 = (bf16[2,2,3,64,256]{4,3,2,1,0:T(8,128)(2,1)}, bf16[2,2,3,64,256]{4,3,2,1,0:T(8,128)(2,1)S(1)}, u32[]{:S(2)}) copy-start(bf16[2,2,3,64,256]{4,3,2,1,0:T(8,128)(2,1)S(1)} %collective-permute-done.7.refs_10_) | copy-start | bytes 1179652
  25.6 14.2 %copy-start.9 = (bf16[2,2,3,64,256]{4,3,2,1,0:T(8,128)(2,1)}, bf16[2,2,3,64,256]{4,3,2,1,0:T(8,128)(2,1)S(1)}, u32[]{:S(2)}) copy-start(bf16[2,2,3,64,256]{4,3,2,1,0:T(8,128)(2,1)S(1)} %collective-permute-done.4.refs_3_) | copy-start | bytes 1179652
  25.7 12.5 %collective-permute-start.12 = (bf16[2,2,3,64,256]{4,3,2,1,0:T(8,128)(2,1)S(1)}, bf16[2,2,3,64,256]{4,3,2,1,0:T(8,128)(2,1)S(1)}, u32[]{:S(2)}, u32[]{:S(2)}) collective-permute-start(bf16[2,2,3,64,256]{4,3,2,1,0:T(8,128)(2,1)S(1)} %pad_maximum_fusion.1), channel_id=1, source_target_pairs={{0,16},{16,0},{1,17},{17,1},{2,18},{18,2},{3,19},{19,3},{4,20},{20... | collective-permute-start | bytes 1179656 | tf_op jit(solution)/shard_map/ppermute | solution.py:87
  26.0 12.1 %collective-permute-start.8 = (bf16[2,2,3,64,256]{4,3,2,1,0:T(8,128)(2,1)S(1)}, bf16[2,2,3,64,256]{4,3,2,1,0:T(8,128)(2,1)S(1)}, u32[]{:S(2)}, u32[]{:S(2)}) collective-permute-start(bf16[2,2,3,64,256]{4,3,2,1,0:T(8,128)(2,1)S(1)} %collective-permute-done.4.refs_3_), channel_id=1, source_target_pairs={{0,4},{1,5},{4,8},{5,9},{8,12},{9,13},{12,14},{13,15},{14,10},{15,... | collective-permute-start | bytes 1179656 | tf_op jit(solution)/shard_map/ppermute | solution.py:81
  26.8 11.4 %collective-permute-start.11 = (bf16[2,2,3,64,256]{4,3,2,1,0:T(8,128)(2,1)S(1)}, bf16[2,2,3,64,256]{4,3,2,1,0:T(8,128)(2,1)S(1)}, u32[]{:S(2)}, u32[]{:S(2)}) collective-permute-start(bf16[2,2,3,64,256]{4,3,2,1,0:T(8,128)(2,1)S(1)} %collective-permute-done.6.refs_4_), channel_id=1, source_target_pairs={{4,0},{5,1},{8,4},{9,5},{12,8},{13,9},{14,12},{15,13},{10,14},{11,... | collective-permute-start | bytes 1179656 | tf_op jit(solution)/shard_map/ppermute | solution.py:82
  28.5 9.1 %collective-permute-start.10 = (bf16[3,1,3,32,256]{4,3,2,1,0:T(8,128)(2,1)S(1)}, bf16[3,1,3,32,256]{4,3,2,1,0:T(8,128)(2,1)S(1)}, u32[]{:S(2)}, u32[]{:S(2)}) collective-permute-start(bf16[3,1,3,32,256]{4,3,2,1,0:T(8,128)(2,1)S(1)} %get-tuple-element.57), channel_id=1, source_target_pairs={{0,1},{1,0},{2,3},{3,2},{4,5},{5,4},{6,7},{7,6},{8,9},{9,8},{10,11... | collective-permute-start | bytes 442376 | tf_op jit(solution)/shard_map/ppermute | solution.py:469
  32.4 17.1 %collective-permute-start.1 = (bf16[2,256,512]{2,1,0:T(8,128)(2,1)}, bf16[2,256,512]{2,1,0:T(8,128)(2,1)S(1)}, u32[]{:S(2)}, u32[]{:S(2)}) collective-permute-start(bf16[2,256,512]{2,1,0:T(8,128)(2,1)} %param.11), channel_id=1, source_target_pairs={{1,2},{2,1},{3,4},{4,3},{5,6},{6,5},{7,8},{8,7},{9,10},{10,9},{11,... | collective-permute-start | bytes 1572872 | tf_op jit(solution)/shard_map/ppermute | solution.py:485
  37.6 21.3 %collective-permute-start.2 = (bf16[2,256,512]{2,1,0:T(8,128)(2,1)}, bf16[2,256,512]{2,1,0:T(8,128)(2,1)S(1)}, u32[]{:S(2)}, u32[]{:S(2)}) collective-permute-start(bf16[2,256,512]{2,1,0:T(8,128)(2,1)} %param.11), channel_id=1, source_target_pairs={{0,1},{1,0},{2,3},{3,2},{4,5},{5,4},{6,7},{7,6},{8,9},{9,8},{10,11... | collective-permute-start | bytes 1572872 | tf_op jit(solution)/shard_map/ppermute | solution.py:486
  38.2 20.7 %copy-start.15 = (bf16[2,256,512]{2,1,0:T(8,128)(2,1)S(1)}, bf16[2,256,512]{2,1,0:T(8,128)(2,1)}, u32[]{:S(2)}) copy-start(bf16[2,256,512]{2,1,0:T(8,128)(2,1)} %param.11) | copy-start | bytes 1572868
  38.2 11.2 %collective-permute-start.14 = (bf16[2,1,3,64,256]{4,3,2,1,0:T(8,128)(2,1)S(1)}, bf16[2,1,3,64,256]{4,3,2,1,0:T(8,128)(2,1)S(1)}, u32[]{:S(2)}, u32[]{:S(2)}) collective-permute-start(bf16[2,1,3,64,256]{4,3,2,1,0:T(8,128)(2,1)S(1)} %slice.70), channel_id=1, source_target_pairs={{4,0},{5,1},{8,4},{9,5},{12,8},{13,9},{14,12},{15,13},{10,14},{11,... | collective-permute-start | bytes 589832 | tf_op jit(solution)/shard_map/ppermute | solution.py:77
  38.3 11.2 %collective-permute-start.13 = (bf16[2,1,3,64,256]{4,3,2,1,0:T(8,128)(2,1)S(1)}, bf16[2,1,3,64,256]{4,3,2,1,0:T(8,128)(2,1)S(1)}, u32[]{:S(2)}, u32[]{:S(2)}) collective-permute-start(bf16[2,1,3,64,256]{4,3,2,1,0:T(8,128)(2,1)S(1)} %slice.69), channel_id=1, source_target_pairs={{0,4},{1,5},{4,8},{5,9},{8,12},{9,13},{12,14},{13,15},{14,10},{15,... | collective-permute-start | bytes 589832 | tf_op jit(solution)/shard_map/ppermute | solution.py:77
  39.8 31.1 %copy-start.14 = (bf16[3,1,3,64,256]{4,3,2,1,0:T(8,128)(2,1)}, bf16[3,1,3,64,256]{4,3,2,1,0:T(8,128)(2,1)S(1)}, u32[]{:S(2)}) copy-start(bf16[3,1,3,64,256]{4,3,2,1,0:T(8,128)(2,1)S(1)} %reverse_select_fusion.1) | copy-start | bytes 884740
  39.9 24.2 %collective-permute-start.17 = (bf16[2,2,3,64,256]{4,3,2,1,0:T(8,128)(2,1)S(1)}, bf16[2,2,3,64,256]{4,3,2,1,0:T(8,128)(2,1)S(1)}, u32[]{:S(2)}, u32[]{:S(2)}) collective-permute-start(bf16[2,2,3,64,256]{4,3,2,1,0:T(8,128)(2,1)S(1)} %pad_maximum_fusion.2), channel_id=1, source_target_pairs={{0,16},{16,0},{1,17},{17,1},{2,18},{18,2},{3,19},{19,3},{4,20},{20... | collective-permute-start | bytes 1179656 | tf_op jit(solution)/shard_map/ppermute | solution.py:87
  49.5 9.4 %collective-permute-start.9 = (bf16[2,256,512]{2,1,0:T(8,128)(2,1)S(1)}, bf16[2,256,512]{2,1,0:T(8,128)(2,1)S(1)}, u32[]{:S(2)}, u32[]{:S(2)}) collective-permute-start(bf16[2,256,512]{2,1,0:T(8,128)(2,1)S(1)} %collective-permute-done.1), channel_id=1, source_target_pairs={{0,1},{1,0},{2,3},{3,2},{4,5},{5,4},{6,7},{7,6},{8,9},{9,8},{10,11... | collective-permute-start | bytes 1572872 | tf_op jit(solution)/shard_map/ppermute | solution.py:493
  49.5 7.8 %collective-permute-start.15 = (bf16[2,1,3,64,256]{4,3,2,1,0:T(8,128)(2,1)S(1)}, bf16[2,1,3,64,256]{4,3,2,1,0:T(8,128)(2,1)S(1)}, u32[]{:S(2)}, u32[]{:S(2)}) collective-permute-start(bf16[2,1,3,64,256]{4,3,2,1,0:T(8,128)(2,1)S(1)} %slice.87.refs_0_), channel_id=1, source_target_pairs={{0,4},{1,5},{4,8},{5,9},{8,12},{9,13},{12,14},{13,15},{14,10},{15,... | collective-permute-start | bytes 589832 | tf_op jit(solution)/shard_map/ppermute | solution.py:81
  50.0 8.5 %collective-permute-start.16 = (bf16[2,1,3,64,256]{4,3,2,1,0:T(8,128)(2,1)S(1)}, bf16[2,1,3,64,256]{4,3,2,1,0:T(8,128)(2,1)S(1)}, u32[]{:S(2)}, u32[]{:S(2)}) collective-permute-start(bf16[2,1,3,64,256]{4,3,2,1,0:T(8,128)(2,1)S(1)} %slice.87.refs_0_), channel_id=1, source_target_pairs={{4,0},{5,1},{8,4},{9,5},{12,8},{13,9},{14,12},{15,13},{10,14},{11,... | collective-permute-start | bytes 589832 | tf_op jit(solution)/shard_map/ppermute | solution.py:82
  57.3 6.9 %collective-permute-start.18 = (bf16[1,2,3,64,256]{4,3,2,1,0:T(8,128)(2,1)S(1)}, bf16[1,2,3,64,256]{4,3,2,1,0:T(8,128)(2,1)S(1)}, u32[]{:S(2)}, u32[]{:S(2)}) collective-permute-start(bf16[1,2,3,64,256]{4,3,2,1,0:T(8,128)(2,1)S(1)} %maximum_bitcast_fusion), channel_id=1, source_target_pairs={{0,16},{16,0},{1,17},{17,1},{2,18},{18,2},{3,19},{19,3},{4,20},{20... | collective-permute-start | bytes 589832 | tf_op jit(solution)/shard_map/ppermute | solution.py:79
  58.5 5.6 %copy-start.8 = (bf16[2,2,3,64,256]{4,3,2,1,0:T(8,128)(2,1)S(1)}, bf16[2,2,3,64,256]{4,3,2,1,0:T(8,128)(2,1)}, u32[]{:S(2)}) copy-start(bf16[2,2,3,64,256]{4,3,2,1,0:T(8,128)(2,1)} %copy-done.7) | copy-start | bytes 1179652
  58.5 5.6 %copy-start.10 = (bf16[2,2,3,64,256]{4,3,2,1,0:T(8,128)(2,1)S(1)}, bf16[2,2,3,64,256]{4,3,2,1,0:T(8,128)(2,1)}, u32[]{:S(2)}) copy-start(bf16[2,2,3,64,256]{4,3,2,1,0:T(8,128)(2,1)} %copy-done.9) | copy-start | bytes 1179652
  58.6 5.6 %copy-start.12 = (bf16[2,2,3,64,256]{4,3,2,1,0:T(8,128)(2,1)S(1)}, bf16[2,2,3,64,256]{4,3,2,1,0:T(8,128)(2,1)}, u32[]{:S(2)}) copy-start(bf16[2,2,3,64,256]{4,3,2,1,0:T(8,128)(2,1)} %copy-done.11) | copy-start | bytes 1179652
  58.6 12.4 %collective-permute-start.21 = (bf16[2,1,3,64,256]{4,3,2,1,0:T(8,128)(2,1)S(1)}, bf16[2,1,3,64,256]{4,3,2,1,0:T(8,128)(2,1)S(1)}, u32[]{:S(2)}, u32[]{:S(2)}) collective-permute-start(bf16[2,1,3,64,256]{4,3,2,1,0:T(8,128)(2,1)S(1)} %pad_maximum_fusion.3), channel_id=1, source_target_pairs={{0,16},{16,0},{1,17},{17,1},{2,18},{18,2},{3,19},{19,3},{4,20},{20... | collective-permute-start | bytes 589832 | tf_op jit(solution)/shard_map/ppermute | solution.py:87
  60.9 10.0 %collective-permute-start.19 = (bf16[2,1,3,64,256]{4,3,2,1,0:T(8,128)(2,1)S(1)}, bf16[2,1,3,64,256]{4,3,2,1,0:T(8,128)(2,1)S(1)}, u32[]{:S(2)}, u32[]{:S(2)}) collective-permute-start(bf16[2,1,3,64,256]{4,3,2,1,0:T(8,128)(2,1)S(1)} %collective-permute-done.15.refs_1_), channel_id=1, source_target_pairs={{0,4},{1,5},{4,8},{5,9},{8,12},{9,13},{12,14},{13,15},{14,10},{15,... | collective-permute-start | bytes 589832 | tf_op jit(solution)/shard_map/ppermute | solution.py:81
  61.4 9.5 %collective-permute-start.20 = (bf16[2,1,3,64,256]{4,3,2,1,0:T(8,128)(2,1)S(1)}, bf16[2,1,3,64,256]{4,3,2,1,0:T(8,128)(2,1)S(1)}, u32[]{:S(2)}, u32[]{:S(2)}) collective-permute-start(bf16[2,1,3,64,256]{4,3,2,1,0:T(8,128)(2,1)S(1)} %collective-permute-done.16.refs_2_), channel_id=1, source_target_pairs={{4,0},{5,1},{8,4},{9,5},{12,8},{13,9},{14,12},{15,13},{10,14},{11,... | collective-permute-start | bytes 589832 | tf_op jit(solution)/shard_map/ppermute | solution.py:82
  70.9 2.5 %copy-start.3 = (bf16[2,1,3,64,256]{4,3,2,1,0:T(8,128)(2,1)}, bf16[2,1,3,64,256]{4,3,2,1,0:T(8,128)(2,1)S(1)}, u32[]{:S(2)}) copy-start(bf16[2,1,3,64,256]{4,3,2,1,0:T(8,128)(2,1)S(1)} %collective-permute-done.21.refs_9_) | copy-start | bytes 589828
  71.0 4.3 %collective-permute-start.22 = (bf16[6,256,256]{2,1,0:T(8,128)(2,1)S(1)}, bf16[6,256,256]{2,1,0:T(8,128)(2,1)S(1)}, u32[]{:S(2)}, u32[]{:S(2)}) collective-permute-start(bf16[6,256,256]{2,1,0:T(8,128)(2,1)S(1)} %get-tuple-element.41.mine), channel_id=1, source_target_pairs={{0,1},{1,0},{2,3},{3,2},{4,5},{5,4},{6,7},{7,6},{8,9},{9,8},{10,11... | collective-permute-start | bytes 2359304 | tf_op jit(solution)/shard_map/ppermute | solution.py:517
  73.1 7.9 %collective-permute-start.25 = (bf16[2,1,3,64,256]{4,3,2,1,0:T(8,128)(2,1)S(1)}, bf16[2,1,3,64,256]{4,3,2,1,0:T(8,128)(2,1)S(1)}, u32[]{:S(2)}, u32[]{:S(2)}) collective-permute-start(bf16[2,1,3,64,256]{4,3,2,1,0:T(8,128)(2,1)S(1)} %pad_maximum_fusion.4), channel_id=1, source_target_pairs={{0,16},{16,0},{1,17},{17,1},{2,18},{18,2},{3,19},{19,3},{4,20},{20... | collective-permute-start | bytes 589832 | tf_op jit(solution)/shard_map/ppermute | solution.py:87
  73.5 8.2 %collective-permute-start.23 = (bf16[2,1,3,64,256]{4,3,2,1,0:T(8,128)(2,1)S(1)}, bf16[2,1,3,64,256]{4,3,2,1,0:T(8,128)(2,1)S(1)}, u32[]{:S(2)}, u32[]{:S(2)}) collective-permute-start(bf16[2,1,3,64,256]{4,3,2,1,0:T(8,128)(2,1)S(1)} %collective-permute-done.19.refs_3_), channel_id=1, source_target_pairs={{0,4},{1,5},{4,8},{5,9},{8,12},{9,13},{12,14},{13,15},{14,10},{15,... | collective-permute-start | bytes 589832 | tf_op jit(solution)/shard_map/ppermute | solution.py:81
  75.2 6.5 %collective-permute-start.24 = (bf16[2,1,3,64,256]{4,3,2,1,0:T(8,128)(2,1)S(1)}, bf16[2,1,3,64,256]{4,3,2,1,0:T(8,128)(2,1)S(1)}, u32[]{:S(2)}, u32[]{:S(2)}) collective-permute-start(bf16[2,1,3,64,256]{4,3,2,1,0:T(8,128)(2,1)S(1)} %collective-permute-done.20.refs_4_), channel_id=1, source_target_pairs={{4,0},{5,1},{8,4},{9,5},{12,8},{13,9},{14,12},{15,13},{10,14},{11,... | collective-permute-start | bytes 589832 | tf_op jit(solution)/shard_map/ppermute | solution.py:82
  81.7 37.2 %copy-start.1 = (bf16[2,1,3,64,256]{4,3,2,1,0:T(8,128)(2,1)}, bf16[2,1,3,64,256]{4,3,2,1,0:T(8,128)(2,1)S(1)}, u32[]{:S(2)}) copy-start(bf16[2,1,3,64,256]{4,3,2,1,0:T(8,128)(2,1)S(1)} %collective-permute-done.24.refs_6_) | copy-start | bytes 589828
  81.7 20.1 %all-to-all-start = ((bf16[16,4,16,256]{3,2,1,0:T(8,128)(2,1)}), bf16[16,4,16,256]{3,2,1,0:T(8,128)(2,1)S(1)}, u32[]{:S(2)}, u32[]{:S(2)}) async-start(bf16[16,4,16,256]{3,2,1,0:T(8,128)(2,1)} %second_conv.1), calls=%async_computation | async-start | bytes 1048576 | tf_op jit(solution)/shard_map/all_to_all | solution.py:537
  101.8 7.0 %copy-start.16 = (bf16[16,4,16,256]{3,2,1,0:T(8,128)(2,1)}, bf16[16,4,16,256]{3,2,1,0:T(8,128)(2,1)S(1)}, u32[]{:S(2)}) copy-start(bf16[16,4,16,256]{3,2,1,0:T(8,128)(2,1)S(1)} %all-to-all-done) | copy-start | bytes 1572868
  101.8 6.6 %collective-permute-start.26 = (bf16[2,1,3,64,256]{4,3,2,1,0:T(8,128)(2,1)S(1)}, bf16[2,1,3,64,256]{4,3,2,1,0:T(8,128)(2,1)S(1)}, u32[]{:S(2)}, u32[]{:S(2)}) collective-permute-start(bf16[2,1,3,64,256]{4,3,2,1,0:T(8,128)(2,1)S(1)} %collective-permute-done.23.refs_5_), channel_id=1, source_target_pairs={{0,4},{1,5},{4,8},{5,9},{8,12},{9,13},{12,14},{13,15},{14,10},{15,... | collective-permute-start | bytes 589832 | tf_op jit(solution)/shard_map/ppermute | solution.py:77
  103.0 15.9 %collective-permute-start.27 = (bf16[2,1,3,64,256]{4,3,2,1,0:T(8,128)(2,1)S(1)}, bf16[2,1,3,64,256]{4,3,2,1,0:T(8,128)(2,1)S(1)}, u32[]{:S(2)}, u32[]{:S(2)}) collective-permute-start(bf16[2,1,3,64,256]{4,3,2,1,0:T(8,128)(2,1)S(1)} %pad_maximum_fusion.5), channel_id=1, source_target_pairs={{0,16},{16,0},{1,17},{17,1},{2,18},{18,2},{3,19},{19,3},{4,20},{20... | collective-permute-start | bytes 589832 | tf_op jit(solution)/shard_map/ppermute | solution.py:87
  108.4 10.5 %collective-permute-start.28 = (bf16[1,1,3,64,256]{4,3,2,1,0:T(8,128)(2,1)S(1)}, bf16[1,1,3,64,256]{4,3,2,1,0:T(8,128)(2,1)S(1)}, u32[]{:S(2)}, u32[]{:S(2)}) collective-permute-start(bf16[1,1,3,64,256]{4,3,2,1,0:T(8,128)(2,1)S(1)} %slice.102), channel_id=1, source_target_pairs={{0,16},{16,0},{1,17},{17,1},{2,18},{18,2},{3,19},{19,3},{4,20},{20... | collective-permute-start | bytes 294920 | tf_op jit(solution)/shard_map/ppermute | solution.py:79
  108.7 10.2 %copy-start.4 = (bf16[2,1,3,64,256]{4,3,2,1,0:T(8,128)(2,1)S(1)}, bf16[2,1,3,64,256]{4,3,2,1,0:T(8,128)(2,1)}, u32[]{:S(2)}) copy-start(bf16[2,1,3,64,256]{4,3,2,1,0:T(8,128)(2,1)} %copy-done.3) | copy-start | bytes 589828
  108.7 10.2 %copy-start.6 = (bf16[2,1,3,64,256]{4,3,2,1,0:T(8,128)(2,1)S(1)}, bf16[2,1,3,64,256]{4,3,2,1,0:T(8,128)(2,1)}, u32[]{:S(2)}) copy-start(bf16[2,1,3,64,256]{4,3,2,1,0:T(8,128)(2,1)} %copy-done.5) | copy-start | bytes 589828
  119.9 3.0 %copy-start.17 = (bf16[16,16,512]{2,1,0:T(8,128)(2,1)S(1)}, bf16[16,16,512]{2,1,0:T(8,128)(2,1)}, u32[]{:S(2)}) copy-start(bf16[16,16,512]{2,1,0:T(8,128)(2,1)} %get-tuple-element.47) | copy-start | bytes 786436
  121.8 18.8 %collective-permute-start.29 = (bf16[3,3,512,256]{3,2,1,0:T(8,128)(2,1)S(1)}, bf16[3,3,512,256]{3,2,1,0:T(8,128)(2,1)}, u32[]{:S(2)}, u32[]{:S(2)}) collective-permute-start(bf16[3,3,512,256]{3,2,1,0:T(8,128)(2,1)S(1)} %assemble.1.mine), channel_id=1, source_target_pairs={{0,1},{1,0},{2,3},{3,2},{4,5},{5,4},{6,7},{7,6},{8,9},{9,8},{10,11... | collective-permute-start | bytes 7077896 | tf_op jit(solution)/shard_map/ppermute | solution.py:572
  135.7 19.0 %all-to-all-start.2 = ((bf16[16,2,16,512]{3,2,1,0:T(8,128)(2,1)}), bf16[16,2,16,512]{3,2,1,0:T(8,128)(2,1)S(1)}, u32[]{:S(2)}, u32[]{:S(2)}) async-start(bf16[16,2,16,512]{3,2,1,0:T(8,128)(2,1)} %get-tuple-element.49), calls=%async_computation.2 | async-start | bytes 1048576 | tf_op jit(solution)/shard_map/all_to_all | solution.py:562
  (3 other events, 2.6 us)

commit v3 on v2

--- a/solution.py
+++ b/solution.py
@@ -47,9 +47,9 @@
 
 
 class Gather:
-    def __init__(self, unit, flip):
+    def __init__(self, unit, flip, whole):
         turned = jnp.where(flip, unit[::-1], unit)
-        self.chips = lax.axis_size("row") // 2
+        self.chips, self.whole = lax.axis_size("row") // 2, whole
         self.up = self.down = turned[:2]
         self.rest = turned[2]
         self.pieces, self.finals, self.batches, self.sent = [self.up], [], [], 1
@@ -75,17 +75,29 @@
             for kernel in range(self.up.shape[1]):
                 value, pairs = ways[kernel % 2]
                 self.finals.append(lax.ppermute(value[:, kernel : kernel + 1], "row", pairs))
-            batch = jnp.concatenate([piece[0] for piece in self.finals], axis=0)[None]
-            self.batches.append(lax.ppermute(batch, "parts", across))
             return
         self.up = lax.ppermute(self.up, "row", forward)
         self.down = lax.ppermute(self.down, "row", backward)
         self.pieces += [self.up, self.down]
-        count = len(self.pieces)
-        if count == self.chips - 1 or count - self.sent >= self.chips // 4:
-            batch = jnp.stack([piece[0] for piece in self.pieces[self.sent :]])
-            self.batches.append(lax.ppermute(batch, "parts", across))
-            self.sent = count
+        near = len(self.pieces) < self.chips - 1
+        if (near and len(self.pieces) - self.sent >= self.chips // 4) or (not near and self.whole):
+            self.cross(slice(None))
+
+    def cross(self, kernels):
+        across = [(i, i ^ 1) for i in range(lax.axis_size("parts"))]
+        thirds = [piece[0, kernels] for piece in self.pieces[self.sent :]]
+        self.batches.append(lax.ppermute(jnp.stack(thirds), "parts", across))
+        self.sent = len(self.pieces)
+
+    def cross_final(self, kernel):
+        across = [(i, i ^ 1) for i in range(lax.axis_size("parts"))]
+        self.batches.append(lax.ppermute(self.finals[kernel][:1], "parts", across))
+
+    def cross_late(self, kernel, since):
+        across = [(i, i ^ 1) for i in range(lax.axis_size("parts"))]
+        late = self.pieces[since:] + self.finals[kernel : kernel + 1]
+        thirds = [piece[0, -1:] for piece in late]
+        return lax.ppermute(jnp.stack(thirds), "parts", across)
 
     def result(self):
         return self.pieces + self.finals + [self.rest] + self.batches
@@ -99,7 +111,8 @@
     pieces = [piece.at[:, index] for piece in refs[:near]] + [finals[index].at[:, 0]]
     thirds = [rest.at[index]]
     for batch in batches:
-        thirds += [batch.at[i, index] for i in range(batch.shape[0])]
+        kernel = min(index, batch.shape[1] - 1)
+        thirds += [batch.at[i, kernel] for i in range(batch.shape[0])]
     first = where[0]
     share = refs[0].shape[3]
     jobs = []
@@ -249,9 +262,10 @@
     return (values * lax.rsqrt(meansq + 1e-06)).astype(BF16)
 
 
-def window_kernel(picks, y2, *refs):
-    sources, (out, edge), (att, wide, thin) = refs[:6], refs[6:8], refs[8:11]
-    weights, sems = refs[11:17], refs[17]
+def window_kernel(per, picks, y2, *refs):
+    sources, outs, sems = refs[:6], refs[6:-10], refs[-1]
+    (att, wide, thin), weights = refs[-10:-7], refs[-7:-1]
+    out, edge = outs[0], outs[-1]
     copies = [
         pltpu.make_async_copy(source, dest, sems.at[i])
         for i, (source, dest) in enumerate(zip(sources, weights))
@@ -259,7 +273,7 @@
     for copy in copies:
         copy.start()
     w_query, w_key, w_value, w_out, w_in, w_down = weights
-    grid, per, _, channels = out.shape
+    grid, channels = out.shape[0], out.shape[2]
     cells = grid * GRID
     current = jnp.concatenate(
         [
@@ -307,35 +321,37 @@
     latent = (current + lowered).astype(BF16)
     wide_values = latent.astype(F32)
     for r in range(per):
-        out[:, r] = latent[r * cells : (r + 1) * cells].reshape(grid, GRID, channels)
+        out[:, r * GRID : (r + 1) * GRID] = latent[r * cells : (r + 1) * cells].reshape(
+            grid, GRID, channels
+        )
     kept = grid // 2
     for lane in range(0, channels, 128):
         wide[...] = wide_values[:, lane : lane + 128]
-        for d in range(edge.shape[0]):
+        for d in range(picks.shape[0]):
             for r in range(per):
                 first = r * cells + (grid // 4) * GRID + picks[d]
                 thin[pl.ds(d * kept * per + r, kept, stride=per), :] = wide[
                     pl.ds(first, kept, stride=GRID), :
                 ]
-        edge[:, :, lane : lane + 128] = thin[...].astype(BF16).reshape(
-            edge.shape[0], kept * per, 128
+        edge[:, edge.shape[1] - kept * per :, lane : lane + 128] = (
+            thin[...].astype(BF16).reshape(picks.shape[0], kept * per, 128)
         )
 
 
-def windows(picks, y2, w_query, w_key, w_value, w_out, w_in, w_down):
+def windows(joined, picks, y2, w_query, w_key, w_value, w_out, w_in, w_down):
     grid, per, channels = y2.shape[0] * y2.shape[2], y2.shape[3], w_query.shape[0]
     cells, units, dests = grid * GRID, w_in.shape[1], picks.shape[0]
     total = per * cells
     kept = per * grid // 2
     flops = 2 * total * channels * (4 * channels + 2 * units + 2 * cells)
+    shapes = [(grid, per * GRID, channels), (dests, kept, channels)]
+    if joined:
+        shapes = [(grid, per * GRID + kept, channels)]
     return pl.pallas_call(
-        window_kernel,
-        out_shape=(
-            jax.ShapeDtypeStruct((grid, per, GRID, channels), BF16),
-            jax.ShapeDtypeStruct((dests, kept, channels), BF16),
-        ),
+        functools.partial(window_kernel, per),
+        out_shape=tuple(jax.ShapeDtypeStruct(shape, BF16) for shape in shapes),
         in_specs=[SMEM, VMEM] + [ANY] * 6,
-        out_specs=(VMEM, VMEM),
+        out_specs=tuple(VMEM for _ in shapes),
         scratch_shapes=[
             pltpu.VMEM((total, channels), BF16),
             pltpu.VMEM((total, 128), F32),
@@ -364,7 +380,7 @@
     framed, rows, channels = field.shape
     width = framed - 2
     for j in range(framed):
-        column = arrived[info[3 + j]]
+        column = arrived[info[3 + j], pl.ds(arrived.shape[1] - rows, rows)]
         if j == 0:
             column = column * info[1].astype(F32).astype(BF16)
         if j == framed - 1:
@@ -407,8 +423,8 @@
             )
 
 
-def upsample(info, arrived, mine, theirs, width):
-    _, rows, channels = arrived.shape
+def upsample(info, arrived, mine, theirs, rows, width):
+    channels = arrived.shape[2]
     framed = width + 2
     return pl.pallas_call(
         upsample_kernel,
@@ -428,18 +444,20 @@
 
 
 def settle_kernel(arrived, earlier, out, spread):
-    groups, per, cells, channels = arrived.shape
+    per, _, channels = out.shape
+    groups = arrived.shape[0]
+    cells = out.shape[1] // groups
     for r in range(per):
         for lane in range(0, channels, 128):
             for c in range(groups):
                 spread[pl.ds(c, cells, stride=groups), :] = arrived[
-                    c, r, :, lane : lane + 128
+                    c, r * cells : (r + 1) * cells, lane : lane + 128
                 ].astype(F32)
             out[r, :, lane : lane + 128] = spread[...].astype(BF16)
 
 
-def settle(arrived, earlier):
-    groups, per, cells, channels = arrived.shape
+def settle(arrived, earlier, per):
+    groups, cells, channels = arrived.shape[0], GRID, arrived.shape[2]
     return pl.pallas_call(
         settle_kernel,
         out_shape=jax.ShapeDtypeStruct((per, groups * cells, channels), BF16),
@@ -474,9 +492,11 @@
             jnp.concatenate([got, mine], axis=depth),
         )
 
-    pair = Gather(unit_of(jnp.stack([conv_first, conv_second], axis=1)), flip)
-    latent_later, conv_later, _ = lax.optimization_barrier((latent, conv_up, pair.up))
-    last = Gather(unit_of(conv_later[:, None]), flip)
+    units = unit_of(jnp.stack([conv_first, conv_second, conv_up], axis=1))
+    pair, last = Gather(units[:, :2], flip, False), Gather(units[:, 2:], flip, True)
+    count = chips // 2
+    pair.step(1)
+    latent_later, _ = lax.optimization_barrier((latent, pair.up))
 
     edges = []
     for i in range(chips - 1):
@@ -484,23 +504,28 @@
     beside = jnp.where(core == 0, latent_later[:2], latent_later[-2:])
     near = lax.ppermute(beside, "row", edges)
     partner = lax.ppermute(latent_later, "row", swap)
-    count = chips // 2
-    for index in range(1, count):
+    far = lax.ppermute(near, "row", swap)
+    for index in range(2, count):
         if len(pair.batches) > 1:
             pair.after(pair.batches[-2])
         pair.step(index)
-    near_later, _ = lax.optimization_barrier((near, pair.up))
-    far = lax.ppermute(near_later, "row", swap)
-    pair.after(pair.batches[-2])
+    since, joint = pair.sent, list(pair.batches)
+    pair.cross(slice(0, 1))
+    last.after(pair.up)
+    last.step(1)
+    pair.after((joint[-1], near))
     pair.step(count)
-    last.after(pair.finals)
-    last.step(1)
+    pair.finals = last.before(pair.finals)
+    pair.cross_final(0)
     field = jnp.where(
         core == 0,
         jnp.concatenate([near, latent, partner, far], axis=0),
         jnp.concatenate([far, partner, latent, near], axis=0),
     )
-    active = last.before(gelu(field.astype(F32)).astype(BF16))
+    active = gelu(field.astype(F32)).astype(BF16)
+    active, pair.finals[1] = lax.optimization_barrier((active, pair.finals[1]))
+    first_pieces = pair.result()
+    pair.batches = joint + [pair.cross_late(1, since)]
     last.after(active)
     last.step(2)
 
@@ -512,12 +537,14 @@
         [jnp.where(flip, 2, 0)[None], owners, jnp.stack([core, top, bottom])]
     ).astype(jnp.int32)
 
-    y1, active2 = first_conv(where, active, field, pair.result(), 2)
+    y1, active2 = first_conv(where, active, field, first_pieces, 3)
     active2 = last.before(active2)
+    active2, pair.batches = lax.optimization_barrier((active2, pair.batches))
+    second_pieces = pair.result()
     theirs = lax.ppermute(active2, "row", swap)
     last.after(active2)
     last.step(3)
-    y2 = second_conv(where, y1, active2, theirs, pair.result(), 2)
+    y2 = second_conv(where, y1, active2, theirs, second_pieces, 4)
 
     y2 = last.before(y2)
     groups = cols // GRID
@@ -547,35 +574,33 @@
     starts = cols // 4 + width * dests - 1
     column = device // subs
     picks = jnp.clip((starts - column + groups - 1) // groups, 0, GRID - 1).astype(jnp.int32)
-    latent_window, edge = windows(
-        picks, owned, w_query, w_key, w_value, w_out, w_in, w_down
-    )
-
-    edge = last.before(edge)
-    edge = edge.reshape(n, per, -1, channels)
-    arrived = lax.all_to_all(edge, "row", split_axis=0, concat_axis=0, tiled=True)
-    arrived, latent_window = lax.optimization_barrier((arrived, latent_window))
-    if subs > 1:
-        arrived = arrived.reshape(groups, subs, GRID // 2, per, channels)
-        arrived = arrived.transpose(0, 2, 1, 3, 4)
-    arrived = arrived.reshape(groups, subs * per * GRID // 2, channels)
-    returned = lax.all_to_all(
-        latent_window,
+    sent = windows(subs == 1, picks, owned, w_query, w_key, w_value, w_out, w_in, w_down)
+
+    sent = last.before(sent)
+    sent, last.finals = lax.optimization_barrier((sent, last.finals))
+    last.cross_final(0)
+    back = lax.all_to_all(
+        sent[0],
         "row",
         split_axis=0,
         concat_axis=0,
         axis_index_groups=index_groups,
         tiled=True,
     )
-    where_later = lax.optimization_barrier((where, edge))[0]
-    up_mine = assemble(where_later, last.result(), chips)
+    central = back
+    rows = subs * per * GRID // 2
+    if subs > 1:
+        central = lax.all_to_all(sent[1], "row", split_axis=0, concat_axis=0, tiled=True)
+        central = central.reshape(groups, subs, GRID // 2, per, channels)
+        central = central.transpose(0, 2, 1, 3, 4).reshape(groups, rows, channels)
+    up_mine = assemble(where, last.result(), chips)
     up_theirs = lax.ppermute(up_mine, "row", swap)
     sources = (cols // 4 + width * device - 1 + jnp.arange(width + 2, dtype=jnp.int32)) % groups
     info = jnp.concatenate(
         [jnp.stack([core, (device > 0).astype(jnp.int32), (device < n - 1).astype(jnp.int32)]), sources]
     ).astype(jnp.int32)
-    upsampled = upsample(info, arrived, up_mine, up_theirs, width)
-    return (settle(returned, upsampled), upsampled)
+    upsampled = upsample(info, central, up_mine, up_theirs, rows, width)
+    return (settle(back, upsampled, per), upsampled)
 
 
 def solution(mesh):

time: 159 us -> 153 us (0.962)
  starting transfers between devices: 42.2 us -> 56.5 us
  blocking collectives: 12.8 us -> 0 us
  waiting for transfers between devices: 59.6 us -> 50 us
  local copies, waits for them, and re-layouts: 5.86 us -> 9.47 us
    all_to_all x1 -> x0, blocking collectives: 12.8 us -> none  [on_device(): lax.all_to_all(edge, 'row', split_axis=0, concat_axis=0, tiled=True)]
    all_to_all x1, waiting for transfers between devices: 9.2 us -> 19.5 us  [on_device(): lax.all_to_all(sent[0], 'row', split_axis=0, concat_axis=0, axis_index_gr...]
    ppermute x1, waiting for transfers between devices: 8.25 us -> 0.93 us  [on_device(): near = lax.ppermute(beside, 'row', edges)]
    ppermute x1, starting transfers between devices: 0.43 us -> 7.03 us  [on_device(): partner = lax.ppermute(latent_later, 'row', swap)]
    ppermute x3, starting transfers between devices: 1.74 us -> 7.99 us  [step(): self.finals.append(lax.ppermute(value[:, kernel:kernel + 1], 'row', pairs))]
    ppermute x6, waiting for transfers between devices: 15.5 us -> 9.65 us  [step(): self.down = lax.ppermute(self.down, 'row', backward)]
    ppermute x6, waiting for transfers between devices: 5.01 us -> 0.06 us  [step(): self.up = lax.ppermute(self.up, 'row', forward)]
    ppermute x2 -> x1, starting transfers between devices: 4.62 us -> 0.74 us  [unit_of(): got = lax.ppermute(given, 'row', swap)]
  transfers between devices with their start and end apart: 32 -> 32, of which waited for: 11 -> 9; matrix products, arithmetic and copies ran while one was open for 4% -> 4% of each run, Pallas kernels for 18% -> 15%
where the time goes in v3:
time: 153 us; the launch traced here: 152 us
  starting transfers between devices  56.5 us (37%)
  waiting for transfers between devices  50 us (33%)
  Pallas kernels  30.7 us (20%)
  local copies, waits for them, and re-layouts  9.47 us (6%)
  other arithmetic  4.56 us (3%)
    all_to_all x1, waiting for transfers between devices, on_device(): lax.all_to_all(sent[0], 'row', split_axis=0, concat_axis=0, axis_index_gr...  19.5 us
    all_to_all x1, waiting for transfers between devices, on_device(): lax.all_to_all(y2, 'row', split_axis=0, concat_axis=0, axis_index_groups=...  12.6 us
    pallas_call x1, Pallas kernels, windows(): pl.pallas_call(functools.partial(window_kernel, per), out_shape=tuple((ja...  10.3 us
    ppermute x6, waiting for transfers between devices, step(): self.down = lax.ppermute(self.down, 'row', backward)  9.65 us
    ppermute x3, starting transfers between devices, step(): self.finals.append(lax.ppermute(value[:, kernel:kernel + 1], 'row', pairs))  7.99 us
    ppermute x6, starting transfers between devices, step(): self.up = lax.ppermute(self.up, 'row', forward)  7.42 us
    ppermute x1, starting transfers between devices, on_device(): partner = lax.ppermute(latent_later, 'row', swap)  7.03 us
    pallas_call x1, Pallas kernels, first_conv(): pl.pallas_call(functools.partial(first_conv_kernel, step), out_shape=(out...  6.58 us
  transfers between devices with their start and end apart: 32, of which 9 were waited for; matrix products, arithmetic and copies ran while one was open for 4% of the time, Pallas kernels for 15%

profile of v3, /device:TPU:9, one launch (start us, length us, event | category | flops | bytes accessed | tf_op | source)
XLA Modules:
  0.0 152.3 jit_solution(8564088659902943154)
XLA Ops:
  0.7 1.2 pad_maximum_fusion
  2.0 0.7 collective-permute-start
  2.7 1.4 collective-permute-done
  4.7 1.5 collective-permute-start.1
  6.2 8.9 %collective-permute-done.6.refs_2_ = bf16[2,2,3,64,256]{4,3,2,1,0:T(8,128)(2,1)S(1)} collective-permute-done((bf16[2,2,3,64,256]{4,3,2,1,0:T(8,128)(2,1)S(1)}, bf16[2,2,3,64,256]{4,3,2,1,0:T(8,128)(2,1)S(1)}, u32[]{:S(2)}, u32[]{:S(2)}) %collective-permute-start.6) | collective-permute-done | bytes 393248 | tf_op jit(solution)/shard_map/ppermute | solution.py:80
  15.2 1.1 collective-permute-start.7
  16.2 1.2 collective-permute-start.8
  18.0 1.0 slice.106
  19.0 6.3 %collective-permute-start.2 = (bf16[2,256,512]{2,1,0:T(8,128)(2,1)}, bf16[2,256,512]{2,1,0:T(8,128)(2,1)S(1)}, u32[]{:S(2)}, u32[]{:S(2)}) collective-permute-start(bf16[2,256,512]{2,1,0:T(8,128)(2,1)} %param.11), channel_id=1, source_target_pairs={{1,2},{2,1},{3,4},{4,3},{5,6},{6,5},{7,8},{8,7},{9,10},{10,9},{11,... | collective-permute-start | bytes 1572872 | tf_op jit(solution)/shard_map/ppermute | solution.py:505
  25.4 0.8 copy-done.13
  26.1 1.3 collective-permute-start.9
  28.5 0.7 collective-permute-start.10
  29.3 0.9 slice_bitcast_fusion.refs_9_
  30.2 7.0 %collective-permute-start.3 = (bf16[2,256,512]{2,1,0:T(8,128)(2,1)}, bf16[2,256,512]{2,1,0:T(8,128)(2,1)S(1)}, u32[]{:S(2)}, u32[]{:S(2)}) collective-permute-start(bf16[2,256,512]{2,1,0:T(8,128)(2,1)} %param.11), channel_id=1, source_target_pairs={{0,1},{1,0},{2,3},{3,2},{4,5},{5,4},{6,7},{7,6},{8,9},{9,8},{10,11... | collective-permute-start | bytes 1572872 | tf_op jit(solution)/shard_map/ppermute | solution.py:506
  37.2 0.9 collective-permute-done.2
  38.2 1.3 collective-permute-start.14
  40.2 4.1 %collective-permute-start.13 = (bf16[2,1,3,64,256]{4,3,2,1,0:T(8,128)(2,1)S(1)}, bf16[2,1,3,64,256]{4,3,2,1,0:T(8,128)(2,1)S(1)}, u32[]{:S(2)}, u32[]{:S(2)}) collective-permute-start(bf16[2,1,3,64,256]{4,3,2,1,0:T(8,128)(2,1)S(1)} %slice.82), channel_id=1, source_target_pairs={{4,0},{5,1},{8,4},{9,5},{12,8},{13,9},{14,12},{15,13},{10,14},{11,... | collective-permute-start | bytes 589832 | tf_op jit(solution)/shard_map/ppermute | solution.py:77
  44.3 3.7 %collective-permute-start.12 = (bf16[2,1,3,64,256]{4,3,2,1,0:T(8,128)(2,1)S(1)}, bf16[2,1,3,64,256]{4,3,2,1,0:T(8,128)(2,1)S(1)}, u32[]{:S(2)}, u32[]{:S(2)}) collective-permute-start(bf16[2,1,3,64,256]{4,3,2,1,0:T(8,128)(2,1)S(1)} %slice.81), channel_id=1, source_target_pairs={{0,4},{1,5},{4,8},{5,9},{8,12},{9,13},{12,14},{13,15},{14,10},{15,... | collective-permute-start | bytes 589832 | tf_op jit(solution)/shard_map/ppermute | solution.py:77
  48.0 0.8 collective-permute-done.15.refs_2_
  48.8 1.2 collective-permute-start.16
  50.0 3.0 %collective-permute-done.13.refs_8_ = bf16[2,1,3,64,256]{4,3,2,1,0:T(8,128)(2,1)S(1)} collective-permute-done((bf16[2,1,3,64,256]{4,3,2,1,0:T(8,128)(2,1)S(1)}, bf16[2,1,3,64,256]{4,3,2,1,0:T(8,128)(2,1)S(1)}, u32[]{:S(2)}, u32[]{:S(2)}) %collective-permute-start.13) | collective-permute-done | bytes 196640 | tf_op jit(solution)/shard_map/ppermute | solution.py:77
  53.0 1.2 collective-permute-start.20
  54.6 2.0 %fusion.5 = (bf16[8,256,512]{2,1,0:T(8,128)(2,1)S(1)}, bf16[8,256,512]{2,1,0:T(8,128)(2,1)S(1)}) fusion(bf16[2,256,512]{2,1,0:T(8,128)(2,1)S(1)} %collective-permute-done.2, bf16[2,256,512]{2,1,0:T(8,128)(2,1)S(1)} %copy-done.18, bf16[2,256,512]{2,1,0:T(8,128)(2,1)S(1)} %collective-permute-done.3, bf16[2,256,512]{2,1,0:T(8,128)(2,1)S(1)} %collective-permute-done.4, ...), kind=kLoop, calls=%fused_computation.9 | loop fusion | flops 17825792 | bytes 6291457 | tf_op jit(solution)/shard_map/convert_element_type | solution.py:525
  56.6 1.2 collective-permute-start.18
  58.2 1.3 collective-permute-start.21
  59.5 1.8 %collective-permute-done.17.refs_13_ = bf16[1,1,3,64,256]{4,3,2,1,0:T(8,128)(2,1)S(1)} collective-permute-done((bf16[1,1,3,64,256]{4,3,2,1,0:T(8,128)(2,1)S(1)}, bf16[1,1,3,64,256]{4,3,2,1,0:T(8,128)(2,1)S(1)}, u32[]{:S(2)}, u32[]{:S(2)}) %collective-permute-start.17) | collective-permute-done | bytes 98336 | tf_op jit(solution)/shard_map/ppermute | solution.py:94
  61.3 6.6 %first_conv.1 = (bf16[6,256,256]{2,1,0:T(8,128)(2,1)S(1)}, bf16[6,256,256]{2,1,0:T(8,128)(2,1)S(1)}) custom-call(s32[12]{0:T(128)S(1)} %concatenate.18.where, bf16[8,256,512]{2,1,0:T(8,128)(2,1)S(1)} %get-tuple-element.37.act, bf16[8,256,512]{2,1,0:T(8,128)(2,1)S(1)} %get-tuple-element.57.lat, bf16[2,2,3,64,256]{4,3,2,1,0:T(8,128)(2,1)S(1)} %slice.101.refs_0_, ...), custom_call_target="tpu_custom_call" | custom-call | flops 3623878656 | bytes 2359296 | tf_op jit(solution)/shard_map/first_conv/pallas_call | solution.py:199
  67.9 3.0 %collective-permute-start.22 = (bf16[6,256,256]{2,1,0:T(8,128)(2,1)S(1)}, bf16[6,256,256]{2,1,0:T(8,128)(2,1)S(1)}, u32[]{:S(2)}, u32[]{:S(2)}) collective-permute-start(bf16[6,256,256]{2,1,0:T(8,128)(2,1)S(1)} %get-tuple-element.45.mine), channel_id=1, source_target_pairs={{0,1},{1,0},{2,3},{3,2},{4,5},{5,4},{6,7},{7,6},{8,9},{9,8},{10,11... | collective-permute-start | bytes 2359304 | tf_op jit(solution)/shard_map/ppermute | solution.py:544
  71.0 1.3 collective-permute-start.25
  72.3 1.7 %collective-permute-start.23 = (bf16[2,1,3,64,256]{4,3,2,1,0:T(8,128)(2,1)S(1)}, bf16[2,1,3,64,256]{4,3,2,1,0:T(8,128)(2,1)S(1)}, u32[]{:S(2)}, u32[]{:S(2)}) collective-permute-start(bf16[2,1,3,64,256]{4,3,2,1,0:T(8,128)(2,1)S(1)} %collective-permute-done.18.refs_3_), channel_id=1, source_target_pairs={{0,4},{1,5},{4,8},{5,9},{8,12},{9,13},{12,14},{13,15},{14,10},{15,... | collective-permute-start | bytes 589832 | tf_op jit(solution)/shard_map/ppermute | solution.py:79
  74.0 5.8 %second_conv.1 = bf16[16,4,16,256]{3,2,1,0:T(8,128)(2,1)} custom-call(s32[12]{0:T(128)S(1)} %concatenate.18.where, bf16[6,256,256]{2,1,0:T(8,128)(2,1)S(1)} %get-tuple-element.40.y1, bf16[6,256,256]{2,1,0:T(8,128)(2,1)S(1)} %get-tuple-element.45.mine, bf16[6,256,256]{2,1,0:T(8,128)(2,1)S(1)} %collective-permute-done.22.theirs, ...), custom_call_target="tpu_custom_call" | custom-call | flops 2415919104 | bytes 2359296 | tf_op jit(solution)/shard_map/second_conv/pallas_call | solution.py:244
  80.5 6.4 %all-to-all-start = ((bf16[16,4,16,256]{3,2,1,0:T(8,128)(2,1)}), bf16[16,4,16,256]{3,2,1,0:T(8,128)(2,1)S(1)}, u32[]{:S(2)}, u32[]{:S(2)}) async-start(bf16[16,4,16,256]{3,2,1,0:T(8,128)(2,1)} %second_conv.1), calls=%async_computation | async-start | bytes 1048576 | tf_op jit(solution)/shard_map/all_to_all | solution.py:564
  87.4 0.9 collective-permute-start.27
  88.4 12.6 %all-to-all-done = bf16[16,4,16,256]{3,2,1,0:T(8,128)(2,1)S(1)} async-done(((bf16[16,4,16,256]{3,2,1,0:T(8,128)(2,1)}), bf16[16,4,16,256]{3,2,1,0:T(8,128)(2,1)S(1)}, u32[]{:S(2)}, u32[]{:S(2)}) %all-to-all-start) | async-done | bytes 524320 | tf_op jit(solution)/shard_map/all_to_all | solution.py:564
  101.8 10.3 %windows.1 = bf16[16,48,512]{2,1,0:T(8,128)(2,1)} custom-call(s32[16]{0:T(128)} %fusion.8.picks, bf16[8,2,2,2,16,256]{5,4,3,2,1,0:T(8,128)(2,1)} %bitcast.14, bf16[512,512]{1,0:T(8,128)(2,1)} %refs_0_.1, bf16[512,512]{1,0:T(8,128)(2,1)} %refs_1_.1, bf16[512,512]{1,0:T(8,128)(2,1)} %refs_2_.1, bf16[512,512]{1,0:T(8,128)(2,1)} %refs_3_.1, ...), custom_call_target="tpu_custom_call" | custom-call | flops 3489660928 | bytes 2097152 | tf_op jit(solution)/shard_map/windows/pallas_call | solution.py:350
  112.1 1.0 collective-permute-start.28
  113.1 0.9 slice_bitcast_fusion.1.refs_8_
  114.0 0.7 copy-done.7
  114.7 1.0 collective-permute-done.28.refs_12_
  115.7 0.9 copy-done.2
  116.6 0.9 copy-done.8
  117.5 1.9 %assemble.1.mine = bf16[3,3,512,256]{3,2,1,0:T(8,128)(2,1)S(1)} custom-call(s32[12]{0:T(128)S(1)} %concatenate.18.where, bf16[2,1,3,64,256]{4,3,2,1,0:T(8,128)(2,1)S(1)} %slice.107.refs_0_, bf16[2,1,3,64,256]{4,3,2,1,0:T(8,128)(2,1)S(1)} %collective-permute-done.14.refs_1_, bf16[2,1,3,64,256]{4,3,2,1,0:T(8,128)(2,1)S(1)} %collective-permute-done.15.refs_2_, ...), custom_call_target="tpu_custom_call" | custom-call | bytes 4718592 | tf_op jit(solution)/shard_map/assemble/pallas_call | solution.py:141
  119.5 2.0 %collective-permute-start.29 = (bf16[3,3,512,256]{3,2,1,0:T(8,128)(2,1)S(1)}, bf16[3,3,512,256]{3,2,1,0:T(8,128)(2,1)}, u32[]{:S(2)}, u32[]{:S(2)}) collective-permute-start(bf16[3,3,512,256]{3,2,1,0:T(8,128)(2,1)S(1)} %assemble.1.mine), channel_id=1, source_target_pairs={{0,1},{1,0},{2,3},{3,2},{4,5},{5,4},{6,7},{7,6},{8,9},{9,8},{10,11... | collective-permute-start | bytes 7077896 | tf_op jit(solution)/shard_map/ppermute | solution.py:597
  121.5 4.1 %all-to-all-start.1 = ((bf16[16,48,512]{2,1,0:T(8,128)(2,1)}), bf16[16,48,512]{2,1,0:T(8,128)(2,1)S(1)}, u32[]{:S(2)}, u32[]{:S(2)}) async-start(bf16[16,48,512]{2,1,0:T(8,128)(2,1)} %windows.1), calls=%async_computation.1 | async-start | bytes 1572864 | tf_op jit(solution)/shard_map/all_to_all | solution.py:582
  125.7 19.5 %all-to-all-done.1.arrived = bf16[16,48,512]{2,1,0:T(8,128)(2,1)S(1)} async-done(((bf16[16,48,512]{2,1,0:T(8,128)(2,1)}), bf16[16,48,512]{2,1,0:T(8,128)(2,1)S(1)}, u32[]{:S(2)}, u32[]{:S(2)}) %all-to-all-start.1) | async-done | bytes 786464 | tf_op jit(solution)/shard_map/all_to_all | solution.py:582
  145.2 4.9 %upsample.1.earlier = bf16[32,16,512]{2,1,0:T(8,128)(2,1)} custom-call(s32[13]{0:T(128)S(1)} %pad_add_fusion.info, bf16[16,48,512]{2,1,0:T(8,128)(2,1)S(1)} %all-to-all-done.1.arrived, bf16[3,3,512,256]{3,2,1,0:T(8,128)(2,1)S(1)} %assemble.1.mine, bf16[3,3,512,256]{3,2,1,0:T(8,128)(2,1)} %collective-permute-done.29.theirs), custom_call_target="tpu_custom_call" | custom-call | flops 754974720 | bytes 4718592 | tf_op jit(solution)/shard_map/upsample/pallas_call | solution.py:429
  150.1 1.0 copy-done
  151.1 1.2 settle.1
  (105 shorter events, 5.9 us)
Async XLA Ops:
  2.0 2.2 %collective-permute-start = (bf16[3,3,3,32,256]{4,3,2,1,0:T(8,128)(2,1)S(1)}, bf16[3,3,3,32,256]{4,3,2,1,0:T(8,128)(2,1)S(1)}, u32[]{:S(2)}, u32[]{:S(2)}) collective-permute-start(bf16[3,3,3,32,256]{4,3,2,1,0:T(8,128)(2,1)S(1)} %get-tuple-element.59), channel_id=1, source_target_pairs={{0,1},{1,0},{2,3},{3,2},{4,5},{5,4},{6,7},{7,6},{8,9},{9,8},{10,11... | collective-permute-start | bytes 1327112 | tf_op jit(solution)/shard_map/ppermute | solution.py:487
  4.4 11.8 %copy-start.15 = (bf16[3,3,3,64,256]{4,3,2,1,0:T(8,128)(2,1)}, bf16[3,3,3,64,256]{4,3,2,1,0:T(8,128)(2,1)S(1)}, u32[]{:S(2)}) copy-start(bf16[3,3,3,64,256]{4,3,2,1,0:T(8,128)(2,1)S(1)} %maximum_select_fusion.1) | copy-start | bytes 2654212
  4.5 13.4 %copy-start.20 = (s32[8]{0:T(128)S(1)}, s32[8]{0:T(128)}, u32[]{:S(2)}) copy-start(s32[8]{0:T(128)} %constant.133.clone) | copy-start | bytes 100
  4.6 12.8 %copy-start.16 = (bf16[3,2,3,64,256]{4,3,2,1,0:T(8,128)(2,1)}, bf16[3,2,3,64,256]{4,3,2,1,0:T(8,128)(2,1)S(1)}, u32[]{:S(2)}) copy-start(bf16[3,2,3,64,256]{4,3,2,1,0:T(8,128)(2,1)S(1)} %reverse_select_fusion) | copy-start | bytes 1769476
  4.7 10.4 %collective-permute-start.6 = (bf16[2,2,3,64,256]{4,3,2,1,0:T(8,128)(2,1)S(1)}, bf16[2,2,3,64,256]{4,3,2,1,0:T(8,128)(2,1)S(1)}, u32[]{:S(2)}, u32[]{:S(2)}) collective-permute-start(bf16[2,2,3,64,256]{4,3,2,1,0:T(8,128)(2,1)S(1)} %slice.101.refs_0_), channel_id=1, source_target_pairs={{4,0},{5,1},{8,4},{9,5},{12,8},{13,9},{14,12},{15,13},{10,14},{11,... | collective-permute-start | bytes 1179656 | tf_op jit(solution)/shard_map/ppermute | solution.py:80
  4.7 10.4 %collective-permute-start.1 = (bf16[2,2,3,64,256]{4,3,2,1,0:T(8,128)(2,1)S(1)}, bf16[2,2,3,64,256]{4,3,2,1,0:T(8,128)(2,1)S(1)}, u32[]{:S(2)}, u32[]{:S(2)}) collective-permute-start(bf16[2,2,3,64,256]{4,3,2,1,0:T(8,128)(2,1)S(1)} %slice.101.refs_0_), channel_id=1, source_target_pairs={{0,4},{1,5},{4,8},{5,9},{8,12},{9,13},{12,14},{13,15},{14,10},{15,... | collective-permute-start | bytes 1179656 | tf_op jit(solution)/shard_map/ppermute | solution.py:79
  15.2 10.1 %collective-permute-start.7 = (bf16[2,2,3,64,256]{4,3,2,1,0:T(8,128)(2,1)S(1)}, bf16[2,2,3,64,256]{4,3,2,1,0:T(8,128)(2,1)S(1)}, u32[]{:S(2)}, u32[]{:S(2)}) collective-permute-start(bf16[2,2,3,64,256]{4,3,2,1,0:T(8,128)(2,1)S(1)} %collective-permute-done.6.refs_2_), channel_id=1, source_target_pairs={{4,0},{5,1},{8,4},{9,5},{12,8},{13,9},{14,12},{15,13},{10,14},{11,... | collective-permute-start | bytes 1179656 | tf_op jit(solution)/shard_map/ppermute | solution.py:80
  16.2 9.1 %collective-permute-start.8 = (bf16[2,2,3,64,256]{4,3,2,1,0:T(8,128)(2,1)S(1)}, bf16[2,2,3,64,256]{4,3,2,1,0:T(8,128)(2,1)S(1)}, u32[]{:S(2)}, u32[]{:S(2)}) collective-permute-start(bf16[2,2,3,64,256]{4,3,2,1,0:T(8,128)(2,1)S(1)} %pad_maximum_fusion.1), channel_id=1, source_target_pairs={{0,16},{16,0},{1,17},{17,1},{2,18},{18,2},{3,19},{19,3},{4,20},{20... | collective-permute-start | bytes 1179656 | tf_op jit(solution)/shard_map/ppermute | solution.py:89
  17.5 8.7 %collective-permute-start.5 = (bf16[2,2,3,64,256]{4,3,2,1,0:T(8,128)(2,1)S(1)}, bf16[2,2,3,64,256]{4,3,2,1,0:T(8,128)(2,1)S(1)}, u32[]{:S(2)}, u32[]{:S(2)}) collective-permute-start(bf16[2,2,3,64,256]{4,3,2,1,0:T(8,128)(2,1)S(1)} %collective-permute-done.1.refs_1_), channel_id=1, source_target_pairs={{0,4},{1,5},{4,8},{5,9},{8,12},{9,13},{12,14},{13,15},{14,10},{15,... | collective-permute-start | bytes 1179656 | tf_op jit(solution)/shard_map/ppermute | solution.py:79
  19.0 19.2 %collective-permute-start.2 = (bf16[2,256,512]{2,1,0:T(8,128)(2,1)}, bf16[2,256,512]{2,1,0:T(8,128)(2,1)S(1)}, u32[]{:S(2)}, u32[]{:S(2)}) collective-permute-start(bf16[2,256,512]{2,1,0:T(8,128)(2,1)} %param.11), channel_id=1, source_target_pairs={{1,2},{2,1},{3,4},{4,3},{5,6},{6,5},{7,8},{8,7},{9,10},{10,9},{11,... | collective-permute-start | bytes 1572872 | tf_op jit(solution)/shard_map/ppermute | solution.py:505
  25.3 19.0 %copy-start.9 = (bf16[2,2,3,64,256]{4,3,2,1,0:T(8,128)(2,1)}, bf16[2,2,3,64,256]{4,3,2,1,0:T(8,128)(2,1)S(1)}, u32[]{:S(2)}) copy-start(bf16[2,2,3,64,256]{4,3,2,1,0:T(8,128)(2,1)S(1)} %collective-permute-done.7.refs_4_) | copy-start | bytes 1179652
  26.1 12.0 %copy-start.11 = (bf16[2,2,3,64,256]{4,3,2,1,0:T(8,128)(2,1)}, bf16[2,2,3,64,256]{4,3,2,1,0:T(8,128)(2,1)S(1)}, u32[]{:S(2)}) copy-start(bf16[2,2,3,64,256]{4,3,2,1,0:T(8,128)(2,1)S(1)} %collective-permute-done.5.refs_3_) | copy-start | bytes 1179652
  26.1 12.0 %collective-permute-start.9 = (bf16[2,2,3,64,256]{4,3,2,1,0:T(8,128)(2,1)S(1)}, bf16[2,2,3,64,256]{4,3,2,1,0:T(8,128)(2,1)S(1)}, u32[]{:S(2)}, u32[]{:S(2)}) collective-permute-start(bf16[2,2,3,64,256]{4,3,2,1,0:T(8,128)(2,1)S(1)} %collective-permute-done.5.refs_3_), channel_id=1, source_target_pairs={{0,4},{1,5},{4,8},{5,9},{8,12},{9,13},{12,14},{13,15},{14,10},{15,... | collective-permute-start | bytes 1179656 | tf_op jit(solution)/shard_map/ppermute | solution.py:79
  27.6 27.0 %copy-start.18 = (bf16[2,256,512]{2,1,0:T(8,128)(2,1)S(1)}, bf16[2,256,512]{2,1,0:T(8,128)(2,1)}, u32[]{:S(2)}) copy-start(bf16[2,256,512]{2,1,0:T(8,128)(2,1)} %param.11) | copy-start | bytes 1572868
  28.2 11.3 %collective-permute-start.11 = (bf16[2,2,3,64,256]{4,3,2,1,0:T(8,128)(2,1)S(1)}, bf16[2,2,3,64,256]{4,3,2,1,0:T(8,128)(2,1)S(1)}, u32[]{:S(2)}, u32[]{:S(2)}) collective-permute-start(bf16[2,2,3,64,256]{4,3,2,1,0:T(8,128)(2,1)S(1)} %pad_maximum_fusion.2), channel_id=1, source_target_pairs={{0,16},{16,0},{1,17},{17,1},{2,18},{18,2},{3,19},{19,3},{4,20},{20... | collective-permute-start | bytes 1179656 | tf_op jit(solution)/shard_map/ppermute | solution.py:89
  28.5 11.6 %collective-permute-start.10 = (bf16[2,2,3,64,256]{4,3,2,1,0:T(8,128)(2,1)S(1)}, bf16[2,2,3,64,256]{4,3,2,1,0:T(8,128)(2,1)S(1)}, u32[]{:S(2)}, u32[]{:S(2)}) collective-permute-start(bf16[2,2,3,64,256]{4,3,2,1,0:T(8,128)(2,1)S(1)} %collective-permute-done.7.refs_4_), channel_id=1, source_target_pairs={{4,0},{5,1},{8,4},{9,5},{12,8},{13,9},{14,12},{15,13},{10,14},{11,... | collective-permute-start | bytes 1179656 | tf_op jit(solution)/shard_map/ppermute | solution.py:80
  30.2 24.4 %collective-permute-start.3 = (bf16[2,256,512]{2,1,0:T(8,128)(2,1)}, bf16[2,256,512]{2,1,0:T(8,128)(2,1)S(1)}, u32[]{:S(2)}, u32[]{:S(2)}) collective-permute-start(bf16[2,256,512]{2,1,0:T(8,128)(2,1)} %param.11), channel_id=1, source_target_pairs={{0,1},{1,0},{2,3},{3,2},{4,5},{5,4},{6,7},{7,6},{8,9},{9,8},{10,11... | collective-permute-start | bytes 1572872 | tf_op jit(solution)/shard_map/ppermute | solution.py:506
  38.2 16.4 %collective-permute-start.4 = (bf16[2,256,512]{2,1,0:T(8,128)(2,1)S(1)}, bf16[2,256,512]{2,1,0:T(8,128)(2,1)S(1)}, u32[]{:S(2)}, u32[]{:S(2)}) collective-permute-start(bf16[2,256,512]{2,1,0:T(8,128)(2,1)S(1)} %collective-permute-done.2), channel_id=1, source_target_pairs={{0,1},{1,0},{2,3},{3,2},{4,5},{5,4},{6,7},{7,6},{8,9},{9,8},{10,11... | collective-permute-start | bytes 1572872 | tf_op jit(solution)/shard_map/ppermute | solution.py:507
  38.2 6.1 %collective-permute-start.14 = (bf16[2,1,3,64,256]{4,3,2,1,0:T(8,128)(2,1)S(1)}, bf16[2,1,3,64,256]{4,3,2,1,0:T(8,128)(2,1)S(1)}, u32[]{:S(2)}, u32[]{:S(2)}) collective-permute-start(bf16[2,1,3,64,256]{4,3,2,1,0:T(8,128)(2,1)S(1)} %slice.107.refs_0_), channel_id=1, source_target_pairs={{0,4},{1,5},{4,8},{5,9},{8,12},{9,13},{12,14},{13,15},{14,10},{15,... | collective-permute-start | bytes 589832 | tf_op jit(solution)/shard_map/ppermute | solution.py:79
  39.6 9.2 %collective-permute-start.15 = (bf16[2,1,3,64,256]{4,3,2,1,0:T(8,128)(2,1)S(1)}, bf16[2,1,3,64,256]{4,3,2,1,0:T(8,128)(2,1)S(1)}, u32[]{:S(2)}, u32[]{:S(2)}) collective-permute-start(bf16[2,1,3,64,256]{4,3,2,1,0:T(8,128)(2,1)S(1)} %slice.107.refs_0_), channel_id=1, source_target_pairs={{4,0},{5,1},{8,4},{9,5},{12,8},{13,9},{14,12},{15,13},{10,14},{11,... | collective-permute-start | bytes 589832 | tf_op jit(solution)/shard_map/ppermute | solution.py:80
  40.2 12.8 %collective-permute-start.13 = (bf16[2,1,3,64,256]{4,3,2,1,0:T(8,128)(2,1)S(1)}, bf16[2,1,3,64,256]{4,3,2,1,0:T(8,128)(2,1)S(1)}, u32[]{:S(2)}, u32[]{:S(2)}) collective-permute-start(bf16[2,1,3,64,256]{4,3,2,1,0:T(8,128)(2,1)S(1)} %slice.82), channel_id=1, source_target_pairs={{4,0},{5,1},{8,4},{9,5},{12,8},{13,9},{14,12},{15,13},{10,14},{11,... | collective-permute-start | bytes 589832 | tf_op jit(solution)/shard_map/ppermute | solution.py:77
  44.3 9.9 %collective-permute-start.12 = (bf16[2,1,3,64,256]{4,3,2,1,0:T(8,128)(2,1)S(1)}, bf16[2,1,3,64,256]{4,3,2,1,0:T(8,128)(2,1)S(1)}, u32[]{:S(2)}, u32[]{:S(2)}) collective-permute-start(bf16[2,1,3,64,256]{4,3,2,1,0:T(8,128)(2,1)S(1)} %slice.81), channel_id=1, source_target_pairs={{0,4},{1,5},{4,8},{5,9},{8,12},{9,13},{12,14},{13,15},{14,10},{15,... | collective-permute-start | bytes 589832 | tf_op jit(solution)/shard_map/ppermute | solution.py:77
  48.8 9.4 %collective-permute-start.16 = (bf16[2,1,3,64,256]{4,3,2,1,0:T(8,128)(2,1)S(1)}, bf16[2,1,3,64,256]{4,3,2,1,0:T(8,128)(2,1)S(1)}, u32[]{:S(2)}, u32[]{:S(2)}) collective-permute-start(bf16[2,1,3,64,256]{4,3,2,1,0:T(8,128)(2,1)S(1)} %pad_maximum_fusion.4), channel_id=1, source_target_pairs={{0,16},{16,0},{1,17},{17,1},{2,18},{18,2},{3,19},{19,3},{4,20},{20... | collective-permute-start | bytes 589832 | tf_op jit(solution)/shard_map/ppermute | solution.py:89
  53.0 14.9 %collective-permute-start.20 = (bf16[2,1,3,64,256]{4,3,2,1,0:T(8,128)(2,1)S(1)}, bf16[2,1,3,64,256]{4,3,2,1,0:T(8,128)(2,1)S(1)}, u32[]{:S(2)}, u32[]{:S(2)}) collective-permute-start(bf16[2,1,3,64,256]{4,3,2,1,0:T(8,128)(2,1)S(1)} %pad_maximum_fusion.5), channel_id=1, source_target_pairs={{0,16},{16,0},{1,17},{17,1},{2,18},{18,2},{3,19},{19,3},{4,20},{20... | collective-permute-start | bytes 589832 | tf_op jit(solution)/shard_map/ppermute | solution.py:89
  54.2 7.1 %copy-start.10 = (bf16[2,2,3,64,256]{4,3,2,1,0:T(8,128)(2,1)S(1)}, bf16[2,2,3,64,256]{4,3,2,1,0:T(8,128)(2,1)}, u32[]{:S(2)}) copy-start(bf16[2,2,3,64,256]{4,3,2,1,0:T(8,128)(2,1)} %copy-done.9) | copy-start | bytes 1179652
  54.2 7.1 %copy-start.12 = (bf16[2,2,3,64,256]{4,3,2,1,0:T(8,128)(2,1)S(1)}, bf16[2,2,3,64,256]{4,3,2,1,0:T(8,128)(2,1)}, u32[]{:S(2)}) copy-start(bf16[2,2,3,64,256]{4,3,2,1,0:T(8,128)(2,1)} %copy-done.11) | copy-start | bytes 1179652
  54.2 7.1 %copy-start.14 = (bf16[2,2,3,64,256]{4,3,2,1,0:T(8,128)(2,1)S(1)}, bf16[2,2,3,64,256]{4,3,2,1,0:T(8,128)(2,1)}, u32[]{:S(2)}) copy-start(bf16[2,2,3,64,256]{4,3,2,1,0:T(8,128)(2,1)} %copy-done.13) | copy-start | bytes 1179652
  54.3 7.0 %collective-permute-start.17 = (bf16[1,1,3,64,256]{4,3,2,1,0:T(8,128)(2,1)S(1)}, bf16[1,1,3,64,256]{4,3,2,1,0:T(8,128)(2,1)S(1)}, u32[]{:S(2)}, u32[]{:S(2)}) collective-permute-start(bf16[1,1,3,64,256]{4,3,2,1,0:T(8,128)(2,1)S(1)} %slice.88), channel_id=1, source_target_pairs={{0,16},{16,0},{1,17},{17,1},{2,18},{18,2},{3,19},{19,3},{4,20},{20... | collective-permute-start | bytes 294920 | tf_op jit(solution)/shard_map/ppermute | solution.py:94
  56.6 11.3 %collective-permute-start.18 = (bf16[2,1,3,64,256]{4,3,2,1,0:T(8,128)(2,1)S(1)}, bf16[2,1,3,64,256]{4,3,2,1,0:T(8,128)(2,1)S(1)}, u32[]{:S(2)}, u32[]{:S(2)}) collective-permute-start(bf16[2,1,3,64,256]{4,3,2,1,0:T(8,128)(2,1)S(1)} %collective-permute-done.14.refs_1_), channel_id=1, source_target_pairs={{0,4},{1,5},{4,8},{5,9},{8,12},{9,13},{12,14},{13,15},{14,10},{15,... | collective-permute-start | bytes 589832 | tf_op jit(solution)/shard_map/ppermute | solution.py:79
  57.8 10.1 %collective-permute-start.19 = (bf16[2,1,3,64,256]{4,3,2,1,0:T(8,128)(2,1)S(1)}, bf16[2,1,3,64,256]{4,3,2,1,0:T(8,128)(2,1)S(1)}, u32[]{:S(2)}, u32[]{:S(2)}) collective-permute-start(bf16[2,1,3,64,256]{4,3,2,1,0:T(8,128)(2,1)S(1)} %collective-permute-done.15.refs_2_), channel_id=1, source_target_pairs={{4,0},{5,1},{8,4},{9,5},{12,8},{13,9},{14,12},{15,13},{10,14},{11,... | collective-permute-start | bytes 589832 | tf_op jit(solution)/shard_map/ppermute | solution.py:80
  58.2 9.7 %collective-permute-start.21 = (bf16[3,1,3,64,256]{4,3,2,1,0:T(8,128)(2,1)S(1)}, bf16[3,1,3,64,256]{4,3,2,1,0:T(8,128)(2,1)S(1)}, u32[]{:S(2)}, u32[]{:S(2)}) collective-permute-start(bf16[3,1,3,64,256]{4,3,2,1,0:T(8,128)(2,1)S(1)} %pad_maximum_fusion.3), channel_id=1, source_target_pairs={{0,16},{16,0},{1,17},{17,1},{2,18},{18,2},{3,19},{19,3},{4,20},{20... | collective-permute-start | bytes 884744 | tf_op jit(solution)/shard_map/ppermute | solution.py:100
  67.9 4.4 %copy-start.3 = (bf16[2,1,3,64,256]{4,3,2,1,0:T(8,128)(2,1)}, bf16[2,1,3,64,256]{4,3,2,1,0:T(8,128)(2,1)S(1)}, u32[]{:S(2)}) copy-start(bf16[2,1,3,64,256]{4,3,2,1,0:T(8,128)(2,1)S(1)} %collective-permute-done.20.refs_9_) | copy-start | bytes 589828
  67.9 6.1 %collective-permute-start.22 = (bf16[6,256,256]{2,1,0:T(8,128)(2,1)S(1)}, bf16[6,256,256]{2,1,0:T(8,128)(2,1)S(1)}, u32[]{:S(2)}, u32[]{:S(2)}) collective-permute-start(bf16[6,256,256]{2,1,0:T(8,128)(2,1)S(1)} %get-tuple-element.45.mine), channel_id=1, source_target_pairs={{0,1},{1,0},{2,3},{3,2},{4,5},{5,4},{6,7},{7,6},{8,9},{9,8},{10,11... | collective-permute-start | bytes 2359304 | tf_op jit(solution)/shard_map/ppermute | solution.py:544
  71.0 8.8 %collective-permute-start.25 = (bf16[2,1,3,64,256]{4,3,2,1,0:T(8,128)(2,1)S(1)}, bf16[2,1,3,64,256]{4,3,2,1,0:T(8,128)(2,1)S(1)}, u32[]{:S(2)}, u32[]{:S(2)}) collective-permute-start(bf16[2,1,3,64,256]{4,3,2,1,0:T(8,128)(2,1)S(1)} %pad_maximum_fusion.6), channel_id=1, source_target_pairs={{0,16},{16,0},{1,17},{17,1},{2,18},{18,2},{3,19},{19,3},{4,20},{20... | collective-permute-start | bytes 589832 | tf_op jit(solution)/shard_map/ppermute | solution.py:89
  72.3 8.2 %collective-permute-start.23 = (bf16[2,1,3,64,256]{4,3,2,1,0:T(8,128)(2,1)S(1)}, bf16[2,1,3,64,256]{4,3,2,1,0:T(8,128)(2,1)S(1)}, u32[]{:S(2)}, u32[]{:S(2)}) collective-permute-start(bf16[2,1,3,64,256]{4,3,2,1,0:T(8,128)(2,1)S(1)} %collective-permute-done.18.refs_3_), channel_id=1, source_target_pairs={{0,4},{1,5},{4,8},{5,9},{8,12},{9,13},{12,14},{13,15},{14,10},{15,... | collective-permute-start | bytes 589832 | tf_op jit(solution)/shard_map/ppermute | solution.py:79
  74.0 6.5 %collective-permute-start.24 = (bf16[2,1,3,64,256]{4,3,2,1,0:T(8,128)(2,1)S(1)}, bf16[2,1,3,64,256]{4,3,2,1,0:T(8,128)(2,1)S(1)}, u32[]{:S(2)}, u32[]{:S(2)}) collective-permute-start(bf16[2,1,3,64,256]{4,3,2,1,0:T(8,128)(2,1)S(1)} %collective-permute-done.19.refs_4_), channel_id=1, source_target_pairs={{4,0},{5,1},{8,4},{9,5},{12,8},{13,9},{14,12},{15,13},{10,14},{11,... | collective-permute-start | bytes 589832 | tf_op jit(solution)/shard_map/ppermute | solution.py:80
  80.5 31.6 %copy-start.1 = (bf16[2,1,3,64,256]{4,3,2,1,0:T(8,128)(2,1)}, bf16[2,1,3,64,256]{4,3,2,1,0:T(8,128)(2,1)S(1)}, u32[]{:S(2)}) copy-start(bf16[2,1,3,64,256]{4,3,2,1,0:T(8,128)(2,1)S(1)} %collective-permute-done.24.refs_6_) | copy-start | bytes 589828
  80.5 20.5 %all-to-all-start = ((bf16[16,4,16,256]{3,2,1,0:T(8,128)(2,1)}), bf16[16,4,16,256]{3,2,1,0:T(8,128)(2,1)S(1)}, u32[]{:S(2)}, u32[]{:S(2)}) async-start(bf16[16,4,16,256]{3,2,1,0:T(8,128)(2,1)} %second_conv.1), calls=%async_computation | async-start | bytes 1048576 | tf_op jit(solution)/shard_map/all_to_all | solution.py:564
  87.4 26.6 %collective-permute-start.27 = (bf16[2,1,3,64,256]{4,3,2,1,0:T(8,128)(2,1)S(1)}, bf16[2,1,3,64,256]{4,3,2,1,0:T(8,128)(2,1)S(1)}, u32[]{:S(2)}, u32[]{:S(2)}) collective-permute-start(bf16[2,1,3,64,256]{4,3,2,1,0:T(8,128)(2,1)S(1)} %pad_maximum_fusion.7), channel_id=1, source_target_pairs={{0,16},{16,0},{1,17},{17,1},{2,18},{18,2},{3,19},{19,3},{4,20},{20... | collective-permute-start | bytes 589832 | tf_op jit(solution)/shard_map/ppermute | solution.py:89
  101.0 11.1 %collective-permute-start.26 = (bf16[2,1,3,64,256]{4,3,2,1,0:T(8,128)(2,1)S(1)}, bf16[2,1,3,64,256]{4,3,2,1,0:T(8,128)(2,1)S(1)}, u32[]{:S(2)}, u32[]{:S(2)}) collective-permute-start(bf16[2,1,3,64,256]{4,3,2,1,0:T(8,128)(2,1)S(1)} %collective-permute-done.23.refs_5_), channel_id=1, source_target_pairs={{0,4},{1,5},{4,8},{5,9},{8,12},{9,13},{12,14},{13,15},{14,10},{15,... | collective-permute-start | bytes 589832 | tf_op jit(solution)/shard_map/ppermute | solution.py:77
  101.8 13.9 %copy-start.4 = (bf16[2,1,3,64,256]{4,3,2,1,0:T(8,128)(2,1)S(1)}, bf16[2,1,3,64,256]{4,3,2,1,0:T(8,128)(2,1)}, u32[]{:S(2)}) copy-start(bf16[2,1,3,64,256]{4,3,2,1,0:T(8,128)(2,1)} %copy-done.3) | copy-start | bytes 589828
  101.8 13.9 %copy-start.6 = (bf16[2,1,3,64,256]{4,3,2,1,0:T(8,128)(2,1)S(1)}, bf16[2,1,3,64,256]{4,3,2,1,0:T(8,128)(2,1)}, u32[]{:S(2)}) copy-start(bf16[2,1,3,64,256]{4,3,2,1,0:T(8,128)(2,1)} %copy-done.5) | copy-start | bytes 589828
  112.1 3.5 %collective-permute-start.28 = (bf16[1,1,3,64,256]{4,3,2,1,0:T(8,128)(2,1)S(1)}, bf16[1,1,3,64,256]{4,3,2,1,0:T(8,128)(2,1)S(1)}, u32[]{:S(2)}, u32[]{:S(2)}) collective-permute-start(bf16[1,1,3,64,256]{4,3,2,1,0:T(8,128)(2,1)S(1)} %slice.99), channel_id=1, source_target_pairs={{0,16},{16,0},{1,17},{17,1},{2,18},{18,2},{3,19},{19,3},{4,20},{20... | collective-permute-start | bytes 294920 | tf_op jit(solution)/shard_map/ppermute | solution.py:94
  115.7 0.9 copy-start.2
  116.6 0.9 copy-start.8
  119.5 25.7 %collective-permute-start.29 = (bf16[3,3,512,256]{3,2,1,0:T(8,128)(2,1)S(1)}, bf16[3,3,512,256]{3,2,1,0:T(8,128)(2,1)}, u32[]{:S(2)}, u32[]{:S(2)}) collective-permute-start(bf16[3,3,512,256]{3,2,1,0:T(8,128)(2,1)S(1)} %assemble.1.mine), channel_id=1, source_target_pairs={{0,1},{1,0},{2,3},{3,2},{4,5},{5,4},{6,7},{7,6},{8,9},{9,8},{10,11... | collective-permute-start | bytes 7077896 | tf_op jit(solution)/shard_map/ppermute | solution.py:597
  121.5 23.7 %all-to-all-start.1 = ((bf16[16,48,512]{2,1,0:T(8,128)(2,1)}), bf16[16,48,512]{2,1,0:T(8,128)(2,1)S(1)}, u32[]{:S(2)}, u32[]{:S(2)}) async-start(bf16[16,48,512]{2,1,0:T(8,128)(2,1)} %windows.1), calls=%async_computation.1 | async-start | bytes 1572864 | tf_op jit(solution)/shard_map/all_to_all | solution.py:582
  150.1 1.0 copy-start
  (5 other events, 3.7 us)

commit v4 on v3

--- a/solution.py
+++ b/solution.py
@@ -103,12 +103,13 @@
         return self.pieces + self.finals + [self.rest] + self.batches
 
 
-def start_copies(where, refs, index, target, sems):
+def start_copies(where, refs, index, target, sems, final=True):
     chips = target.shape[2] // refs[0].shape[3]
-    near, kernels = chips - 1, refs[0].shape[1]
+    near, kernels = chips - 1, refs[0].shape[1] if final else 0
     finals, rest = refs[near : near + kernels], refs[near + kernels]
     batches = refs[near + kernels + 1 :]
-    pieces = [piece.at[:, index] for piece in refs[:near]] + [finals[index].at[:, 0]]
+    pieces = [piece.at[:, index] for piece in refs[:near]]
+    pieces += [piece.at[:, 0] for piece in finals[index : index + 1]]
     thirds = [rest.at[index]]
     for batch in batches:
         kernel = min(index, batch.shape[1] - 1)
@@ -131,7 +132,7 @@
 
 def assemble_kernel(where, *refs):
     target, sems = refs[-2:]
-    for copy in start_copies(where, refs[:-2], 0, target, sems):
+    for copy in start_copies(where, refs[:-2], 0, target, sems, False):
         copy.wait()
 
 
@@ -368,7 +369,8 @@
     )(picks, y2, w_query, w_key, w_value, w_out, w_in, w_down)
 
 
-def upsample_kernel(info, arrived, mine, theirs, out, field, weights, spread, sems):
+def upsample_kernel(info, where, arrived, mine, theirs, *refs):
+    ends, (out, field, weights, spread, sems) = refs[:4], refs[4:]
     taps, depth, half = mine.shape[0], mine.shape[2], mine.shape[3]
     core = info[0]
     copies = []
@@ -387,6 +389,19 @@
             column = column * info[2].astype(F32).astype(BF16)
         field[j] = column
     for copy in copies:
+        copy.wait()
+    share = ends[0].shape[3]
+    far = where[where.shape[0] - 4]
+    depth_rows = pl.ds(pl.multiple_of(far * share, share), share)
+    late = []
+    for side, (pair, third) in ((core, ends[:2]), (1 - core, ends[2:])):
+        lanes = pl.ds(pl.multiple_of(side * half, half), half)
+        for source, tap in ((pair.at[0, 0], where[0]), (pair.at[1, 0], 1), (third.at[0, 0], 2 - where[0])):
+            target = weights.at[tap, :, depth_rows, lanes]
+            late.append(pltpu.make_async_copy(source, target, sems.at[2 + len(late)]))
+    for copy in late:
+        copy.start()
+    for copy in late:
         copy.wait()
     flat = field[...].reshape(framed * rows, channels)
     size = width * rows
@@ -423,24 +438,24 @@
             )
 
 
-def upsample(info, arrived, mine, theirs, rows, width):
+def upsample(info, where, arrived, mine, theirs, ends, rows, width):
     channels = arrived.shape[2]
     framed = width + 2
     return pl.pallas_call(
         upsample_kernel,
         out_shape=jax.ShapeDtypeStruct((2 * rows, 2 * width, channels), BF16),
-        in_specs=[SMEM, VMEM, ANY, ANY],
+        in_specs=[SMEM, SMEM, VMEM] + [ANY] * 6,
         out_specs=VMEM,
         scratch_shapes=[
             pltpu.VMEM((framed, rows, channels), BF16),
             pltpu.VMEM((3, 3, channels, channels), BF16),
             pltpu.VMEM((4 * rows * width, 128), F32),
-            pltpu.SemaphoreType.DMA((2,)),
+            pltpu.SemaphoreType.DMA((8,)),
         ],
         compiler_params=params(40),
         cost_estimate=cost(18 * framed * rows * channels * channels, 18 * channels * channels),
         name="upsample",
-    )(info, arrived, mine, theirs)
+    )(info, where, arrived, mine, theirs, *ends)
 
 
 def settle_kernel(arrived, earlier, out, spread):
@@ -543,7 +558,8 @@
     second_pieces = pair.result()
     theirs = lax.ppermute(active2, "row", swap)
     last.after(active2)
-    last.step(3)
+    for index in range(3, count):
+        last.step(index)
     y2 = second_conv(where, y1, active2, theirs, second_pieces, 4)
 
     y2 = last.before(y2)
@@ -564,9 +580,11 @@
     owned = lax.all_to_all(
         y2, "row", split_axis=0, concat_axis=0, axis_index_groups=index_groups, tiled=True
     )
+    up_mine = assemble(where, last.result(), chips)
+    owned, _ = lax.optimization_barrier((owned, up_mine))
+    up_theirs = lax.ppermute(up_mine, "row", swap)
     last.after(owned)
-    for index in range(4, count + 1):
-        last.step(index)
+    last.step(count)
     sides = 2 if subs == 1 else 1
     owned = owned.reshape(GRID // 2, sides, 2, per, GRID, channels // sides)
     width = cols // 2 // n
@@ -593,13 +611,13 @@
         central = lax.all_to_all(sent[1], "row", split_axis=0, concat_axis=0, tiled=True)
         central = central.reshape(groups, subs, GRID // 2, per, channels)
         central = central.transpose(0, 2, 1, 3, 4).reshape(groups, rows, channels)
-    up_mine = assemble(where, last.result(), chips)
-    up_theirs = lax.ppermute(up_mine, "row", swap)
+    ends = [last.finals[0], last.batches[-1]]
+    ends += [lax.ppermute(end, "row", swap) for end in ends]
     sources = (cols // 4 + width * device - 1 + jnp.arange(width + 2, dtype=jnp.int32)) % groups
     info = jnp.concatenate(
         [jnp.stack([core, (device > 0).astype(jnp.int32), (device < n - 1).astype(jnp.int32)]), sources]
     ).astype(jnp.int32)
-    upsampled = upsample(info, central, up_mine, up_theirs, rows, width)
+    upsampled = upsample(info, where, central, up_mine, up_theirs, ends, rows, width)
     return (settle(back, upsampled, per), upsampled)
 
 

time: 153 us -> 146 us (0.954)
  waiting for transfers between devices: 50 us -> 38.5 us
  local copies, waits for them, and re-layouts: 9.47 us -> 12.2 us
  starting transfers between devices: 56.5 us -> 58.3 us
    all_to_all x1, waiting for transfers between devices: 12.6 us -> 1.68 us  [on_device(): lax.all_to_all(y2, 'row', split_axis=0, concat_axis=0, axis_index_groups=...]
    all_to_all x1, waiting for transfers between devices: 19.5 us -> 12.3 us  [on_device(): lax.all_to_all(sent[0], 'row', split_axis=0, concat_axis=0, axis_index_gr...]
    ppermute x6, waiting for transfers between devices: 0.02 us -> 4.24 us  [cross(): self.batches.append(lax.ppermute(jnp.stack(thirds), 'parts', across))]
    unnamed x42 -> x44, local copies, waits for them, and re-layouts: 6.23 us -> 8.98 us
    ppermute x2, waiting for transfers between devices: 2.79 us -> 4.94 us  [cross_final(): self.batches.append(lax.ppermute(self.finals[kernel][:1], 'parts', across))]
  transfers between devices with their start and end apart: 32 -> 34, of which waited for: 9 -> 11; matrix products, arithmetic and copies ran while one was open for 4% -> 4% of each run, Pallas kernels for 15% -> 17%
where the time goes in v4:
time: 146 us; the launch traced here: 145 us
  starting transfers between devices  58.3 us (40%)
  waiting for transfers between devices  38.5 us (26%)
  Pallas kernels  30.6 us (21%)
  local copies, waits for them, and re-layouts  12.2 us (8%)
  other arithmetic  4.54 us (3%)
    all_to_all x1, waiting for transfers between devices, on_device(): lax.all_to_all(sent[0], 'row', split_axis=0, concat_axis=0, axis_index_gr...  12.3 us
    pallas_call x1, Pallas kernels, windows(): pl.pallas_call(functools.partial(window_kernel, per), out_shape=tuple((ja...  10.3 us
    ppermute x6, waiting for transfers between devices, step(): self.down = lax.ppermute(self.down, 'row', backward)  9.65 us
    unnamed x44, local copies, waits for them, and re-layouts  8.98 us
    ppermute x3, starting transfers between devices, step(): self.finals.append(lax.ppermute(value[:, kernel:kernel + 1], 'row', pairs))  8.03 us
    ppermute x6, starting transfers between devices, step(): self.up = lax.ppermute(self.up, 'row', forward)  7.42 us
    ppermute x1, starting transfers between devices, on_device(): partner = lax.ppermute(latent_later, 'row', swap)  6.99 us
    all_to_all x1, starting transfers between devices, on_device(): lax.all_to_all(y2, 'row', split_axis=0, concat_axis=0, axis_index_groups=...  6.69 us
  transfers between devices with their start and end apart: 34, of which 11 were waited for; matrix products, arithmetic and copies ran while one was open for 4% of the time, Pallas kernels for 17%

profile of v4, /device:TPU:9, one launch (start us, length us, event | category | flops | bytes accessed | tf_op | source)
XLA Modules:
  0.0 145.3 jit_solution(602713411914088652)
XLA Ops:
  0.7 1.2 pad_maximum_fusion
  2.7 1.4 collective-permute-done
  4.7 1.5 collective-permute-start.1
  6.2 8.9 %collective-permute-done.6.refs_2_ = bf16[2,2,3,64,256]{4,3,2,1,0:T(8,128)(2,1)S(1)} collective-permute-done((bf16[2,2,3,64,256]{4,3,2,1,0:T(8,128)(2,1)S(1)}, bf16[2,2,3,64,256]{4,3,2,1,0:T(8,128)(2,1)S(1)}, u32[]{:S(2)}, u32[]{:S(2)}) %collective-permute-start.6) | collective-permute-done | bytes 393248 | tf_op jit(solution)/shard_map/ppermute | solution.py:80
  15.2 1.1 collective-permute-start.7
  16.2 1.2 collective-permute-start.8
  18.0 1.0 slice.106
  19.0 6.3 %collective-permute-start.2 = (bf16[2,256,512]{2,1,0:T(8,128)(2,1)}, bf16[2,256,512]{2,1,0:T(8,128)(2,1)S(1)}, u32[]{:S(2)}, u32[]{:S(2)}) collective-permute-start(bf16[2,256,512]{2,1,0:T(8,128)(2,1)} %param.11), channel_id=1, source_target_pairs={{1,2},{2,1},{3,4},{4,3},{5,6},{6,5},{7,8},{8,7},{9,10},{10,9},{11,... | collective-permute-start | bytes 1572872 | tf_op jit(solution)/shard_map/ppermute | solution.py:520
  26.1 1.3 collective-permute-start.9
  29.3 0.9 slice_bitcast_fusion.refs_9_
  30.2 7.0 %collective-permute-start.3 = (bf16[2,256,512]{2,1,0:T(8,128)(2,1)}, bf16[2,256,512]{2,1,0:T(8,128)(2,1)S(1)}, u32[]{:S(2)}, u32[]{:S(2)}) collective-permute-start(bf16[2,256,512]{2,1,0:T(8,128)(2,1)} %param.11), channel_id=1, source_target_pairs={{0,1},{1,0},{2,3},{3,2},{4,5},{5,4},{6,7},{7,6},{8,9},{9,8},{10,11... | collective-permute-start | bytes 1572872 | tf_op jit(solution)/shard_map/ppermute | solution.py:521
  37.2 1.0 collective-permute-done.2
  38.2 1.3 collective-permute-start.14
  40.1 4.2 %collective-permute-start.13 = (bf16[2,1,3,64,256]{4,3,2,1,0:T(8,128)(2,1)S(1)}, bf16[2,1,3,64,256]{4,3,2,1,0:T(8,128)(2,1)S(1)}, u32[]{:S(2)}, u32[]{:S(2)}) collective-permute-start(bf16[2,1,3,64,256]{4,3,2,1,0:T(8,128)(2,1)S(1)} %slice.82), channel_id=1, source_target_pairs={{4,0},{5,1},{8,4},{9,5},{12,8},{13,9},{14,12},{15,13},{10,14},{11,... | collective-permute-start | bytes 589832 | tf_op jit(solution)/shard_map/ppermute | solution.py:77
  44.3 3.6 %collective-permute-start.12 = (bf16[2,1,3,64,256]{4,3,2,1,0:T(8,128)(2,1)S(1)}, bf16[2,1,3,64,256]{4,3,2,1,0:T(8,128)(2,1)S(1)}, u32[]{:S(2)}, u32[]{:S(2)}) collective-permute-start(bf16[2,1,3,64,256]{4,3,2,1,0:T(8,128)(2,1)S(1)} %slice.81), channel_id=1, source_target_pairs={{0,4},{1,5},{4,8},{5,9},{8,12},{9,13},{12,14},{13,15},{14,10},{15,... | collective-permute-start | bytes 589832 | tf_op jit(solution)/shard_map/ppermute | solution.py:77
  48.8 1.2 collective-permute-start.16
  50.0 3.0 %collective-permute-done.13.refs_8_ = bf16[2,1,3,64,256]{4,3,2,1,0:T(8,128)(2,1)S(1)} collective-permute-done((bf16[2,1,3,64,256]{4,3,2,1,0:T(8,128)(2,1)S(1)}, bf16[2,1,3,64,256]{4,3,2,1,0:T(8,128)(2,1)S(1)}, u32[]{:S(2)}, u32[]{:S(2)}) %collective-permute-start.13) | collective-permute-done | bytes 196640 | tf_op jit(solution)/shard_map/ppermute | solution.py:77
  53.0 1.2 collective-permute-start.20
  54.6 2.0 %fusion.5 = (bf16[8,256,512]{2,1,0:T(8,128)(2,1)S(1)}, bf16[8,256,512]{2,1,0:T(8,128)(2,1)S(1)}) fusion(bf16[2,256,512]{2,1,0:T(8,128)(2,1)S(1)} %collective-permute-done.2, bf16[2,256,512]{2,1,0:T(8,128)(2,1)S(1)} %copy-done.20, bf16[2,256,512]{2,1,0:T(8,128)(2,1)S(1)} %collective-permute-done.3, bf16[2,256,512]{2,1,0:T(8,128)(2,1)S(1)} %collective-permute-done.4, ...), kind=kLoop, calls=%fused_computation.9 | loop fusion | flops 17825792 | bytes 6291457 | tf_op jit(solution)/shard_map/convert_element_type | solution.py:540
  56.6 1.2 collective-permute-start.18
  58.2 1.3 collective-permute-start.21
  59.5 1.8 %collective-permute-done.17.refs_13_ = bf16[1,1,3,64,256]{4,3,2,1,0:T(8,128)(2,1)S(1)} collective-permute-done((bf16[1,1,3,64,256]{4,3,2,1,0:T(8,128)(2,1)S(1)}, bf16[1,1,3,64,256]{4,3,2,1,0:T(8,128)(2,1)S(1)}, u32[]{:S(2)}, u32[]{:S(2)}) %collective-permute-start.17) | collective-permute-done | bytes 98336 | tf_op jit(solution)/shard_map/ppermute | solution.py:94
  61.3 6.6 %first_conv.1 = (bf16[6,256,256]{2,1,0:T(8,128)(2,1)S(1)}, bf16[6,256,256]{2,1,0:T(8,128)(2,1)S(1)}) custom-call(s32[12]{0:T(128)S(1)} %concatenate.18.where, bf16[8,256,512]{2,1,0:T(8,128)(2,1)S(1)} %get-tuple-element.38.act, bf16[8,256,512]{2,1,0:T(8,128)(2,1)S(1)} %get-tuple-element.59.lat, bf16[2,2,3,64,256]{4,3,2,1,0:T(8,128)(2,1)S(1)} %slice.101.refs_0_, ...), custom_call_target="tpu_custom_call" | custom-call | flops 3623878656 | bytes 2359296 | tf_op jit(solution)/shard_map/first_conv/pallas_call | solution.py:200
  67.9 3.0 %collective-permute-start.22 = (bf16[6,256,256]{2,1,0:T(8,128)(2,1)S(1)}, bf16[6,256,256]{2,1,0:T(8,128)(2,1)S(1)}, u32[]{:S(2)}, u32[]{:S(2)}) collective-permute-start(bf16[6,256,256]{2,1,0:T(8,128)(2,1)S(1)} %get-tuple-element.46.mine), channel_id=1, source_target_pairs={{0,1},{1,0},{2,3},{3,2},{4,5},{5,4},{6,7},{7,6},{8,9},{9,8},{10,11... | collective-permute-start | bytes 2359304 | tf_op jit(solution)/shard_map/ppermute | solution.py:559
  71.0 1.3 collective-permute-start.25
  72.3 1.7 %collective-permute-start.23 = (bf16[2,1,3,64,256]{4,3,2,1,0:T(8,128)(2,1)S(1)}, bf16[2,1,3,64,256]{4,3,2,1,0:T(8,128)(2,1)S(1)}, u32[]{:S(2)}, u32[]{:S(2)}) collective-permute-start(bf16[2,1,3,64,256]{4,3,2,1,0:T(8,128)(2,1)S(1)} %collective-permute-done.18.refs_3_), channel_id=1, source_target_pairs={{0,4},{1,5},{4,8},{5,9},{8,12},{9,13},{12,14},{13,15},{14,10},{15,... | collective-permute-start | bytes 589832 | tf_op jit(solution)/shard_map/ppermute | solution.py:79
  74.0 5.8 %second_conv.1 = bf16[16,4,16,256]{3,2,1,0:T(8,128)(2,1)} custom-call(s32[12]{0:T(128)S(1)} %concatenate.18.where, bf16[6,256,256]{2,1,0:T(8,128)(2,1)S(1)} %get-tuple-element.41.y1, bf16[6,256,256]{2,1,0:T(8,128)(2,1)S(1)} %get-tuple-element.46.mine, bf16[6,256,256]{2,1,0:T(8,128)(2,1)S(1)} %collective-permute-done.22.theirs, ...), custom_call_target="tpu_custom_call" | custom-call | flops 2415919104 | bytes 2359296 | tf_op jit(solution)/shard_map/second_conv/pallas_call | solution.py:245
  80.5 6.7 %all-to-all-start = ((bf16[16,4,16,256]{3,2,1,0:T(8,128)(2,1)}), bf16[16,4,16,256]{3,2,1,0:T(8,128)(2,1)}, u32[]{:S(2)}, u32[]{:S(2)}) async-start(bf16[16,4,16,256]{3,2,1,0:T(8,128)(2,1)} %second_conv.1), calls=%async_computation | async-start | bytes 1048576 | tf_op jit(solution)/shard_map/all_to_all | solution.py:580
  87.3 1.2 collective-permute-start.26
  88.4 0.9 slice_bitcast_fusion.1.refs_7_
  89.3 4.2 %collective-permute-done.26.refs_10_ = bf16[2,1,3,64,256]{4,3,2,1,0:T(8,128)(2,1)S(1)} collective-permute-done((bf16[2,1,3,64,256]{4,3,2,1,0:T(8,128)(2,1)S(1)}, bf16[2,1,3,64,256]{4,3,2,1,0:T(8,128)(2,1)S(1)}, u32[]{:S(2)}, u32[]{:S(2)}) %collective-permute-start.26) | collective-permute-done | bytes 196640 | tf_op jit(solution)/shard_map/ppermute | solution.py:89
  93.6 0.9 copy-done.2
  94.5 0.9 copy-done.4
  95.4 0.9 copy-done.6
  96.3 1.8 %assemble.1.mine = bf16[3,3,512,256]{3,2,1,0:T(8,128)(2,1)S(1)} custom-call(s32[12]{0:T(128)S(1)} %concatenate.18.where, bf16[2,1,3,64,256]{4,3,2,1,0:T(8,128)(2,1)S(1)} %slice.107.refs_0_, bf16[2,1,3,64,256]{4,3,2,1,0:T(8,128)(2,1)S(1)} %collective-permute-done.14.refs_1_, bf16[2,1,3,64,256]{4,3,2,1,0:T(8,128)(2,1)S(1)} %collective-permute-done.15.refs_2_, ...), custom_call_target="tpu_custom_call" | custom-call | bytes 4718592 | tf_op jit(solution)/shard_map/assemble/pallas_call | solution.py:142
  98.1 1.2 collective-permute-start.28
  99.8 1.7 %all-to-all-done = bf16[16,4,16,256]{3,2,1,0:T(8,128)(2,1)} async-done(((bf16[16,4,16,256]{3,2,1,0:T(8,128)(2,1)}), bf16[16,4,16,256]{3,2,1,0:T(8,128)(2,1)}, u32[]{:S(2)}, u32[]{:S(2)}) %all-to-all-start) | async-done | bytes 524320 | tf_op jit(solution)/shard_map/all_to_all | solution.py:580
  101.7 10.3 %windows.1 = bf16[16,48,512]{2,1,0:T(8,128)(2,1)} custom-call(s32[16]{0:T(128)} %fusion.8.picks, bf16[8,2,2,2,16,256]{5,4,3,2,1,0:T(8,128)(2,1)} %bitcast.9.y2, bf16[512,512]{1,0:T(8,128)(2,1)} %refs_0_.1, bf16[512,512]{1,0:T(8,128)(2,1)} %refs_1_.1, bf16[512,512]{1,0:T(8,128)(2,1)} %refs_2_.1, bf16[512,512]{1,0:T(8,128)(2,1)} %refs_3_.1, ...), custom_call_target="tpu_custom_call" | custom-call | flops 3489660928 | bytes 2097152 | tf_op jit(solution)/shard_map/windows/pallas_call | solution.py:351
  112.0 4.8 %all-to-all-start.1 = ((bf16[16,48,512]{2,1,0:T(8,128)(2,1)}), bf16[16,48,512]{2,1,0:T(8,128)(2,1)S(1)}, u32[]{:S(2)}, u32[]{:S(2)}) async-start(bf16[16,48,512]{2,1,0:T(8,128)(2,1)} %windows.1), calls=%async_computation.1 | async-start | bytes 1572864 | tf_op jit(solution)/shard_map/all_to_all | solution.py:600
  117.2 1.1 collective-permute-start.29
  118.3 3.1 %collective-permute-done.29.refs_1_ = bf16[1,1,3,64,256]{4,3,2,1,0:T(8,128)(2,1)S(1)} collective-permute-done((bf16[1,1,3,64,256]{4,3,2,1,0:T(8,128)(2,1)S(1)}, bf16[1,1,3,64,256]{4,3,2,1,0:T(8,128)(2,1)S(1)}, u32[]{:S(2)}, u32[]{:S(2)}) %collective-permute-start.29) | collective-permute-done | bytes 98336 | tf_op jit(solution)/shard_map/ppermute | solution.py:94
  121.4 1.0 collective-permute-start.31
  124.0 12.3 %all-to-all-done.1.arrived = bf16[16,48,512]{2,1,0:T(8,128)(2,1)S(1)} async-done(((bf16[16,48,512]{2,1,0:T(8,128)(2,1)}), bf16[16,48,512]{2,1,0:T(8,128)(2,1)S(1)}, u32[]{:S(2)}, u32[]{:S(2)}) %all-to-all-start.1) | async-done | bytes 786464 | tf_op jit(solution)/shard_map/all_to_all | solution.py:600
  136.3 0.9 copy-done.12
  137.2 0.9 copy-done.14
  138.1 5.0 %upsample.1.earlier = bf16[32,16,512]{2,1,0:T(8,128)(2,1)} custom-call(s32[13]{0:T(128)S(1)} %pad_add_fusion.info, s32[12]{0:T(128)S(1)} %concatenate.18.where, bf16[16,48,512]{2,1,0:T(8,128)(2,1)S(1)} %all-to-all-done.1.arrived, bf16[3,3,512,256]{3,2,1,0:T(8,128)(2,1)S(1)} %assemble.1.mine, bf16[3,3,512,256]{3,2,1,0:T(8,128)(2,1)} %collective-permute-done.28.theirs, ...), custom_call_target="tpu_custom_call" | custom-call | flops 754974720 | bytes 4718592 | tf_op jit(solution)/shard_map/upsample/pallas_call | solution.py:444
  143.1 1.0 copy-done
  144.1 1.2 settle.1
  (111 shorter events, 10.3 us)
Async XLA Ops:
  2.0 2.2 %collective-permute-start = (bf16[3,3,3,32,256]{4,3,2,1,0:T(8,128)(2,1)S(1)}, bf16[3,3,3,32,256]{4,3,2,1,0:T(8,128)(2,1)S(1)}, u32[]{:S(2)}, u32[]{:S(2)}) collective-permute-start(bf16[3,3,3,32,256]{4,3,2,1,0:T(8,128)(2,1)S(1)} %get-tuple-element.61), channel_id=1, source_target_pairs={{0,1},{1,0},{2,3},{3,2},{4,5},{5,4},{6,7},{7,6},{8,9},{9,8},{10,11... | collective-permute-start | bytes 1327112 | tf_op jit(solution)/shard_map/ppermute | solution.py:502
  4.4 11.8 %copy-start.17 = (bf16[3,3,3,64,256]{4,3,2,1,0:T(8,128)(2,1)}, bf16[3,3,3,64,256]{4,3,2,1,0:T(8,128)(2,1)S(1)}, u32[]{:S(2)}) copy-start(bf16[3,3,3,64,256]{4,3,2,1,0:T(8,128)(2,1)S(1)} %maximum_select_fusion.1) | copy-start | bytes 2654212
  4.5 13.4 %copy-start.21 = (s32[8]{0:T(128)S(1)}, s32[8]{0:T(128)}, u32[]{:S(2)}) copy-start(s32[8]{0:T(128)} %constant.133.clone) | copy-start | bytes 100
  4.6 12.8 %copy-start.18 = (bf16[3,2,3,64,256]{4,3,2,1,0:T(8,128)(2,1)}, bf16[3,2,3,64,256]{4,3,2,1,0:T(8,128)(2,1)S(1)}, u32[]{:S(2)}) copy-start(bf16[3,2,3,64,256]{4,3,2,1,0:T(8,128)(2,1)S(1)} %reverse_select_fusion) | copy-start | bytes 1769476
  4.7 10.4 %collective-permute-start.6 = (bf16[2,2,3,64,256]{4,3,2,1,0:T(8,128)(2,1)S(1)}, bf16[2,2,3,64,256]{4,3,2,1,0:T(8,128)(2,1)S(1)}, u32[]{:S(2)}, u32[]{:S(2)}) collective-permute-start(bf16[2,2,3,64,256]{4,3,2,1,0:T(8,128)(2,1)S(1)} %slice.101.refs_0_), channel_id=1, source_target_pairs={{4,0},{5,1},{8,4},{9,5},{12,8},{13,9},{14,12},{15,13},{10,14},{11,... | collective-permute-start | bytes 1179656 | tf_op jit(solution)/shard_map/ppermute | solution.py:80
  4.7 10.4 %collective-permute-start.1 = (bf16[2,2,3,64,256]{4,3,2,1,0:T(8,128)(2,1)S(1)}, bf16[2,2,3,64,256]{4,3,2,1,0:T(8,128)(2,1)S(1)}, u32[]{:S(2)}, u32[]{:S(2)}) collective-permute-start(bf16[2,2,3,64,256]{4,3,2,1,0:T(8,128)(2,1)S(1)} %slice.101.refs_0_), channel_id=1, source_target_pairs={{0,4},{1,5},{4,8},{5,9},{8,12},{9,13},{12,14},{13,15},{14,10},{15,... | collective-permute-start | bytes 1179656 | tf_op jit(solution)/shard_map/ppermute | solution.py:79
  15.2 10.1 %collective-permute-start.7 = (bf16[2,2,3,64,256]{4,3,2,1,0:T(8,128)(2,1)S(1)}, bf16[2,2,3,64,256]{4,3,2,1,0:T(8,128)(2,1)S(1)}, u32[]{:S(2)}, u32[]{:S(2)}) collective-permute-start(bf16[2,2,3,64,256]{4,3,2,1,0:T(8,128)(2,1)S(1)} %collective-permute-done.6.refs_2_), channel_id=1, source_target_pairs={{4,0},{5,1},{8,4},{9,5},{12,8},{13,9},{14,12},{15,13},{10,14},{11,... | collective-permute-start | bytes 1179656 | tf_op jit(solution)/shard_map/ppermute | solution.py:80
  16.2 9.1 %collective-permute-start.8 = (bf16[2,2,3,64,256]{4,3,2,1,0:T(8,128)(2,1)S(1)}, bf16[2,2,3,64,256]{4,3,2,1,0:T(8,128)(2,1)S(1)}, u32[]{:S(2)}, u32[]{:S(2)}) collective-permute-start(bf16[2,2,3,64,256]{4,3,2,1,0:T(8,128)(2,1)S(1)} %pad_maximum_fusion.1), channel_id=1, source_target_pairs={{0,16},{16,0},{1,17},{17,1},{2,18},{18,2},{3,19},{19,3},{4,20},{20... | collective-permute-start | bytes 1179656 | tf_op jit(solution)/shard_map/ppermute | solution.py:89
  17.5 8.7 %collective-permute-start.5 = (bf16[2,2,3,64,256]{4,3,2,1,0:T(8,128)(2,1)S(1)}, bf16[2,2,3,64,256]{4,3,2,1,0:T(8,128)(2,1)S(1)}, u32[]{:S(2)}, u32[]{:S(2)}) collective-permute-start(bf16[2,2,3,64,256]{4,3,2,1,0:T(8,128)(2,1)S(1)} %collective-permute-done.1.refs_1_), channel_id=1, source_target_pairs={{0,4},{1,5},{4,8},{5,9},{8,12},{9,13},{12,14},{13,15},{14,10},{15,... | collective-permute-start | bytes 1179656 | tf_op jit(solution)/shard_map/ppermute | solution.py:79
  19.0 19.2 %collective-permute-start.2 = (bf16[2,256,512]{2,1,0:T(8,128)(2,1)}, bf16[2,256,512]{2,1,0:T(8,128)(2,1)S(1)}, u32[]{:S(2)}, u32[]{:S(2)}) collective-permute-start(bf16[2,256,512]{2,1,0:T(8,128)(2,1)} %param.11), channel_id=1, source_target_pairs={{1,2},{2,1},{3,4},{4,3},{5,6},{6,5},{7,8},{8,7},{9,10},{10,9},{11,... | collective-permute-start | bytes 1572872 | tf_op jit(solution)/shard_map/ppermute | solution.py:520
  25.3 19.0 %copy-start.7 = (bf16[2,2,3,64,256]{4,3,2,1,0:T(8,128)(2,1)}, bf16[2,2,3,64,256]{4,3,2,1,0:T(8,128)(2,1)S(1)}, u32[]{:S(2)}) copy-start(bf16[2,2,3,64,256]{4,3,2,1,0:T(8,128)(2,1)S(1)} %collective-permute-done.7.refs_4_) | copy-start | bytes 1179652
  26.1 12.0 %copy-start.9 = (bf16[2,2,3,64,256]{4,3,2,1,0:T(8,128)(2,1)}, bf16[2,2,3,64,256]{4,3,2,1,0:T(8,128)(2,1)S(1)}, u32[]{:S(2)}) copy-start(bf16[2,2,3,64,256]{4,3,2,1,0:T(8,128)(2,1)S(1)} %collective-permute-done.5.refs_3_) | copy-start | bytes 1179652
  26.1 12.0 %collective-permute-start.9 = (bf16[2,2,3,64,256]{4,3,2,1,0:T(8,128)(2,1)S(1)}, bf16[2,2,3,64,256]{4,3,2,1,0:T(8,128)(2,1)S(1)}, u32[]{:S(2)}, u32[]{:S(2)}) collective-permute-start(bf16[2,2,3,64,256]{4,3,2,1,0:T(8,128)(2,1)S(1)} %collective-permute-done.5.refs_3_), channel_id=1, source_target_pairs={{0,4},{1,5},{4,8},{5,9},{8,12},{9,13},{12,14},{13,15},{14,10},{15,... | collective-permute-start | bytes 1179656 | tf_op jit(solution)/shard_map/ppermute | solution.py:79
  27.6 27.0 %copy-start.20 = (bf16[2,256,512]{2,1,0:T(8,128)(2,1)S(1)}, bf16[2,256,512]{2,1,0:T(8,128)(2,1)}, u32[]{:S(2)}) copy-start(bf16[2,256,512]{2,1,0:T(8,128)(2,1)} %param.11) | copy-start | bytes 1572868
  28.2 11.3 %collective-permute-start.11 = (bf16[2,2,3,64,256]{4,3,2,1,0:T(8,128)(2,1)S(1)}, bf16[2,2,3,64,256]{4,3,2,1,0:T(8,128)(2,1)S(1)}, u32[]{:S(2)}, u32[]{:S(2)}) collective-permute-start(bf16[2,2,3,64,256]{4,3,2,1,0:T(8,128)(2,1)S(1)} %pad_maximum_fusion.2), channel_id=1, source_target_pairs={{0,16},{16,0},{1,17},{17,1},{2,18},{18,2},{3,19},{19,3},{4,20},{20... | collective-permute-start | bytes 1179656 | tf_op jit(solution)/shard_map/ppermute | solution.py:89
  28.5 11.5 %collective-permute-start.10 = (bf16[2,2,3,64,256]{4,3,2,1,0:T(8,128)(2,1)S(1)}, bf16[2,2,3,64,256]{4,3,2,1,0:T(8,128)(2,1)S(1)}, u32[]{:S(2)}, u32[]{:S(2)}) collective-permute-start(bf16[2,2,3,64,256]{4,3,2,1,0:T(8,128)(2,1)S(1)} %collective-permute-done.7.refs_4_), channel_id=1, source_target_pairs={{4,0},{5,1},{8,4},{9,5},{12,8},{13,9},{14,12},{15,13},{10,14},{11,... | collective-permute-start | bytes 1179656 | tf_op jit(solution)/shard_map/ppermute | solution.py:80
  30.2 24.4 %collective-permute-start.3 = (bf16[2,256,512]{2,1,0:T(8,128)(2,1)}, bf16[2,256,512]{2,1,0:T(8,128)(2,1)S(1)}, u32[]{:S(2)}, u32[]{:S(2)}) collective-permute-start(bf16[2,256,512]{2,1,0:T(8,128)(2,1)} %param.11), channel_id=1, source_target_pairs={{0,1},{1,0},{2,3},{3,2},{4,5},{5,4},{6,7},{7,6},{8,9},{9,8},{10,11... | collective-permute-start | bytes 1572872 | tf_op jit(solution)/shard_map/ppermute | solution.py:521
  38.2 16.4 %collective-permute-start.4 = (bf16[2,256,512]{2,1,0:T(8,128)(2,1)S(1)}, bf16[2,256,512]{2,1,0:T(8,128)(2,1)S(1)}, u32[]{:S(2)}, u32[]{:S(2)}) collective-permute-start(bf16[2,256,512]{2,1,0:T(8,128)(2,1)S(1)} %collective-permute-done.2), channel_id=1, source_target_pairs={{0,1},{1,0},{2,3},{3,2},{4,5},{5,4},{6,7},{7,6},{8,9},{9,8},{10,11... | collective-permute-start | bytes 1572872 | tf_op jit(solution)/shard_map/ppermute | solution.py:522
  38.2 6.2 %collective-permute-start.14 = (bf16[2,1,3,64,256]{4,3,2,1,0:T(8,128)(2,1)S(1)}, bf16[2,1,3,64,256]{4,3,2,1,0:T(8,128)(2,1)S(1)}, u32[]{:S(2)}, u32[]{:S(2)}) collective-permute-start(bf16[2,1,3,64,256]{4,3,2,1,0:T(8,128)(2,1)S(1)} %slice.107.refs_0_), channel_id=1, source_target_pairs={{0,4},{1,5},{4,8},{5,9},{8,12},{9,13},{12,14},{13,15},{14,10},{15,... | collective-permute-start | bytes 589832 | tf_op jit(solution)/shard_map/ppermute | solution.py:79
  39.6 9.2 %collective-permute-start.15 = (bf16[2,1,3,64,256]{4,3,2,1,0:T(8,128)(2,1)S(1)}, bf16[2,1,3,64,256]{4,3,2,1,0:T(8,128)(2,1)S(1)}, u32[]{:S(2)}, u32[]{:S(2)}) collective-permute-start(bf16[2,1,3,64,256]{4,3,2,1,0:T(8,128)(2,1)S(1)} %slice.107.refs_0_), channel_id=1, source_target_pairs={{4,0},{5,1},{8,4},{9,5},{12,8},{13,9},{14,12},{15,13},{10,14},{11,... | collective-permute-start | bytes 589832 | tf_op jit(solution)/shard_map/ppermute | solution.py:80
  40.1 12.9 %collective-permute-start.13 = (bf16[2,1,3,64,256]{4,3,2,1,0:T(8,128)(2,1)S(1)}, bf16[2,1,3,64,256]{4,3,2,1,0:T(8,128)(2,1)S(1)}, u32[]{:S(2)}, u32[]{:S(2)}) collective-permute-start(bf16[2,1,3,64,256]{4,3,2,1,0:T(8,128)(2,1)S(1)} %slice.82), channel_id=1, source_target_pairs={{4,0},{5,1},{8,4},{9,5},{12,8},{13,9},{14,12},{15,13},{10,14},{11,... | collective-permute-start | bytes 589832 | tf_op jit(solution)/shard_map/ppermute | solution.py:77
  44.3 9.9 %collective-permute-start.12 = (bf16[2,1,3,64,256]{4,3,2,1,0:T(8,128)(2,1)S(1)}, bf16[2,1,3,64,256]{4,3,2,1,0:T(8,128)(2,1)S(1)}, u32[]{:S(2)}, u32[]{:S(2)}) collective-permute-start(bf16[2,1,3,64,256]{4,3,2,1,0:T(8,128)(2,1)S(1)} %slice.81), channel_id=1, source_target_pairs={{0,4},{1,5},{4,8},{5,9},{8,12},{9,13},{12,14},{13,15},{14,10},{15,... | collective-permute-start | bytes 589832 | tf_op jit(solution)/shard_map/ppermute | solution.py:77
  48.8 9.4 %collective-permute-start.16 = (bf16[2,1,3,64,256]{4,3,2,1,0:T(8,128)(2,1)S(1)}, bf16[2,1,3,64,256]{4,3,2,1,0:T(8,128)(2,1)S(1)}, u32[]{:S(2)}, u32[]{:S(2)}) collective-permute-start(bf16[2,1,3,64,256]{4,3,2,1,0:T(8,128)(2,1)S(1)} %pad_maximum_fusion.4), channel_id=1, source_target_pairs={{0,16},{16,0},{1,17},{17,1},{2,18},{18,2},{3,19},{19,3},{4,20},{20... | collective-permute-start | bytes 589832 | tf_op jit(solution)/shard_map/ppermute | solution.py:89
  53.0 14.9 %collective-permute-start.20 = (bf16[2,1,3,64,256]{4,3,2,1,0:T(8,128)(2,1)S(1)}, bf16[2,1,3,64,256]{4,3,2,1,0:T(8,128)(2,1)S(1)}, u32[]{:S(2)}, u32[]{:S(2)}) collective-permute-start(bf16[2,1,3,64,256]{4,3,2,1,0:T(8,128)(2,1)S(1)} %pad_maximum_fusion.5), channel_id=1, source_target_pairs={{0,16},{16,0},{1,17},{17,1},{2,18},{18,2},{3,19},{19,3},{4,20},{20... | collective-permute-start | bytes 589832 | tf_op jit(solution)/shard_map/ppermute | solution.py:89
  54.2 7.1 %copy-start.8 = (bf16[2,2,3,64,256]{4,3,2,1,0:T(8,128)(2,1)S(1)}, bf16[2,2,3,64,256]{4,3,2,1,0:T(8,128)(2,1)}, u32[]{:S(2)}) copy-start(bf16[2,2,3,64,256]{4,3,2,1,0:T(8,128)(2,1)} %copy-done.7) | copy-start | bytes 1179652
  54.2 7.1 %copy-start.10 = (bf16[2,2,3,64,256]{4,3,2,1,0:T(8,128)(2,1)S(1)}, bf16[2,2,3,64,256]{4,3,2,1,0:T(8,128)(2,1)}, u32[]{:S(2)}) copy-start(bf16[2,2,3,64,256]{4,3,2,1,0:T(8,128)(2,1)} %copy-done.9) | copy-start | bytes 1179652
  54.2 7.1 %copy-start.16 = (bf16[2,2,3,64,256]{4,3,2,1,0:T(8,128)(2,1)S(1)}, bf16[2,2,3,64,256]{4,3,2,1,0:T(8,128)(2,1)}, u32[]{:S(2)}) copy-start(bf16[2,2,3,64,256]{4,3,2,1,0:T(8,128)(2,1)} %copy-done.15) | copy-start | bytes 1179652
  54.3 7.0 %collective-permute-start.17 = (bf16[1,1,3,64,256]{4,3,2,1,0:T(8,128)(2,1)S(1)}, bf16[1,1,3,64,256]{4,3,2,1,0:T(8,128)(2,1)S(1)}, u32[]{:S(2)}, u32[]{:S(2)}) collective-permute-start(bf16[1,1,3,64,256]{4,3,2,1,0:T(8,128)(2,1)S(1)} %slice.88), channel_id=1, source_target_pairs={{0,16},{16,0},{1,17},{17,1},{2,18},{18,2},{3,19},{19,3},{4,20},{20... | collective-permute-start | bytes 294920 | tf_op jit(solution)/shard_map/ppermute | solution.py:94
  56.6 11.3 %collective-permute-start.18 = (bf16[2,1,3,64,256]{4,3,2,1,0:T(8,128)(2,1)S(1)}, bf16[2,1,3,64,256]{4,3,2,1,0:T(8,128)(2,1)S(1)}, u32[]{:S(2)}, u32[]{:S(2)}) collective-permute-start(bf16[2,1,3,64,256]{4,3,2,1,0:T(8,128)(2,1)S(1)} %collective-permute-done.14.refs_1_), channel_id=1, source_target_pairs={{0,4},{1,5},{4,8},{5,9},{8,12},{9,13},{12,14},{13,15},{14,10},{15,... | collective-permute-start | bytes 589832 | tf_op jit(solution)/shard_map/ppermute | solution.py:79
  57.8 10.1 %collective-permute-start.19 = (bf16[2,1,3,64,256]{4,3,2,1,0:T(8,128)(2,1)S(1)}, bf16[2,1,3,64,256]{4,3,2,1,0:T(8,128)(2,1)S(1)}, u32[]{:S(2)}, u32[]{:S(2)}) collective-permute-start(bf16[2,1,3,64,256]{4,3,2,1,0:T(8,128)(2,1)S(1)} %collective-permute-done.15.refs_2_), channel_id=1, source_target_pairs={{4,0},{5,1},{8,4},{9,5},{12,8},{13,9},{14,12},{15,13},{10,14},{11,... | collective-permute-start | bytes 589832 | tf_op jit(solution)/shard_map/ppermute | solution.py:80
  58.2 9.7 %collective-permute-start.21 = (bf16[3,1,3,64,256]{4,3,2,1,0:T(8,128)(2,1)S(1)}, bf16[3,1,3,64,256]{4,3,2,1,0:T(8,128)(2,1)S(1)}, u32[]{:S(2)}, u32[]{:S(2)}) collective-permute-start(bf16[3,1,3,64,256]{4,3,2,1,0:T(8,128)(2,1)S(1)} %pad_maximum_fusion.3), channel_id=1, source_target_pairs={{0,16},{16,0},{1,17},{17,1},{2,18},{18,2},{3,19},{19,3},{4,20},{20... | collective-permute-start | bytes 884744 | tf_op jit(solution)/shard_map/ppermute | solution.py:100
  67.9 4.4 %copy-start.3 = (bf16[2,1,3,64,256]{4,3,2,1,0:T(8,128)(2,1)}, bf16[2,1,3,64,256]{4,3,2,1,0:T(8,128)(2,1)S(1)}, u32[]{:S(2)}) copy-start(bf16[2,1,3,64,256]{4,3,2,1,0:T(8,128)(2,1)S(1)} %collective-permute-done.20.refs_8_) | copy-start | bytes 589828
  67.9 6.1 %collective-permute-start.22 = (bf16[6,256,256]{2,1,0:T(8,128)(2,1)S(1)}, bf16[6,256,256]{2,1,0:T(8,128)(2,1)S(1)}, u32[]{:S(2)}, u32[]{:S(2)}) collective-permute-start(bf16[6,256,256]{2,1,0:T(8,128)(2,1)S(1)} %get-tuple-element.46.mine), channel_id=1, source_target_pairs={{0,1},{1,0},{2,3},{3,2},{4,5},{5,4},{6,7},{7,6},{8,9},{9,8},{10,11... | collective-permute-start | bytes 2359304 | tf_op jit(solution)/shard_map/ppermute | solution.py:559
  71.0 8.8 %collective-permute-start.25 = (bf16[2,1,3,64,256]{4,3,2,1,0:T(8,128)(2,1)S(1)}, bf16[2,1,3,64,256]{4,3,2,1,0:T(8,128)(2,1)S(1)}, u32[]{:S(2)}, u32[]{:S(2)}) collective-permute-start(bf16[2,1,3,64,256]{4,3,2,1,0:T(8,128)(2,1)S(1)} %pad_maximum_fusion.6), channel_id=1, source_target_pairs={{0,16},{16,0},{1,17},{17,1},{2,18},{18,2},{3,19},{19,3},{4,20},{20... | collective-permute-start | bytes 589832 | tf_op jit(solution)/shard_map/ppermute | solution.py:89
  72.3 8.2 %collective-permute-start.23 = (bf16[2,1,3,64,256]{4,3,2,1,0:T(8,128)(2,1)S(1)}, bf16[2,1,3,64,256]{4,3,2,1,0:T(8,128)(2,1)S(1)}, u32[]{:S(2)}, u32[]{:S(2)}) collective-permute-start(bf16[2,1,3,64,256]{4,3,2,1,0:T(8,128)(2,1)S(1)} %collective-permute-done.18.refs_3_), channel_id=1, source_target_pairs={{0,4},{1,5},{4,8},{5,9},{8,12},{9,13},{12,14},{13,15},{14,10},{15,... | collective-permute-start | bytes 589832 | tf_op jit(solution)/shard_map/ppermute | solution.py:79
  74.0 6.5 %collective-permute-start.24 = (bf16[2,1,3,64,256]{4,3,2,1,0:T(8,128)(2,1)S(1)}, bf16[2,1,3,64,256]{4,3,2,1,0:T(8,128)(2,1)S(1)}, u32[]{:S(2)}, u32[]{:S(2)}) collective-permute-start(bf16[2,1,3,64,256]{4,3,2,1,0:T(8,128)(2,1)S(1)} %collective-permute-done.19.refs_4_), channel_id=1, source_target_pairs={{4,0},{5,1},{8,4},{9,5},{12,8},{13,9},{14,12},{15,13},{10,14},{11,... | collective-permute-start | bytes 589832 | tf_op jit(solution)/shard_map/ppermute | solution.py:80
  80.5 8.8 %copy-start.1 = (bf16[2,1,3,64,256]{4,3,2,1,0:T(8,128)(2,1)}, bf16[2,1,3,64,256]{4,3,2,1,0:T(8,128)(2,1)S(1)}, u32[]{:S(2)}) copy-start(bf16[2,1,3,64,256]{4,3,2,1,0:T(8,128)(2,1)S(1)} %collective-permute-done.24.refs_6_) | copy-start | bytes 589828
  80.5 21.0 %all-to-all-start = ((bf16[16,4,16,256]{3,2,1,0:T(8,128)(2,1)}), bf16[16,4,16,256]{3,2,1,0:T(8,128)(2,1)}, u32[]{:S(2)}, u32[]{:S(2)}) async-start(bf16[16,4,16,256]{3,2,1,0:T(8,128)(2,1)} %second_conv.1), calls=%async_computation | async-start | bytes 1048576 | tf_op jit(solution)/shard_map/all_to_all | solution.py:580
  87.3 6.3 %collective-permute-start.26 = (bf16[2,1,3,64,256]{4,3,2,1,0:T(8,128)(2,1)S(1)}, bf16[2,1,3,64,256]{4,3,2,1,0:T(8,128)(2,1)S(1)}, u32[]{:S(2)}, u32[]{:S(2)}) collective-permute-start(bf16[2,1,3,64,256]{4,3,2,1,0:T(8,128)(2,1)S(1)} %pad_maximum_fusion.7), channel_id=1, source_target_pairs={{0,16},{16,0},{1,17},{17,1},{2,18},{18,2},{3,19},{19,3},{4,20},{20... | collective-permute-start | bytes 589832 | tf_op jit(solution)/shard_map/ppermute | solution.py:89
  93.6 0.9 copy-start.2
  94.5 0.9 copy-start.4
  98.1 25.9 %collective-permute-start.28 = (bf16[3,3,512,256]{3,2,1,0:T(8,128)(2,1)S(1)}, bf16[3,3,512,256]{3,2,1,0:T(8,128)(2,1)}, u32[]{:S(2)}, u32[]{:S(2)}) collective-permute-start(bf16[3,3,512,256]{3,2,1,0:T(8,128)(2,1)S(1)} %assemble.1.mine), channel_id=1, source_target_pairs={{0,1},{1,0},{2,3},{3,2},{4,5},{5,4},{6,7},{7,6},{8,9},{9,8},{10,11... | collective-permute-start | bytes 7077896 | tf_op jit(solution)/shard_map/ppermute | solution.py:585
  101.5 10.5 %collective-permute-start.27 = (bf16[2,1,3,64,256]{4,3,2,1,0:T(8,128)(2,1)S(1)}, bf16[2,1,3,64,256]{4,3,2,1,0:T(8,128)(2,1)S(1)}, u32[]{:S(2)}, u32[]{:S(2)}) collective-permute-start(bf16[2,1,3,64,256]{4,3,2,1,0:T(8,128)(2,1)S(1)} %collective-permute-done.23.refs_5_), channel_id=1, source_target_pairs={{0,4},{1,5},{4,8},{5,9},{8,12},{9,13},{12,14},{13,15},{14,10},{15,... | collective-permute-start | bytes 589832 | tf_op jit(solution)/shard_map/ppermute | solution.py:77
  112.0 24.3 %all-to-all-start.1 = ((bf16[16,48,512]{2,1,0:T(8,128)(2,1)}), bf16[16,48,512]{2,1,0:T(8,128)(2,1)S(1)}, u32[]{:S(2)}, u32[]{:S(2)}) async-start(bf16[16,48,512]{2,1,0:T(8,128)(2,1)} %windows.1), calls=%async_computation.1 | async-start | bytes 1572864 | tf_op jit(solution)/shard_map/all_to_all | solution.py:600
  116.8 7.2 %collective-permute-start.30 = (bf16[2,1,3,64,256]{4,3,2,1,0:T(8,128)(2,1)S(1)}, bf16[2,1,3,64,256]{4,3,2,1,0:T(8,128)(2,1)S(1)}, u32[]{:S(2)}, u32[]{:S(2)}) collective-permute-start(bf16[2,1,3,64,256]{4,3,2,1,0:T(8,128)(2,1)S(1)} %collective-permute-done.27.refs_0_), channel_id=1, source_target_pairs={{0,1},{1,0},{2,3},{3,2},{4,5},{5,4},{6,7},{7,6},{8,9},{9,8},{10,11... | collective-permute-start | bytes 589832 | tf_op jit(solution)/shard_map/ppermute | solution.py:615
  117.2 4.2 %collective-permute-start.29 = (bf16[1,1,3,64,256]{4,3,2,1,0:T(8,128)(2,1)S(1)}, bf16[1,1,3,64,256]{4,3,2,1,0:T(8,128)(2,1)S(1)}, u32[]{:S(2)}, u32[]{:S(2)}) collective-permute-start(bf16[1,1,3,64,256]{4,3,2,1,0:T(8,128)(2,1)S(1)} %slice.99), channel_id=1, source_target_pairs={{0,16},{16,0},{1,17},{17,1},{2,18},{18,2},{3,19},{19,3},{4,20},{20... | collective-permute-start | bytes 294920 | tf_op jit(solution)/shard_map/ppermute | solution.py:94
  121.4 1.9 %collective-permute-start.31 = (bf16[1,1,3,64,256]{4,3,2,1,0:T(8,128)(2,1)S(1)}, bf16[1,1,3,64,256]{4,3,2,1,0:T(8,128)(2,1)S(1)}, u32[]{:S(2)}, u32[]{:S(2)}) collective-permute-start(bf16[1,1,3,64,256]{4,3,2,1,0:T(8,128)(2,1)S(1)} %collective-permute-done.29.refs_1_), channel_id=1, source_target_pairs={{0,1},{1,0},{2,3},{3,2},{4,5},{5,4},{6,7},{7,6},{8,9},{9,8},{10,11... | collective-permute-start | bytes 294920 | tf_op jit(solution)/shard_map/ppermute | solution.py:615
  143.1 1.0 copy-start
  (8 other events, 6.2 us)

commit v5 on v4

--- a/solution.py
+++ b/solution.py
@@ -370,7 +370,8 @@
 
 
 def upsample_kernel(info, where, arrived, mine, theirs, *refs):
-    ends, (out, field, weights, spread, sems) = refs[:4], refs[4:]
+    ends, outs, (lines, field, weights, spread, sems) = refs[:4], refs[4:-5], refs[-5:]
+    out = outs[0]
     taps, depth, half = mine.shape[0], mine.shape[2], mine.shape[3]
     core = info[0]
     copies = []
@@ -381,6 +382,8 @@
         copy.start()
     framed, rows, channels = field.shape
     width = framed - 2
+    for settled in outs[1:]:
+        settle_kernel(arrived, None, settled, lines)
     for j in range(framed):
         column = arrived[info[3 + j], pl.ds(arrived.shape[1] - rows, rows)]
         if j == 0:
@@ -438,15 +441,19 @@
             )
 
 
-def upsample(info, where, arrived, mine, theirs, ends, rows, width):
+def upsample(info, where, arrived, mine, theirs, ends, rows, width, per):
     channels = arrived.shape[2]
-    framed = width + 2
+    framed, line = width + 2, arrived.shape[0] * GRID
+    shapes = [(2 * rows, 2 * width, channels)]
+    if arrived.shape[1] > rows:
+        shapes.append((per, line, channels))
     return pl.pallas_call(
         upsample_kernel,
-        out_shape=jax.ShapeDtypeStruct((2 * rows, 2 * width, channels), BF16),
+        out_shape=tuple(jax.ShapeDtypeStruct(shape, BF16) for shape in shapes),
         in_specs=[SMEM, SMEM, VMEM] + [ANY] * 6,
-        out_specs=VMEM,
+        out_specs=tuple(VMEM for _ in shapes),
         scratch_shapes=[
+            pltpu.VMEM((line, 128), F32),
             pltpu.VMEM((framed, rows, channels), BF16),
             pltpu.VMEM((3, 3, channels, channels), BF16),
             pltpu.VMEM((4 * rows * width, 128), F32),
@@ -528,7 +535,7 @@
     pair.cross(slice(0, 1))
     last.after(pair.up)
     last.step(1)
-    pair.after((joint[-1], near))
+    pair.after((joint[-1], near, partner))
     pair.step(count)
     pair.finals = last.before(pair.finals)
     pair.cross_final(0)
@@ -617,8 +624,11 @@
     info = jnp.concatenate(
         [jnp.stack([core, (device > 0).astype(jnp.int32), (device < n - 1).astype(jnp.int32)]), sources]
     ).astype(jnp.int32)
-    upsampled = upsample(info, where, central, up_mine, up_theirs, ends, rows, width)
-    return (settle(back, upsampled, per), upsampled)
+    upsampled, *settled = upsample(
+        info, where, central, up_mine, up_theirs, ends, rows, width, per
+    )
+    latent_out = settled[0] if settled else settle(back, upsampled, per)
+    return (latent_out, upsampled)
 
 
 def solution(mesh):

time: 146 us -> 145 us (level)
  waiting for transfers between devices: 38.5 us -> 48 us
  starting transfers between devices: 58.3 us -> 51.9 us
  local copies, waits for them, and re-layouts: 12.2 us -> 8.93 us
    ppermute x1, starting transfers between devices: 6.99 us -> 0.07 us  [on_device(): partner = lax.ppermute(latent_later, 'row', swap)]
    ppermute x1, waiting for transfers between devices: 0.98 us -> 7.86 us  [on_device(): near = lax.ppermute(beside, 'row', edges)]
    unnamed x44 -> x42, local copies, waits for them, and re-layouts: 8.98 us -> 6.57 us
    ppermute x6, starting transfers between devices: 6.39 us -> 4.3 us  [cross(): self.batches.append(lax.ppermute(jnp.stack(thirds), 'parts', across))]
    ppermute x6, starting transfers between devices: 2.71 us -> 4.6 us  [step(): self.down = lax.ppermute(self.down, 'row', backward)]
    ppermute x6, starting transfers between devices: 7.42 us -> 5.85 us  [step(): self.up = lax.ppermute(self.up, 'row', forward)]
    pallas_call x2 -> x1, Pallas kernels: 6.18 us -> 4.98 us  [upsample(): pl.pallas_call(upsample_kernel, out_shape=tuple((jax.ShapeDtypeStruct(sha...]
  transfers between devices with their start and end apart: 34 -> 34, of which waited for: 11 -> 14; matrix products, arithmetic and copies ran while one was open for 4% -> 4% of each run, Pallas kernels for 17% -> 17%
where the time goes in v5:
time: 145 us; the launch traced here: 144 us
  starting transfers between devices  51.9 us (36%)
  waiting for transfers between devices  48 us (33%)
  Pallas kernels  29.4 us (20%)
  local copies, waits for them, and re-layouts  8.93 us (6%)
  other arithmetic  4.54 us (3%)
    all_to_all x1, waiting for transfers between devices, on_device(): lax.all_to_all(sent[0], 'row', split_axis=0, concat_axis=0, axis_index_gr...  12.3 us
    ppermute x6, waiting for transfers between devices, step(): self.down = lax.ppermute(self.down, 'row', backward)  10.4 us
    pallas_call x1, Pallas kernels, windows(): pl.pallas_call(functools.partial(window_kernel, per), out_shape=tuple((ja...  10.3 us
    ppermute x3, starting transfers between devices, step(): self.finals.append(lax.ppermute(value[:, kernel:kernel + 1], 'row', pairs))  8.63 us
    ppermute x1, waiting for transfers between devices, on_device(): near = lax.ppermute(beside, 'row', edges)  7.86 us
    pallas_call x1, Pallas kernels, first_conv(): pl.pallas_call(functools.partial(first_conv_kernel, step), out_shape=(out...  6.57 us
    unnamed x42, local copies, waits for them, and re-layouts  6.57 us
    all_to_all x1, starting transfers between devices, on_device(): lax.all_to_all(y2, 'row', split_axis=0, concat_axis=0, axis_index_groups=...  6.51 us
  transfers between devices with their start and end apart: 34, of which 14 were waited for; matrix products, arithmetic and copies ran while one was open for 4% of the time, Pallas kernels for 17%

profile of v5, /device:TPU:9, one launch (start us, length us, event | category | flops | bytes accessed | tf_op | source)
XLA Modules:
  0.0 144.0 jit_solution(4801985436799462234)
XLA Ops:
  0.7 1.2 pad_maximum_fusion
  2.0 0.7 collective-permute-start
  2.7 1.4 collective-permute-done
  4.7 1.5 %collective-permute-start.1 = (bf16[2,2,3,64,256]{4,3,2,1,0:T(8,128)(2,1)S(1)}, bf16[2,2,3,64,256]{4,3,2,1,0:T(8,128)(2,1)S(1)}, u32[]{:S(2)}, u32[]{:S(2)}) collective-permute-start(bf16[2,2,3,64,256]{4,3,2,1,0:T(8,128)(2,1)S(1)} %slice.101.refs_0_), channel_id=1, source_target_pairs={{0,4},{1,5},{4,8},{5,9},{8,12},{9,13},{12,14},{13,15},{14,10},{15,... | collective-permute-start | bytes 1179656 | tf_op jit(solution)/shard_map/ppermute | solution.py:79
  6.2 8.9 %collective-permute-done.6.refs_2_ = bf16[2,2,3,64,256]{4,3,2,1,0:T(8,128)(2,1)S(1)} collective-permute-done((bf16[2,2,3,64,256]{4,3,2,1,0:T(8,128)(2,1)S(1)}, bf16[2,2,3,64,256]{4,3,2,1,0:T(8,128)(2,1)S(1)}, u32[]{:S(2)}, u32[]{:S(2)}) %collective-permute-start.6) | collective-permute-done | bytes 393248 | tf_op jit(solution)/shard_map/ppermute | solution.py:80
  15.2 1.3 collective-permute-start.5
  16.7 1.2 collective-permute-start.8
  18.0 6.5 %collective-permute-start.2 = (bf16[2,256,512]{2,1,0:T(8,128)(2,1)}, bf16[2,256,512]{2,1,0:T(8,128)(2,1)S(1)}, u32[]{:S(2)}, u32[]{:S(2)}) collective-permute-start(bf16[2,256,512]{2,1,0:T(8,128)(2,1)} %param.11), channel_id=1, source_target_pairs={{1,2},{2,1},{3,4},{4,3},{5,6},{6,5},{7,8},{8,7},{9,10},{10,9},{11,... | collective-permute-start | bytes 1572872 | tf_op jit(solution)/shard_map/ppermute | solution.py:527
  24.6 0.8 collective-permute-done.7.refs_4_
  25.5 1.3 collective-permute-start.9
  27.1 1.3 collective-permute-start.11
  28.5 1.0 slice_bitcast_fusion.refs_9_
  29.5 7.9 %collective-permute-done.2 = bf16[2,256,512]{2,1,0:T(8,128)(2,1)S(1)} collective-permute-done((bf16[2,256,512]{2,1,0:T(8,128)(2,1)}, bf16[2,256,512]{2,1,0:T(8,128)(2,1)S(1)}, u32[]{:S(2)}, u32[]{:S(2)}) %collective-permute-start.2) | collective-permute-done | bytes 524320 | tf_op jit(solution)/shard_map/ppermute | solution.py:527
  37.4 0.7 collective-permute-done.10.refs_6_
  38.1 1.2 collective-permute-start.12
  39.3 7.2 %collective-permute-start.13 = (bf16[2,1,3,64,256]{4,3,2,1,0:T(8,128)(2,1)S(1)}, bf16[2,1,3,64,256]{4,3,2,1,0:T(8,128)(2,1)S(1)}, u32[]{:S(2)}, u32[]{:S(2)}) collective-permute-start(bf16[2,1,3,64,256]{4,3,2,1,0:T(8,128)(2,1)S(1)} %slice.82), channel_id=1, source_target_pairs={{4,0},{5,1},{8,4},{9,5},{12,8},{13,9},{14,12},{15,13},{10,14},{11,... | collective-permute-start | bytes 589832 | tf_op jit(solution)/shard_map/ppermute | solution.py:77
  46.5 1.9 %collective-permute-start.15 = (bf16[2,1,3,64,256]{4,3,2,1,0:T(8,128)(2,1)S(1)}, bf16[2,1,3,64,256]{4,3,2,1,0:T(8,128)(2,1)S(1)}, u32[]{:S(2)}, u32[]{:S(2)}) collective-permute-start(bf16[2,1,3,64,256]{4,3,2,1,0:T(8,128)(2,1)S(1)} %slice.107.refs_0_), channel_id=1, source_target_pairs={{4,0},{5,1},{8,4},{9,5},{12,8},{13,9},{14,12},{15,13},{10,14},{11,... | collective-permute-start | bytes 589832 | tf_op jit(solution)/shard_map/ppermute | solution.py:80
  48.5 3.2 %collective-permute-done.12.refs_7_ = bf16[2,1,3,64,256]{4,3,2,1,0:T(8,128)(2,1)S(1)} collective-permute-done((bf16[2,1,3,64,256]{4,3,2,1,0:T(8,128)(2,1)S(1)}, bf16[2,1,3,64,256]{4,3,2,1,0:T(8,128)(2,1)S(1)}, u32[]{:S(2)}, u32[]{:S(2)}) %collective-permute-start.12) | collective-permute-done | bytes 196640 | tf_op jit(solution)/shard_map/ppermute | solution.py:77
  51.6 1.4 collective-permute-start.16
  53.0 1.2 collective-permute-done.14.refs_1_
  54.2 2.4 %collective-permute-start.17 = (bf16[1,1,3,64,256]{4,3,2,1,0:T(8,128)(2,1)S(1)}, bf16[1,1,3,64,256]{4,3,2,1,0:T(8,128)(2,1)S(1)}, u32[]{:S(2)}, u32[]{:S(2)}) collective-permute-start(bf16[1,1,3,64,256]{4,3,2,1,0:T(8,128)(2,1)S(1)} %slice.88), channel_id=1, source_target_pairs={{0,16},{16,0},{1,17},{17,1},{2,18},{18,2},{3,19},{19,3},{4,20},{20... | collective-permute-start | bytes 294920 | tf_op jit(solution)/shard_map/ppermute | solution.py:94
  56.8 2.0 %fusion.5 = (bf16[8,256,512]{2,1,0:T(8,128)(2,1)S(1)}, bf16[8,256,512]{2,1,0:T(8,128)(2,1)S(1)}) fusion(bf16[2,256,512]{2,1,0:T(8,128)(2,1)S(1)} %collective-permute-done.2, bf16[2,256,512]{2,1,0:T(8,128)(2,1)S(1)} %copy-done.19, bf16[2,256,512]{2,1,0:T(8,128)(2,1)S(1)} %collective-permute-done.3, bf16[2,256,512]{2,1,0:T(8,128)(2,1)S(1)} %collective-permute-done.4, ...), kind=kLoop, calls=%fused_computation.9 | loop fusion | flops 17825792 | bytes 6291457 | tf_op jit(solution)/shard_map/convert_element_type | solution.py:547
  58.9 2.3 %collective-permute-start.19 = (bf16[2,1,3,64,256]{4,3,2,1,0:T(8,128)(2,1)S(1)}, bf16[2,1,3,64,256]{4,3,2,1,0:T(8,128)(2,1)S(1)}, u32[]{:S(2)}, u32[]{:S(2)}) collective-permute-start(bf16[2,1,3,64,256]{4,3,2,1,0:T(8,128)(2,1)S(1)} %collective-permute-done.15.refs_2_), channel_id=1, source_target_pairs={{4,0},{5,1},{8,4},{9,5},{12,8},{13,9},{14,12},{15,13},{10,14},{11,... | collective-permute-start | bytes 589832 | tf_op jit(solution)/shard_map/ppermute | solution.py:80
  61.3 1.5 %collective-permute-start.21 = (bf16[3,1,3,64,256]{4,3,2,1,0:T(8,128)(2,1)S(1)}, bf16[3,1,3,64,256]{4,3,2,1,0:T(8,128)(2,1)S(1)}, u32[]{:S(2)}, u32[]{:S(2)}) collective-permute-start(bf16[3,1,3,64,256]{4,3,2,1,0:T(8,128)(2,1)S(1)} %pad_maximum_fusion.3), channel_id=1, source_target_pairs={{0,16},{16,0},{1,17},{17,1},{2,18},{18,2},{3,19},{19,3},{4,20},{20... | collective-permute-start | bytes 884744 | tf_op jit(solution)/shard_map/ppermute | solution.py:100
  62.8 6.6 %first_conv.1 = (bf16[6,256,256]{2,1,0:T(8,128)(2,1)S(1)}, bf16[6,256,256]{2,1,0:T(8,128)(2,1)S(1)}) custom-call(s32[12]{0:T(128)S(1)} %concatenate.19.where, bf16[8,256,512]{2,1,0:T(8,128)(2,1)S(1)} %get-tuple-element.40.act, bf16[8,256,512]{2,1,0:T(8,128)(2,1)S(1)} %get-tuple-element.63.lat, bf16[2,2,3,64,256]{4,3,2,1,0:T(8,128)(2,1)S(1)} %slice.101.refs_0_, ...), custom_call_target="tpu_custom_call" | custom-call | flops 3623878656 | bytes 2359296 | tf_op jit(solution)/shard_map/first_conv/pallas_call | solution.py:200
  69.4 3.5 %collective-permute-start.22 = (bf16[6,256,256]{2,1,0:T(8,128)(2,1)S(1)}, bf16[6,256,256]{2,1,0:T(8,128)(2,1)S(1)}, u32[]{:S(2)}, u32[]{:S(2)}) collective-permute-start(bf16[6,256,256]{2,1,0:T(8,128)(2,1)S(1)} %get-tuple-element.48.mine), channel_id=1, source_target_pairs={{0,1},{1,0},{2,3},{3,2},{4,5},{5,4},{6,7},{7,6},{8,9},{9,8},{10,11... | collective-permute-start | bytes 2359304 | tf_op jit(solution)/shard_map/ppermute | solution.py:566
  73.3 1.7 %collective-permute-start.23 = (bf16[2,1,3,64,256]{4,3,2,1,0:T(8,128)(2,1)S(1)}, bf16[2,1,3,64,256]{4,3,2,1,0:T(8,128)(2,1)S(1)}, u32[]{:S(2)}, u32[]{:S(2)}) collective-permute-start(bf16[2,1,3,64,256]{4,3,2,1,0:T(8,128)(2,1)S(1)} %collective-permute-done.18.refs_3_), channel_id=1, source_target_pairs={{0,4},{1,5},{4,8},{5,9},{8,12},{9,13},{12,14},{13,15},{14,10},{15,... | collective-permute-start | bytes 589832 | tf_op jit(solution)/shard_map/ppermute | solution.py:79
  75.0 5.8 %second_conv.1 = bf16[16,4,16,256]{3,2,1,0:T(8,128)(2,1)} custom-call(s32[12]{0:T(128)S(1)} %concatenate.19.where, bf16[6,256,256]{2,1,0:T(8,128)(2,1)S(1)} %get-tuple-element.43.y1, bf16[6,256,256]{2,1,0:T(8,128)(2,1)S(1)} %get-tuple-element.48.mine, bf16[6,256,256]{2,1,0:T(8,128)(2,1)S(1)} %collective-permute-done.22.theirs, ...), custom_call_target="tpu_custom_call" | custom-call | flops 2415919104 | bytes 2359296 | tf_op jit(solution)/shard_map/second_conv/pallas_call | solution.py:245
  80.8 0.7 copy-done.4
  81.5 6.5 %all-to-all-start = ((bf16[16,4,16,256]{3,2,1,0:T(8,128)(2,1)}), bf16[16,4,16,256]{3,2,1,0:T(8,128)(2,1)}, u32[]{:S(2)}, u32[]{:S(2)}) async-start(bf16[16,4,16,256]{3,2,1,0:T(8,128)(2,1)} %second_conv.1), calls=%async_computation | async-start | bytes 1048576 | tf_op jit(solution)/shard_map/all_to_all | solution.py:587
  88.2 0.9 slice_bitcast_fusion.1.refs_7_
  89.1 5.3 %collective-permute-done.26.refs_10_ = bf16[2,1,3,64,256]{4,3,2,1,0:T(8,128)(2,1)S(1)} collective-permute-done((bf16[2,1,3,64,256]{4,3,2,1,0:T(8,128)(2,1)S(1)}, bf16[2,1,3,64,256]{4,3,2,1,0:T(8,128)(2,1)S(1)}, u32[]{:S(2)}, u32[]{:S(2)}) %collective-permute-start.26) | collective-permute-done | bytes 196640 | tf_op jit(solution)/shard_map/ppermute | solution.py:89
  94.4 0.9 copy-done.1
  95.3 0.9 copy-done.3
  96.2 0.9 copy-done.5
  97.2 1.8 %assemble.1.mine = bf16[3,3,512,256]{3,2,1,0:T(8,128)(2,1)S(1)} custom-call(s32[12]{0:T(128)S(1)} %concatenate.19.where, bf16[2,1,3,64,256]{4,3,2,1,0:T(8,128)(2,1)S(1)} %slice.107.refs_0_, bf16[2,1,3,64,256]{4,3,2,1,0:T(8,128)(2,1)S(1)} %collective-permute-done.14.refs_1_, bf16[2,1,3,64,256]{4,3,2,1,0:T(8,128)(2,1)S(1)} %collective-permute-done.15.refs_2_, ...), custom_call_target="tpu_custom_call" | custom-call | bytes 4718592 | tf_op jit(solution)/shard_map/assemble/pallas_call | solution.py:142
  98.9 1.2 collective-permute-start.28
  100.6 1.6 %all-to-all-done = bf16[16,4,16,256]{3,2,1,0:T(8,128)(2,1)} async-done(((bf16[16,4,16,256]{3,2,1,0:T(8,128)(2,1)}), bf16[16,4,16,256]{3,2,1,0:T(8,128)(2,1)}, u32[]{:S(2)}, u32[]{:S(2)}) %all-to-all-start) | async-done | bytes 524320 | tf_op jit(solution)/shard_map/all_to_all | solution.py:587
  102.5 10.3 %windows.1 = bf16[16,48,512]{2,1,0:T(8,128)(2,1)} custom-call(s32[16]{0:T(128)} %fusion.8.picks, bf16[8,2,2,2,16,256]{5,4,3,2,1,0:T(8,128)(2,1)} %bitcast.11.y2, bf16[512,512]{1,0:T(8,128)(2,1)} %refs_0_.1, bf16[512,512]{1,0:T(8,128)(2,1)} %refs_1_.1, bf16[512,512]{1,0:T(8,128)(2,1)} %refs_2_.1, bf16[512,512]{1,0:T(8,128)(2,1)} %refs_3_.1, ...), custom_call_target="tpu_custom_call" | custom-call | flops 3489660928 | bytes 2097152 | tf_op jit(solution)/shard_map/windows/pallas_call | solution.py:351
  112.8 4.8 %all-to-all-start.1 = ((bf16[16,48,512]{2,1,0:T(8,128)(2,1)}), bf16[16,48,512]{2,1,0:T(8,128)(2,1)S(1)}, u32[]{:S(2)}, u32[]{:S(2)}) async-start(bf16[16,48,512]{2,1,0:T(8,128)(2,1)} %windows.1), calls=%async_computation.1 | async-start | bytes 1572864 | tf_op jit(solution)/shard_map/all_to_all | solution.py:607
  118.0 4.2 %collective-permute-done.29.refs_1_ = bf16[1,1,3,64,256]{4,3,2,1,0:T(8,128)(2,1)S(1)} collective-permute-done((bf16[1,1,3,64,256]{4,3,2,1,0:T(8,128)(2,1)S(1)}, bf16[1,1,3,64,256]{4,3,2,1,0:T(8,128)(2,1)S(1)}, u32[]{:S(2)}, u32[]{:S(2)}) %collective-permute-start.29) | collective-permute-done | bytes 98336 | tf_op jit(solution)/shard_map/ppermute | solution.py:94
  122.2 1.0 collective-permute-start.31
  123.2 0.6 copy-done.10
  124.2 0.6 copy-done.12
  124.8 12.3 %all-to-all-done.1.arrived = bf16[16,48,512]{2,1,0:T(8,128)(2,1)S(1)} async-done(((bf16[16,48,512]{2,1,0:T(8,128)(2,1)}), bf16[16,48,512]{2,1,0:T(8,128)(2,1)S(1)}, u32[]{:S(2)}, u32[]{:S(2)}) %all-to-all-start.1) | async-done | bytes 786464 | tf_op jit(solution)/shard_map/all_to_all | solution.py:607
  137.1 0.9 copy-done.11
  138.0 0.9 copy-done.13
  138.9 5.0 %upsample.1 = (bf16[32,16,512]{2,1,0:T(8,128)(2,1)}, bf16[2,256,512]{2,1,0:T(8,128)(2,1)}) custom-call(s32[13]{0:T(128)S(1)} %pad_add_fusion.info, s32[12]{0:T(128)S(1)} %concatenate.19.where, bf16[16,48,512]{2,1,0:T(8,128)(2,1)S(1)} %all-to-all-done.1.arrived, bf16[3,3,512,256]{3,2,1,0:T(8,128)(2,1)S(1)} %assemble.1.mine, ...), custom_call_target="tpu_custom_call" | custom-call | flops 754974720 | bytes 4718592 | tf_op jit(solution)/shard_map/upsample/pallas_call | solution.py:450
  (109 shorter events, 4.0 us)
Async XLA Ops:
  2.0 2.2 %collective-permute-start = (bf16[3,3,3,32,256]{4,3,2,1,0:T(8,128)(2,1)S(1)}, bf16[3,3,3,32,256]{4,3,2,1,0:T(8,128)(2,1)S(1)}, u32[]{:S(2)}, u32[]{:S(2)}) collective-permute-start(bf16[3,3,3,32,256]{4,3,2,1,0:T(8,128)(2,1)S(1)} %get-tuple-element.65), channel_id=1, source_target_pairs={{0,1},{1,0},{2,3},{3,2},{4,5},{5,4},{6,7},{7,6},{8,9},{9,8},{10,11... | collective-permute-start | bytes 1327112 | tf_op jit(solution)/shard_map/ppermute | solution.py:509
  4.4 12.1 %copy-start.16 = (bf16[3,3,3,64,256]{4,3,2,1,0:T(8,128)(2,1)}, bf16[3,3,3,64,256]{4,3,2,1,0:T(8,128)(2,1)S(1)}, u32[]{:S(2)}) copy-start(bf16[3,3,3,64,256]{4,3,2,1,0:T(8,128)(2,1)S(1)} %maximum_select_fusion.1) | copy-start | bytes 2654212
  4.5 13.4 %copy-start.20 = (s32[8]{0:T(128)S(1)}, s32[8]{0:T(128)}, u32[]{:S(2)}) copy-start(s32[8]{0:T(128)} %constant.133.clone) | copy-start | bytes 100
  4.6 12.1 %copy-start.17 = (bf16[3,2,3,64,256]{4,3,2,1,0:T(8,128)(2,1)}, bf16[3,2,3,64,256]{4,3,2,1,0:T(8,128)(2,1)S(1)}, u32[]{:S(2)}) copy-start(bf16[3,2,3,64,256]{4,3,2,1,0:T(8,128)(2,1)S(1)} %reverse_select_fusion) | copy-start | bytes 1769476
  4.7 10.4 %collective-permute-start.6 = (bf16[2,2,3,64,256]{4,3,2,1,0:T(8,128)(2,1)S(1)}, bf16[2,2,3,64,256]{4,3,2,1,0:T(8,128)(2,1)S(1)}, u32[]{:S(2)}, u32[]{:S(2)}) collective-permute-start(bf16[2,2,3,64,256]{4,3,2,1,0:T(8,128)(2,1)S(1)} %slice.101.refs_0_), channel_id=1, source_target_pairs={{4,0},{5,1},{8,4},{9,5},{12,8},{13,9},{14,12},{15,13},{10,14},{11,... | collective-permute-start | bytes 1179656 | tf_op jit(solution)/shard_map/ppermute | solution.py:80
  4.7 10.4 %collective-permute-start.1 = (bf16[2,2,3,64,256]{4,3,2,1,0:T(8,128)(2,1)S(1)}, bf16[2,2,3,64,256]{4,3,2,1,0:T(8,128)(2,1)S(1)}, u32[]{:S(2)}, u32[]{:S(2)}) collective-permute-start(bf16[2,2,3,64,256]{4,3,2,1,0:T(8,128)(2,1)S(1)} %slice.101.refs_0_), channel_id=1, source_target_pairs={{0,4},{1,5},{4,8},{5,9},{8,12},{9,13},{12,14},{13,15},{14,10},{15,... | collective-permute-start | bytes 1179656 | tf_op jit(solution)/shard_map/ppermute | solution.py:79
  15.2 9.5 %collective-permute-start.5 = (bf16[2,2,3,64,256]{4,3,2,1,0:T(8,128)(2,1)S(1)}, bf16[2,2,3,64,256]{4,3,2,1,0:T(8,128)(2,1)S(1)}, u32[]{:S(2)}, u32[]{:S(2)}) collective-permute-start(bf16[2,2,3,64,256]{4,3,2,1,0:T(8,128)(2,1)S(1)} %collective-permute-done.1.refs_1_), channel_id=1, source_target_pairs={{0,4},{1,5},{4,8},{5,9},{8,12},{9,13},{12,14},{13,15},{14,10},{15,... | collective-permute-start | bytes 1179656 | tf_op jit(solution)/shard_map/ppermute | solution.py:79
  16.5 9.0 %collective-permute-start.7 = (bf16[2,2,3,64,256]{4,3,2,1,0:T(8,128)(2,1)S(1)}, bf16[2,2,3,64,256]{4,3,2,1,0:T(8,128)(2,1)S(1)}, u32[]{:S(2)}, u32[]{:S(2)}) collective-permute-start(bf16[2,2,3,64,256]{4,3,2,1,0:T(8,128)(2,1)S(1)} %collective-permute-done.6.refs_2_), channel_id=1, source_target_pairs={{4,0},{5,1},{8,4},{9,5},{12,8},{13,9},{14,12},{15,13},{10,14},{11,... | collective-permute-start | bytes 1179656 | tf_op jit(solution)/shard_map/ppermute | solution.py:80
  16.7 8.8 %collective-permute-start.8 = (bf16[2,2,3,64,256]{4,3,2,1,0:T(8,128)(2,1)S(1)}, bf16[2,2,3,64,256]{4,3,2,1,0:T(8,128)(2,1)S(1)}, u32[]{:S(2)}, u32[]{:S(2)}) collective-permute-start(bf16[2,2,3,64,256]{4,3,2,1,0:T(8,128)(2,1)S(1)} %pad_maximum_fusion.1), channel_id=1, source_target_pairs={{0,16},{16,0},{1,17},{17,1},{2,18},{18,2},{3,19},{19,3},{4,20},{20... | collective-permute-start | bytes 1179656 | tf_op jit(solution)/shard_map/ppermute | solution.py:89
  18.0 10.4 %slice-start = ((bf16[3,3,3,64,256]{4,3,2,1,0:T(8,128)(2,1)}), bf16[3,1,3,64,256]{4,3,2,1,0:T(8,128)(2,1)S(1)}, s32[]{:S(2)}) async-start(bf16[3,3,3,64,256]{4,3,2,1,0:T(8,128)(2,1)} %copy-done.16), calls=%async_computation.2 | async-start | bytes 589824 | tf_op jit(solution)/shard_map/slice | solution.py:518
  18.0 19.4 %collective-permute-start.2 = (bf16[2,256,512]{2,1,0:T(8,128)(2,1)}, bf16[2,256,512]{2,1,0:T(8,128)(2,1)S(1)}, u32[]{:S(2)}, u32[]{:S(2)}) collective-permute-start(bf16[2,256,512]{2,1,0:T(8,128)(2,1)} %param.11), channel_id=1, source_target_pairs={{1,2},{2,1},{3,4},{4,3},{5,6},{6,5},{7,8},{8,7},{9,10},{10,9},{11,... | collective-permute-start | bytes 1572872 | tf_op jit(solution)/shard_map/ppermute | solution.py:527
  24.5 12.9 %collective-permute-start.3 = (bf16[2,256,512]{2,1,0:T(8,128)(2,1)}, bf16[2,256,512]{2,1,0:T(8,128)(2,1)S(1)}, u32[]{:S(2)}, u32[]{:S(2)}) collective-permute-start(bf16[2,256,512]{2,1,0:T(8,128)(2,1)} %param.11), channel_id=1, source_target_pairs={{0,1},{1,0},{2,3},{3,2},{4,5},{5,4},{6,7},{7,6},{8,9},{9,8},{10,11... | collective-permute-start | bytes 1572872 | tf_op jit(solution)/shard_map/ppermute | solution.py:528
  24.6 14.7 %copy-start.6 = (bf16[2,2,3,64,256]{4,3,2,1,0:T(8,128)(2,1)}, bf16[2,2,3,64,256]{4,3,2,1,0:T(8,128)(2,1)S(1)}, u32[]{:S(2)}) copy-start(bf16[2,2,3,64,256]{4,3,2,1,0:T(8,128)(2,1)S(1)} %collective-permute-done.5.refs_3_) | copy-start | bytes 1179652
  25.5 23.0 %copy-start.8 = (bf16[2,2,3,64,256]{4,3,2,1,0:T(8,128)(2,1)}, bf16[2,2,3,64,256]{4,3,2,1,0:T(8,128)(2,1)S(1)}, u32[]{:S(2)}) copy-start(bf16[2,2,3,64,256]{4,3,2,1,0:T(8,128)(2,1)S(1)} %collective-permute-done.7.refs_4_) | copy-start | bytes 1179652
  25.5 2.8 %copy-start.14 = (bf16[2,2,3,64,256]{4,3,2,1,0:T(8,128)(2,1)}, bf16[2,2,3,64,256]{4,3,2,1,0:T(8,128)(2,1)S(1)}, u32[]{:S(2)}) copy-start(bf16[2,2,3,64,256]{4,3,2,1,0:T(8,128)(2,1)S(1)} %collective-permute-done.8.refs_10_) | copy-start | bytes 1179652
  25.5 11.8 %collective-permute-start.9 = (bf16[2,2,3,64,256]{4,3,2,1,0:T(8,128)(2,1)S(1)}, bf16[2,2,3,64,256]{4,3,2,1,0:T(8,128)(2,1)S(1)}, u32[]{:S(2)}, u32[]{:S(2)}) collective-permute-start(bf16[2,2,3,64,256]{4,3,2,1,0:T(8,128)(2,1)S(1)} %collective-permute-done.5.refs_3_), channel_id=1, source_target_pairs={{0,4},{1,5},{4,8},{5,9},{8,12},{9,13},{12,14},{13,15},{14,10},{15,... | collective-permute-start | bytes 1179656 | tf_op jit(solution)/shard_map/ppermute | solution.py:79
  26.8 11.2 %collective-permute-start.10 = (bf16[2,2,3,64,256]{4,3,2,1,0:T(8,128)(2,1)S(1)}, bf16[2,2,3,64,256]{4,3,2,1,0:T(8,128)(2,1)S(1)}, u32[]{:S(2)}, u32[]{:S(2)}) collective-permute-start(bf16[2,2,3,64,256]{4,3,2,1,0:T(8,128)(2,1)S(1)} %collective-permute-done.7.refs_4_), channel_id=1, source_target_pairs={{4,0},{5,1},{8,4},{9,5},{12,8},{13,9},{14,12},{15,13},{10,14},{11,... | collective-permute-start | bytes 1179656 | tf_op jit(solution)/shard_map/ppermute | solution.py:80
  27.1 29.7 %copy-start.19 = (bf16[2,256,512]{2,1,0:T(8,128)(2,1)S(1)}, bf16[2,256,512]{2,1,0:T(8,128)(2,1)}, u32[]{:S(2)}) copy-start(bf16[2,256,512]{2,1,0:T(8,128)(2,1)} %param.11) | copy-start | bytes 1572868
  27.1 10.9 %collective-permute-start.11 = (bf16[2,2,3,64,256]{4,3,2,1,0:T(8,128)(2,1)S(1)}, bf16[2,2,3,64,256]{4,3,2,1,0:T(8,128)(2,1)S(1)}, u32[]{:S(2)}, u32[]{:S(2)}) collective-permute-start(bf16[2,2,3,64,256]{4,3,2,1,0:T(8,128)(2,1)S(1)} %pad_maximum_fusion.2), channel_id=1, source_target_pairs={{0,16},{16,0},{1,17},{17,1},{2,18},{18,2},{3,19},{19,3},{4,20},{20... | collective-permute-start | bytes 1179656 | tf_op jit(solution)/shard_map/ppermute | solution.py:89
  28.4 30.4 %copy-start.18 = (bf16[3,1,3,64,256]{4,3,2,1,0:T(8,128)(2,1)}, bf16[3,1,3,64,256]{4,3,2,1,0:T(8,128)(2,1)S(1)}, u32[]{:S(2)}) copy-start(bf16[3,1,3,64,256]{4,3,2,1,0:T(8,128)(2,1)S(1)} %reverse_select_fusion.1) | copy-start | bytes 884740
  37.4 19.5 %collective-permute-start.4 = (bf16[2,256,512]{2,1,0:T(8,128)(2,1)S(1)}, bf16[2,256,512]{2,1,0:T(8,128)(2,1)S(1)}, u32[]{:S(2)}, u32[]{:S(2)}) collective-permute-start(bf16[2,256,512]{2,1,0:T(8,128)(2,1)S(1)} %collective-permute-done.2), channel_id=1, source_target_pairs={{0,1},{1,0},{2,3},{3,2},{4,5},{5,4},{6,7},{7,6},{8,9},{9,8},{10,11... | collective-permute-start | bytes 1572872 | tf_op jit(solution)/shard_map/ppermute | solution.py:529
  38.1 13.6 %collective-permute-start.12 = (bf16[2,1,3,64,256]{4,3,2,1,0:T(8,128)(2,1)S(1)}, bf16[2,1,3,64,256]{4,3,2,1,0:T(8,128)(2,1)S(1)}, u32[]{:S(2)}, u32[]{:S(2)}) collective-permute-start(bf16[2,1,3,64,256]{4,3,2,1,0:T(8,128)(2,1)S(1)} %slice.81), channel_id=1, source_target_pairs={{0,4},{1,5},{4,8},{5,9},{8,12},{9,13},{12,14},{13,15},{14,10},{15,... | collective-permute-start | bytes 589832 | tf_op jit(solution)/shard_map/ppermute | solution.py:77
  39.3 13.7 %collective-permute-start.13 = (bf16[2,1,3,64,256]{4,3,2,1,0:T(8,128)(2,1)S(1)}, bf16[2,1,3,64,256]{4,3,2,1,0:T(8,128)(2,1)S(1)}, u32[]{:S(2)}, u32[]{:S(2)}) collective-permute-start(bf16[2,1,3,64,256]{4,3,2,1,0:T(8,128)(2,1)S(1)} %slice.82), channel_id=1, source_target_pairs={{4,0},{5,1},{8,4},{9,5},{12,8},{13,9},{14,12},{15,13},{10,14},{11,... | collective-permute-start | bytes 589832 | tf_op jit(solution)/shard_map/ppermute | solution.py:77
  46.5 7.7 %collective-permute-start.14 = (bf16[2,1,3,64,256]{4,3,2,1,0:T(8,128)(2,1)S(1)}, bf16[2,1,3,64,256]{4,3,2,1,0:T(8,128)(2,1)S(1)}, u32[]{:S(2)}, u32[]{:S(2)}) collective-permute-start(bf16[2,1,3,64,256]{4,3,2,1,0:T(8,128)(2,1)S(1)} %slice.107.refs_0_), channel_id=1, source_target_pairs={{0,4},{1,5},{4,8},{5,9},{8,12},{9,13},{12,14},{13,15},{14,10},{15,... | collective-permute-start | bytes 589832 | tf_op jit(solution)/shard_map/ppermute | solution.py:79
  46.5 7.7 %collective-permute-start.15 = (bf16[2,1,3,64,256]{4,3,2,1,0:T(8,128)(2,1)S(1)}, bf16[2,1,3,64,256]{4,3,2,1,0:T(8,128)(2,1)S(1)}, u32[]{:S(2)}, u32[]{:S(2)}) collective-permute-start(bf16[2,1,3,64,256]{4,3,2,1,0:T(8,128)(2,1)S(1)} %slice.107.refs_0_), channel_id=1, source_target_pairs={{4,0},{5,1},{8,4},{9,5},{12,8},{13,9},{14,12},{15,13},{10,14},{11,... | collective-permute-start | bytes 589832 | tf_op jit(solution)/shard_map/ppermute | solution.py:80
  51.6 9.6 %collective-permute-start.16 = (bf16[2,1,3,64,256]{4,3,2,1,0:T(8,128)(2,1)S(1)}, bf16[2,1,3,64,256]{4,3,2,1,0:T(8,128)(2,1)S(1)}, u32[]{:S(2)}, u32[]{:S(2)}) collective-permute-start(bf16[2,1,3,64,256]{4,3,2,1,0:T(8,128)(2,1)S(1)} %pad_maximum_fusion.4), channel_id=1, source_target_pairs={{0,16},{16,0},{1,17},{17,1},{2,18},{18,2},{3,19},{19,3},{4,20},{20... | collective-permute-start | bytes 589832 | tf_op jit(solution)/shard_map/ppermute | solution.py:89
  54.2 8.5 %collective-permute-start.17 = (bf16[1,1,3,64,256]{4,3,2,1,0:T(8,128)(2,1)S(1)}, bf16[1,1,3,64,256]{4,3,2,1,0:T(8,128)(2,1)S(1)}, u32[]{:S(2)}, u32[]{:S(2)}) collective-permute-start(bf16[1,1,3,64,256]{4,3,2,1,0:T(8,128)(2,1)S(1)} %slice.88), channel_id=1, source_target_pairs={{0,16},{16,0},{1,17},{17,1},{2,18},{18,2},{3,19},{19,3},{4,20},{20... | collective-permute-start | bytes 294920 | tf_op jit(solution)/shard_map/ppermute | solution.py:94
  56.7 6.1 %copy-start.7 = (bf16[2,2,3,64,256]{4,3,2,1,0:T(8,128)(2,1)S(1)}, bf16[2,2,3,64,256]{4,3,2,1,0:T(8,128)(2,1)}, u32[]{:S(2)}) copy-start(bf16[2,2,3,64,256]{4,3,2,1,0:T(8,128)(2,1)} %copy-done.6) | copy-start | bytes 1179652
  56.7 6.0 %copy-start.9 = (bf16[2,2,3,64,256]{4,3,2,1,0:T(8,128)(2,1)S(1)}, bf16[2,2,3,64,256]{4,3,2,1,0:T(8,128)(2,1)}, u32[]{:S(2)}) copy-start(bf16[2,2,3,64,256]{4,3,2,1,0:T(8,128)(2,1)} %copy-done.8) | copy-start | bytes 1179652
  56.7 6.0 %copy-start.15 = (bf16[2,2,3,64,256]{4,3,2,1,0:T(8,128)(2,1)S(1)}, bf16[2,2,3,64,256]{4,3,2,1,0:T(8,128)(2,1)}, u32[]{:S(2)}) copy-start(bf16[2,2,3,64,256]{4,3,2,1,0:T(8,128)(2,1)} %copy-done.14) | copy-start | bytes 1179652
  56.7 12.6 %collective-permute-start.20 = (bf16[2,1,3,64,256]{4,3,2,1,0:T(8,128)(2,1)S(1)}, bf16[2,1,3,64,256]{4,3,2,1,0:T(8,128)(2,1)S(1)}, u32[]{:S(2)}, u32[]{:S(2)}) collective-permute-start(bf16[2,1,3,64,256]{4,3,2,1,0:T(8,128)(2,1)S(1)} %pad_maximum_fusion.5), channel_id=1, source_target_pairs={{0,16},{16,0},{1,17},{17,1},{2,18},{18,2},{3,19},{19,3},{4,20},{20... | collective-permute-start | bytes 589832 | tf_op jit(solution)/shard_map/ppermute | solution.py:89
  58.9 10.5 %collective-permute-start.18 = (bf16[2,1,3,64,256]{4,3,2,1,0:T(8,128)(2,1)S(1)}, bf16[2,1,3,64,256]{4,3,2,1,0:T(8,128)(2,1)S(1)}, u32[]{:S(2)}, u32[]{:S(2)}) collective-permute-start(bf16[2,1,3,64,256]{4,3,2,1,0:T(8,128)(2,1)S(1)} %collective-permute-done.14.refs_1_), channel_id=1, source_target_pairs={{0,4},{1,5},{4,8},{5,9},{8,12},{9,13},{12,14},{13,15},{14,10},{15,... | collective-permute-start | bytes 589832 | tf_op jit(solution)/shard_map/ppermute | solution.py:79
  58.9 10.4 %collective-permute-start.19 = (bf16[2,1,3,64,256]{4,3,2,1,0:T(8,128)(2,1)S(1)}, bf16[2,1,3,64,256]{4,3,2,1,0:T(8,128)(2,1)S(1)}, u32[]{:S(2)}, u32[]{:S(2)}) collective-permute-start(bf16[2,1,3,64,256]{4,3,2,1,0:T(8,128)(2,1)S(1)} %collective-permute-done.15.refs_2_), channel_id=1, source_target_pairs={{4,0},{5,1},{8,4},{9,5},{12,8},{13,9},{14,12},{15,13},{10,14},{11,... | collective-permute-start | bytes 589832 | tf_op jit(solution)/shard_map/ppermute | solution.py:80
  61.3 8.1 %collective-permute-start.21 = (bf16[3,1,3,64,256]{4,3,2,1,0:T(8,128)(2,1)S(1)}, bf16[3,1,3,64,256]{4,3,2,1,0:T(8,128)(2,1)S(1)}, u32[]{:S(2)}, u32[]{:S(2)}) collective-permute-start(bf16[3,1,3,64,256]{4,3,2,1,0:T(8,128)(2,1)S(1)} %pad_maximum_fusion.3), channel_id=1, source_target_pairs={{0,16},{16,0},{1,17},{17,1},{2,18},{18,2},{3,19},{19,3},{4,20},{20... | collective-permute-start | bytes 884744 | tf_op jit(solution)/shard_map/ppermute | solution.py:100
  69.4 3.9 %copy-start.2 = (bf16[2,1,3,64,256]{4,3,2,1,0:T(8,128)(2,1)}, bf16[2,1,3,64,256]{4,3,2,1,0:T(8,128)(2,1)S(1)}, u32[]{:S(2)}) copy-start(bf16[2,1,3,64,256]{4,3,2,1,0:T(8,128)(2,1)S(1)} %collective-permute-done.20.refs_8_) | copy-start | bytes 589828
  69.4 5.6 %collective-permute-start.22 = (bf16[6,256,256]{2,1,0:T(8,128)(2,1)S(1)}, bf16[6,256,256]{2,1,0:T(8,128)(2,1)S(1)}, u32[]{:S(2)}, u32[]{:S(2)}) collective-permute-start(bf16[6,256,256]{2,1,0:T(8,128)(2,1)S(1)} %get-tuple-element.48.mine), channel_id=1, source_target_pairs={{0,1},{1,0},{2,3},{3,2},{4,5},{5,4},{6,7},{7,6},{8,9},{9,8},{10,11... | collective-permute-start | bytes 2359304 | tf_op jit(solution)/shard_map/ppermute | solution.py:566
  72.9 7.9 %collective-permute-start.25 = (bf16[2,1,3,64,256]{4,3,2,1,0:T(8,128)(2,1)S(1)}, bf16[2,1,3,64,256]{4,3,2,1,0:T(8,128)(2,1)S(1)}, u32[]{:S(2)}, u32[]{:S(2)}) collective-permute-start(bf16[2,1,3,64,256]{4,3,2,1,0:T(8,128)(2,1)S(1)} %pad_maximum_fusion.6), channel_id=1, source_target_pairs={{0,16},{16,0},{1,17},{17,1},{2,18},{18,2},{3,19},{19,3},{4,20},{20... | collective-permute-start | bytes 589832 | tf_op jit(solution)/shard_map/ppermute | solution.py:89
  73.3 8.2 %collective-permute-start.23 = (bf16[2,1,3,64,256]{4,3,2,1,0:T(8,128)(2,1)S(1)}, bf16[2,1,3,64,256]{4,3,2,1,0:T(8,128)(2,1)S(1)}, u32[]{:S(2)}, u32[]{:S(2)}) collective-permute-start(bf16[2,1,3,64,256]{4,3,2,1,0:T(8,128)(2,1)S(1)} %collective-permute-done.18.refs_3_), channel_id=1, source_target_pairs={{0,4},{1,5},{4,8},{5,9},{8,12},{9,13},{12,14},{13,15},{14,10},{15,... | collective-permute-start | bytes 589832 | tf_op jit(solution)/shard_map/ppermute | solution.py:79
  75.0 6.5 %collective-permute-start.24 = (bf16[2,1,3,64,256]{4,3,2,1,0:T(8,128)(2,1)S(1)}, bf16[2,1,3,64,256]{4,3,2,1,0:T(8,128)(2,1)S(1)}, u32[]{:S(2)}, u32[]{:S(2)}) collective-permute-start(bf16[2,1,3,64,256]{4,3,2,1,0:T(8,128)(2,1)S(1)} %collective-permute-done.19.refs_4_), channel_id=1, source_target_pairs={{4,0},{5,1},{8,4},{9,5},{12,8},{13,9},{14,12},{15,13},{10,14},{11,... | collective-permute-start | bytes 589832 | tf_op jit(solution)/shard_map/ppermute | solution.py:80
  81.5 7.6 %copy-start = (bf16[2,1,3,64,256]{4,3,2,1,0:T(8,128)(2,1)}, bf16[2,1,3,64,256]{4,3,2,1,0:T(8,128)(2,1)S(1)}, u32[]{:S(2)}) copy-start(bf16[2,1,3,64,256]{4,3,2,1,0:T(8,128)(2,1)S(1)} %collective-permute-done.24.refs_6_) | copy-start | bytes 589828
  81.5 20.8 %all-to-all-start = ((bf16[16,4,16,256]{3,2,1,0:T(8,128)(2,1)}), bf16[16,4,16,256]{3,2,1,0:T(8,128)(2,1)}, u32[]{:S(2)}, u32[]{:S(2)}) async-start(bf16[16,4,16,256]{3,2,1,0:T(8,128)(2,1)} %second_conv.1), calls=%async_computation | async-start | bytes 1048576 | tf_op jit(solution)/shard_map/all_to_all | solution.py:587
  88.1 6.3 %collective-permute-start.26 = (bf16[2,1,3,64,256]{4,3,2,1,0:T(8,128)(2,1)S(1)}, bf16[2,1,3,64,256]{4,3,2,1,0:T(8,128)(2,1)S(1)}, u32[]{:S(2)}, u32[]{:S(2)}) collective-permute-start(bf16[2,1,3,64,256]{4,3,2,1,0:T(8,128)(2,1)S(1)} %pad_maximum_fusion.7), channel_id=1, source_target_pairs={{0,16},{16,0},{1,17},{17,1},{2,18},{18,2},{3,19},{19,3},{4,20},{20... | collective-permute-start | bytes 589832 | tf_op jit(solution)/shard_map/ppermute | solution.py:89
  98.9 25.9 %collective-permute-start.28 = (bf16[3,3,512,256]{3,2,1,0:T(8,128)(2,1)S(1)}, bf16[3,3,512,256]{3,2,1,0:T(8,128)(2,1)}, u32[]{:S(2)}, u32[]{:S(2)}) collective-permute-start(bf16[3,3,512,256]{3,2,1,0:T(8,128)(2,1)S(1)} %assemble.1.mine), channel_id=1, source_target_pairs={{0,1},{1,0},{2,3},{3,2},{4,5},{5,4},{6,7},{7,6},{8,9},{9,8},{10,11... | collective-permute-start | bytes 7077896 | tf_op jit(solution)/shard_map/ppermute | solution.py:592
  102.3 10.5 %collective-permute-start.27 = (bf16[2,1,3,64,256]{4,3,2,1,0:T(8,128)(2,1)S(1)}, bf16[2,1,3,64,256]{4,3,2,1,0:T(8,128)(2,1)S(1)}, u32[]{:S(2)}, u32[]{:S(2)}) collective-permute-start(bf16[2,1,3,64,256]{4,3,2,1,0:T(8,128)(2,1)S(1)} %collective-permute-done.23.refs_5_), channel_id=1, source_target_pairs={{0,4},{1,5},{4,8},{5,9},{8,12},{9,13},{12,14},{13,15},{14,10},{15,... | collective-permute-start | bytes 589832 | tf_op jit(solution)/shard_map/ppermute | solution.py:77
  112.8 24.3 %all-to-all-start.1 = ((bf16[16,48,512]{2,1,0:T(8,128)(2,1)}), bf16[16,48,512]{2,1,0:T(8,128)(2,1)S(1)}, u32[]{:S(2)}, u32[]{:S(2)}) async-start(bf16[16,48,512]{2,1,0:T(8,128)(2,1)} %windows.1), calls=%async_computation.1 | async-start | bytes 1572864 | tf_op jit(solution)/shard_map/all_to_all | solution.py:607
  117.6 6.4 %collective-permute-start.30 = (bf16[2,1,3,64,256]{4,3,2,1,0:T(8,128)(2,1)S(1)}, bf16[2,1,3,64,256]{4,3,2,1,0:T(8,128)(2,1)S(1)}, u32[]{:S(2)}, u32[]{:S(2)}) collective-permute-start(bf16[2,1,3,64,256]{4,3,2,1,0:T(8,128)(2,1)S(1)} %collective-permute-done.27.refs_0_), channel_id=1, source_target_pairs={{0,1},{1,0},{2,3},{3,2},{4,5},{5,4},{6,7},{7,6},{8,9},{9,8},{10,11... | collective-permute-start | bytes 589832 | tf_op jit(solution)/shard_map/ppermute | solution.py:622
  118.0 4.2 %collective-permute-start.29 = (bf16[1,1,3,64,256]{4,3,2,1,0:T(8,128)(2,1)S(1)}, bf16[1,1,3,64,256]{4,3,2,1,0:T(8,128)(2,1)S(1)}, u32[]{:S(2)}, u32[]{:S(2)}) collective-permute-start(bf16[1,1,3,64,256]{4,3,2,1,0:T(8,128)(2,1)S(1)} %slice.99), channel_id=1, source_target_pairs={{0,16},{16,0},{1,17},{17,1},{2,18},{18,2},{3,19},{19,3},{4,20},{20... | collective-permute-start | bytes 294920 | tf_op jit(solution)/shard_map/ppermute | solution.py:94
  122.2 1.9 %collective-permute-start.31 = (bf16[1,1,3,64,256]{4,3,2,1,0:T(8,128)(2,1)S(1)}, bf16[1,1,3,64,256]{4,3,2,1,0:T(8,128)(2,1)S(1)}, u32[]{:S(2)}, u32[]{:S(2)}) collective-permute-start(bf16[1,1,3,64,256]{4,3,2,1,0:T(8,128)(2,1)S(1)} %collective-permute-done.29.refs_1_), channel_id=1, source_target_pairs={{0,1},{1,0},{2,3},{3,2},{4,5},{5,4},{6,7},{7,6},{8,9},{9,8},{10,11... | collective-permute-start | bytes 294920 | tf_op jit(solution)/shard_map/ppermute | solution.py:622
  (8 other events, 6.5 us)

commit v6 on v5

--- a/solution.py
+++ b/solution.py
@@ -305,8 +305,8 @@
                     keep, key, (((1,), (1,)), ((), ())), preferred_element_type=F32
                 )
                 lifted = jnp.exp(scores - jnp.max(scores, axis=-1, keepdims=True))
-                probs = lifted * (1.0 / jnp.sum(lifted, axis=-1, keepdims=True))
-                halves.append(dot(probs.astype(BF16), value))
+                share = 1.0 / jnp.sum(lifted, axis=-1, keepdims=True)
+                halves.append(dot(lifted.astype(BF16), value) * share)
             att[spot] = jnp.where(low, halves[0], halves[1]).astype(BF16)
     for copy in copies[3:]:
         copy.wait()

time: 145 us -> 144 us (level)
  transfers between devices with their start and end apart: 34 -> 34, of which waited for: 14 -> 14; matrix products, arithmetic and copies ran while one was open for 4% -> 4% of each run, Pallas kernels for 17% -> 16%
where the time goes in v6:
time: 144 us; the launch traced here: 143 us
  starting transfers between devices  51.9 us (36%)
  waiting for transfers between devices  48 us (33%)
  Pallas kernels  28.6 us (20%)
  local copies, waits for them, and re-layouts  8.93 us (6%)
  other arithmetic  4.54 us (3%)
    all_to_all x1, waiting for transfers between devices, on_device(): lax.all_to_all(sent[0], 'row', split_axis=0, concat_axis=0, axis_index_gr...  12.3 us
    ppermute x6, waiting for transfers between devices, step(): self.down = lax.ppermute(self.down, 'row', backward)  10.4 us
    pallas_call x1, Pallas kernels, windows(): pl.pallas_call(functools.partial(window_kernel, per), out_shape=tuple((ja...  9.49 us
    ppermute x3, starting transfers between devices, step(): self.finals.append(lax.ppermute(value[:, kernel:kernel + 1], 'row', pairs))  8.63 us
    ppermute x1, waiting for transfers between devices, on_device(): near = lax.ppermute(beside, 'row', edges)  7.86 us
    pallas_call x1, Pallas kernels, first_conv(): pl.pallas_call(functools.partial(first_conv_kernel, step), out_shape=(out...  6.57 us
    unnamed x42, local copies, waits for them, and re-layouts  6.57 us
    all_to_all x1, starting transfers between devices, on_device(): lax.all_to_all(y2, 'row', split_axis=0, concat_axis=0, axis_index_groups=...  6.51 us
  transfers between devices with their start and end apart: 34, of which 14 were waited for; matrix products, arithmetic and copies ran while one was open for 4% of the time, Pallas kernels for 16%

profile of v6, /device:TPU:9, one launch (start us, length us, event | category | flops | bytes accessed | tf_op | source)
XLA Modules:
  0.0 143.3 jit_solution(18074434623074614706)
XLA Ops:
  0.7 1.2 pad_maximum_fusion
  2.0 0.7 collective-permute-start
  2.7 1.4 collective-permute-done
  4.7 1.5 %collective-permute-start.1 = (bf16[2,2,3,64,256]{4,3,2,1,0:T(8,128)(2,1)S(1)}, bf16[2,2,3,64,256]{4,3,2,1,0:T(8,128)(2,1)S(1)}, u32[]{:S(2)}, u32[]{:S(2)}) collective-permute-start(bf16[2,2,3,64,256]{4,3,2,1,0:T(8,128)(2,1)S(1)} %slice.101.refs_0_), channel_id=1, source_target_pairs={{0,4},{1,5},{4,8},{5,9},{8,12},{9,13},{12,14},{13,15},{14,10},{15,... | collective-permute-start | bytes 1179656 | tf_op jit(solution)/shard_map/ppermute | solution.py:79
  6.2 8.9 %collective-permute-done.6.refs_2_ = bf16[2,2,3,64,256]{4,3,2,1,0:T(8,128)(2,1)S(1)} collective-permute-done((bf16[2,2,3,64,256]{4,3,2,1,0:T(8,128)(2,1)S(1)}, bf16[2,2,3,64,256]{4,3,2,1,0:T(8,128)(2,1)S(1)}, u32[]{:S(2)}, u32[]{:S(2)}) %collective-permute-start.6) | collective-permute-done | bytes 393248 | tf_op jit(solution)/shard_map/ppermute | solution.py:80
  15.2 1.3 collective-permute-start.5
  16.7 1.2 collective-permute-start.8
  18.0 6.5 %collective-permute-start.2 = (bf16[2,256,512]{2,1,0:T(8,128)(2,1)}, bf16[2,256,512]{2,1,0:T(8,128)(2,1)S(1)}, u32[]{:S(2)}, u32[]{:S(2)}) collective-permute-start(bf16[2,256,512]{2,1,0:T(8,128)(2,1)} %param.11), channel_id=1, source_target_pairs={{1,2},{2,1},{3,4},{4,3},{5,6},{6,5},{7,8},{8,7},{9,10},{10,9},{11,... | collective-permute-start | bytes 1572872 | tf_op jit(solution)/shard_map/ppermute | solution.py:527
  24.6 0.8 collective-permute-done.7.refs_4_
  25.5 1.3 collective-permute-start.9
  27.1 1.3 collective-permute-start.11
  28.5 1.0 slice_bitcast_fusion.refs_9_
  29.5 7.9 %collective-permute-done.2 = bf16[2,256,512]{2,1,0:T(8,128)(2,1)S(1)} collective-permute-done((bf16[2,256,512]{2,1,0:T(8,128)(2,1)}, bf16[2,256,512]{2,1,0:T(8,128)(2,1)S(1)}, u32[]{:S(2)}, u32[]{:S(2)}) %collective-permute-start.2) | collective-permute-done | bytes 524320 | tf_op jit(solution)/shard_map/ppermute | solution.py:527
  37.4 0.7 collective-permute-done.10.refs_6_
  38.1 1.2 collective-permute-start.12
  39.3 7.2 %collective-permute-start.13 = (bf16[2,1,3,64,256]{4,3,2,1,0:T(8,128)(2,1)S(1)}, bf16[2,1,3,64,256]{4,3,2,1,0:T(8,128)(2,1)S(1)}, u32[]{:S(2)}, u32[]{:S(2)}) collective-permute-start(bf16[2,1,3,64,256]{4,3,2,1,0:T(8,128)(2,1)S(1)} %slice.82), channel_id=1, source_target_pairs={{4,0},{5,1},{8,4},{9,5},{12,8},{13,9},{14,12},{15,13},{10,14},{11,... | collective-permute-start | bytes 589832 | tf_op jit(solution)/shard_map/ppermute | solution.py:77
  46.5 1.9 %collective-permute-start.15 = (bf16[2,1,3,64,256]{4,3,2,1,0:T(8,128)(2,1)S(1)}, bf16[2,1,3,64,256]{4,3,2,1,0:T(8,128)(2,1)S(1)}, u32[]{:S(2)}, u32[]{:S(2)}) collective-permute-start(bf16[2,1,3,64,256]{4,3,2,1,0:T(8,128)(2,1)S(1)} %slice.107.refs_0_), channel_id=1, source_target_pairs={{4,0},{5,1},{8,4},{9,5},{12,8},{13,9},{14,12},{15,13},{10,14},{11,... | collective-permute-start | bytes 589832 | tf_op jit(solution)/shard_map/ppermute | solution.py:80
  48.5 3.2 %collective-permute-done.12.refs_7_ = bf16[2,1,3,64,256]{4,3,2,1,0:T(8,128)(2,1)S(1)} collective-permute-done((bf16[2,1,3,64,256]{4,3,2,1,0:T(8,128)(2,1)S(1)}, bf16[2,1,3,64,256]{4,3,2,1,0:T(8,128)(2,1)S(1)}, u32[]{:S(2)}, u32[]{:S(2)}) %collective-permute-start.12) | collective-permute-done | bytes 196640 | tf_op jit(solution)/shard_map/ppermute | solution.py:77
  51.6 1.4 collective-permute-start.16
  53.0 1.2 collective-permute-done.14.refs_1_
  54.2 2.4 %collective-permute-start.17 = (bf16[1,1,3,64,256]{4,3,2,1,0:T(8,128)(2,1)S(1)}, bf16[1,1,3,64,256]{4,3,2,1,0:T(8,128)(2,1)S(1)}, u32[]{:S(2)}, u32[]{:S(2)}) collective-permute-start(bf16[1,1,3,64,256]{4,3,2,1,0:T(8,128)(2,1)S(1)} %slice.88), channel_id=1, source_target_pairs={{0,16},{16,0},{1,17},{17,1},{2,18},{18,2},{3,19},{19,3},{4,20},{20... | collective-permute-start | bytes 294920 | tf_op jit(solution)/shard_map/ppermute | solution.py:94
  56.8 2.0 %fusion.5 = (bf16[8,256,512]{2,1,0:T(8,128)(2,1)S(1)}, bf16[8,256,512]{2,1,0:T(8,128)(2,1)S(1)}) fusion(bf16[2,256,512]{2,1,0:T(8,128)(2,1)S(1)} %collective-permute-done.2, bf16[2,256,512]{2,1,0:T(8,128)(2,1)S(1)} %copy-done.19, bf16[2,256,512]{2,1,0:T(8,128)(2,1)S(1)} %collective-permute-done.3, bf16[2,256,512]{2,1,0:T(8,128)(2,1)S(1)} %collective-permute-done.4, ...), kind=kLoop, calls=%fused_computation.9 | loop fusion | flops 17825792 | bytes 6291457 | tf_op jit(solution)/shard_map/convert_element_type | solution.py:547
  58.9 2.3 %collective-permute-start.19 = (bf16[2,1,3,64,256]{4,3,2,1,0:T(8,128)(2,1)S(1)}, bf16[2,1,3,64,256]{4,3,2,1,0:T(8,128)(2,1)S(1)}, u32[]{:S(2)}, u32[]{:S(2)}) collective-permute-start(bf16[2,1,3,64,256]{4,3,2,1,0:T(8,128)(2,1)S(1)} %collective-permute-done.15.refs_2_), channel_id=1, source_target_pairs={{4,0},{5,1},{8,4},{9,5},{12,8},{13,9},{14,12},{15,13},{10,14},{11,... | collective-permute-start | bytes 589832 | tf_op jit(solution)/shard_map/ppermute | solution.py:80
  61.3 1.5 %collective-permute-start.21 = (bf16[3,1,3,64,256]{4,3,2,1,0:T(8,128)(2,1)S(1)}, bf16[3,1,3,64,256]{4,3,2,1,0:T(8,128)(2,1)S(1)}, u32[]{:S(2)}, u32[]{:S(2)}) collective-permute-start(bf16[3,1,3,64,256]{4,3,2,1,0:T(8,128)(2,1)S(1)} %pad_maximum_fusion.3), channel_id=1, source_target_pairs={{0,16},{16,0},{1,17},{17,1},{2,18},{18,2},{3,19},{19,3},{4,20},{20... | collective-permute-start | bytes 884744 | tf_op jit(solution)/shard_map/ppermute | solution.py:100
  62.8 6.6 %first_conv.1 = (bf16[6,256,256]{2,1,0:T(8,128)(2,1)S(1)}, bf16[6,256,256]{2,1,0:T(8,128)(2,1)S(1)}) custom-call(s32[12]{0:T(128)S(1)} %concatenate.19.where, bf16[8,256,512]{2,1,0:T(8,128)(2,1)S(1)} %get-tuple-element.40.act, bf16[8,256,512]{2,1,0:T(8,128)(2,1)S(1)} %get-tuple-element.63.lat, bf16[2,2,3,64,256]{4,3,2,1,0:T(8,128)(2,1)S(1)} %slice.101.refs_0_, ...), custom_call_target="tpu_custom_call" | custom-call | flops 3623878656 | bytes 2359296 | tf_op jit(solution)/shard_map/first_conv/pallas_call | solution.py:200
  69.4 3.5 %collective-permute-start.22 = (bf16[6,256,256]{2,1,0:T(8,128)(2,1)S(1)}, bf16[6,256,256]{2,1,0:T(8,128)(2,1)S(1)}, u32[]{:S(2)}, u32[]{:S(2)}) collective-permute-start(bf16[6,256,256]{2,1,0:T(8,128)(2,1)S(1)} %get-tuple-element.48.mine), channel_id=1, source_target_pairs={{0,1},{1,0},{2,3},{3,2},{4,5},{5,4},{6,7},{7,6},{8,9},{9,8},{10,11... | collective-permute-start | bytes 2359304 | tf_op jit(solution)/shard_map/ppermute | solution.py:566
  73.3 1.7 %collective-permute-start.23 = (bf16[2,1,3,64,256]{4,3,2,1,0:T(8,128)(2,1)S(1)}, bf16[2,1,3,64,256]{4,3,2,1,0:T(8,128)(2,1)S(1)}, u32[]{:S(2)}, u32[]{:S(2)}) collective-permute-start(bf16[2,1,3,64,256]{4,3,2,1,0:T(8,128)(2,1)S(1)} %collective-permute-done.18.refs_3_), channel_id=1, source_target_pairs={{0,4},{1,5},{4,8},{5,9},{8,12},{9,13},{12,14},{13,15},{14,10},{15,... | collective-permute-start | bytes 589832 | tf_op jit(solution)/shard_map/ppermute | solution.py:79
  75.0 5.8 %second_conv.1 = bf16[16,4,16,256]{3,2,1,0:T(8,128)(2,1)} custom-call(s32[12]{0:T(128)S(1)} %concatenate.19.where, bf16[6,256,256]{2,1,0:T(8,128)(2,1)S(1)} %get-tuple-element.43.y1, bf16[6,256,256]{2,1,0:T(8,128)(2,1)S(1)} %get-tuple-element.48.mine, bf16[6,256,256]{2,1,0:T(8,128)(2,1)S(1)} %collective-permute-done.22.theirs, ...), custom_call_target="tpu_custom_call" | custom-call | flops 2415919104 | bytes 2359296 | tf_op jit(solution)/shard_map/second_conv/pallas_call | solution.py:245
  80.8 0.7 copy-done.4
  81.5 6.5 %all-to-all-start = ((bf16[16,4,16,256]{3,2,1,0:T(8,128)(2,1)}), bf16[16,4,16,256]{3,2,1,0:T(8,128)(2,1)}, u32[]{:S(2)}, u32[]{:S(2)}) async-start(bf16[16,4,16,256]{3,2,1,0:T(8,128)(2,1)} %second_conv.1), calls=%async_computation | async-start | bytes 1048576 | tf_op jit(solution)/shard_map/all_to_all | solution.py:587
  88.2 0.9 slice_bitcast_fusion.1.refs_7_
  89.1 5.3 %collective-permute-done.26.refs_10_ = bf16[2,1,3,64,256]{4,3,2,1,0:T(8,128)(2,1)S(1)} collective-permute-done((bf16[2,1,3,64,256]{4,3,2,1,0:T(8,128)(2,1)S(1)}, bf16[2,1,3,64,256]{4,3,2,1,0:T(8,128)(2,1)S(1)}, u32[]{:S(2)}, u32[]{:S(2)}) %collective-permute-start.26) | collective-permute-done | bytes 196640 | tf_op jit(solution)/shard_map/ppermute | solution.py:89
  94.4 0.9 copy-done.1
  95.3 0.9 copy-done.3
  96.2 0.9 copy-done.5
  97.2 1.8 %assemble.1.mine = bf16[3,3,512,256]{3,2,1,0:T(8,128)(2,1)S(1)} custom-call(s32[12]{0:T(128)S(1)} %concatenate.19.where, bf16[2,1,3,64,256]{4,3,2,1,0:T(8,128)(2,1)S(1)} %slice.107.refs_0_, bf16[2,1,3,64,256]{4,3,2,1,0:T(8,128)(2,1)S(1)} %collective-permute-done.14.refs_1_, bf16[2,1,3,64,256]{4,3,2,1,0:T(8,128)(2,1)S(1)} %collective-permute-done.15.refs_2_, ...), custom_call_target="tpu_custom_call" | custom-call | bytes 4718592 | tf_op jit(solution)/shard_map/assemble/pallas_call | solution.py:142
  98.9 1.2 collective-permute-start.28
  100.6 1.6 %all-to-all-done = bf16[16,4,16,256]{3,2,1,0:T(8,128)(2,1)} async-done(((bf16[16,4,16,256]{3,2,1,0:T(8,128)(2,1)}), bf16[16,4,16,256]{3,2,1,0:T(8,128)(2,1)}, u32[]{:S(2)}, u32[]{:S(2)}) %all-to-all-start) | async-done | bytes 524320 | tf_op jit(solution)/shard_map/all_to_all | solution.py:587
  102.5 9.5 %windows.1 = bf16[16,48,512]{2,1,0:T(8,128)(2,1)} custom-call(s32[16]{0:T(128)} %fusion.8.picks, bf16[8,2,2,2,16,256]{5,4,3,2,1,0:T(8,128)(2,1)} %bitcast.11.y2, bf16[512,512]{1,0:T(8,128)(2,1)} %refs_0_.1, bf16[512,512]{1,0:T(8,128)(2,1)} %refs_1_.1, bf16[512,512]{1,0:T(8,128)(2,1)} %refs_2_.1, bf16[512,512]{1,0:T(8,128)(2,1)} %refs_3_.1, ...), custom_call_target="tpu_custom_call" | custom-call | flops 3489660928 | bytes 2097152 | tf_op jit(solution)/shard_map/windows/pallas_call | solution.py:351
  112.0 4.8 %all-to-all-start.1 = ((bf16[16,48,512]{2,1,0:T(8,128)(2,1)}), bf16[16,48,512]{2,1,0:T(8,128)(2,1)S(1)}, u32[]{:S(2)}, u32[]{:S(2)}) async-start(bf16[16,48,512]{2,1,0:T(8,128)(2,1)} %windows.1), calls=%async_computation.1 | async-start | bytes 1572864 | tf_op jit(solution)/shard_map/all_to_all | solution.py:607
  117.2 4.2 %collective-permute-done.29.refs_1_ = bf16[1,1,3,64,256]{4,3,2,1,0:T(8,128)(2,1)S(1)} collective-permute-done((bf16[1,1,3,64,256]{4,3,2,1,0:T(8,128)(2,1)S(1)}, bf16[1,1,3,64,256]{4,3,2,1,0:T(8,128)(2,1)S(1)}, u32[]{:S(2)}, u32[]{:S(2)}) %collective-permute-start.29) | collective-permute-done | bytes 98336 | tf_op jit(solution)/shard_map/ppermute | solution.py:94
  121.5 1.0 collective-permute-start.31
  122.4 0.6 copy-done.10
  123.4 0.6 copy-done.12
  124.0 12.3 %all-to-all-done.1.arrived = bf16[16,48,512]{2,1,0:T(8,128)(2,1)S(1)} async-done(((bf16[16,48,512]{2,1,0:T(8,128)(2,1)}), bf16[16,48,512]{2,1,0:T(8,128)(2,1)S(1)}, u32[]{:S(2)}, u32[]{:S(2)}) %all-to-all-start.1) | async-done | bytes 786464 | tf_op jit(solution)/shard_map/all_to_all | solution.py:607
  136.3 0.9 copy-done.11
  137.2 0.9 copy-done.13
  138.1 5.0 %upsample.1 = (bf16[32,16,512]{2,1,0:T(8,128)(2,1)}, bf16[2,256,512]{2,1,0:T(8,128)(2,1)}) custom-call(s32[13]{0:T(128)S(1)} %pad_add_fusion.info, s32[12]{0:T(128)S(1)} %concatenate.19.where, bf16[16,48,512]{2,1,0:T(8,128)(2,1)S(1)} %all-to-all-done.1.arrived, bf16[3,3,512,256]{3,2,1,0:T(8,128)(2,1)S(1)} %assemble.1.mine, ...), custom_call_target="tpu_custom_call" | custom-call | flops 754974720 | bytes 4718592 | tf_op jit(solution)/shard_map/upsample/pallas_call | solution.py:450
  (109 shorter events, 4.0 us)
Async XLA Ops:
  2.0 2.2 %collective-permute-start = (bf16[3,3,3,32,256]{4,3,2,1,0:T(8,128)(2,1)S(1)}, bf16[3,3,3,32,256]{4,3,2,1,0:T(8,128)(2,1)S(1)}, u32[]{:S(2)}, u32[]{:S(2)}) collective-permute-start(bf16[3,3,3,32,256]{4,3,2,1,0:T(8,128)(2,1)S(1)} %get-tuple-element.65), channel_id=1, source_target_pairs={{0,1},{1,0},{2,3},{3,2},{4,5},{5,4},{6,7},{7,6},{8,9},{9,8},{10,11... | collective-permute-start | bytes 1327112 | tf_op jit(solution)/shard_map/ppermute | solution.py:509
  4.4 12.1 %copy-start.16 = (bf16[3,3,3,64,256]{4,3,2,1,0:T(8,128)(2,1)}, bf16[3,3,3,64,256]{4,3,2,1,0:T(8,128)(2,1)S(1)}, u32[]{:S(2)}) copy-start(bf16[3,3,3,64,256]{4,3,2,1,0:T(8,128)(2,1)S(1)} %maximum_select_fusion.1) | copy-start | bytes 2654212
  4.5 13.4 %copy-start.20 = (s32[8]{0:T(128)S(1)}, s32[8]{0:T(128)}, u32[]{:S(2)}) copy-start(s32[8]{0:T(128)} %constant.133.clone) | copy-start | bytes 100
  4.6 12.1 %copy-start.17 = (bf16[3,2,3,64,256]{4,3,2,1,0:T(8,128)(2,1)}, bf16[3,2,3,64,256]{4,3,2,1,0:T(8,128)(2,1)S(1)}, u32[]{:S(2)}) copy-start(bf16[3,2,3,64,256]{4,3,2,1,0:T(8,128)(2,1)S(1)} %reverse_select_fusion) | copy-start | bytes 1769476
  4.7 10.4 %collective-permute-start.6 = (bf16[2,2,3,64,256]{4,3,2,1,0:T(8,128)(2,1)S(1)}, bf16[2,2,3,64,256]{4,3,2,1,0:T(8,128)(2,1)S(1)}, u32[]{:S(2)}, u32[]{:S(2)}) collective-permute-start(bf16[2,2,3,64,256]{4,3,2,1,0:T(8,128)(2,1)S(1)} %slice.101.refs_0_), channel_id=1, source_target_pairs={{4,0},{5,1},{8,4},{9,5},{12,8},{13,9},{14,12},{15,13},{10,14},{11,... | collective-permute-start | bytes 1179656 | tf_op jit(solution)/shard_map/ppermute | solution.py:80
  4.7 10.4 %collective-permute-start.1 = (bf16[2,2,3,64,256]{4,3,2,1,0:T(8,128)(2,1)S(1)}, bf16[2,2,3,64,256]{4,3,2,1,0:T(8,128)(2,1)S(1)}, u32[]{:S(2)}, u32[]{:S(2)}) collective-permute-start(bf16[2,2,3,64,256]{4,3,2,1,0:T(8,128)(2,1)S(1)} %slice.101.refs_0_), channel_id=1, source_target_pairs={{0,4},{1,5},{4,8},{5,9},{8,12},{9,13},{12,14},{13,15},{14,10},{15,... | collective-permute-start | bytes 1179656 | tf_op jit(solution)/shard_map/ppermute | solution.py:79
  15.2 9.5 %collective-permute-start.5 = (bf16[2,2,3,64,256]{4,3,2,1,0:T(8,128)(2,1)S(1)}, bf16[2,2,3,64,256]{4,3,2,1,0:T(8,128)(2,1)S(1)}, u32[]{:S(2)}, u32[]{:S(2)}) collective-permute-start(bf16[2,2,3,64,256]{4,3,2,1,0:T(8,128)(2,1)S(1)} %collective-permute-done.1.refs_1_), channel_id=1, source_target_pairs={{0,4},{1,5},{4,8},{5,9},{8,12},{9,13},{12,14},{13,15},{14,10},{15,... | collective-permute-start | bytes 1179656 | tf_op jit(solution)/shard_map/ppermute | solution.py:79
  16.5 9.0 %collective-permute-start.7 = (bf16[2,2,3,64,256]{4,3,2,1,0:T(8,128)(2,1)S(1)}, bf16[2,2,3,64,256]{4,3,2,1,0:T(8,128)(2,1)S(1)}, u32[]{:S(2)}, u32[]{:S(2)}) collective-permute-start(bf16[2,2,3,64,256]{4,3,2,1,0:T(8,128)(2,1)S(1)} %collective-permute-done.6.refs_2_), channel_id=1, source_target_pairs={{4,0},{5,1},{8,4},{9,5},{12,8},{13,9},{14,12},{15,13},{10,14},{11,... | collective-permute-start | bytes 1179656 | tf_op jit(solution)/shard_map/ppermute | solution.py:80
  16.7 8.8 %collective-permute-start.8 = (bf16[2,2,3,64,256]{4,3,2,1,0:T(8,128)(2,1)S(1)}, bf16[2,2,3,64,256]{4,3,2,1,0:T(8,128)(2,1)S(1)}, u32[]{:S(2)}, u32[]{:S(2)}) collective-permute-start(bf16[2,2,3,64,256]{4,3,2,1,0:T(8,128)(2,1)S(1)} %pad_maximum_fusion.1), channel_id=1, source_target_pairs={{0,16},{16,0},{1,17},{17,1},{2,18},{18,2},{3,19},{19,3},{4,20},{20... | collective-permute-start | bytes 1179656 | tf_op jit(solution)/shard_map/ppermute | solution.py:89
  18.0 10.4 %slice-start = ((bf16[3,3,3,64,256]{4,3,2,1,0:T(8,128)(2,1)}), bf16[3,1,3,64,256]{4,3,2,1,0:T(8,128)(2,1)S(1)}, s32[]{:S(2)}) async-start(bf16[3,3,3,64,256]{4,3,2,1,0:T(8,128)(2,1)} %copy-done.16), calls=%async_computation.2 | async-start | bytes 589824 | tf_op jit(solution)/shard_map/slice | solution.py:518
  18.0 19.4 %collective-permute-start.2 = (bf16[2,256,512]{2,1,0:T(8,128)(2,1)}, bf16[2,256,512]{2,1,0:T(8,128)(2,1)S(1)}, u32[]{:S(2)}, u32[]{:S(2)}) collective-permute-start(bf16[2,256,512]{2,1,0:T(8,128)(2,1)} %param.11), channel_id=1, source_target_pairs={{1,2},{2,1},{3,4},{4,3},{5,6},{6,5},{7,8},{8,7},{9,10},{10,9},{11,... | collective-permute-start | bytes 1572872 | tf_op jit(solution)/shard_map/ppermute | solution.py:527
  24.5 12.9 %collective-permute-start.3 = (bf16[2,256,512]{2,1,0:T(8,128)(2,1)}, bf16[2,256,512]{2,1,0:T(8,128)(2,1)S(1)}, u32[]{:S(2)}, u32[]{:S(2)}) collective-permute-start(bf16[2,256,512]{2,1,0:T(8,128)(2,1)} %param.11), channel_id=1, source_target_pairs={{0,1},{1,0},{2,3},{3,2},{4,5},{5,4},{6,7},{7,6},{8,9},{9,8},{10,11... | collective-permute-start | bytes 1572872 | tf_op jit(solution)/shard_map/ppermute | solution.py:528
  24.6 14.7 %copy-start.6 = (bf16[2,2,3,64,256]{4,3,2,1,0:T(8,128)(2,1)}, bf16[2,2,3,64,256]{4,3,2,1,0:T(8,128)(2,1)S(1)}, u32[]{:S(2)}) copy-start(bf16[2,2,3,64,256]{4,3,2,1,0:T(8,128)(2,1)S(1)} %collective-permute-done.5.refs_3_) | copy-start | bytes 1179652
  25.5 23.0 %copy-start.8 = (bf16[2,2,3,64,256]{4,3,2,1,0:T(8,128)(2,1)}, bf16[2,2,3,64,256]{4,3,2,1,0:T(8,128)(2,1)S(1)}, u32[]{:S(2)}) copy-start(bf16[2,2,3,64,256]{4,3,2,1,0:T(8,128)(2,1)S(1)} %collective-permute-done.7.refs_4_) | copy-start | bytes 1179652
  25.5 2.8 %copy-start.14 = (bf16[2,2,3,64,256]{4,3,2,1,0:T(8,128)(2,1)}, bf16[2,2,3,64,256]{4,3,2,1,0:T(8,128)(2,1)S(1)}, u32[]{:S(2)}) copy-start(bf16[2,2,3,64,256]{4,3,2,1,0:T(8,128)(2,1)S(1)} %collective-permute-done.8.refs_10_) | copy-start | bytes 1179652
  25.5 11.8 %collective-permute-start.9 = (bf16[2,2,3,64,256]{4,3,2,1,0:T(8,128)(2,1)S(1)}, bf16[2,2,3,64,256]{4,3,2,1,0:T(8,128)(2,1)S(1)}, u32[]{:S(2)}, u32[]{:S(2)}) collective-permute-start(bf16[2,2,3,64,256]{4,3,2,1,0:T(8,128)(2,1)S(1)} %collective-permute-done.5.refs_3_), channel_id=1, source_target_pairs={{0,4},{1,5},{4,8},{5,9},{8,12},{9,13},{12,14},{13,15},{14,10},{15,... | collective-permute-start | bytes 1179656 | tf_op jit(solution)/shard_map/ppermute | solution.py:79
  26.8 11.2 %collective-permute-start.10 = (bf16[2,2,3,64,256]{4,3,2,1,0:T(8,128)(2,1)S(1)}, bf16[2,2,3,64,256]{4,3,2,1,0:T(8,128)(2,1)S(1)}, u32[]{:S(2)}, u32[]{:S(2)}) collective-permute-start(bf16[2,2,3,64,256]{4,3,2,1,0:T(8,128)(2,1)S(1)} %collective-permute-done.7.refs_4_), channel_id=1, source_target_pairs={{4,0},{5,1},{8,4},{9,5},{12,8},{13,9},{14,12},{15,13},{10,14},{11,... | collective-permute-start | bytes 1179656 | tf_op jit(solution)/shard_map/ppermute | solution.py:80
  27.1 29.7 %copy-start.19 = (bf16[2,256,512]{2,1,0:T(8,128)(2,1)S(1)}, bf16[2,256,512]{2,1,0:T(8,128)(2,1)}, u32[]{:S(2)}) copy-start(bf16[2,256,512]{2,1,0:T(8,128)(2,1)} %param.11) | copy-start | bytes 1572868
  27.1 10.9 %collective-permute-start.11 = (bf16[2,2,3,64,256]{4,3,2,1,0:T(8,128)(2,1)S(1)}, bf16[2,2,3,64,256]{4,3,2,1,0:T(8,128)(2,1)S(1)}, u32[]{:S(2)}, u32[]{:S(2)}) collective-permute-start(bf16[2,2,3,64,256]{4,3,2,1,0:T(8,128)(2,1)S(1)} %pad_maximum_fusion.2), channel_id=1, source_target_pairs={{0,16},{16,0},{1,17},{17,1},{2,18},{18,2},{3,19},{19,3},{4,20},{20... | collective-permute-start | bytes 1179656 | tf_op jit(solution)/shard_map/ppermute | solution.py:89
  28.4 30.4 %copy-start.18 = (bf16[3,1,3,64,256]{4,3,2,1,0:T(8,128)(2,1)}, bf16[3,1,3,64,256]{4,3,2,1,0:T(8,128)(2,1)S(1)}, u32[]{:S(2)}) copy-start(bf16[3,1,3,64,256]{4,3,2,1,0:T(8,128)(2,1)S(1)} %reverse_select_fusion.1) | copy-start | bytes 884740
  37.4 19.5 %collective-permute-start.4 = (bf16[2,256,512]{2,1,0:T(8,128)(2,1)S(1)}, bf16[2,256,512]{2,1,0:T(8,128)(2,1)S(1)}, u32[]{:S(2)}, u32[]{:S(2)}) collective-permute-start(bf16[2,256,512]{2,1,0:T(8,128)(2,1)S(1)} %collective-permute-done.2), channel_id=1, source_target_pairs={{0,1},{1,0},{2,3},{3,2},{4,5},{5,4},{6,7},{7,6},{8,9},{9,8},{10,11... | collective-permute-start | bytes 1572872 | tf_op jit(solution)/shard_map/ppermute | solution.py:529
  38.1 13.6 %collective-permute-start.12 = (bf16[2,1,3,64,256]{4,3,2,1,0:T(8,128)(2,1)S(1)}, bf16[2,1,3,64,256]{4,3,2,1,0:T(8,128)(2,1)S(1)}, u32[]{:S(2)}, u32[]{:S(2)}) collective-permute-start(bf16[2,1,3,64,256]{4,3,2,1,0:T(8,128)(2,1)S(1)} %slice.81), channel_id=1, source_target_pairs={{0,4},{1,5},{4,8},{5,9},{8,12},{9,13},{12,14},{13,15},{14,10},{15,... | collective-permute-start | bytes 589832 | tf_op jit(solution)/shard_map/ppermute | solution.py:77
  39.3 13.7 %collective-permute-start.13 = (bf16[2,1,3,64,256]{4,3,2,1,0:T(8,128)(2,1)S(1)}, bf16[2,1,3,64,256]{4,3,2,1,0:T(8,128)(2,1)S(1)}, u32[]{:S(2)}, u32[]{:S(2)}) collective-permute-start(bf16[2,1,3,64,256]{4,3,2,1,0:T(8,128)(2,1)S(1)} %slice.82), channel_id=1, source_target_pairs={{4,0},{5,1},{8,4},{9,5},{12,8},{13,9},{14,12},{15,13},{10,14},{11,... | collective-permute-start | bytes 589832 | tf_op jit(solution)/shard_map/ppermute | solution.py:77
  46.5 7.7 %collective-permute-start.14 = (bf16[2,1,3,64,256]{4,3,2,1,0:T(8,128)(2,1)S(1)}, bf16[2,1,3,64,256]{4,3,2,1,0:T(8,128)(2,1)S(1)}, u32[]{:S(2)}, u32[]{:S(2)}) collective-permute-start(bf16[2,1,3,64,256]{4,3,2,1,0:T(8,128)(2,1)S(1)} %slice.107.refs_0_), channel_id=1, source_target_pairs={{0,4},{1,5},{4,8},{5,9},{8,12},{9,13},{12,14},{13,15},{14,10},{15,... | collective-permute-start | bytes 589832 | tf_op jit(solution)/shard_map/ppermute | solution.py:79
  46.5 7.7 %collective-permute-start.15 = (bf16[2,1,3,64,256]{4,3,2,1,0:T(8,128)(2,1)S(1)}, bf16[2,1,3,64,256]{4,3,2,1,0:T(8,128)(2,1)S(1)}, u32[]{:S(2)}, u32[]{:S(2)}) collective-permute-start(bf16[2,1,3,64,256]{4,3,2,1,0:T(8,128)(2,1)S(1)} %slice.107.refs_0_), channel_id=1, source_target_pairs={{4,0},{5,1},{8,4},{9,5},{12,8},{13,9},{14,12},{15,13},{10,14},{11,... | collective-permute-start | bytes 589832 | tf_op jit(solution)/shard_map/ppermute | solution.py:80
  51.6 9.6 %collective-permute-start.16 = (bf16[2,1,3,64,256]{4,3,2,1,0:T(8,128)(2,1)S(1)}, bf16[2,1,3,64,256]{4,3,2,1,0:T(8,128)(2,1)S(1)}, u32[]{:S(2)}, u32[]{:S(2)}) collective-permute-start(bf16[2,1,3,64,256]{4,3,2,1,0:T(8,128)(2,1)S(1)} %pad_maximum_fusion.4), channel_id=1, source_target_pairs={{0,16},{16,0},{1,17},{17,1},{2,18},{18,2},{3,19},{19,3},{4,20},{20... | collective-permute-start | bytes 589832 | tf_op jit(solution)/shard_map/ppermute | solution.py:89
  54.2 8.5 %collective-permute-start.17 = (bf16[1,1,3,64,256]{4,3,2,1,0:T(8,128)(2,1)S(1)}, bf16[1,1,3,64,256]{4,3,2,1,0:T(8,128)(2,1)S(1)}, u32[]{:S(2)}, u32[]{:S(2)}) collective-permute-start(bf16[1,1,3,64,256]{4,3,2,1,0:T(8,128)(2,1)S(1)} %slice.88), channel_id=1, source_target_pairs={{0,16},{16,0},{1,17},{17,1},{2,18},{18,2},{3,19},{19,3},{4,20},{20... | collective-permute-start | bytes 294920 | tf_op jit(solution)/shard_map/ppermute | solution.py:94
  56.7 6.1 %copy-start.7 = (bf16[2,2,3,64,256]{4,3,2,1,0:T(8,128)(2,1)S(1)}, bf16[2,2,3,64,256]{4,3,2,1,0:T(8,128)(2,1)}, u32[]{:S(2)}) copy-start(bf16[2,2,3,64,256]{4,3,2,1,0:T(8,128)(2,1)} %copy-done.6) | copy-start | bytes 1179652
  56.7 6.0 %copy-start.9 = (bf16[2,2,3,64,256]{4,3,2,1,0:T(8,128)(2,1)S(1)}, bf16[2,2,3,64,256]{4,3,2,1,0:T(8,128)(2,1)}, u32[]{:S(2)}) copy-start(bf16[2,2,3,64,256]{4,3,2,1,0:T(8,128)(2,1)} %copy-done.8) | copy-start | bytes 1179652
  56.7 6.0 %copy-start.15 = (bf16[2,2,3,64,256]{4,3,2,1,0:T(8,128)(2,1)S(1)}, bf16[2,2,3,64,256]{4,3,2,1,0:T(8,128)(2,1)}, u32[]{:S(2)}) copy-start(bf16[2,2,3,64,256]{4,3,2,1,0:T(8,128)(2,1)} %copy-done.14) | copy-start | bytes 1179652
  56.7 12.6 %collective-permute-start.20 = (bf16[2,1,3,64,256]{4,3,2,1,0:T(8,128)(2,1)S(1)}, bf16[2,1,3,64,256]{4,3,2,1,0:T(8,128)(2,1)S(1)}, u32[]{:S(2)}, u32[]{:S(2)}) collective-permute-start(bf16[2,1,3,64,256]{4,3,2,1,0:T(8,128)(2,1)S(1)} %pad_maximum_fusion.5), channel_id=1, source_target_pairs={{0,16},{16,0},{1,17},{17,1},{2,18},{18,2},{3,19},{19,3},{4,20},{20... | collective-permute-start | bytes 589832 | tf_op jit(solution)/shard_map/ppermute | solution.py:89
  58.9 10.5 %collective-permute-start.18 = (bf16[2,1,3,64,256]{4,3,2,1,0:T(8,128)(2,1)S(1)}, bf16[2,1,3,64,256]{4,3,2,1,0:T(8,128)(2,1)S(1)}, u32[]{:S(2)}, u32[]{:S(2)}) collective-permute-start(bf16[2,1,3,64,256]{4,3,2,1,0:T(8,128)(2,1)S(1)} %collective-permute-done.14.refs_1_), channel_id=1, source_target_pairs={{0,4},{1,5},{4,8},{5,9},{8,12},{9,13},{12,14},{13,15},{14,10},{15,... | collective-permute-start | bytes 589832 | tf_op jit(solution)/shard_map/ppermute | solution.py:79
  58.9 10.4 %collective-permute-start.19 = (bf16[2,1,3,64,256]{4,3,2,1,0:T(8,128)(2,1)S(1)}, bf16[2,1,3,64,256]{4,3,2,1,0:T(8,128)(2,1)S(1)}, u32[]{:S(2)}, u32[]{:S(2)}) collective-permute-start(bf16[2,1,3,64,256]{4,3,2,1,0:T(8,128)(2,1)S(1)} %collective-permute-done.15.refs_2_), channel_id=1, source_target_pairs={{4,0},{5,1},{8,4},{9,5},{12,8},{13,9},{14,12},{15,13},{10,14},{11,... | collective-permute-start | bytes 589832 | tf_op jit(solution)/shard_map/ppermute | solution.py:80
  61.3 8.1 %collective-permute-start.21 = (bf16[3,1,3,64,256]{4,3,2,1,0:T(8,128)(2,1)S(1)}, bf16[3,1,3,64,256]{4,3,2,1,0:T(8,128)(2,1)S(1)}, u32[]{:S(2)}, u32[]{:S(2)}) collective-permute-start(bf16[3,1,3,64,256]{4,3,2,1,0:T(8,128)(2,1)S(1)} %pad_maximum_fusion.3), channel_id=1, source_target_pairs={{0,16},{16,0},{1,17},{17,1},{2,18},{18,2},{3,19},{19,3},{4,20},{20... | collective-permute-start | bytes 884744 | tf_op jit(solution)/shard_map/ppermute | solution.py:100
  69.4 3.9 %copy-start.2 = (bf16[2,1,3,64,256]{4,3,2,1,0:T(8,128)(2,1)}, bf16[2,1,3,64,256]{4,3,2,1,0:T(8,128)(2,1)S(1)}, u32[]{:S(2)}) copy-start(bf16[2,1,3,64,256]{4,3,2,1,0:T(8,128)(2,1)S(1)} %collective-permute-done.20.refs_8_) | copy-start | bytes 589828
  69.4 5.6 %collective-permute-start.22 = (bf16[6,256,256]{2,1,0:T(8,128)(2,1)S(1)}, bf16[6,256,256]{2,1,0:T(8,128)(2,1)S(1)}, u32[]{:S(2)}, u32[]{:S(2)}) collective-permute-start(bf16[6,256,256]{2,1,0:T(8,128)(2,1)S(1)} %get-tuple-element.48.mine), channel_id=1, source_target_pairs={{0,1},{1,0},{2,3},{3,2},{4,5},{5,4},{6,7},{7,6},{8,9},{9,8},{10,11... | collective-permute-start | bytes 2359304 | tf_op jit(solution)/shard_map/ppermute | solution.py:566
  72.9 7.9 %collective-permute-start.25 = (bf16[2,1,3,64,256]{4,3,2,1,0:T(8,128)(2,1)S(1)}, bf16[2,1,3,64,256]{4,3,2,1,0:T(8,128)(2,1)S(1)}, u32[]{:S(2)}, u32[]{:S(2)}) collective-permute-start(bf16[2,1,3,64,256]{4,3,2,1,0:T(8,128)(2,1)S(1)} %pad_maximum_fusion.6), channel_id=1, source_target_pairs={{0,16},{16,0},{1,17},{17,1},{2,18},{18,2},{3,19},{19,3},{4,20},{20... | collective-permute-start | bytes 589832 | tf_op jit(solution)/shard_map/ppermute | solution.py:89
  73.3 8.2 %collective-permute-start.23 = (bf16[2,1,3,64,256]{4,3,2,1,0:T(8,128)(2,1)S(1)}, bf16[2,1,3,64,256]{4,3,2,1,0:T(8,128)(2,1)S(1)}, u32[]{:S(2)}, u32[]{:S(2)}) collective-permute-start(bf16[2,1,3,64,256]{4,3,2,1,0:T(8,128)(2,1)S(1)} %collective-permute-done.18.refs_3_), channel_id=1, source_target_pairs={{0,4},{1,5},{4,8},{5,9},{8,12},{9,13},{12,14},{13,15},{14,10},{15,... | collective-permute-start | bytes 589832 | tf_op jit(solution)/shard_map/ppermute | solution.py:79
  75.0 6.5 %collective-permute-start.24 = (bf16[2,1,3,64,256]{4,3,2,1,0:T(8,128)(2,1)S(1)}, bf16[2,1,3,64,256]{4,3,2,1,0:T(8,128)(2,1)S(1)}, u32[]{:S(2)}, u32[]{:S(2)}) collective-permute-start(bf16[2,1,3,64,256]{4,3,2,1,0:T(8,128)(2,1)S(1)} %collective-permute-done.19.refs_4_), channel_id=1, source_target_pairs={{4,0},{5,1},{8,4},{9,5},{12,8},{13,9},{14,12},{15,13},{10,14},{11,... | collective-permute-start | bytes 589832 | tf_op jit(solution)/shard_map/ppermute | solution.py:80
  81.5 7.6 %copy-start = (bf16[2,1,3,64,256]{4,3,2,1,0:T(8,128)(2,1)}, bf16[2,1,3,64,256]{4,3,2,1,0:T(8,128)(2,1)S(1)}, u32[]{:S(2)}) copy-start(bf16[2,1,3,64,256]{4,3,2,1,0:T(8,128)(2,1)S(1)} %collective-permute-done.24.refs_6_) | copy-start | bytes 589828
  81.5 20.8 %all-to-all-start = ((bf16[16,4,16,256]{3,2,1,0:T(8,128)(2,1)}), bf16[16,4,16,256]{3,2,1,0:T(8,128)(2,1)}, u32[]{:S(2)}, u32[]{:S(2)}) async-start(bf16[16,4,16,256]{3,2,1,0:T(8,128)(2,1)} %second_conv.1), calls=%async_computation | async-start | bytes 1048576 | tf_op jit(solution)/shard_map/all_to_all | solution.py:587
  88.1 6.3 %collective-permute-start.26 = (bf16[2,1,3,64,256]{4,3,2,1,0:T(8,128)(2,1)S(1)}, bf16[2,1,3,64,256]{4,3,2,1,0:T(8,128)(2,1)S(1)}, u32[]{:S(2)}, u32[]{:S(2)}) collective-permute-start(bf16[2,1,3,64,256]{4,3,2,1,0:T(8,128)(2,1)S(1)} %pad_maximum_fusion.7), channel_id=1, source_target_pairs={{0,16},{16,0},{1,17},{17,1},{2,18},{18,2},{3,19},{19,3},{4,20},{20... | collective-permute-start | bytes 589832 | tf_op jit(solution)/shard_map/ppermute | solution.py:89
  98.9 25.1 %collective-permute-start.28 = (bf16[3,3,512,256]{3,2,1,0:T(8,128)(2,1)S(1)}, bf16[3,3,512,256]{3,2,1,0:T(8,128)(2,1)}, u32[]{:S(2)}, u32[]{:S(2)}) collective-permute-start(bf16[3,3,512,256]{3,2,1,0:T(8,128)(2,1)S(1)} %assemble.1.mine), channel_id=1, source_target_pairs={{0,1},{1,0},{2,3},{3,2},{4,5},{5,4},{6,7},{7,6},{8,9},{9,8},{10,11... | collective-permute-start | bytes 7077896 | tf_op jit(solution)/shard_map/ppermute | solution.py:592
  102.3 9.7 %collective-permute-start.27 = (bf16[2,1,3,64,256]{4,3,2,1,0:T(8,128)(2,1)S(1)}, bf16[2,1,3,64,256]{4,3,2,1,0:T(8,128)(2,1)S(1)}, u32[]{:S(2)}, u32[]{:S(2)}) collective-permute-start(bf16[2,1,3,64,256]{4,3,2,1,0:T(8,128)(2,1)S(1)} %collective-permute-done.23.refs_5_), channel_id=1, source_target_pairs={{0,4},{1,5},{4,8},{5,9},{8,12},{9,13},{12,14},{13,15},{14,10},{15,... | collective-permute-start | bytes 589832 | tf_op jit(solution)/shard_map/ppermute | solution.py:77
  112.0 24.3 %all-to-all-start.1 = ((bf16[16,48,512]{2,1,0:T(8,128)(2,1)}), bf16[16,48,512]{2,1,0:T(8,128)(2,1)S(1)}, u32[]{:S(2)}, u32[]{:S(2)}) async-start(bf16[16,48,512]{2,1,0:T(8,128)(2,1)} %windows.1), calls=%async_computation.1 | async-start | bytes 1572864 | tf_op jit(solution)/shard_map/all_to_all | solution.py:607
  116.8 6.4 %collective-permute-start.30 = (bf16[2,1,3,64,256]{4,3,2,1,0:T(8,128)(2,1)S(1)}, bf16[2,1,3,64,256]{4,3,2,1,0:T(8,128)(2,1)S(1)}, u32[]{:S(2)}, u32[]{:S(2)}) collective-permute-start(bf16[2,1,3,64,256]{4,3,2,1,0:T(8,128)(2,1)S(1)} %collective-permute-done.27.refs_0_), channel_id=1, source_target_pairs={{0,1},{1,0},{2,3},{3,2},{4,5},{5,4},{6,7},{7,6},{8,9},{9,8},{10,11... | collective-permute-start | bytes 589832 | tf_op jit(solution)/shard_map/ppermute | solution.py:622
  117.2 4.2 %collective-permute-start.29 = (bf16[1,1,3,64,256]{4,3,2,1,0:T(8,128)(2,1)S(1)}, bf16[1,1,3,64,256]{4,3,2,1,0:T(8,128)(2,1)S(1)}, u32[]{:S(2)}, u32[]{:S(2)}) collective-permute-start(bf16[1,1,3,64,256]{4,3,2,1,0:T(8,128)(2,1)S(1)} %slice.99), channel_id=1, source_target_pairs={{0,16},{16,0},{1,17},{17,1},{2,18},{18,2},{3,19},{19,3},{4,20},{20... | collective-permute-start | bytes 294920 | tf_op jit(solution)/shard_map/ppermute | solution.py:94
  121.5 1.9 %collective-permute-start.31 = (bf16[1,1,3,64,256]{4,3,2,1,0:T(8,128)(2,1)S(1)}, bf16[1,1,3,64,256]{4,3,2,1,0:T(8,128)(2,1)S(1)}, u32[]{:S(2)}, u32[]{:S(2)}) collective-permute-start(bf16[1,1,3,64,256]{4,3,2,1,0:T(8,128)(2,1)S(1)} %collective-permute-done.29.refs_1_), channel_id=1, source_target_pairs={{0,1},{1,0},{2,3},{3,2},{4,5},{5,4},{6,7},{7,6},{8,9},{9,8},{10,11... | collective-permute-start | bytes 294920 | tf_op jit(solution)/shard_map/ppermute | solution.py:622
  (8 other events, 6.5 us)

commit v7 on v6

--- a/solution.py
+++ b/solution.py
@@ -308,14 +308,16 @@
                 share = 1.0 / jnp.sum(lifted, axis=-1, keepdims=True)
                 halves.append(dot(lifted.astype(BF16), value) * share)
             att[spot] = jnp.where(low, halves[0], halves[1]).astype(BF16)
-    for copy in copies[3:]:
-        copy.wait()
+    copies[3].wait()
     current = (current + dot(att[...], w_out[...])).astype(BF16).astype(F32)
     normed = rms_round(current)
     units = w_in.shape[1]
+    chunk = units // 2
     lowered = None
-    for start in range(0, units, channels):
-        span = slice(start, start + channels)
+    for copy in copies[4:]:
+        copy.wait()
+    for start in range(0, units, chunk):
+        span = slice(start, start + chunk)
         hidden = gelu(dot(normed, w_in[:, span])).astype(BF16)
         term = dot(hidden, w_down[span, :])
         lowered = term if lowered is None else lowered + term

time: 144 us -> 144 us (level)
  no operation moved by 1% of the time
where the time goes in v7:
time: 144 us; the launch traced here: 143 us
  starting transfers between devices  51.9 us (36%)
  waiting for transfers between devices  48 us (33%)
  Pallas kernels  28.5 us (20%)
  local copies, waits for them, and re-layouts  8.93 us (6%)
  other arithmetic  4.54 us (3%)
    all_to_all x1, waiting for transfers between devices, on_device(): lax.all_to_all(sent[0], 'row', split_axis=0, concat_axis=0, axis_index_gr...  12.3 us
    ppermute x6, waiting for transfers between devices, step(): self.down = lax.ppermute(self.down, 'row', backward)  10.4 us
    pallas_call x1, Pallas kernels, windows(): pl.pallas_call(functools.partial(window_kernel, per), out_shape=tuple((ja...  9.35 us
    ppermute x3, starting transfers between devices, step(): self.finals.append(lax.ppermute(value[:, kernel:kernel + 1], 'row', pairs))  8.63 us
    ppermute x1, waiting for transfers between devices, on_device(): near = lax.ppermute(beside, 'row', edges)  7.86 us
    pallas_call x1, Pallas kernels, first_conv(): pl.pallas_call(functools.partial(first_conv_kernel, step), out_shape=(out...  6.57 us
    unnamed x42, local copies, waits for them, and re-layouts  6.57 us
    all_to_all x1, starting transfers between devices, on_device(): lax.all_to_all(y2, 'row', split_axis=0, concat_axis=0, axis_index_groups=...  6.51 us
  transfers between devices with their start and end apart: 34, of which 14 were waited for; matrix products, arithmetic and copies ran while one was open for 4% of the time, Pallas kernels for 16%

profile of v7, /device:TPU:9, one launch (start us, length us, event | category | flops | bytes accessed | tf_op | source)
XLA Modules:
  0.0 143.1 jit_solution(10320164219246080934)
XLA Ops:
  0.7 1.2 pad_maximum_fusion
  2.0 0.7 collective-permute-start
  2.7 1.4 collective-permute-done
  4.7 1.5 %collective-permute-start.1 = (bf16[2,2,3,64,256]{4,3,2,1,0:T(8,128)(2,1)S(1)}, bf16[2,2,3,64,256]{4,3,2,1,0:T(8,128)(2,1)S(1)}, u32[]{:S(2)}, u32[]{:S(2)}) collective-permute-start(bf16[2,2,3,64,256]{4,3,2,1,0:T(8,128)(2,1)S(1)} %slice.101.refs_0_), channel_id=1, source_target_pairs={{0,4},{1,5},{4,8},{5,9},{8,12},{9,13},{12,14},{13,15},{14,10},{15,... | collective-permute-start | bytes 1179656 | tf_op jit(solution)/shard_map/ppermute | solution.py:79
  6.2 8.9 %collective-permute-done.6.refs_2_ = bf16[2,2,3,64,256]{4,3,2,1,0:T(8,128)(2,1)S(1)} collective-permute-done((bf16[2,2,3,64,256]{4,3,2,1,0:T(8,128)(2,1)S(1)}, bf16[2,2,3,64,256]{4,3,2,1,0:T(8,128)(2,1)S(1)}, u32[]{:S(2)}, u32[]{:S(2)}) %collective-permute-start.6) | collective-permute-done | bytes 393248 | tf_op jit(solution)/shard_map/ppermute | solution.py:80
  15.2 1.3 collective-permute-start.5
  16.7 1.2 collective-permute-start.8
  18.0 6.5 %collective-permute-start.2 = (bf16[2,256,512]{2,1,0:T(8,128)(2,1)}, bf16[2,256,512]{2,1,0:T(8,128)(2,1)S(1)}, u32[]{:S(2)}, u32[]{:S(2)}) collective-permute-start(bf16[2,256,512]{2,1,0:T(8,128)(2,1)} %param.11), channel_id=1, source_target_pairs={{1,2},{2,1},{3,4},{4,3},{5,6},{6,5},{7,8},{8,7},{9,10},{10,9},{11,... | collective-permute-start | bytes 1572872 | tf_op jit(solution)/shard_map/ppermute | solution.py:529
  24.6 0.8 collective-permute-done.7.refs_4_
  25.5 1.3 collective-permute-start.9
  27.1 1.3 collective-permute-start.11
  28.5 1.0 slice_bitcast_fusion.refs_9_
  29.5 7.9 %collective-permute-done.2 = bf16[2,256,512]{2,1,0:T(8,128)(2,1)S(1)} collective-permute-done((bf16[2,256,512]{2,1,0:T(8,128)(2,1)}, bf16[2,256,512]{2,1,0:T(8,128)(2,1)S(1)}, u32[]{:S(2)}, u32[]{:S(2)}) %collective-permute-start.2) | collective-permute-done | bytes 524320 | tf_op jit(solution)/shard_map/ppermute | solution.py:529
  37.4 0.7 collective-permute-done.10.refs_6_
  38.1 1.2 collective-permute-start.12
  39.3 7.2 %collective-permute-start.13 = (bf16[2,1,3,64,256]{4,3,2,1,0:T(8,128)(2,1)S(1)}, bf16[2,1,3,64,256]{4,3,2,1,0:T(8,128)(2,1)S(1)}, u32[]{:S(2)}, u32[]{:S(2)}) collective-permute-start(bf16[2,1,3,64,256]{4,3,2,1,0:T(8,128)(2,1)S(1)} %slice.82), channel_id=1, source_target_pairs={{4,0},{5,1},{8,4},{9,5},{12,8},{13,9},{14,12},{15,13},{10,14},{11,... | collective-permute-start | bytes 589832 | tf_op jit(solution)/shard_map/ppermute | solution.py:77
  46.5 1.9 %collective-permute-start.15 = (bf16[2,1,3,64,256]{4,3,2,1,0:T(8,128)(2,1)S(1)}, bf16[2,1,3,64,256]{4,3,2,1,0:T(8,128)(2,1)S(1)}, u32[]{:S(2)}, u32[]{:S(2)}) collective-permute-start(bf16[2,1,3,64,256]{4,3,2,1,0:T(8,128)(2,1)S(1)} %slice.107.refs_0_), channel_id=1, source_target_pairs={{4,0},{5,1},{8,4},{9,5},{12,8},{13,9},{14,12},{15,13},{10,14},{11,... | collective-permute-start | bytes 589832 | tf_op jit(solution)/shard_map/ppermute | solution.py:80
  48.5 3.2 %collective-permute-done.12.refs_7_ = bf16[2,1,3,64,256]{4,3,2,1,0:T(8,128)(2,1)S(1)} collective-permute-done((bf16[2,1,3,64,256]{4,3,2,1,0:T(8,128)(2,1)S(1)}, bf16[2,1,3,64,256]{4,3,2,1,0:T(8,128)(2,1)S(1)}, u32[]{:S(2)}, u32[]{:S(2)}) %collective-permute-start.12) | collective-permute-done | bytes 196640 | tf_op jit(solution)/shard_map/ppermute | solution.py:77
  51.6 1.4 collective-permute-start.16
  53.0 1.2 collective-permute-done.14.refs_1_
  54.2 2.4 %collective-permute-start.17 = (bf16[1,1,3,64,256]{4,3,2,1,0:T(8,128)(2,1)S(1)}, bf16[1,1,3,64,256]{4,3,2,1,0:T(8,128)(2,1)S(1)}, u32[]{:S(2)}, u32[]{:S(2)}) collective-permute-start(bf16[1,1,3,64,256]{4,3,2,1,0:T(8,128)(2,1)S(1)} %slice.88), channel_id=1, source_target_pairs={{0,16},{16,0},{1,17},{17,1},{2,18},{18,2},{3,19},{19,3},{4,20},{20... | collective-permute-start | bytes 294920 | tf_op jit(solution)/shard_map/ppermute | solution.py:94
  56.8 2.0 %fusion.5 = (bf16[8,256,512]{2,1,0:T(8,128)(2,1)S(1)}, bf16[8,256,512]{2,1,0:T(8,128)(2,1)S(1)}) fusion(bf16[2,256,512]{2,1,0:T(8,128)(2,1)S(1)} %collective-permute-done.2, bf16[2,256,512]{2,1,0:T(8,128)(2,1)S(1)} %copy-done.19, bf16[2,256,512]{2,1,0:T(8,128)(2,1)S(1)} %collective-permute-done.3, bf16[2,256,512]{2,1,0:T(8,128)(2,1)S(1)} %collective-permute-done.4, ...), kind=kLoop, calls=%fused_computation.9 | loop fusion | flops 17825792 | bytes 6291457 | tf_op jit(solution)/shard_map/convert_element_type | solution.py:549
  58.9 2.3 %collective-permute-start.19 = (bf16[2,1,3,64,256]{4,3,2,1,0:T(8,128)(2,1)S(1)}, bf16[2,1,3,64,256]{4,3,2,1,0:T(8,128)(2,1)S(1)}, u32[]{:S(2)}, u32[]{:S(2)}) collective-permute-start(bf16[2,1,3,64,256]{4,3,2,1,0:T(8,128)(2,1)S(1)} %collective-permute-done.15.refs_2_), channel_id=1, source_target_pairs={{4,0},{5,1},{8,4},{9,5},{12,8},{13,9},{14,12},{15,13},{10,14},{11,... | collective-permute-start | bytes 589832 | tf_op jit(solution)/shard_map/ppermute | solution.py:80
  61.3 1.5 %collective-permute-start.21 = (bf16[3,1,3,64,256]{4,3,2,1,0:T(8,128)(2,1)S(1)}, bf16[3,1,3,64,256]{4,3,2,1,0:T(8,128)(2,1)S(1)}, u32[]{:S(2)}, u32[]{:S(2)}) collective-permute-start(bf16[3,1,3,64,256]{4,3,2,1,0:T(8,128)(2,1)S(1)} %pad_maximum_fusion.3), channel_id=1, source_target_pairs={{0,16},{16,0},{1,17},{17,1},{2,18},{18,2},{3,19},{19,3},{4,20},{20... | collective-permute-start | bytes 884744 | tf_op jit(solution)/shard_map/ppermute | solution.py:100
  62.8 6.6 %first_conv.1 = (bf16[6,256,256]{2,1,0:T(8,128)(2,1)S(1)}, bf16[6,256,256]{2,1,0:T(8,128)(2,1)S(1)}) custom-call(s32[12]{0:T(128)S(1)} %concatenate.19.where, bf16[8,256,512]{2,1,0:T(8,128)(2,1)S(1)} %get-tuple-element.40.act, bf16[8,256,512]{2,1,0:T(8,128)(2,1)S(1)} %get-tuple-element.63.lat, bf16[2,2,3,64,256]{4,3,2,1,0:T(8,128)(2,1)S(1)} %slice.101.refs_0_, ...), custom_call_target="tpu_custom_call" | custom-call | flops 3623878656 | bytes 2359296 | tf_op jit(solution)/shard_map/first_conv/pallas_call | solution.py:200
  69.4 3.5 %collective-permute-start.22 = (bf16[6,256,256]{2,1,0:T(8,128)(2,1)S(1)}, bf16[6,256,256]{2,1,0:T(8,128)(2,1)S(1)}, u32[]{:S(2)}, u32[]{:S(2)}) collective-permute-start(bf16[6,256,256]{2,1,0:T(8,128)(2,1)S(1)} %get-tuple-element.48.mine), channel_id=1, source_target_pairs={{0,1},{1,0},{2,3},{3,2},{4,5},{5,4},{6,7},{7,6},{8,9},{9,8},{10,11... | collective-permute-start | bytes 2359304 | tf_op jit(solution)/shard_map/ppermute | solution.py:568
  73.3 1.7 %collective-permute-start.23 = (bf16[2,1,3,64,256]{4,3,2,1,0:T(8,128)(2,1)S(1)}, bf16[2,1,3,64,256]{4,3,2,1,0:T(8,128)(2,1)S(1)}, u32[]{:S(2)}, u32[]{:S(2)}) collective-permute-start(bf16[2,1,3,64,256]{4,3,2,1,0:T(8,128)(2,1)S(1)} %collective-permute-done.18.refs_3_), channel_id=1, source_target_pairs={{0,4},{1,5},{4,8},{5,9},{8,12},{9,13},{12,14},{13,15},{14,10},{15,... | collective-permute-start | bytes 589832 | tf_op jit(solution)/shard_map/ppermute | solution.py:79
  75.0 5.8 %second_conv.1 = bf16[16,4,16,256]{3,2,1,0:T(8,128)(2,1)} custom-call(s32[12]{0:T(128)S(1)} %concatenate.19.where, bf16[6,256,256]{2,1,0:T(8,128)(2,1)S(1)} %get-tuple-element.43.y1, bf16[6,256,256]{2,1,0:T(8,128)(2,1)S(1)} %get-tuple-element.48.mine, bf16[6,256,256]{2,1,0:T(8,128)(2,1)S(1)} %collective-permute-done.22.theirs, ...), custom_call_target="tpu_custom_call" | custom-call | flops 2415919104 | bytes 2359296 | tf_op jit(solution)/shard_map/second_conv/pallas_call | solution.py:245
  80.8 0.7 copy-done.4
  81.5 6.5 %all-to-all-start = ((bf16[16,4,16,256]{3,2,1,0:T(8,128)(2,1)}), bf16[16,4,16,256]{3,2,1,0:T(8,128)(2,1)}, u32[]{:S(2)}, u32[]{:S(2)}) async-start(bf16[16,4,16,256]{3,2,1,0:T(8,128)(2,1)} %second_conv.1), calls=%async_computation | async-start | bytes 1048576 | tf_op jit(solution)/shard_map/all_to_all | solution.py:589
  88.2 0.9 slice_bitcast_fusion.1.refs_7_
  89.1 5.3 %collective-permute-done.26.refs_10_ = bf16[2,1,3,64,256]{4,3,2,1,0:T(8,128)(2,1)S(1)} collective-permute-done((bf16[2,1,3,64,256]{4,3,2,1,0:T(8,128)(2,1)S(1)}, bf16[2,1,3,64,256]{4,3,2,1,0:T(8,128)(2,1)S(1)}, u32[]{:S(2)}, u32[]{:S(2)}) %collective-permute-start.26) | collective-permute-done | bytes 196640 | tf_op jit(solution)/shard_map/ppermute | solution.py:89
  94.4 0.9 copy-done.1
  95.3 0.9 copy-done.3
  96.2 0.9 copy-done.5
  97.2 1.8 %assemble.1.mine = bf16[3,3,512,256]{3,2,1,0:T(8,128)(2,1)S(1)} custom-call(s32[12]{0:T(128)S(1)} %concatenate.19.where, bf16[2,1,3,64,256]{4,3,2,1,0:T(8,128)(2,1)S(1)} %slice.107.refs_0_, bf16[2,1,3,64,256]{4,3,2,1,0:T(8,128)(2,1)S(1)} %collective-permute-done.14.refs_1_, bf16[2,1,3,64,256]{4,3,2,1,0:T(8,128)(2,1)S(1)} %collective-permute-done.15.refs_2_, ...), custom_call_target="tpu_custom_call" | custom-call | bytes 4718592 | tf_op jit(solution)/shard_map/assemble/pallas_call | solution.py:142
  98.9 1.2 collective-permute-start.28
  100.6 1.6 %all-to-all-done = bf16[16,4,16,256]{3,2,1,0:T(8,128)(2,1)} async-done(((bf16[16,4,16,256]{3,2,1,0:T(8,128)(2,1)}), bf16[16,4,16,256]{3,2,1,0:T(8,128)(2,1)}, u32[]{:S(2)}, u32[]{:S(2)}) %all-to-all-start) | async-done | bytes 524320 | tf_op jit(solution)/shard_map/all_to_all | solution.py:589
  102.5 9.4 %windows.1 = bf16[16,48,512]{2,1,0:T(8,128)(2,1)} custom-call(s32[16]{0:T(128)} %fusion.8.picks, bf16[8,2,2,2,16,256]{5,4,3,2,1,0:T(8,128)(2,1)} %bitcast.11.y2, bf16[512,512]{1,0:T(8,128)(2,1)} %refs_0_.1, bf16[512,512]{1,0:T(8,128)(2,1)} %refs_1_.1, bf16[512,512]{1,0:T(8,128)(2,1)} %refs_2_.1, bf16[512,512]{1,0:T(8,128)(2,1)} %refs_3_.1, ...), custom_call_target="tpu_custom_call" | custom-call | flops 3489660928 | bytes 2097152 | tf_op jit(solution)/shard_map/windows/pallas_call | solution.py:353
  111.9 4.8 %all-to-all-start.1 = ((bf16[16,48,512]{2,1,0:T(8,128)(2,1)}), bf16[16,48,512]{2,1,0:T(8,128)(2,1)S(1)}, u32[]{:S(2)}, u32[]{:S(2)}) async-start(bf16[16,48,512]{2,1,0:T(8,128)(2,1)} %windows.1), calls=%async_computation.1 | async-start | bytes 1572864 | tf_op jit(solution)/shard_map/all_to_all | solution.py:609
  117.1 4.2 %collective-permute-done.29.refs_1_ = bf16[1,1,3,64,256]{4,3,2,1,0:T(8,128)(2,1)S(1)} collective-permute-done((bf16[1,1,3,64,256]{4,3,2,1,0:T(8,128)(2,1)S(1)}, bf16[1,1,3,64,256]{4,3,2,1,0:T(8,128)(2,1)S(1)}, u32[]{:S(2)}, u32[]{:S(2)}) %collective-permute-start.29) | collective-permute-done | bytes 98336 | tf_op jit(solution)/shard_map/ppermute | solution.py:94
  121.3 1.0 collective-permute-start.31
  122.3 0.6 copy-done.10
  123.2 0.6 copy-done.12
  123.9 12.3 %all-to-all-done.1.arrived = bf16[16,48,512]{2,1,0:T(8,128)(2,1)S(1)} async-done(((bf16[16,48,512]{2,1,0:T(8,128)(2,1)}), bf16[16,48,512]{2,1,0:T(8,128)(2,1)S(1)}, u32[]{:S(2)}, u32[]{:S(2)}) %all-to-all-start.1) | async-done | bytes 786464 | tf_op jit(solution)/shard_map/all_to_all | solution.py:609
  136.2 0.9 copy-done.11
  137.1 0.9 copy-done.13
  138.0 5.0 %upsample.1 = (bf16[32,16,512]{2,1,0:T(8,128)(2,1)}, bf16[2,256,512]{2,1,0:T(8,128)(2,1)}) custom-call(s32[13]{0:T(128)S(1)} %pad_add_fusion.info, s32[12]{0:T(128)S(1)} %concatenate.19.where, bf16[16,48,512]{2,1,0:T(8,128)(2,1)S(1)} %all-to-all-done.1.arrived, bf16[3,3,512,256]{3,2,1,0:T(8,128)(2,1)S(1)} %assemble.1.mine, ...), custom_call_target="tpu_custom_call" | custom-call | flops 754974720 | bytes 4718592 | tf_op jit(solution)/shard_map/upsample/pallas_call | solution.py:452
  (109 shorter events, 4.0 us)
Async XLA Ops:
  2.0 2.2 %collective-permute-start = (bf16[3,3,3,32,256]{4,3,2,1,0:T(8,128)(2,1)S(1)}, bf16[3,3,3,32,256]{4,3,2,1,0:T(8,128)(2,1)S(1)}, u32[]{:S(2)}, u32[]{:S(2)}) collective-permute-start(bf16[3,3,3,32,256]{4,3,2,1,0:T(8,128)(2,1)S(1)} %get-tuple-element.65), channel_id=1, source_target_pairs={{0,1},{1,0},{2,3},{3,2},{4,5},{5,4},{6,7},{7,6},{8,9},{9,8},{10,11... | collective-permute-start | bytes 1327112 | tf_op jit(solution)/shard_map/ppermute | solution.py:511
  4.4 12.1 %copy-start.16 = (bf16[3,3,3,64,256]{4,3,2,1,0:T(8,128)(2,1)}, bf16[3,3,3,64,256]{4,3,2,1,0:T(8,128)(2,1)S(1)}, u32[]{:S(2)}) copy-start(bf16[3,3,3,64,256]{4,3,2,1,0:T(8,128)(2,1)S(1)} %maximum_select_fusion.1) | copy-start | bytes 2654212
  4.5 13.4 %copy-start.20 = (s32[8]{0:T(128)S(1)}, s32[8]{0:T(128)}, u32[]{:S(2)}) copy-start(s32[8]{0:T(128)} %constant.133.clone) | copy-start | bytes 100
  4.6 12.1 %copy-start.17 = (bf16[3,2,3,64,256]{4,3,2,1,0:T(8,128)(2,1)}, bf16[3,2,3,64,256]{4,3,2,1,0:T(8,128)(2,1)S(1)}, u32[]{:S(2)}) copy-start(bf16[3,2,3,64,256]{4,3,2,1,0:T(8,128)(2,1)S(1)} %reverse_select_fusion) | copy-start | bytes 1769476
  4.7 10.4 %collective-permute-start.6 = (bf16[2,2,3,64,256]{4,3,2,1,0:T(8,128)(2,1)S(1)}, bf16[2,2,3,64,256]{4,3,2,1,0:T(8,128)(2,1)S(1)}, u32[]{:S(2)}, u32[]{:S(2)}) collective-permute-start(bf16[2,2,3,64,256]{4,3,2,1,0:T(8,128)(2,1)S(1)} %slice.101.refs_0_), channel_id=1, source_target_pairs={{4,0},{5,1},{8,4},{9,5},{12,8},{13,9},{14,12},{15,13},{10,14},{11,... | collective-permute-start | bytes 1179656 | tf_op jit(solution)/shard_map/ppermute | solution.py:80
  4.7 10.4 %collective-permute-start.1 = (bf16[2,2,3,64,256]{4,3,2,1,0:T(8,128)(2,1)S(1)}, bf16[2,2,3,64,256]{4,3,2,1,0:T(8,128)(2,1)S(1)}, u32[]{:S(2)}, u32[]{:S(2)}) collective-permute-start(bf16[2,2,3,64,256]{4,3,2,1,0:T(8,128)(2,1)S(1)} %slice.101.refs_0_), channel_id=1, source_target_pairs={{0,4},{1,5},{4,8},{5,9},{8,12},{9,13},{12,14},{13,15},{14,10},{15,... | collective-permute-start | bytes 1179656 | tf_op jit(solution)/shard_map/ppermute | solution.py:79
  15.2 9.5 %collective-permute-start.5 = (bf16[2,2,3,64,256]{4,3,2,1,0:T(8,128)(2,1)S(1)}, bf16[2,2,3,64,256]{4,3,2,1,0:T(8,128)(2,1)S(1)}, u32[]{:S(2)}, u32[]{:S(2)}) collective-permute-start(bf16[2,2,3,64,256]{4,3,2,1,0:T(8,128)(2,1)S(1)} %collective-permute-done.1.refs_1_), channel_id=1, source_target_pairs={{0,4},{1,5},{4,8},{5,9},{8,12},{9,13},{12,14},{13,15},{14,10},{15,... | collective-permute-start | bytes 1179656 | tf_op jit(solution)/shard_map/ppermute | solution.py:79
  16.5 9.0 %collective-permute-start.7 = (bf16[2,2,3,64,256]{4,3,2,1,0:T(8,128)(2,1)S(1)}, bf16[2,2,3,64,256]{4,3,2,1,0:T(8,128)(2,1)S(1)}, u32[]{:S(2)}, u32[]{:S(2)}) collective-permute-start(bf16[2,2,3,64,256]{4,3,2,1,0:T(8,128)(2,1)S(1)} %collective-permute-done.6.refs_2_), channel_id=1, source_target_pairs={{4,0},{5,1},{8,4},{9,5},{12,8},{13,9},{14,12},{15,13},{10,14},{11,... | collective-permute-start | bytes 1179656 | tf_op jit(solution)/shard_map/ppermute | solution.py:80
  16.7 8.8 %collective-permute-start.8 = (bf16[2,2,3,64,256]{4,3,2,1,0:T(8,128)(2,1)S(1)}, bf16[2,2,3,64,256]{4,3,2,1,0:T(8,128)(2,1)S(1)}, u32[]{:S(2)}, u32[]{:S(2)}) collective-permute-start(bf16[2,2,3,64,256]{4,3,2,1,0:T(8,128)(2,1)S(1)} %pad_maximum_fusion.1), channel_id=1, source_target_pairs={{0,16},{16,0},{1,17},{17,1},{2,18},{18,2},{3,19},{19,3},{4,20},{20... | collective-permute-start | bytes 1179656 | tf_op jit(solution)/shard_map/ppermute | solution.py:89
  18.0 10.4 %slice-start = ((bf16[3,3,3,64,256]{4,3,2,1,0:T(8,128)(2,1)}), bf16[3,1,3,64,256]{4,3,2,1,0:T(8,128)(2,1)S(1)}, s32[]{:S(2)}) async-start(bf16[3,3,3,64,256]{4,3,2,1,0:T(8,128)(2,1)} %copy-done.16), calls=%async_computation.2 | async-start | bytes 589824 | tf_op jit(solution)/shard_map/slice | solution.py:520
  18.0 19.4 %collective-permute-start.2 = (bf16[2,256,512]{2,1,0:T(8,128)(2,1)}, bf16[2,256,512]{2,1,0:T(8,128)(2,1)S(1)}, u32[]{:S(2)}, u32[]{:S(2)}) collective-permute-start(bf16[2,256,512]{2,1,0:T(8,128)(2,1)} %param.11), channel_id=1, source_target_pairs={{1,2},{2,1},{3,4},{4,3},{5,6},{6,5},{7,8},{8,7},{9,10},{10,9},{11,... | collective-permute-start | bytes 1572872 | tf_op jit(solution)/shard_map/ppermute | solution.py:529
  24.5 12.9 %collective-permute-start.3 = (bf16[2,256,512]{2,1,0:T(8,128)(2,1)}, bf16[2,256,512]{2,1,0:T(8,128)(2,1)S(1)}, u32[]{:S(2)}, u32[]{:S(2)}) collective-permute-start(bf16[2,256,512]{2,1,0:T(8,128)(2,1)} %param.11), channel_id=1, source_target_pairs={{0,1},{1,0},{2,3},{3,2},{4,5},{5,4},{6,7},{7,6},{8,9},{9,8},{10,11... | collective-permute-start | bytes 1572872 | tf_op jit(solution)/shard_map/ppermute | solution.py:530
  24.6 14.7 %copy-start.6 = (bf16[2,2,3,64,256]{4,3,2,1,0:T(8,128)(2,1)}, bf16[2,2,3,64,256]{4,3,2,1,0:T(8,128)(2,1)S(1)}, u32[]{:S(2)}) copy-start(bf16[2,2,3,64,256]{4,3,2,1,0:T(8,128)(2,1)S(1)} %collective-permute-done.5.refs_3_) | copy-start | bytes 1179652
  25.5 23.0 %copy-start.8 = (bf16[2,2,3,64,256]{4,3,2,1,0:T(8,128)(2,1)}, bf16[2,2,3,64,256]{4,3,2,1,0:T(8,128)(2,1)S(1)}, u32[]{:S(2)}) copy-start(bf16[2,2,3,64,256]{4,3,2,1,0:T(8,128)(2,1)S(1)} %collective-permute-done.7.refs_4_) | copy-start | bytes 1179652
  25.5 2.8 %copy-start.14 = (bf16[2,2,3,64,256]{4,3,2,1,0:T(8,128)(2,1)}, bf16[2,2,3,64,256]{4,3,2,1,0:T(8,128)(2,1)S(1)}, u32[]{:S(2)}) copy-start(bf16[2,2,3,64,256]{4,3,2,1,0:T(8,128)(2,1)S(1)} %collective-permute-done.8.refs_10_) | copy-start | bytes 1179652
  25.5 11.8 %collective-permute-start.9 = (bf16[2,2,3,64,256]{4,3,2,1,0:T(8,128)(2,1)S(1)}, bf16[2,2,3,64,256]{4,3,2,1,0:T(8,128)(2,1)S(1)}, u32[]{:S(2)}, u32[]{:S(2)}) collective-permute-start(bf16[2,2,3,64,256]{4,3,2,1,0:T(8,128)(2,1)S(1)} %collective-permute-done.5.refs_3_), channel_id=1, source_target_pairs={{0,4},{1,5},{4,8},{5,9},{8,12},{9,13},{12,14},{13,15},{14,10},{15,... | collective-permute-start | bytes 1179656 | tf_op jit(solution)/shard_map/ppermute | solution.py:79
  26.8 11.2 %collective-permute-start.10 = (bf16[2,2,3,64,256]{4,3,2,1,0:T(8,128)(2,1)S(1)}, bf16[2,2,3,64,256]{4,3,2,1,0:T(8,128)(2,1)S(1)}, u32[]{:S(2)}, u32[]{:S(2)}) collective-permute-start(bf16[2,2,3,64,256]{4,3,2,1,0:T(8,128)(2,1)S(1)} %collective-permute-done.7.refs_4_), channel_id=1, source_target_pairs={{4,0},{5,1},{8,4},{9,5},{12,8},{13,9},{14,12},{15,13},{10,14},{11,... | collective-permute-start | bytes 1179656 | tf_op jit(solution)/shard_map/ppermute | solution.py:80
  27.1 29.7 %copy-start.19 = (bf16[2,256,512]{2,1,0:T(8,128)(2,1)S(1)}, bf16[2,256,512]{2,1,0:T(8,128)(2,1)}, u32[]{:S(2)}) copy-start(bf16[2,256,512]{2,1,0:T(8,128)(2,1)} %param.11) | copy-start | bytes 1572868
  27.1 10.9 %collective-permute-start.11 = (bf16[2,2,3,64,256]{4,3,2,1,0:T(8,128)(2,1)S(1)}, bf16[2,2,3,64,256]{4,3,2,1,0:T(8,128)(2,1)S(1)}, u32[]{:S(2)}, u32[]{:S(2)}) collective-permute-start(bf16[2,2,3,64,256]{4,3,2,1,0:T(8,128)(2,1)S(1)} %pad_maximum_fusion.2), channel_id=1, source_target_pairs={{0,16},{16,0},{1,17},{17,1},{2,18},{18,2},{3,19},{19,3},{4,20},{20... | collective-permute-start | bytes 1179656 | tf_op jit(solution)/shard_map/ppermute | solution.py:89
  28.4 30.4 %copy-start.18 = (bf16[3,1,3,64,256]{4,3,2,1,0:T(8,128)(2,1)}, bf16[3,1,3,64,256]{4,3,2,1,0:T(8,128)(2,1)S(1)}, u32[]{:S(2)}) copy-start(bf16[3,1,3,64,256]{4,3,2,1,0:T(8,128)(2,1)S(1)} %reverse_select_fusion.1) | copy-start | bytes 884740
  37.4 19.5 %collective-permute-start.4 = (bf16[2,256,512]{2,1,0:T(8,128)(2,1)S(1)}, bf16[2,256,512]{2,1,0:T(8,128)(2,1)S(1)}, u32[]{:S(2)}, u32[]{:S(2)}) collective-permute-start(bf16[2,256,512]{2,1,0:T(8,128)(2,1)S(1)} %collective-permute-done.2), channel_id=1, source_target_pairs={{0,1},{1,0},{2,3},{3,2},{4,5},{5,4},{6,7},{7,6},{8,9},{9,8},{10,11... | collective-permute-start | bytes 1572872 | tf_op jit(solution)/shard_map/ppermute | solution.py:531
  38.1 13.6 %collective-permute-start.12 = (bf16[2,1,3,64,256]{4,3,2,1,0:T(8,128)(2,1)S(1)}, bf16[2,1,3,64,256]{4,3,2,1,0:T(8,128)(2,1)S(1)}, u32[]{:S(2)}, u32[]{:S(2)}) collective-permute-start(bf16[2,1,3,64,256]{4,3,2,1,0:T(8,128)(2,1)S(1)} %slice.81), channel_id=1, source_target_pairs={{0,4},{1,5},{4,8},{5,9},{8,12},{9,13},{12,14},{13,15},{14,10},{15,... | collective-permute-start | bytes 589832 | tf_op jit(solution)/shard_map/ppermute | solution.py:77
  39.3 13.7 %collective-permute-start.13 = (bf16[2,1,3,64,256]{4,3,2,1,0:T(8,128)(2,1)S(1)}, bf16[2,1,3,64,256]{4,3,2,1,0:T(8,128)(2,1)S(1)}, u32[]{:S(2)}, u32[]{:S(2)}) collective-permute-start(bf16[2,1,3,64,256]{4,3,2,1,0:T(8,128)(2,1)S(1)} %slice.82), channel_id=1, source_target_pairs={{4,0},{5,1},{8,4},{9,5},{12,8},{13,9},{14,12},{15,13},{10,14},{11,... | collective-permute-start | bytes 589832 | tf_op jit(solution)/shard_map/ppermute | solution.py:77
  46.5 7.7 %collective-permute-start.14 = (bf16[2,1,3,64,256]{4,3,2,1,0:T(8,128)(2,1)S(1)}, bf16[2,1,3,64,256]{4,3,2,1,0:T(8,128)(2,1)S(1)}, u32[]{:S(2)}, u32[]{:S(2)}) collective-permute-start(bf16[2,1,3,64,256]{4,3,2,1,0:T(8,128)(2,1)S(1)} %slice.107.refs_0_), channel_id=1, source_target_pairs={{0,4},{1,5},{4,8},{5,9},{8,12},{9,13},{12,14},{13,15},{14,10},{15,... | collective-permute-start | bytes 589832 | tf_op jit(solution)/shard_map/ppermute | solution.py:79
  46.5 7.7 %collective-permute-start.15 = (bf16[2,1,3,64,256]{4,3,2,1,0:T(8,128)(2,1)S(1)}, bf16[2,1,3,64,256]{4,3,2,1,0:T(8,128)(2,1)S(1)}, u32[]{:S(2)}, u32[]{:S(2)}) collective-permute-start(bf16[2,1,3,64,256]{4,3,2,1,0:T(8,128)(2,1)S(1)} %slice.107.refs_0_), channel_id=1, source_target_pairs={{4,0},{5,1},{8,4},{9,5},{12,8},{13,9},{14,12},{15,13},{10,14},{11,... | collective-permute-start | bytes 589832 | tf_op jit(solution)/shard_map/ppermute | solution.py:80
  51.6 9.6 %collective-permute-start.16 = (bf16[2,1,3,64,256]{4,3,2,1,0:T(8,128)(2,1)S(1)}, bf16[2,1,3,64,256]{4,3,2,1,0:T(8,128)(2,1)S(1)}, u32[]{:S(2)}, u32[]{:S(2)}) collective-permute-start(bf16[2,1,3,64,256]{4,3,2,1,0:T(8,128)(2,1)S(1)} %pad_maximum_fusion.4), channel_id=1, source_target_pairs={{0,16},{16,0},{1,17},{17,1},{2,18},{18,2},{3,19},{19,3},{4,20},{20... | collective-permute-start | bytes 589832 | tf_op jit(solution)/shard_map/ppermute | solution.py:89
  54.2 8.5 %collective-permute-start.17 = (bf16[1,1,3,64,256]{4,3,2,1,0:T(8,128)(2,1)S(1)}, bf16[1,1,3,64,256]{4,3,2,1,0:T(8,128)(2,1)S(1)}, u32[]{:S(2)}, u32[]{:S(2)}) collective-permute-start(bf16[1,1,3,64,256]{4,3,2,1,0:T(8,128)(2,1)S(1)} %slice.88), channel_id=1, source_target_pairs={{0,16},{16,0},{1,17},{17,1},{2,18},{18,2},{3,19},{19,3},{4,20},{20... | collective-permute-start | bytes 294920 | tf_op jit(solution)/shard_map/ppermute | solution.py:94
  56.7 6.1 %copy-start.7 = (bf16[2,2,3,64,256]{4,3,2,1,0:T(8,128)(2,1)S(1)}, bf16[2,2,3,64,256]{4,3,2,1,0:T(8,128)(2,1)}, u32[]{:S(2)}) copy-start(bf16[2,2,3,64,256]{4,3,2,1,0:T(8,128)(2,1)} %copy-done.6) | copy-start | bytes 1179652
  56.7 6.0 %copy-start.9 = (bf16[2,2,3,64,256]{4,3,2,1,0:T(8,128)(2,1)S(1)}, bf16[2,2,3,64,256]{4,3,2,1,0:T(8,128)(2,1)}, u32[]{:S(2)}) copy-start(bf16[2,2,3,64,256]{4,3,2,1,0:T(8,128)(2,1)} %copy-done.8) | copy-start | bytes 1179652
  56.7 6.0 %copy-start.15 = (bf16[2,2,3,64,256]{4,3,2,1,0:T(8,128)(2,1)S(1)}, bf16[2,2,3,64,256]{4,3,2,1,0:T(8,128)(2,1)}, u32[]{:S(2)}) copy-start(bf16[2,2,3,64,256]{4,3,2,1,0:T(8,128)(2,1)} %copy-done.14) | copy-start | bytes 1179652
  56.7 12.6 %collective-permute-start.20 = (bf16[2,1,3,64,256]{4,3,2,1,0:T(8,128)(2,1)S(1)}, bf16[2,1,3,64,256]{4,3,2,1,0:T(8,128)(2,1)S(1)}, u32[]{:S(2)}, u32[]{:S(2)}) collective-permute-start(bf16[2,1,3,64,256]{4,3,2,1,0:T(8,128)(2,1)S(1)} %pad_maximum_fusion.5), channel_id=1, source_target_pairs={{0,16},{16,0},{1,17},{17,1},{2,18},{18,2},{3,19},{19,3},{4,20},{20... | collective-permute-start | bytes 589832 | tf_op jit(solution)/shard_map/ppermute | solution.py:89
  58.9 10.5 %collective-permute-start.18 = (bf16[2,1,3,64,256]{4,3,2,1,0:T(8,128)(2,1)S(1)}, bf16[2,1,3,64,256]{4,3,2,1,0:T(8,128)(2,1)S(1)}, u32[]{:S(2)}, u32[]{:S(2)}) collective-permute-start(bf16[2,1,3,64,256]{4,3,2,1,0:T(8,128)(2,1)S(1)} %collective-permute-done.14.refs_1_), channel_id=1, source_target_pairs={{0,4},{1,5},{4,8},{5,9},{8,12},{9,13},{12,14},{13,15},{14,10},{15,... | collective-permute-start | bytes 589832 | tf_op jit(solution)/shard_map/ppermute | solution.py:79
  58.9 10.4 %collective-permute-start.19 = (bf16[2,1,3,64,256]{4,3,2,1,0:T(8,128)(2,1)S(1)}, bf16[2,1,3,64,256]{4,3,2,1,0:T(8,128)(2,1)S(1)}, u32[]{:S(2)}, u32[]{:S(2)}) collective-permute-start(bf16[2,1,3,64,256]{4,3,2,1,0:T(8,128)(2,1)S(1)} %collective-permute-done.15.refs_2_), channel_id=1, source_target_pairs={{4,0},{5,1},{8,4},{9,5},{12,8},{13,9},{14,12},{15,13},{10,14},{11,... | collective-permute-start | bytes 589832 | tf_op jit(solution)/shard_map/ppermute | solution.py:80
  61.3 8.1 %collective-permute-start.21 = (bf16[3,1,3,64,256]{4,3,2,1,0:T(8,128)(2,1)S(1)}, bf16[3,1,3,64,256]{4,3,2,1,0:T(8,128)(2,1)S(1)}, u32[]{:S(2)}, u32[]{:S(2)}) collective-permute-start(bf16[3,1,3,64,256]{4,3,2,1,0:T(8,128)(2,1)S(1)} %pad_maximum_fusion.3), channel_id=1, source_target_pairs={{0,16},{16,0},{1,17},{17,1},{2,18},{18,2},{3,19},{19,3},{4,20},{20... | collective-permute-start | bytes 884744 | tf_op jit(solution)/shard_map/ppermute | solution.py:100
  69.4 3.9 %copy-start.2 = (bf16[2,1,3,64,256]{4,3,2,1,0:T(8,128)(2,1)}, bf16[2,1,3,64,256]{4,3,2,1,0:T(8,128)(2,1)S(1)}, u32[]{:S(2)}) copy-start(bf16[2,1,3,64,256]{4,3,2,1,0:T(8,128)(2,1)S(1)} %collective-permute-done.20.refs_8_) | copy-start | bytes 589828
  69.4 5.6 %collective-permute-start.22 = (bf16[6,256,256]{2,1,0:T(8,128)(2,1)S(1)}, bf16[6,256,256]{2,1,0:T(8,128)(2,1)S(1)}, u32[]{:S(2)}, u32[]{:S(2)}) collective-permute-start(bf16[6,256,256]{2,1,0:T(8,128)(2,1)S(1)} %get-tuple-element.48.mine), channel_id=1, source_target_pairs={{0,1},{1,0},{2,3},{3,2},{4,5},{5,4},{6,7},{7,6},{8,9},{9,8},{10,11... | collective-permute-start | bytes 2359304 | tf_op jit(solution)/shard_map/ppermute | solution.py:568
  72.9 7.9 %collective-permute-start.25 = (bf16[2,1,3,64,256]{4,3,2,1,0:T(8,128)(2,1)S(1)}, bf16[2,1,3,64,256]{4,3,2,1,0:T(8,128)(2,1)S(1)}, u32[]{:S(2)}, u32[]{:S(2)}) collective-permute-start(bf16[2,1,3,64,256]{4,3,2,1,0:T(8,128)(2,1)S(1)} %pad_maximum_fusion.6), channel_id=1, source_target_pairs={{0,16},{16,0},{1,17},{17,1},{2,18},{18,2},{3,19},{19,3},{4,20},{20... | collective-permute-start | bytes 589832 | tf_op jit(solution)/shard_map/ppermute | solution.py:89
  73.3 8.2 %collective-permute-start.23 = (bf16[2,1,3,64,256]{4,3,2,1,0:T(8,128)(2,1)S(1)}, bf16[2,1,3,64,256]{4,3,2,1,0:T(8,128)(2,1)S(1)}, u32[]{:S(2)}, u32[]{:S(2)}) collective-permute-start(bf16[2,1,3,64,256]{4,3,2,1,0:T(8,128)(2,1)S(1)} %collective-permute-done.18.refs_3_), channel_id=1, source_target_pairs={{0,4},{1,5},{4,8},{5,9},{8,12},{9,13},{12,14},{13,15},{14,10},{15,... | collective-permute-start | bytes 589832 | tf_op jit(solution)/shard_map/ppermute | solution.py:79
  75.0 6.5 %collective-permute-start.24 = (bf16[2,1,3,64,256]{4,3,2,1,0:T(8,128)(2,1)S(1)}, bf16[2,1,3,64,256]{4,3,2,1,0:T(8,128)(2,1)S(1)}, u32[]{:S(2)}, u32[]{:S(2)}) collective-permute-start(bf16[2,1,3,64,256]{4,3,2,1,0:T(8,128)(2,1)S(1)} %collective-permute-done.19.refs_4_), channel_id=1, source_target_pairs={{4,0},{5,1},{8,4},{9,5},{12,8},{13,9},{14,12},{15,13},{10,14},{11,... | collective-permute-start | bytes 589832 | tf_op jit(solution)/shard_map/ppermute | solution.py:80
  81.5 7.6 %copy-start = (bf16[2,1,3,64,256]{4,3,2,1,0:T(8,128)(2,1)}, bf16[2,1,3,64,256]{4,3,2,1,0:T(8,128)(2,1)S(1)}, u32[]{:S(2)}) copy-start(bf16[2,1,3,64,256]{4,3,2,1,0:T(8,128)(2,1)S(1)} %collective-permute-done.24.refs_6_) | copy-start | bytes 589828
  81.5 20.8 %all-to-all-start = ((bf16[16,4,16,256]{3,2,1,0:T(8,128)(2,1)}), bf16[16,4,16,256]{3,2,1,0:T(8,128)(2,1)}, u32[]{:S(2)}, u32[]{:S(2)}) async-start(bf16[16,4,16,256]{3,2,1,0:T(8,128)(2,1)} %second_conv.1), calls=%async_computation | async-start | bytes 1048576 | tf_op jit(solution)/shard_map/all_to_all | solution.py:589
  88.1 6.3 %collective-permute-start.26 = (bf16[2,1,3,64,256]{4,3,2,1,0:T(8,128)(2,1)S(1)}, bf16[2,1,3,64,256]{4,3,2,1,0:T(8,128)(2,1)S(1)}, u32[]{:S(2)}, u32[]{:S(2)}) collective-permute-start(bf16[2,1,3,64,256]{4,3,2,1,0:T(8,128)(2,1)S(1)} %pad_maximum_fusion.7), channel_id=1, source_target_pairs={{0,16},{16,0},{1,17},{17,1},{2,18},{18,2},{3,19},{19,3},{4,20},{20... | collective-permute-start | bytes 589832 | tf_op jit(solution)/shard_map/ppermute | solution.py:89
  98.9 24.9 %collective-permute-start.28 = (bf16[3,3,512,256]{3,2,1,0:T(8,128)(2,1)S(1)}, bf16[3,3,512,256]{3,2,1,0:T(8,128)(2,1)}, u32[]{:S(2)}, u32[]{:S(2)}) collective-permute-start(bf16[3,3,512,256]{3,2,1,0:T(8,128)(2,1)S(1)} %assemble.1.mine), channel_id=1, source_target_pairs={{0,1},{1,0},{2,3},{3,2},{4,5},{5,4},{6,7},{7,6},{8,9},{9,8},{10,11... | collective-permute-start | bytes 7077896 | tf_op jit(solution)/shard_map/ppermute | solution.py:594
  102.3 9.6 %collective-permute-start.27 = (bf16[2,1,3,64,256]{4,3,2,1,0:T(8,128)(2,1)S(1)}, bf16[2,1,3,64,256]{4,3,2,1,0:T(8,128)(2,1)S(1)}, u32[]{:S(2)}, u32[]{:S(2)}) collective-permute-start(bf16[2,1,3,64,256]{4,3,2,1,0:T(8,128)(2,1)S(1)} %collective-permute-done.23.refs_5_), channel_id=1, source_target_pairs={{0,4},{1,5},{4,8},{5,9},{8,12},{9,13},{12,14},{13,15},{14,10},{15,... | collective-permute-start | bytes 589832 | tf_op jit(solution)/shard_map/ppermute | solution.py:77
  111.9 24.3 %all-to-all-start.1 = ((bf16[16,48,512]{2,1,0:T(8,128)(2,1)}), bf16[16,48,512]{2,1,0:T(8,128)(2,1)S(1)}, u32[]{:S(2)}, u32[]{:S(2)}) async-start(bf16[16,48,512]{2,1,0:T(8,128)(2,1)} %windows.1), calls=%async_computation.1 | async-start | bytes 1572864 | tf_op jit(solution)/shard_map/all_to_all | solution.py:609
  116.7 6.4 %collective-permute-start.30 = (bf16[2,1,3,64,256]{4,3,2,1,0:T(8,128)(2,1)S(1)}, bf16[2,1,3,64,256]{4,3,2,1,0:T(8,128)(2,1)S(1)}, u32[]{:S(2)}, u32[]{:S(2)}) collective-permute-start(bf16[2,1,3,64,256]{4,3,2,1,0:T(8,128)(2,1)S(1)} %collective-permute-done.27.refs_0_), channel_id=1, source_target_pairs={{0,1},{1,0},{2,3},{3,2},{4,5},{5,4},{6,7},{7,6},{8,9},{9,8},{10,11... | collective-permute-start | bytes 589832 | tf_op jit(solution)/shard_map/ppermute | solution.py:624
  117.1 4.2 %collective-permute-start.29 = (bf16[1,1,3,64,256]{4,3,2,1,0:T(8,128)(2,1)S(1)}, bf16[1,1,3,64,256]{4,3,2,1,0:T(8,128)(2,1)S(1)}, u32[]{:S(2)}, u32[]{:S(2)}) collective-permute-start(bf16[1,1,3,64,256]{4,3,2,1,0:T(8,128)(2,1)S(1)} %slice.99), channel_id=1, source_target_pairs={{0,16},{16,0},{1,17},{17,1},{2,18},{18,2},{3,19},{19,3},{4,20},{20... | collective-permute-start | bytes 294920 | tf_op jit(solution)/shard_map/ppermute | solution.py:94
  121.3 1.9 %collective-permute-start.31 = (bf16[1,1,3,64,256]{4,3,2,1,0:T(8,128)(2,1)S(1)}, bf16[1,1,3,64,256]{4,3,2,1,0:T(8,128)(2,1)S(1)}, u32[]{:S(2)}, u32[]{:S(2)}) collective-permute-start(bf16[1,1,3,64,256]{4,3,2,1,0:T(8,128)(2,1)S(1)} %collective-permute-done.29.refs_1_), channel_id=1, source_target_pairs={{0,1},{1,0},{2,3},{3,2},{4,5},{5,4},{6,7},{7,6},{8,9},{9,8},{10,11... | collective-permute-start | bytes 294920 | tf_op jit(solution)/shard_map/ppermute | solution.py:624
  (8 other events, 6.5 us)
